TPU v7x, 32 devices: a whole 2x2x4 slice. The times are simulated.
32 devices in a mesh: grp: 2 (over x), dp: 8 (over z, y), tp: 2 (over core).
Axes of the slice: x: 2, y: 2, z: 4, core: 2. Of those that a mesh axis runs over, the one named last changes fastest.
Arguments:
- tokens: bfloat16 [8192, 8192], P(('grp', 'dp'), 'tp'), parts along dimension 0, may hold values from -5 to 7
- norm_gain: bfloat16 [8192], P('tp'), may hold values from 0.6 to 8
- lengths: int32 [16], P('grp'), parts along dimension 0, may hold values from 1 to 1536, 4096 in all
- w_query: bfloat16 [8192, 1024], P(None, 'tp'), may hold values from -0.049939416 to 0.049939416
- w_key: bfloat16 [8192, 128], replicated, may hold values from -0.049939416 to 0.049939416
- w_value: bfloat16 [8192, 128], replicated, may hold values from -0.0625 to 0.0625
- w_out: bfloat16 [1024, 8192], P('tp'), may hold values from -0.1875 to 0.1875
Outputs:
- mixed: bfloat16 [8192, 8192], P(('grp', 'dp'), 'tp'), parts along dimension 0
There are 2 independent parts, one for each index of `grp`. A program takes and returns all parts, laid end to end along the dimension named above; an argument that names none is the same for every part. Nothing has to cross between parts.
All inputs are finite; a program needn't handle non-finite values.
Results may differ from a plain program's by a relative error of at most 0.012.
The roundings to bfloat16 on the way count: a program that leaves them out, or rounds other values in their place, can miss the bound.
Values may be sent and summed in bfloat16 or wider, within the bound.
No kernel may reach another device: no remote copies, remote signals or barrier semaphores. Data moves between devices by JAX's collectives and lax.ppermute only.
A program may use at most 128 MiB of HBM per device.

v0:
```python
import functools
import math

import jax
import jax.numpy as jnp
from jax import lax
from jax.experimental import pallas as pl
from jax.experimental.pallas import tpu as pltpu
from jax.sharding import PartitionSpec as P

HEAD = 128
MOST = 1536
LANES = 128
SWAP = [(0, 1), (1, 0)]
MIB = 1024 * 1024
EXP2_SCALE = math.log2(math.e) / HEAD**0.5


def in_hbm(*arrays):
    return [pltpu.with_memory_space_constraint(array, pltpu.HBM) for array in arrays]


def params(mib):
    return pltpu.CompilerParams(vmem_limit_bytes=mib * MIB)


SCALAR = pl.BlockSpec(memory_space=pltpu.SMEM)
WHOLE = pl.BlockSpec(memory_space=pltpu.VMEM)


def prepare_kernel(gain_ref, tokens_hbm, wk_hbm, wv_hbm, wq_hbm, sums_ref, tokens_ref, wkv_ref, wq_ref, sems):
    rows, width = tokens_ref.shape
    step = 1024
    chunks = width // step
    loads = [
        pltpu.make_async_copy(tokens_hbm.at[:, c * step : (c + 1) * step], tokens_ref.at[:, c * step : (c + 1) * step], sems.at[c])
        for c in range(chunks)
    ]
    loads += [
        pltpu.make_async_copy(wk_hbm, wkv_ref.at[:, :HEAD], sems.at[chunks]),
        pltpu.make_async_copy(wv_hbm, wkv_ref.at[:, HEAD:], sems.at[chunks + 1]),
        pltpu.make_async_copy(wq_hbm, wq_ref, sems.at[chunks + 2]),
    ]
    for load in loads:
        load.start()
    sums_ref[rows:, :] = gain_ref[...].astype(jnp.float32)
    for c in range(chunks):
        loads[c].wait()
        total = sums_ref[0:rows, :] if c else jnp.zeros((rows, LANES), jnp.float32)
        for j in range(c * step // LANES, (c + 1) * step // LANES):
            wide = tokens_ref[:, j * LANES : (j + 1) * LANES].astype(jnp.float32)
            total = total + wide * wide
        sums_ref[0:rows, :] = total
    for load in loads[chunks:]:
        load.wait()


def prepare(tokens, gain, wk, wv, wq):
    rows, width = tokens.shape
    gain_rows = gain.shape[0]
    hbm = pl.BlockSpec(memory_space=pltpu.HBM)
    return pl.pallas_call(
        prepare_kernel,
        in_specs=[WHOLE] + [hbm] * 4,
        out_specs=[WHOLE] * 4,
        out_shape=[
            jax.ShapeDtypeStruct((rows + gain_rows, LANES), jnp.float32),
            jax.ShapeDtypeStruct(tokens.shape, tokens.dtype),
            jax.ShapeDtypeStruct((wk.shape[0], 2 * HEAD), wk.dtype),
            jax.ShapeDtypeStruct(wq.shape, wq.dtype),
        ],
        scratch_shapes=[pltpu.SemaphoreType.DMA((width // 1024 + 3,))],
        compiler_params=params(8),
        cost_estimate=pl.CostEstimate(flops=rows * width * 2, bytes_accessed=16 * MIB, transcendentals=0),
        name="prepare",
    )(gain, *in_hbm(tokens, wk, wv, wq))


def inverse_norm(mine, other, model):
    mean = jnp.sum(mine + other, axis=1, keepdims=True) * (1.0 / model)
    return jnp.broadcast_to(lax.rsqrt(mean + 1e-05), mine.shape)


def normalize(block, inverse, gains_ref, gain_row):
    parts = []
    for j in range(block.shape[1] // LANES):
        wide = block[:, j * LANES : (j + 1) * LANES].astype(jnp.float32)
        gain = gains_ref[gain_row + j : gain_row + j + 1, :]
        parts.append((wide * inverse * gain).astype(jnp.bfloat16))
    return jnp.concatenate(parts, axis=1)


def turn(x, cosine, sine):
    return (x * cosine + pltpu.roll(x, HEAD // 2, 1) * sine).astype(jnp.bfloat16)


def keys_kernel(
    half_ref, mine_ref, other_ref, smine_ref, sother_ref, cos_ref, sin_ref, wkv_ref, wout_ref, kv_ref, wsend_ref, sem
):
    rows, width = mine_ref.shape
    part_rows = rows // 2
    step = 1024
    me = half_ref[0]
    send_start = pl.multiple_of((1 - me) * width, width)
    send = pltpu.make_async_copy(wout_ref.at[:, pl.ds(send_start, width)], wsend_ref, sem)
    send.start()
    here = pl.ds(pl.multiple_of(me * part_rows, part_rows), part_rows)
    inverse = inverse_norm(smine_ref[here, :], sother_ref[here, :], 2 * width)
    total = jnp.zeros((part_rows, 2 * HEAD), jnp.float32)
    for part in range(2):
        tokens_ref, sums_ref = ((mine_ref, smine_ref), (other_ref, sother_ref))[part]
        base = (me if part == 0 else 1 - me) * width
        for c in range(width // step):
            block = tokens_ref[here, c * step : (c + 1) * step]
            normed = normalize(block, inverse, sums_ref, rows + c * (step // LANES))
            depth = pl.ds(pl.multiple_of(base + c * step, step), step)
            total = total + jnp.dot(normed, wkv_ref[depth, :], preferred_element_type=jnp.float32)
    kv_ref[:, :HEAD] = turn(total[:, :HEAD], cos_ref[here, :], sin_ref[here, :])
    kv_ref[:, HEAD:] = total[:, HEAD:].astype(jnp.bfloat16)
    send.wait()


def keys_values(half, tokens, tokens_other, sums, sums_other, tables, wkv, w_out):
    rows, width = tokens.shape
    part = rows // 2
    hbm = pl.BlockSpec(memory_space=pltpu.HBM)
    return pl.pallas_call(
        keys_kernel,
        in_specs=[SCALAR] + [WHOLE] * 7 + [hbm],
        out_specs=[WHOLE, WHOLE],
        out_shape=[
            jax.ShapeDtypeStruct((part, 2 * HEAD), jnp.bfloat16),
            jax.ShapeDtypeStruct((w_out.shape[0], width), w_out.dtype),
        ],
        scratch_shapes=[pltpu.SemaphoreType.DMA],
        compiler_params=params(8),
        cost_estimate=pl.CostEstimate(
            flops=4 * rows * width * HEAD * 2, bytes_accessed=rows * width * 2, transcendentals=0
        ),
        name="keys_values",
    )(half, tokens, tokens_other, sums, sums_other, *tables, wkv, *in_hbm(w_out))


def queries_kernel(half_ref, mine_ref, other_ref, smine_ref, sother_ref, cos_ref, sin_ref, wq_ref, wout_ref, q_ref, wkeep_ref, acc, sem):
    rows, width = mine_ref.shape
    step = 1024
    me = half_ref[0]
    keep = pltpu.make_async_copy(wout_ref.at[:, pl.ds(pl.multiple_of(me * width, width), width)], wkeep_ref, sem)
    keep.start()
    inverse = inverse_norm(smine_ref[0:rows, :], sother_ref[0:rows, :], 2 * width)
    for part in range(2):
        tokens_ref, sums_ref = ((mine_ref, smine_ref), (other_ref, sother_ref))[part]
        base = (me if part == 0 else 1 - me) * width
        for c in range(width // step):
            normed = normalize(tokens_ref[:, c * step : (c + 1) * step], inverse, sums_ref, rows + c * (step // LANES))
            depth = pl.ds(pl.multiple_of(base + c * step, step), step)
            term = jnp.dot(normed, wq_ref[depth, :], preferred_element_type=jnp.float32)
            if part == 0 and c == 0:
                acc[...] = term
            else:
                acc[...] += term
    for h in range(q_ref.shape[1] // HEAD):
        lanes = slice(h * HEAD, (h + 1) * HEAD)
        q_ref[:, lanes] = turn(acc[:, lanes], cos_ref[...], sin_ref[...])
    keep.wait()


def project_queries(half, tokens, tokens_other, sums, sums_other, tables, wq, w_out):
    rows, width = tokens.shape
    nq = wq.shape[1]
    return pl.pallas_call(
        queries_kernel,
        in_specs=[SCALAR] + [WHOLE] * 7 + [pl.BlockSpec(memory_space=pltpu.HBM)],
        out_specs=[WHOLE, WHOLE],
        out_shape=[
            jax.ShapeDtypeStruct((rows, nq), jnp.bfloat16),
            jax.ShapeDtypeStruct((w_out.shape[0], width), w_out.dtype),
        ],
        scratch_shapes=[pltpu.VMEM((rows, nq), jnp.float32), pltpu.SemaphoreType.DMA],
        compiler_params=params(8),
        cost_estimate=pl.CostEstimate(flops=4 * rows * width * nq, bytes_accessed=rows * width * 4, transcendentals=0),
        name="queries",
    )(half, tokens, tokens_other, sums, sums_other, *tables, wq, *in_hbm(w_out))


def attend_kernel(reach, half_ref, starts_ref, q_ref, *rest):
    blocks = rest[: 2 * (reach + 1)]
    ctx_ref, keys, values, scores, acc, tops, sums = rest[2 * (reach + 1) :]
    rows = q_ref.shape[0]
    tile_rows = ctx_ref.shape[0]
    heads = q_ref.shape[1] // HEAD
    span = scores.shape[2]
    t = pl.program_id(0)

    @pl.when(t == 0)
    def _():
        part = rows // 2
        for b, block in enumerate(blocks):
            which = half_ref[0] if b % 2 == 0 else 1 - half_ref[0]
            at = pl.ds(pl.multiple_of((b // 2) * rows + which * part, part), part)
            keys[at, :] = block[:, :HEAD]
            values[at, :] = block[:, HEAD:]

    first_row = reach * rows + t * tile_rows
    row = first_row + lax.broadcasted_iota(jnp.int32, (tile_rows, span), 0)
    begin = jnp.zeros((tile_rows, span), jnp.int32)
    lowest = jnp.int32(0)
    for d in range(starts_ref.shape[0]):
        start = starts_ref[d]
        begin = jnp.where(row >= start, jnp.maximum(begin, start), begin)
        lowest = jnp.where(first_row >= start, jnp.maximum(lowest, start), lowest)
    lane = lax.broadcasted_iota(jnp.int32, (tile_rows, span), 1)
    low = lowest // span
    high = (first_row + tile_rows - 1) // span + 1
    q_rows = pl.ds(pl.multiple_of(t * tile_rows, tile_rows), tile_rows)

    tops[...] = jnp.full(tops.shape, -1e30, jnp.float32)
    sums[...] = jnp.zeros(sums.shape, jnp.float32)
    acc[...] = jnp.zeros(acc.shape, jnp.float32)

    def score(i, carry):
        place = lane + i * span
        allowed = (place >= begin) & (place <= row)
        block_keys = keys[pl.ds(pl.multiple_of(i * span, span), span), :]
        for h in range(heads):
            s = lax.dot_general(
                q_ref[q_rows, h * HEAD : (h + 1) * HEAD],
                block_keys,
                (((1,), (1,)), ((), ())),
                preferred_element_type=jnp.float32,
            )
            s = jnp.where(allowed, s, -1e30)
            scores[i, h * tile_rows : (h + 1) * tile_rows, :] = s
            top = tops[h * tile_rows : (h + 1) * tile_rows, :]
            for j in range(span // LANES):
                top = jnp.maximum(top, s[:, j * LANES : (j + 1) * LANES])
            tops[h * tile_rows : (h + 1) * tile_rows, :] = top
        return carry

    lax.fori_loop(low, high, score, 0)
    top = jnp.max(tops[...], axis=1, keepdims=True)
    tops[...] = jnp.broadcast_to(top * EXP2_SCALE, tops.shape)

    def weigh(i, carry):
        block_values = values[pl.ds(pl.multiple_of(i * span, span), span), :]
        for h in range(heads):
            part = slice(h * tile_rows, (h + 1) * tile_rows)
            top = tops[part, :]
            total = sums[part, :]
            rounded = []
            for j in range(span // LANES):
                w = jnp.exp2(scores[i, part, j * LANES : (j + 1) * LANES] * EXP2_SCALE - top)
                total = total + w
                rounded.append(w.astype(jnp.bfloat16))
            sums[part, :] = total
            acc[part, :] += jnp.dot(
                jnp.concatenate(rounded, axis=1), block_values, preferred_element_type=jnp.float32
            )
        return carry

    lax.fori_loop(low, high, weigh, 0)
    for h in range(heads):
        part = slice(h * tile_rows, (h + 1) * tile_rows)
        total = jnp.sum(sums[part, :], axis=1, keepdims=True)
        ctx_ref[:, h * HEAD : (h + 1) * HEAD] = (acc[part, :] / total).astype(jnp.bfloat16)


def attend(half, starts, queries, blocks):
    rows, width = queries.shape
    reach = len(blocks) // 2 - 1
    tile_rows, span = 128, 256
    heads = width // HEAD
    places = (reach + 1) * rows
    whole = lambda t, s, u: (0, 0)
    return pl.pallas_call(
        functools.partial(attend_kernel, reach),
        grid_spec=pltpu.PrefetchScalarGridSpec(
            num_scalar_prefetch=2,
            grid=(rows // tile_rows,),
            in_specs=[pl.BlockSpec((rows, width), whole)] + [pl.BlockSpec((rows // 2, 2 * HEAD), whole)] * len(blocks),
            out_specs=pl.BlockSpec((tile_rows, width), lambda t, s, u: (t, 0)),
            scratch_shapes=[
                pltpu.VMEM((places, HEAD), jnp.bfloat16),
                pltpu.VMEM((places, HEAD), jnp.bfloat16),
                pltpu.VMEM((places // span, heads * tile_rows, span), jnp.float32),
                pltpu.VMEM((heads * tile_rows, HEAD), jnp.float32),
                pltpu.VMEM((heads * tile_rows, LANES), jnp.float32),
                pltpu.VMEM((heads * tile_rows, LANES), jnp.float32),
            ],
        ),
        out_shape=jax.ShapeDtypeStruct((rows, width), jnp.bfloat16),
        compiler_params=params(16),
        cost_estimate=pl.CostEstimate(
            flops=4 * rows * width * places, bytes_accessed=rows * width * 8, transcendentals=rows * heads * places
        ),
        name="attend",
    )(half, starts, queries, *blocks)


def output_kernel(tokens_ref, mine_ref, other_ref, w_mine_ref, w_other_ref, out_ref):
    step = out_ref.shape[1]
    here = pl.ds(pl.multiple_of(pl.program_id(0) * step, step), step)
    mine = jnp.dot(mine_ref[...], w_mine_ref[:, here], preferred_element_type=jnp.float32).astype(jnp.bfloat16)
    other = jnp.dot(other_ref[...], w_other_ref[:, here], preferred_element_type=jnp.float32).astype(jnp.bfloat16)
    out = tokens_ref[:, here].astype(jnp.float32) + mine.astype(jnp.float32) + other.astype(jnp.float32)
    out_ref[...] = out.astype(jnp.bfloat16)


def output(tokens, mine, other, w_mine, w_other):
    rows, width = tokens.shape
    depth = mine.shape[1]
    step = 512
    return pl.pallas_call(
        output_kernel,
        grid=(width // step,),
        in_specs=[WHOLE] * 5,
        out_specs=pl.BlockSpec((rows, step), lambda j: (0, j)),
        out_shape=jax.ShapeDtypeStruct((rows, width), jnp.bfloat16),
        compiler_params=params(16),
        cost_estimate=pl.CostEstimate(
            flops=4 * rows * width * depth, bytes_accessed=(4 * rows + 4 * depth) * width, transcendentals=0
        ),
        name="output",
    )(tokens, mine, other, w_mine, w_other)


def shift(value, axis, steps):
    count = lax.axis_size(axis)
    return lax.ppermute(value, axis, [(source, source + steps) for source in range(count - steps)])


def rotary_tables(lengths, places):
    doc_ends = jnp.cumsum(lengths)
    first_rows = jnp.max(jnp.where(places[:, None] >= doc_ends[None, :], doc_ends[None, :], 0), axis=1)
    within = places - first_rows
    half = HEAD // 2
    frequency = 500000.0 ** (-jnp.arange(half, dtype=jnp.float32) * 2.0 / HEAD)
    frequency = jnp.concatenate([frequency, frequency])
    angles = within.astype(jnp.float32)[:, None] * frequency[None, :]
    sign = jnp.where(jnp.arange(HEAD) < half, -1.0, 1.0)
    return jnp.cos(angles), jnp.sin(angles) * sign[None, :]


def local(tokens, norm_gain, lengths, w_query, w_key, w_value, w_out):
    rows, width = tokens.shape
    me = lax.axis_index("tp")
    mine_half = me[None].astype(jnp.int32)
    first_here = lax.axis_index("dp") * rows
    reach = (rows + MOST - 2) // rows

    tokens_other = lax.ppermute(tokens, "tp", SWAP)
    sums, tokens, wkv, wq = prepare(tokens, norm_gain.reshape(-1, LANES), w_key, w_value, w_query)
    sums_other = lax.ppermute(sums, "tp", SWAP)
    tables = rotary_tables(lengths, first_here + jnp.arange(rows, dtype=jnp.int32))

    kv, w_send = keys_values(mine_half, tokens, tokens_other, sums, sums_other, tables, wkv, w_out)
    parts = [shift(kv, "dp", d) for d in range(reach, 0, -1)]
    own_other = lax.ppermute(kv, "tp", SWAP)
    w_other = lax.ppermute(w_send, "tp", SWAP)
    queries, w_mine = project_queries(mine_half, tokens, tokens_other, sums, sums_other, tables, wq, w_out)
    parts, queries = lax.optimization_barrier((parts, queries))
    blocks = []
    for part in parts:
        blocks += [part, lax.ppermute(part, "tp", SWAP)]
    blocks += [kv, own_other]
    starts = jnp.cumsum(lengths) - lengths - first_here + reach * rows
    context = attend(mine_half, starts.astype(jnp.int32), queries, blocks)
    context_other = lax.ppermute(context, "tp", SWAP)
    return output(tokens, context, context_other, w_mine, w_other)


def solution(mesh):
    placed = (P(("grp", "dp"), "tp"), P("tp"), P("grp"), P(None, "tp"), P(), P(), P("tp", None))
    return jax.shard_map(
        local, mesh=mesh, in_specs=placed, out_specs=P(("grp", "dp"), "tp"), check_vma=False
    )
```

profile of v0, /device:TPU:9, one launch (start us, length us, event | category | flops | bytes accessed | tf_op | source)
XLA Modules:
  0.0 68.4 jit_solution(968980147026456680)
XLA Ops:
  0.0 0.7 collective-permute-start
  0.7 0.7 %copy-done.7 = bf16[4096]{0:T(1024)(128)(2,1)S(1)} copy-done((bf16[4096]{0:T(1024)(128)(2,1)S(1)}, bf16[4096]{0:T(1024)(128)(2,1)}, u32[]{:S(2)}) %copy-start.7) | copy-done | bytes 8216
  1.4 6.0 %prepare.1 = (f32[544,128]{1,0:T(8,128)S(1)}, bf16[512,4096]{1,0:T(8,128)(2,1)S(1)}, bf16[8192,256]{1,0:T(8,128)(2,1)S(1)}, bf16[8192,512]{1,0:T(8,128)(2,1)S(1)}) custom-call(bf16[32,128]{1,0:T(8,128)(2,1)S(1)} %bitcast.5, bf16[512,4096]{1,0:T(8,128)(2,1)} %tokens_hbm.1, bf16[8192,128]{1,0:T(8,128)(2,1)} %wk_hbm.1, bf16[8192,128]{1,0:T(8,128)(2,1)} %wv_hbm.1, ...), custom_call_target="tpu_custom_call" | custom-call | flops 4194304 | bytes 16777216 | tf_op jit(solution)/shard_map/prepare/pallas_call | solution.py:62
  7.4 2.0 %copy-done = bf16[512,4096]{1,0:T(8,128)(2,1)} copy-done((bf16[512,4096]{1,0:T(8,128)(2,1)}, bf16[512,4096]{1,0:T(8,128)(2,1)S(1)}, u32[]{:S(2)}) %copy-start) | copy-done | bytes 4194328
  9.4 3.2 %copy-done.3 = bf16[8192,512]{1,0:T(8,128)(2,1)} copy-done((bf16[8192,512]{1,0:T(8,128)(2,1)}, bf16[8192,512]{1,0:T(8,128)(2,1)S(1)}, u32[]{:S(2)}) %copy-start.3) | copy-done | bytes 8388632
  12.6 1.9 %copy-done.5 = bf16[8192,256]{1,0:T(8,128)(2,1)} copy-done((bf16[8192,256]{1,0:T(8,128)(2,1)}, bf16[8192,256]{1,0:T(8,128)(2,1)S(1)}, u32[]{:S(2)}) %copy-start.5) | copy-done | bytes 4194328
  14.9 1.0 %fusion = (f32[512,128]{1,0:T(8,128)S(1)}, f32[512,128]{1,0:T(8,128)S(1)}) fusion(f32[128]{0:T(128)S(1)} %get-tuple-element.31, f32[128]{0:T(128)S(1)} %get-tuple-element.32, f32[512]{0:T(512)S(1)} %subtract_convert_fusion), kind=kLoop, calls=%fused_computation.2 | loop fusion | flops 131072 | bytes 527360 | tf_op jit(solution)/shard_map/mul | solution.py:341
  16.1 2.2 %copy-done.1 = bf16[512,4096]{1,0:T(8,128)(2,1)S(1)} copy-done((bf16[512,4096]{1,0:T(8,128)(2,1)S(1)}, bf16[512,4096]{1,0:T(8,128)(2,1)}, u32[]{:S(2)}) %copy-start.1) | copy-done | bytes 4194328
  18.3 2.2 %copy-done.6 = bf16[8192,256]{1,0:T(8,128)(2,1)S(1)} copy-done((bf16[8192,256]{1,0:T(8,128)(2,1)S(1)}, bf16[8192,256]{1,0:T(8,128)(2,1)}, u32[]{:S(2)}) %copy-start.6) | copy-done | bytes 4194328
  20.5 5.8 %keys_values.1 = (bf16[256,256]{1,0:T(8,128)(2,1)S(1)}, bf16[512,4096]{1,0:T(8,128)(2,1)S(1)}) custom-call(s32[1]{0:T(128)} %bitcast.1.half_ref, bf16[512,4096]{1,0:T(8,128)(2,1)S(1)} %copy-done.1, bf16[512,4096]{1,0:T(8,128)(2,1)} %collective-permute-done.other_ref, f32[544,128]{1,0:T(8,128)S(1)} %get-tuple-element.18.smine_ref, ...), custom_call_target="tpu_custom_call" | custom-call | flops 2147483648 | bytes 4194304 | tf_op jit(solution)/shard_map/keys_values/pallas_call | solution.py:127
  26.3 0.4 collective-permute-start.10
  26.9 3.1 %collective-permute-start.4 = (bf16[256,256]{1,0:T(8,128)(2,1)S(1)}, bf16[256,256]{1,0:T(8,128)(2,1)S(1)}, u32[]{:S(2)}, u32[]{:S(2)}) collective-permute-start(bf16[256,256]{1,0:T(8,128)(2,1)S(1)} %get-tuple-element.20.rest_6_), channel_id=1, source_target_pairs={{0,2},{2,4},{4,6},{6,8},{8,10},{10,12},{12,14},{1,3},{3,5},{5,7},{... | collective-permute-start | bytes 393224 | tf_op jit(solution)/shard_map/ppermute | solution.py:329
  30.0 3.2 %collective-permute-start.3 = (bf16[256,256]{1,0:T(8,128)(2,1)S(1)}, bf16[256,256]{1,0:T(8,128)(2,1)S(1)}, u32[]{:S(2)}, u32[]{:S(2)}) collective-permute-start(bf16[256,256]{1,0:T(8,128)(2,1)S(1)} %get-tuple-element.20.rest_6_), channel_id=1, source_target_pairs={{0,4},{2,6},{4,8},{6,10},{8,12},{10,14},{1,5},{3,7},{5,9},{7,11},{... | collective-permute-start | bytes 393224 | tf_op jit(solution)/shard_map/ppermute | solution.py:329
  33.2 2.9 %collective-permute-start.2 = (bf16[256,256]{1,0:T(8,128)(2,1)S(1)}, bf16[256,256]{1,0:T(8,128)(2,1)S(1)}, u32[]{:S(2)}, u32[]{:S(2)}) collective-permute-start(bf16[256,256]{1,0:T(8,128)(2,1)S(1)} %get-tuple-element.20.rest_6_), channel_id=1, source_target_pairs={{0,6},{2,8},{4,10},{6,12},{8,14},{1,7},{3,9},{5,11},{7,13},{9,15},... | collective-permute-start | bytes 393224 | tf_op jit(solution)/shard_map/ppermute | solution.py:329
  36.1 8.1 %queries.1 = (bf16[512,512]{1,0:T(8,128)(2,1)S(1)}, bf16[512,4096]{1,0:T(8,128)(2,1)S(1)}) custom-call(s32[1]{0:T(128)} %bitcast.1.half_ref, bf16[512,4096]{1,0:T(8,128)(2,1)S(1)} %copy-done.1, bf16[512,4096]{1,0:T(8,128)(2,1)} %collective-permute-done.other_ref, f32[544,128]{1,0:T(8,128)S(1)} %get-tuple-element.18.smine_ref, ...), custom_call_target="tpu_custom_call" | custom-call | flops 4294967296 | bytes 8388608 | tf_op jit(solution)/shard_map/queries/pallas_call | solution.py:171
  44.3 1.0 %collective-permute-start.5 = (bf16[256,256]{1,0:T(8,128)(2,1)S(1)}, bf16[256,256]{1,0:T(8,128)(2,1)S(1)}, u32[]{:S(2)}, u32[]{:S(2)}) collective-permute-start(bf16[256,256]{1,0:T(8,128)(2,1)S(1)} %collective-permute-done.2.rest_0_), channel_id=1, source_target_pairs={{0,1},{1,0},{2,3},{3,2},{4,5},{5,4},{6,7},{7,6},{8,9},{9,8},{10,11... | collective-permute-start | bytes 393224 | tf_op jit(solution)/shard_map/ppermute | solution.py:364
  45.4 0.4 collective-permute-start.7
  45.8 0.5 collective-permute-done.5.rest_1_
  46.3 0.4 collective-permute-done.6.rest_3_
  46.6 0.2 collective-permute-done.7.rest_5_
  46.8 12.7 %attend.1.mine_ref = bf16[512,512]{1,0:T(8,128)(2,1)S(1)} custom-call(s32[1]{0:T(128)} %bitcast.1.half_ref, s32[8]{0:T(128)S(1)} %subtract_add_fusion.starts_ref, bf16[512,512]{1,0:T(8,128)(2,1)S(1)} %get-tuple-element.23.q_ref, bf16[256,256]{1,0:T(8,128)(2,1)S(1)} %collective-permute-done.2.rest_0_, bf16[256,256]{1,0:T(8,128)(2,1)S(1)} %collective-permute-done.5.rest_1_, ...), custom_call_target="tpu_custom_call" | custom-call | flops 2147483648 | bytes 2097152 | tf_op jit(solution)/shard_map/attend/pallas_call | solution.py:275
  59.5 0.4 collective-permute-start.9
  59.9 1.6 %collective-permute-done.9.other_ref = bf16[512,512]{1,0:T(8,128)(2,1)S(1)} collective-permute-done((bf16[512,512]{1,0:T(8,128)(2,1)S(1)}, bf16[512,512]{1,0:T(8,128)(2,1)S(1)}, u32[]{:S(2)}, u32[]{:S(2)}) %collective-permute-start.9) | collective-permute-done | bytes 524320 | tf_op jit(solution)/shard_map/ppermute | solution.py:368
  61.5 6.9 %output.1 = bf16[512,4096]{1,0:T(8,128)(2,1)} custom-call(bf16[512,4096]{1,0:T(8,128)(2,1)S(1)} %copy-done.2, bf16[512,512]{1,0:T(8,128)(2,1)S(1)} %attend.1.mine_ref, bf16[512,512]{1,0:T(8,128)(2,1)S(1)} %collective-permute-done.9.other_ref, bf16[512,4096]{1,0:T(8,128)(2,1)S(1)} %get-tuple-element.27.w_mine_ref, ...), custom_call_target="tpu_custom_call" | custom-call | flops 4294967296 | bytes 16777216 | tf_op jit(solution)/shard_map/output/pallas_call | solution.py:313
  (29 shorter events, 0.8 us)
Async XLA Ops:
  0.0 16.1 %collective-permute-start = (bf16[512,4096]{1,0:T(8,128)(2,1)}, bf16[512,4096]{1,0:T(8,128)(2,1)}, u32[]{:S(2)}, u32[]{:S(2)}) collective-permute-start(bf16[512,4096]{1,0:T(8,128)(2,1)} %tokens_hbm.1), channel_id=1, source_target_pairs={{0,1},{1,0},{2,3},{3,2},{4,5},{5,4},{6,7},{7,6},{8,9},{9,8},{10,11... | collective-permute-start | bytes 12582920 | tf_op jit(solution)/shard_map/ppermute | solution.py:351
  0.7 0.7 %copy-start.7 = (bf16[4096]{0:T(1024)(128)(2,1)S(1)}, bf16[4096]{0:T(1024)(128)(2,1)}, u32[]{:S(2)}) copy-start(bf16[4096]{0:T(1024)(128)(2,1)} %param.8) | copy-start | bytes 24580
  1.4 13.1 %copy-start.8 = (s32[8]{0:T(128)S(1)}, s32[8]{0:T(128)}, u32[]{:S(2)}) copy-start(s32[8]{0:T(128)} %param.9) | copy-start | bytes 100
  7.3 2.0 %copy-start = (bf16[512,4096]{1,0:T(8,128)(2,1)}, bf16[512,4096]{1,0:T(8,128)(2,1)S(1)}, u32[]{:S(2)}) copy-start(bf16[512,4096]{1,0:T(8,128)(2,1)S(1)} %get-tuple-element.17.mine_ref.tokens_ref) | copy-start | bytes 12582916
  9.4 3.2 %copy-start.3 = (bf16[8192,512]{1,0:T(8,128)(2,1)}, bf16[8192,512]{1,0:T(8,128)(2,1)S(1)}, u32[]{:S(2)}) copy-start(bf16[8192,512]{1,0:T(8,128)(2,1)S(1)} %get-tuple-element.21.wq_ref) | copy-start | bytes 25165828
  12.6 1.9 %copy-start.5 = (bf16[8192,256]{1,0:T(8,128)(2,1)}, bf16[8192,256]{1,0:T(8,128)(2,1)S(1)}, u32[]{:S(2)}) copy-start(bf16[8192,256]{1,0:T(8,128)(2,1)S(1)} %get-tuple-element.19.wkv_ref) | copy-start | bytes 12582916
  14.5 1.6 %collective-permute-start.1 = (f32[544,128]{1,0:T(8,128)S(1)}, f32[544,128]{1,0:T(8,128)S(1)}, u32[]{:S(2)}, u32[]{:S(2)}) collective-permute-start(f32[544,128]{1,0:T(8,128)S(1)} %get-tuple-element.18.smine_ref), channel_id=1, source_target_pairs={{0,1},{1,0},{2,3},{3,2},{4,5},{5,4},{6,7},{7,6},{8,9},{9,8},{10,11... | collective-permute-start | bytes 835592 | tf_op jit(solution)/shard_map/ppermute | solution.py:353
  16.1 2.2 %copy-start.1 = (bf16[512,4096]{1,0:T(8,128)(2,1)S(1)}, bf16[512,4096]{1,0:T(8,128)(2,1)}, u32[]{:S(2)}) copy-start(bf16[512,4096]{1,0:T(8,128)(2,1)} %copy-done) | copy-start | bytes 12582916
  18.3 2.2 %copy-start.6 = (bf16[8192,256]{1,0:T(8,128)(2,1)S(1)}, bf16[8192,256]{1,0:T(8,128)(2,1)}, u32[]{:S(2)}) copy-start(bf16[8192,256]{1,0:T(8,128)(2,1)} %copy-done.5) | copy-start | bytes 12582916
  20.5 15.7 %copy-start.4 = (bf16[8192,512]{1,0:T(8,128)(2,1)S(1)}, bf16[8192,512]{1,0:T(8,128)(2,1)}, u32[]{:S(2)}) copy-start(bf16[8192,512]{1,0:T(8,128)(2,1)} %copy-done.3) | copy-start | bytes 25165828
  26.3 35.2 %collective-permute-start.10 = (bf16[512,4096]{1,0:T(8,128)(2,1)S(1)}, bf16[512,4096]{1,0:T(8,128)(2,1)S(1)}, u32[]{:S(2)}, u32[]{:S(2)}) collective-permute-start(bf16[512,4096]{1,0:T(8,128)(2,1)S(1)} %get-tuple-element.28), channel_id=1, source_target_pairs={{0,1},{1,0},{2,3},{3,2},{4,5},{5,4},{6,7},{7,6},{8,9},{9,8},{10,11... | collective-permute-start | bytes 12582920 | tf_op jit(solution)/shard_map/ppermute | solution.py:359
  26.7 19.1 %collective-permute-start.8 = (bf16[256,256]{1,0:T(8,128)(2,1)S(1)}, bf16[256,256]{1,0:T(8,128)(2,1)S(1)}, u32[]{:S(2)}, u32[]{:S(2)}) collective-permute-start(bf16[256,256]{1,0:T(8,128)(2,1)S(1)} %get-tuple-element.20.rest_6_), channel_id=1, source_target_pairs={{0,1},{1,0},{2,3},{3,2},{4,5},{5,4},{6,7},{7,6},{8,9},{9,8},{10,11... | collective-permute-start | bytes 393224 | tf_op jit(solution)/shard_map/ppermute | solution.py:358
  26.9 17.4 %collective-permute-start.4 = (bf16[256,256]{1,0:T(8,128)(2,1)S(1)}, bf16[256,256]{1,0:T(8,128)(2,1)S(1)}, u32[]{:S(2)}, u32[]{:S(2)}) collective-permute-start(bf16[256,256]{1,0:T(8,128)(2,1)S(1)} %get-tuple-element.20.rest_6_), channel_id=1, source_target_pairs={{0,2},{2,4},{4,6},{6,8},{8,10},{10,12},{12,14},{1,3},{3,5},{5,7},{... | collective-permute-start | bytes 393224 | tf_op jit(solution)/shard_map/ppermute | solution.py:329
  30.0 14.3 %collective-permute-start.3 = (bf16[256,256]{1,0:T(8,128)(2,1)S(1)}, bf16[256,256]{1,0:T(8,128)(2,1)S(1)}, u32[]{:S(2)}, u32[]{:S(2)}) collective-permute-start(bf16[256,256]{1,0:T(8,128)(2,1)S(1)} %get-tuple-element.20.rest_6_), channel_id=1, source_target_pairs={{0,4},{2,6},{4,8},{6,10},{8,12},{10,14},{1,5},{3,7},{5,9},{7,11},{... | collective-permute-start | bytes 393224 | tf_op jit(solution)/shard_map/ppermute | solution.py:329
  33.2 11.1 %collective-permute-start.2 = (bf16[256,256]{1,0:T(8,128)(2,1)S(1)}, bf16[256,256]{1,0:T(8,128)(2,1)S(1)}, u32[]{:S(2)}, u32[]{:S(2)}) collective-permute-start(bf16[256,256]{1,0:T(8,128)(2,1)S(1)} %get-tuple-element.20.rest_6_), channel_id=1, source_target_pairs={{0,6},{2,8},{4,10},{6,12},{8,14},{1,7},{3,9},{5,11},{7,13},{9,15},... | collective-permute-start | bytes 393224 | tf_op jit(solution)/shard_map/ppermute | solution.py:329
  44.3 17.2 %copy-start.2 = (bf16[512,4096]{1,0:T(8,128)(2,1)S(1)}, bf16[512,4096]{1,0:T(8,128)(2,1)}, u32[]{:S(2)}) copy-start(bf16[512,4096]{1,0:T(8,128)(2,1)} %copy-done) | copy-start | bytes 12582916
  44.3 2.0 %collective-permute-start.5 = (bf16[256,256]{1,0:T(8,128)(2,1)S(1)}, bf16[256,256]{1,0:T(8,128)(2,1)S(1)}, u32[]{:S(2)}, u32[]{:S(2)}) collective-permute-start(bf16[256,256]{1,0:T(8,128)(2,1)S(1)} %collective-permute-done.2.rest_0_), channel_id=1, source_target_pairs={{0,1},{1,0},{2,3},{3,2},{4,5},{5,4},{6,7},{7,6},{8,9},{9,8},{10,11... | collective-permute-start | bytes 393224 | tf_op jit(solution)/shard_map/ppermute | solution.py:364
  45.3 1.3 %collective-permute-start.6 = (bf16[256,256]{1,0:T(8,128)(2,1)S(1)}, bf16[256,256]{1,0:T(8,128)(2,1)S(1)}, u32[]{:S(2)}, u32[]{:S(2)}) collective-permute-start(bf16[256,256]{1,0:T(8,128)(2,1)S(1)} %collective-permute-done.3.rest_2_), channel_id=1, source_target_pairs={{0,1},{1,0},{2,3},{3,2},{4,5},{5,4},{6,7},{7,6},{8,9},{9,8},{10,11... | collective-permute-start | bytes 393224 | tf_op jit(solution)/shard_map/ppermute | solution.py:364
  45.4 1.5 %collective-permute-start.7 = (bf16[256,256]{1,0:T(8,128)(2,1)S(1)}, bf16[256,256]{1,0:T(8,128)(2,1)S(1)}, u32[]{:S(2)}, u32[]{:S(2)}) collective-permute-start(bf16[256,256]{1,0:T(8,128)(2,1)S(1)} %collective-permute-done.4.rest_4_), channel_id=1, source_target_pairs={{0,1},{1,0},{2,3},{3,2},{4,5},{5,4},{6,7},{7,6},{8,9},{9,8},{10,11... | collective-permute-start | bytes 393224 | tf_op jit(solution)/shard_map/ppermute | solution.py:364
  59.5 2.0 %collective-permute-start.9 = (bf16[512,512]{1,0:T(8,128)(2,1)S(1)}, bf16[512,512]{1,0:T(8,128)(2,1)S(1)}, u32[]{:S(2)}, u32[]{:S(2)}) collective-permute-start(bf16[512,512]{1,0:T(8,128)(2,1)S(1)} %attend.1.mine_ref), channel_id=1, source_target_pairs={{0,1},{1,0},{2,3},{3,2},{4,5},{5,4},{6,7},{7,6},{8,9},{9,8},{10,11... | collective-permute-start | bytes 1572872 | tf_op jit(solution)/shard_map/ppermute | solution.py:368
where the time goes:
time: 68.4 us
  Pallas kernels  39.5 us (58%)
  starting transfers between devices  12.3 us (18%)
  local copies, waits for them, and re-layouts  12.2 us (18%)
  waiting for transfers between devices  2.8 us (4%)
  other arithmetic  1.37 us (2%)
    pallas_call x1, Pallas kernels, attend(): pl.pallas_call(functools.partial(attend_kernel, reach), grid_spec=pltpu.P...  12.7 us
    unnamed x18, local copies, waits for them, and re-layouts  12.2 us
    ppermute x3, starting transfers between devices, shift(): lax.ppermute(value, axis, [(source, source + steps) for source in range(c...  9.22 us
    pallas_call x1, Pallas kernels, project_queries(): pl.pallas_call(queries_kernel, in_specs=[SCALAR] + [WHOLE] * 7 + [pl.Bloc...  8.14 us
    pallas_call x1, Pallas kernels, output(): pl.pallas_call(output_kernel, grid=(width // step,), in_specs=[WHOLE] * 5...  6.93 us
    pallas_call x1, Pallas kernels, prepare(): pl.pallas_call(prepare_kernel, in_specs=[WHOLE] + [hbm] * 4, out_specs=[W...  5.95 us
    pallas_call x1, Pallas kernels, keys_values(): pl.pallas_call(keys_kernel, in_specs=[SCALAR] + [WHOLE] * 7 + [hbm], out_...  5.84 us
    ppermute x1, waiting for transfers between devices, local(): context_other = lax.ppermute(context, 'tp', SWAP)  1.59 us
  transfers between devices with their start and end apart: 11, of which 5 were waited for; matrix products, arithmetic and copies ran while one was open for 2% of the time, Pallas kernels for 39%

commit v1 on v0

v1 whole, which is shorter than its diff:
```python
import functools
import math

import jax
import jax.numpy as jnp
from jax import lax
from jax.experimental import pallas as pl
from jax.experimental.pallas import tpu as pltpu
from jax.sharding import PartitionSpec as P

HEAD = 128
MOST = 1536
LANES = 128
SWAP = [(0, 1), (1, 0)]
MIB = 1024 * 1024
EXP2_SCALE = math.log2(math.e) / HEAD**0.5


def in_hbm(*arrays):
    return [pltpu.with_memory_space_constraint(array, pltpu.HBM) for array in arrays]


def params(mib):
    return pltpu.CompilerParams(vmem_limit_bytes=mib * MIB)


SCALAR = pl.BlockSpec(memory_space=pltpu.SMEM)
WHOLE = pl.BlockSpec(memory_space=pltpu.VMEM)


def first_of_document(info_ref, row):
    begin = jnp.full(row.shape, info_ref[1], jnp.int32)
    for d in range(2, info_ref.shape[0]):
        begin = jnp.where(row >= info_ref[d], info_ref[d], begin)
    return begin


def prepare_kernel(
    info_ref, gain_ref, frequency_ref, tokens_hbm, wk_hbm, wv_hbm, wq_hbm, sums_ref, tokens_ref, wkv_ref, wq_ref, cos_ref, sin_ref, sems
):
    rows, width = tokens_ref.shape
    step = 1024
    chunks = width // step
    loads = [
        pltpu.make_async_copy(tokens_hbm.at[:, c * step : (c + 1) * step], tokens_ref.at[:, c * step : (c + 1) * step], sems.at[c])
        for c in range(chunks)
    ]
    loads += [
        pltpu.make_async_copy(wk_hbm, wkv_ref.at[:, :HEAD], sems.at[chunks]),
        pltpu.make_async_copy(wv_hbm, wkv_ref.at[:, HEAD:], sems.at[chunks + 1]),
        pltpu.make_async_copy(wq_hbm, wq_ref, sems.at[chunks + 2]),
    ]
    for load in loads:
        load.start()
    sums_ref[rows:, :] = gain_ref[...].astype(jnp.float32)
    for c in range(chunks):
        loads[c].wait()
        total = sums_ref[0:rows, :] if c else jnp.zeros((rows, LANES), jnp.float32)
        for j in range(c * step // LANES, (c + 1) * step // LANES):
            wide = tokens_ref[:, j * LANES : (j + 1) * LANES].astype(jnp.float32)
            total = total + wide * wide
        sums_ref[0:rows, :] = total
    row = lax.broadcasted_iota(jnp.int32, (rows, HEAD), 0)
    begin = first_of_document(info_ref, row)
    angles = (row - begin).astype(jnp.float32) * frequency_ref[...]
    lane = lax.broadcasted_iota(jnp.int32, (rows, HEAD), 1)
    cos_ref[...] = jnp.cos(angles)
    sine = jnp.sin(angles)
    sin_ref[...] = jnp.where(lane < HEAD // 2, -sine, sine)
    for load in loads[chunks:]:
        load.wait()


def prepare(info, gain, frequency, tokens, wk, wv, wq):
    rows, width = tokens.shape
    gain_rows = gain.shape[0]
    hbm = pl.BlockSpec(memory_space=pltpu.HBM)
    return pl.pallas_call(
        prepare_kernel,
        in_specs=[SCALAR, WHOLE, WHOLE] + [hbm] * 4,
        out_specs=[WHOLE] * 6,
        out_shape=[
            jax.ShapeDtypeStruct((rows + gain_rows, LANES), jnp.float32),
            jax.ShapeDtypeStruct(tokens.shape, tokens.dtype),
            jax.ShapeDtypeStruct((wk.shape[0], 2 * HEAD), wk.dtype),
            jax.ShapeDtypeStruct(wq.shape, wq.dtype),
            jax.ShapeDtypeStruct((rows, HEAD), jnp.float32),
            jax.ShapeDtypeStruct((rows, HEAD), jnp.float32),
        ],
        scratch_shapes=[pltpu.SemaphoreType.DMA((width // 1024 + 3,))],
        compiler_params=params(20),
        cost_estimate=pl.CostEstimate(flops=rows * width * 2, bytes_accessed=16 * MIB, transcendentals=0),
        name="prepare",
    )(info, gain, frequency, *in_hbm(tokens, wk, wv, wq))


def inverse_norm(mine, other, model):
    mean = jnp.sum(mine + other, axis=1, keepdims=True) * (1.0 / model)
    return jnp.broadcast_to(lax.rsqrt(mean + 1e-05), mine.shape)


def normalize(block, inverse, gains_ref, gain_row):
    parts = []
    for j in range(block.shape[1] // LANES):
        wide = block[:, j * LANES : (j + 1) * LANES].astype(jnp.float32)
        gain = gains_ref[gain_row + j : gain_row + j + 1, :]
        parts.append((wide * inverse * gain).astype(jnp.bfloat16))
    return jnp.concatenate(parts, axis=1)


def turn(x, cosine, sine):
    return (x * cosine + pltpu.roll(x, HEAD // 2, 1) * sine).astype(jnp.bfloat16)


def keys_kernel(
    info_ref, mine_ref, other_ref, smine_ref, sother_ref, cos_ref, sin_ref, wkv_ref, wout_ref, kv_ref, wsend_ref, sem
):
    rows, width = mine_ref.shape
    part_rows = rows // 2
    step = 1024
    me = info_ref[0]
    send_start = pl.multiple_of((1 - me) * width, width)
    send = pltpu.make_async_copy(wout_ref.at[:, pl.ds(send_start, width)], wsend_ref, sem)
    send.start()
    here = pl.ds(pl.multiple_of(me * part_rows, part_rows), part_rows)
    inverse = inverse_norm(smine_ref[here, :], sother_ref[here, :], 2 * width)
    totals = [jnp.zeros((part_rows, 2 * HEAD), jnp.float32)] * 2
    for c in range(width // step):
        for part in range(2):
            tokens_ref, sums_ref = ((mine_ref, smine_ref), (other_ref, sother_ref))[part]
            base = (me if part == 0 else 1 - me) * width
            block = tokens_ref[here, c * step : (c + 1) * step]
            normed = normalize(block, inverse, sums_ref, rows + c * (step // LANES))
            depth = pl.ds(pl.multiple_of(base + c * step, step), step)
            totals[part] = totals[part] + jnp.dot(normed, wkv_ref[depth, :], preferred_element_type=jnp.float32)
    total = totals[0] + totals[1]
    kv_ref[:, :HEAD] = turn(total[:, :HEAD], cos_ref[here, :], sin_ref[here, :])
    kv_ref[:, HEAD:] = total[:, HEAD:].astype(jnp.bfloat16)
    send.wait()


def keys_values(info, tokens, tokens_other, sums, sums_other, tables, wkv, w_out):
    rows, width = tokens.shape
    part = rows // 2
    hbm = pl.BlockSpec(memory_space=pltpu.HBM)
    return pl.pallas_call(
        keys_kernel,
        in_specs=[SCALAR] + [WHOLE] * 7 + [hbm],
        out_specs=[WHOLE, WHOLE],
        out_shape=[
            jax.ShapeDtypeStruct((part, 2 * HEAD), jnp.bfloat16),
            jax.ShapeDtypeStruct((w_out.shape[0], width), w_out.dtype),
        ],
        scratch_shapes=[pltpu.SemaphoreType.DMA],
        compiler_params=params(20),
        cost_estimate=pl.CostEstimate(
            flops=4 * rows * width * HEAD * 2, bytes_accessed=rows * width * 2, transcendentals=0
        ),
        name="keys_values",
    )(info, tokens, tokens_other, sums, sums_other, *tables, wkv, *in_hbm(w_out))


def queries_kernel(info_ref, mine_ref, other_ref, smine_ref, sother_ref, cos_ref, sin_ref, wq_ref, wout_ref, q_ref, wkeep_ref, acc, sem):
    rows, width = mine_ref.shape
    step = 1024
    me = info_ref[0]
    keep = pltpu.make_async_copy(wout_ref.at[:, pl.ds(pl.multiple_of(me * width, width), width)], wkeep_ref, sem)
    keep.start()
    inverse = inverse_norm(smine_ref[0:rows, :], sother_ref[0:rows, :], 2 * width)
    for c in range(width // step):
        for part in range(2):
            tokens_ref, sums_ref = ((mine_ref, smine_ref), (other_ref, sother_ref))[part]
            base = (me if part == 0 else 1 - me) * width
            normed = normalize(tokens_ref[:, c * step : (c + 1) * step], inverse, sums_ref, rows + c * (step // LANES))
            depth = pl.ds(pl.multiple_of(base + c * step, step), step)
            term = jnp.dot(normed, wq_ref[depth, :], preferred_element_type=jnp.float32)
            if c == 0:
                acc[part] = term
            else:
                acc[part] += term
    for h in range(q_ref.shape[1] // HEAD):
        lanes = slice(h * HEAD, (h + 1) * HEAD)
        q_ref[:, lanes] = turn(acc[0, :, lanes] + acc[1, :, lanes], cos_ref[...], sin_ref[...])
    keep.wait()


def project_queries(info, tokens, tokens_other, sums, sums_other, tables, wq, w_out):
    rows, width = tokens.shape
    nq = wq.shape[1]
    return pl.pallas_call(
        queries_kernel,
        in_specs=[SCALAR] + [WHOLE] * 7 + [pl.BlockSpec(memory_space=pltpu.HBM)],
        out_specs=[WHOLE, WHOLE],
        out_shape=[
            jax.ShapeDtypeStruct((rows, nq), jnp.bfloat16),
            jax.ShapeDtypeStruct((w_out.shape[0], width), w_out.dtype),
        ],
        scratch_shapes=[pltpu.VMEM((2, rows, nq), jnp.float32), pltpu.SemaphoreType.DMA],
        compiler_params=params(20),
        cost_estimate=pl.CostEstimate(flops=4 * rows * width * nq, bytes_accessed=rows * width * 4, transcendentals=0),
        name="queries",
    )(info, tokens, tokens_other, sums, sums_other, *tables, wq, *in_hbm(w_out))


def attend_kernel(reach, info_ref, q_ref, *rest):
    blocks = rest[: 2 * (reach + 1)]
    ctx_ref, keys, values, stacked, scores, acc, tops, sums = rest[2 * (reach + 1) :]
    rows = q_ref.shape[0]
    tile_rows = ctx_ref.shape[0]
    heads = q_ref.shape[1] // HEAD
    span = scores.shape[2]
    t = pl.program_id(0)

    @pl.when(t == 0)
    def _():
        part = rows // 2
        for b, block in enumerate(blocks):
            which = info_ref[0] if b % 2 == 0 else 1 - info_ref[0]
            at = pl.ds(pl.multiple_of((b // 2) * rows + which * part, part), part)
            keys[at, :] = block[:, :HEAD]
            values[at, :] = block[:, HEAD:]

    behind = reach * rows
    first_row = t * tile_rows
    row = first_row + lax.broadcasted_iota(jnp.int32, (tile_rows, span), 0)
    begin = first_of_document(info_ref, row) + behind
    row = row + behind
    lowest = info_ref[1]
    for d in range(2, info_ref.shape[0]):
        lowest = jnp.where(first_row >= info_ref[d], info_ref[d], lowest)
    lane = lax.broadcasted_iota(jnp.int32, (tile_rows, span), 1)
    low = (lowest + behind) // span
    high = (first_row + behind + tile_rows - 1) // span + 1
    q_rows = pl.ds(pl.multiple_of(first_row, tile_rows), tile_rows)
    for h in range(heads):
        stacked[h * tile_rows : (h + 1) * tile_rows, :] = q_ref[q_rows, h * HEAD : (h + 1) * HEAD]

    tops[...] = jnp.full(tops.shape, -1e30, jnp.float32)
    sums[...] = jnp.zeros(sums.shape, jnp.float32)
    acc[...] = jnp.zeros(acc.shape, jnp.float32)

    def score(i, carry):
        place = lane + i * span
        allowed = (place >= begin) & (place <= row)
        s = lax.dot_general(
            stacked[...],
            keys[pl.ds(pl.multiple_of(i * span, span), span), :],
            (((1,), (1,)), ((), ())),
            preferred_element_type=jnp.float32,
        )
        for h in range(heads):
            part = slice(h * tile_rows, (h + 1) * tile_rows)
            masked = jnp.where(allowed, s[part, :], -1e30)
            scores[i, part, :] = masked
            top = tops[part, :]
            for j in range(span // LANES):
                top = jnp.maximum(top, masked[:, j * LANES : (j + 1) * LANES])
            tops[part, :] = top
        return carry

    lax.fori_loop(low, high, score, 0)
    top = jnp.max(tops[...], axis=1, keepdims=True)
    tops[...] = jnp.broadcast_to(top * EXP2_SCALE, tops.shape)

    def weigh(i, carry):
        top = tops[...]
        total = sums[...]
        rounded = []
        for j in range(span // LANES):
            w = jnp.exp2(scores[i, :, j * LANES : (j + 1) * LANES] * EXP2_SCALE - top)
            total = total + w
            rounded.append(w.astype(jnp.bfloat16))
        sums[...] = total
        acc[...] += jnp.dot(
            jnp.concatenate(rounded, axis=1),
            values[pl.ds(pl.multiple_of(i * span, span), span), :],
            preferred_element_type=jnp.float32,
        )
        return carry

    lax.fori_loop(low, high, weigh, 0)
    for h in range(heads):
        part = slice(h * tile_rows, (h + 1) * tile_rows)
        total = jnp.sum(sums[part, :], axis=1, keepdims=True)
        ctx_ref[:, h * HEAD : (h + 1) * HEAD] = (acc[part, :] / total).astype(jnp.bfloat16)


def attend(info, queries, blocks):
    rows, width = queries.shape
    reach = len(blocks) // 2 - 1
    tile_rows, span = 128, 512
    heads = width // HEAD
    places = (reach + 1) * rows
    tall = heads * tile_rows
    return pl.pallas_call(
        functools.partial(attend_kernel, reach),
        grid=(rows // tile_rows,),
        in_specs=[SCALAR] + [WHOLE] * (1 + len(blocks)),
        out_specs=pl.BlockSpec((tile_rows, width), lambda t: (t, 0)),
        scratch_shapes=[
            pltpu.VMEM((places, HEAD), jnp.bfloat16),
            pltpu.VMEM((places, HEAD), jnp.bfloat16),
            pltpu.VMEM((tall, HEAD), jnp.bfloat16),
            pltpu.VMEM((places // span, tall, span), jnp.float32),
            pltpu.VMEM((tall, HEAD), jnp.float32),
            pltpu.VMEM((tall, LANES), jnp.float32),
            pltpu.VMEM((tall, LANES), jnp.float32),
        ],
        out_shape=jax.ShapeDtypeStruct((rows, width), jnp.bfloat16),
        compiler_params=params(20),
        cost_estimate=pl.CostEstimate(
            flops=4 * rows * width * places, bytes_accessed=rows * width * 8, transcendentals=rows * heads * places
        ),
        name="attend",
    )(info, queries, *blocks)


def output_kernel(tokens_ref, mine_ref, other_ref, w_mine_ref, w_other_ref, out_ref):
    step = out_ref.shape[1]
    here = pl.ds(pl.multiple_of(pl.program_id(0) * step, step), step)
    mine = jnp.dot(mine_ref[...], w_mine_ref[:, here], preferred_element_type=jnp.float32).astype(jnp.bfloat16)
    other = jnp.dot(other_ref[...], w_other_ref[:, here], preferred_element_type=jnp.float32).astype(jnp.bfloat16)
    out = tokens_ref[:, here].astype(jnp.float32) + mine.astype(jnp.float32) + other.astype(jnp.float32)
    out_ref[...] = out.astype(jnp.bfloat16)


def output(tokens, mine, other, w_mine, w_other):
    rows, width = tokens.shape
    depth = mine.shape[1]
    step = 1024
    return pl.pallas_call(
        output_kernel,
        grid=(width // step,),
        in_specs=[WHOLE] * 5,
        out_specs=pl.BlockSpec((rows, step), lambda j: (0, j)),
        out_shape=jax.ShapeDtypeStruct((rows, width), jnp.bfloat16),
        compiler_params=params(20),
        cost_estimate=pl.CostEstimate(
            flops=4 * rows * width * depth, bytes_accessed=(4 * rows + 4 * depth) * width, transcendentals=0
        ),
        name="output",
    )(tokens, mine, other, w_mine, w_other)


def shift(value, axis, steps):
    count = lax.axis_size(axis)
    return lax.ppermute(value, axis, [(source, source + steps) for source in range(count - steps)])


def local(tokens, norm_gain, lengths, w_query, w_key, w_value, w_out):
    rows = tokens.shape[0]
    first_here = lax.axis_index("dp") * rows
    reach = (rows + MOST - 2) // rows
    half = HEAD // 2
    frequency = 500000.0 ** (-jnp.arange(half, dtype=jnp.float32) * 2.0 / HEAD)
    frequency = jnp.concatenate([frequency, frequency])[None, :]
    starts = jnp.cumsum(lengths) - lengths - first_here
    info = jnp.concatenate([lax.axis_index("tp")[None], starts]).astype(jnp.int32)

    tokens_other = lax.ppermute(tokens, "tp", SWAP)
    sums, tokens, wkv, wq, *tables = prepare(
        info, norm_gain.reshape(-1, LANES), frequency, tokens, w_key, w_value, w_query
    )
    sums_other = lax.ppermute(sums, "tp", SWAP)

    kv, w_send = keys_values(info, tokens, tokens_other, sums, sums_other, tables, wkv, w_out)
    parts = [shift(kv, "dp", d) for d in range(reach, 0, -1)]
    own_other = lax.ppermute(kv, "tp", SWAP)
    w_other = lax.ppermute(w_send, "tp", SWAP)
    queries, w_mine = project_queries(info, tokens, tokens_other, sums, sums_other, tables, wq, w_out)
    parts, queries = lax.optimization_barrier((parts, queries))
    blocks = []
    for part in parts:
        blocks += [part, lax.ppermute(part, "tp", SWAP)]
    blocks += [kv, own_other]
    context = attend(info, queries, blocks)
    context_other = lax.ppermute(context, "tp", SWAP)
    return output(tokens, context, context_other, w_mine, w_other)


def solution(mesh):
    placed = (P(("grp", "dp"), "tp"), P("tp"), P("grp"), P(None, "tp"), P(), P(), P("tp", None))
    return jax.shard_map(
        local, mesh=mesh, in_specs=placed, out_specs=P(("grp", "dp"), "tp"), check_vma=False
    )
```

time: 68.4 us -> 54.8 us (0.80)
  the two profiles are of different devices: /device:TPU:9 before, /device:TPU:13 now
where the time goes in v1:
time: 54.8 us; the launch traced here: 53.9 us
  Pallas kernels  35.7 us (65%)
  starting transfers between devices  11.6 us (21%)
  waiting for transfers between devices  4.16 us (8%)
  other arithmetic  1.66 us (3%)
  local copies, waits for them, and re-layouts  0.7 us (1%)
    pallas_call x1, Pallas kernels, attend(): pl.pallas_call(functools.partial(attend_kernel, reach), grid=(rows // til...  10 us
    ppermute x3, starting transfers between devices, shift(): lax.ppermute(value, axis, [(source, source + steps) for source in range(c...  8.59 us
    pallas_call x1, Pallas kernels, project_queries(): pl.pallas_call(queries_kernel, in_specs=[SCALAR] + [WHOLE] * 7 + [pl.Bloc...  7.58 us
    pallas_call x1, Pallas kernels, prepare(): pl.pallas_call(prepare_kernel, in_specs=[SCALAR, WHOLE, WHOLE] + [hbm] *...  6.49 us
    pallas_call x1, Pallas kernels, output(): pl.pallas_call(output_kernel, grid=(width // step,), in_specs=[WHOLE] * 5...  6.43 us
    pallas_call x1, Pallas kernels, keys_values(): pl.pallas_call(keys_kernel, in_specs=[SCALAR] + [WHOLE] * 7 + [hbm], out_...  5.23 us
    ppermute x1, waiting for transfers between devices, local(): context_other = lax.ppermute(context, 'tp', SWAP)  1.58 us
    ppermute x1, waiting for transfers between devices, local(): sums_other = lax.ppermute(sums, 'tp', SWAP)  1.55 us
  transfers between devices with their start and end apart: 11, of which 5 were waited for; matrix products, arithmetic and copies ran while one was open for 3% of the time, Pallas kernels for 45%

profile of v1, /device:TPU:13, one launch (start us, length us, event | category | flops | bytes accessed | tf_op | source)
XLA Modules:
  0.0 53.9 jit_solution(14109032739964508441)
XLA Ops:
  0.0 0.7 %collective-permute-start = (bf16[512,4096]{1,0:T(8,128)(2,1)}, bf16[512,4096]{1,0:T(8,128)(2,1)}, u32[]{:S(2)}, u32[]{:S(2)}) collective-permute-start(bf16[512,4096]{1,0:T(8,128)(2,1)} %tokens_hbm.1), channel_id=1, source_target_pairs={{0,1},{1,0},{2,3},{3,2},{4,5},{5,4},{6,7},{7,6},{8,9},{9,8},{10,11... | collective-permute-start | bytes 12582920 | tf_op jit(solution)/shard_map/ppermute | solution.py:360
  0.7 0.8 %reduce-window.9 = s32[8,1]{0,1:T(1,128)S(1)} reduce-window(s32[8,1]{0,1:T(1,128)} %bitcast.10, s32[]{:T(128)} %constant.16.clone.1), window={size=8x1 pad=7_0x0_0}, to_apply=%region_0.0 | reduce-window | flops 56 | bytes 68 | tf_op jit(solution)/shard_map/reduce-window.4
  1.5 0.1 maximum_bitcast_fusion.frequency_ref
  1.6 0.7 %fusion = s32[8]{0:T(128)S(1)} fusion(s32[8]{0:T(128)} %param.9, s32[8,1]{0,1:T(1,128)S(1)} %reduce-window.9, s32[]{:T(128)S(6)} %mul.2), kind=kLoop, calls=%fused_computation.3 | loop fusion | flops 16 | bytes 100 | tf_op jit(solution)/shard_map/sub | solution.py:357
  2.3 0.7 %copy-done = bf16[4096]{0:T(1024)(128)(2,1)S(1)} copy-done((bf16[4096]{0:T(1024)(128)(2,1)S(1)}, bf16[4096]{0:T(1024)(128)(2,1)}, u32[]{:S(2)}) %copy-start) | copy-done | bytes 8216
  3.0 6.5 %prepare.1 = (f32[544,128]{1,0:T(8,128)S(1)}, bf16[512,4096]{1,0:T(8,128)(2,1)S(1)}, bf16[8192,256]{1,0:T(8,128)(2,1)S(1)}, bf16[8192,512]{1,0:T(8,128)(2,1)S(1)...) custom-call(s32[9]{0:T(128)S(1)} %pad_add_fusion.info_ref, bf16[32,128]{1,0:T(8,128)(2,1)S(1)} %bitcast.9, ...), custom_call_target="tpu_custom_call" | custom-call | flops 4194304 | bytes 16777216 | tf_op jit(solution)/shard_map/prepare/pallas_call | solution.py:78
  9.6 1.5 %collective-permute-done.1.sother_ref = f32[544,128]{1,0:T(8,128)S(1)} collective-permute-done((f32[544,128]{1,0:T(8,128)S(1)}, f32[544,128]{1,0:T(8,128)S(1)}, u32[]{:S(2)}, u32[]{:S(2)}) %collective-permute-start.1) | collective-permute-done | bytes 278560 | tf_op jit(solution)/shard_map/ppermute | solution.py:364
  11.2 5.2 %keys_values.1 = (bf16[256,256]{1,0:T(8,128)(2,1)S(1)}, bf16[512,4096]{1,0:T(8,128)(2,1)S(1)}) custom-call(s32[9]{0:T(128)S(1)} %pad_add_fusion.info_ref, bf16[512,4096]{1,0:T(8,128)(2,1)S(1)} %get-tuple-element.19.mine_ref.tokens_ref, bf16[512,4096]{1,0:T(8,128)(2,1)} %collective-permute-done.other_ref, f32[544,128]{1,0:T(8,128)S(1)} %get-tuple-element.20.smine_ref, ...), custom_call_target="tpu_custom_call" | custom-call | flops 2147483648 | bytes 4194304 | tf_op jit(solution)/shard_map/keys_values/pallas_call | solution.py:146
  16.4 0.2 collective-permute-start.10
  16.6 0.4 collective-permute-start.8
  17.0 3.1 %collective-permute-start.4 = (bf16[256,256]{1,0:T(8,128)(2,1)S(1)}, bf16[256,256]{1,0:T(8,128)(2,1)S(1)}, u32[]{:S(2)}, u32[]{:S(2)}) collective-permute-start(bf16[256,256]{1,0:T(8,128)(2,1)S(1)} %get-tuple-element.24.rest_6_), channel_id=1, source_target_pairs={{0,2},{2,4},{4,6},{6,8},{8,10},{10,12},{12,14},{1,3},{3,5},{5,7},{... | collective-permute-start | bytes 393224 | tf_op jit(solution)/shard_map/ppermute | solution.py:347
  20.1 3.2 %collective-permute-start.3 = (bf16[256,256]{1,0:T(8,128)(2,1)S(1)}, bf16[256,256]{1,0:T(8,128)(2,1)S(1)}, u32[]{:S(2)}, u32[]{:S(2)}) collective-permute-start(bf16[256,256]{1,0:T(8,128)(2,1)S(1)} %get-tuple-element.24.rest_6_), channel_id=1, source_target_pairs={{0,4},{2,6},{4,8},{6,10},{8,12},{10,14},{1,5},{3,7},{5,9},{7,11},{... | collective-permute-start | bytes 393224 | tf_op jit(solution)/shard_map/ppermute | solution.py:347
  23.3 2.2 %collective-permute-start.2 = (bf16[256,256]{1,0:T(8,128)(2,1)S(1)}, bf16[256,256]{1,0:T(8,128)(2,1)S(1)}, u32[]{:S(2)}, u32[]{:S(2)}) collective-permute-start(bf16[256,256]{1,0:T(8,128)(2,1)S(1)} %get-tuple-element.24.rest_6_), channel_id=1, source_target_pairs={{0,6},{2,8},{4,10},{6,12},{8,14},{1,7},{3,9},{5,11},{7,13},{9,15},... | collective-permute-start | bytes 393224 | tf_op jit(solution)/shard_map/ppermute | solution.py:347
  25.6 7.6 %queries.1 = (bf16[512,512]{1,0:T(8,128)(2,1)S(1)}, bf16[512,4096]{1,0:T(8,128)(2,1)S(1)}) custom-call(s32[9]{0:T(128)S(1)} %pad_add_fusion.info_ref, bf16[512,4096]{1,0:T(8,128)(2,1)S(1)} %get-tuple-element.19.mine_ref.tokens_ref, bf16[512,4096]{1,0:T(8,128)(2,1)} %collective-permute-done.other_ref, f32[544,128]{1,0:T(8,128)S(1)} %get-tuple-element.20.smine_ref, ...), custom_call_target="tpu_custom_call" | custom-call | flops 4294967296 | bytes 8388608 | tf_op jit(solution)/shard_map/queries/pallas_call | solution.py:190
  33.2 0.8 %collective-permute-start.5 = (bf16[256,256]{1,0:T(8,128)(2,1)S(1)}, bf16[256,256]{1,0:T(8,128)(2,1)S(1)}, u32[]{:S(2)}, u32[]{:S(2)}) collective-permute-start(bf16[256,256]{1,0:T(8,128)(2,1)S(1)} %collective-permute-done.2.rest_0_), channel_id=1, source_target_pairs={{0,1},{1,0},{2,3},{3,2},{4,5},{5,4},{6,7},{7,6},{8,9},{9,8},{10,11... | collective-permute-start | bytes 393224 | tf_op jit(solution)/shard_map/ppermute | solution.py:374
  34.0 0.1 collective-permute-start.6
  34.1 0.4 collective-permute-start.7
  34.5 0.5 collective-permute-done.5.rest_1_
  35.0 0.4 collective-permute-done.6.rest_3_
  35.3 0.2 collective-permute-done.7.rest_5_
  35.5 10.0 %attend.1.mine_ref = bf16[512,512]{1,0:T(8,128)(2,1)S(1)} custom-call(s32[9]{0:T(128)S(1)} %pad_add_fusion.info_ref, bf16[512,512]{1,0:T(8,128)(2,1)S(1)} %get-tuple-element.27.q_ref, bf16[256,256]{1,0:T(8,128)(2,1)S(1)} %collective-permute-done.2.rest_0_, bf16[256,256]{1,0:T(8,128)(2,1)S(1)} %collective-permute-done.5.rest_1_, ...), custom_call_target="tpu_custom_call" | custom-call | flops 2147483648 | bytes 2097152 | tf_op jit(solution)/shard_map/attend/pallas_call | solution.py:295
  45.5 0.4 collective-permute-start.9
  45.9 1.6 %collective-permute-done.9.other_ref = bf16[512,512]{1,0:T(8,128)(2,1)S(1)} collective-permute-done((bf16[512,512]{1,0:T(8,128)(2,1)S(1)}, bf16[512,512]{1,0:T(8,128)(2,1)S(1)}, u32[]{:S(2)}, u32[]{:S(2)}) %collective-permute-start.9) | collective-permute-done | bytes 524320 | tf_op jit(solution)/shard_map/ppermute | solution.py:377
  47.5 6.4 %output.1 = bf16[512,4096]{1,0:T(8,128)(2,1)} custom-call(bf16[512,4096]{1,0:T(8,128)(2,1)S(1)} %get-tuple-element.19.mine_ref.tokens_ref, bf16[512,512]{1,0:T(8,128)(2,1)S(1)} %attend.1.mine_ref, bf16[512,512]{1,0:T(8,128)(2,1)S(1)} %collective-permute-done.9.other_ref, bf16[512,4096]{1,0:T(8,128)(2,1)S(1)} %get-tuple-element.31.w_mine_ref, ...), custom_call_target="tpu_custom_call" | custom-call | flops 4294967296 | bytes 16777216 | tf_op jit(solution)/shard_map/output/pallas_call | solution.py:331
  (10 shorter events, 0.2 us)
Async XLA Ops:
  0.0 11.2 %collective-permute-start = (bf16[512,4096]{1,0:T(8,128)(2,1)}, bf16[512,4096]{1,0:T(8,128)(2,1)}, u32[]{:S(2)}, u32[]{:S(2)}) collective-permute-start(bf16[512,4096]{1,0:T(8,128)(2,1)} %tokens_hbm.1), channel_id=1, source_target_pairs={{0,1},{1,0},{2,3},{3,2},{4,5},{5,4},{6,7},{7,6},{8,9},{9,8},{10,11... | collective-permute-start | bytes 12582920 | tf_op jit(solution)/shard_map/ppermute | solution.py:360
  2.3 0.7 %copy-start = (bf16[4096]{0:T(1024)(128)(2,1)S(1)}, bf16[4096]{0:T(1024)(128)(2,1)}, u32[]{:S(2)}) copy-start(bf16[4096]{0:T(1024)(128)(2,1)} %param.8) | copy-start | bytes 24580
  9.5 1.6 %collective-permute-start.1 = (f32[544,128]{1,0:T(8,128)S(1)}, f32[544,128]{1,0:T(8,128)S(1)}, u32[]{:S(2)}, u32[]{:S(2)}) collective-permute-start(f32[544,128]{1,0:T(8,128)S(1)} %get-tuple-element.20.smine_ref), channel_id=1, source_target_pairs={{0,1},{1,0},{2,3},{3,2},{4,5},{5,4},{6,7},{7,6},{8,9},{9,8},{10,11... | collective-permute-start | bytes 835592 | tf_op jit(solution)/shard_map/ppermute | solution.py:364
  16.4 31.1 %collective-permute-start.10 = (bf16[512,4096]{1,0:T(8,128)(2,1)S(1)}, bf16[512,4096]{1,0:T(8,128)(2,1)S(1)}, u32[]{:S(2)}, u32[]{:S(2)}) collective-permute-start(bf16[512,4096]{1,0:T(8,128)(2,1)S(1)} %get-tuple-element.32), channel_id=1, source_target_pairs={{0,1},{1,0},{2,3},{3,2},{4,5},{5,4},{6,7},{7,6},{8,9},{9,8},{10,11... | collective-permute-start | bytes 12582920 | tf_op jit(solution)/shard_map/ppermute | solution.py:369
  16.6 17.9 %collective-permute-start.8 = (bf16[256,256]{1,0:T(8,128)(2,1)S(1)}, bf16[256,256]{1,0:T(8,128)(2,1)S(1)}, u32[]{:S(2)}, u32[]{:S(2)}) collective-permute-start(bf16[256,256]{1,0:T(8,128)(2,1)S(1)} %get-tuple-element.24.rest_6_), channel_id=1, source_target_pairs={{0,1},{1,0},{2,3},{3,2},{4,5},{5,4},{6,7},{7,6},{8,9},{9,8},{10,11... | collective-permute-start | bytes 393224 | tf_op jit(solution)/shard_map/ppermute | solution.py:368
  17.0 16.2 %collective-permute-start.4 = (bf16[256,256]{1,0:T(8,128)(2,1)S(1)}, bf16[256,256]{1,0:T(8,128)(2,1)S(1)}, u32[]{:S(2)}, u32[]{:S(2)}) collective-permute-start(bf16[256,256]{1,0:T(8,128)(2,1)S(1)} %get-tuple-element.24.rest_6_), channel_id=1, source_target_pairs={{0,2},{2,4},{4,6},{6,8},{8,10},{10,12},{12,14},{1,3},{3,5},{5,7},{... | collective-permute-start | bytes 393224 | tf_op jit(solution)/shard_map/ppermute | solution.py:347
  20.1 13.1 %collective-permute-start.3 = (bf16[256,256]{1,0:T(8,128)(2,1)S(1)}, bf16[256,256]{1,0:T(8,128)(2,1)S(1)}, u32[]{:S(2)}, u32[]{:S(2)}) collective-permute-start(bf16[256,256]{1,0:T(8,128)(2,1)S(1)} %get-tuple-element.24.rest_6_), channel_id=1, source_target_pairs={{0,4},{2,6},{4,8},{6,10},{8,12},{10,14},{1,5},{3,7},{5,9},{7,11},{... | collective-permute-start | bytes 393224 | tf_op jit(solution)/shard_map/ppermute | solution.py:347
  23.3 9.9 %collective-permute-start.2 = (bf16[256,256]{1,0:T(8,128)(2,1)S(1)}, bf16[256,256]{1,0:T(8,128)(2,1)S(1)}, u32[]{:S(2)}, u32[]{:S(2)}) collective-permute-start(bf16[256,256]{1,0:T(8,128)(2,1)S(1)} %get-tuple-element.24.rest_6_), channel_id=1, source_target_pairs={{0,6},{2,8},{4,10},{6,12},{8,14},{1,7},{3,9},{5,11},{7,13},{9,15},... | collective-permute-start | bytes 393224 | tf_op jit(solution)/shard_map/ppermute | solution.py:347
  33.2 1.8 %collective-permute-start.5 = (bf16[256,256]{1,0:T(8,128)(2,1)S(1)}, bf16[256,256]{1,0:T(8,128)(2,1)S(1)}, u32[]{:S(2)}, u32[]{:S(2)}) collective-permute-start(bf16[256,256]{1,0:T(8,128)(2,1)S(1)} %collective-permute-done.2.rest_0_), channel_id=1, source_target_pairs={{0,1},{1,0},{2,3},{3,2},{4,5},{5,4},{6,7},{7,6},{8,9},{9,8},{10,11... | collective-permute-start | bytes 393224 | tf_op jit(solution)/shard_map/ppermute | solution.py:374
  34.0 1.3 %collective-permute-start.6 = (bf16[256,256]{1,0:T(8,128)(2,1)S(1)}, bf16[256,256]{1,0:T(8,128)(2,1)S(1)}, u32[]{:S(2)}, u32[]{:S(2)}) collective-permute-start(bf16[256,256]{1,0:T(8,128)(2,1)S(1)} %collective-permute-done.3.rest_2_), channel_id=1, source_target_pairs={{0,1},{1,0},{2,3},{3,2},{4,5},{5,4},{6,7},{7,6},{8,9},{9,8},{10,11... | collective-permute-start | bytes 393224 | tf_op jit(solution)/shard_map/ppermute | solution.py:374
  34.1 1.5 %collective-permute-start.7 = (bf16[256,256]{1,0:T(8,128)(2,1)S(1)}, bf16[256,256]{1,0:T(8,128)(2,1)S(1)}, u32[]{:S(2)}, u32[]{:S(2)}) collective-permute-start(bf16[256,256]{1,0:T(8,128)(2,1)S(1)} %collective-permute-done.4.rest_4_), channel_id=1, source_target_pairs={{0,1},{1,0},{2,3},{3,2},{4,5},{5,4},{6,7},{7,6},{8,9},{9,8},{10,11... | collective-permute-start | bytes 393224 | tf_op jit(solution)/shard_map/ppermute | solution.py:374
  45.5 2.0 %collective-permute-start.9 = (bf16[512,512]{1,0:T(8,128)(2,1)S(1)}, bf16[512,512]{1,0:T(8,128)(2,1)S(1)}, u32[]{:S(2)}, u32[]{:S(2)}) collective-permute-start(bf16[512,512]{1,0:T(8,128)(2,1)S(1)} %attend.1.mine_ref), channel_id=1, source_target_pairs={{0,1},{1,0},{2,3},{3,2},{4,5},{5,4},{6,7},{7,6},{8,9},{9,8},{10,11... | collective-permute-start | bytes 1572872 | tf_op jit(solution)/shard_map/ppermute | solution.py:377

commit v2 on v1

v2 whole, which is shorter than its diff:
```python
import functools
import math

import jax
import jax.numpy as jnp
from jax import lax
from jax.experimental import pallas as pl
from jax.experimental.pallas import tpu as pltpu
from jax.sharding import PartitionSpec as P

HEAD = 128
MOST = 1536
LANES = 128
SWAP = [(0, 1), (1, 0)]
MIB = 1024 * 1024
EXP2_SCALE = math.log2(math.e) / HEAD**0.5

SCALAR = pl.BlockSpec(memory_space=pltpu.SMEM)
WHOLE = pl.BlockSpec(memory_space=pltpu.VMEM)
HBM = pl.BlockSpec(memory_space=pltpu.HBM)


def in_hbm(*arrays):
    return [pltpu.with_memory_space_constraint(array, pltpu.HBM) for array in arrays]


def params(mib):
    return pltpu.CompilerParams(vmem_limit_bytes=mib * MIB)


def cost(flops, moved):
    return pl.CostEstimate(flops=flops, bytes_accessed=moved, transcendentals=0)


def shaped(shape, dtype):
    return jax.ShapeDtypeStruct(shape, dtype)


def first_of_document(place_ref, lengths_ref, row):
    start = -place_ref[1]
    begin = jnp.full(row.shape, start, jnp.int32)
    for d in range(lengths_ref.shape[0] - 1):
        start = start + lengths_ref[d]
        begin = jnp.where(row >= start, start, begin)
    return begin


def squares_kernel(place_ref, frequency_ref, gain_ref, tokens_hbm, sums_ref, tokens_ref, sems):
    rows, width = tokens_ref.shape
    chunks = sems.shape[0]
    step = width // chunks
    loads = []
    for c in range(chunks):
        part = (slice(None), slice(c * step, (c + 1) * step))
        loads.append(pltpu.make_async_copy(tokens_hbm.at[part], tokens_ref.at[part], sems.at[c]))
        loads[c].start()
    sums_ref[rows:, :] = gain_ref[...].astype(jnp.float32)
    for c in range(chunks):
        loads[c].wait()
        total = sums_ref[0:rows, :] if c else jnp.zeros((rows, LANES), jnp.float32)
        for j in range(c * step // LANES, (c + 1) * step // LANES):
            wide = tokens_ref[:, j * LANES : (j + 1) * LANES].astype(jnp.float32)
            total = total + wide * wide
        sums_ref[0:rows, :] = total


def squares(place, frequency, gain, tokens):
    rows, width = tokens.shape
    return pl.pallas_call(
        squares_kernel,
        in_specs=[SCALAR, WHOLE, WHOLE, HBM],
        out_specs=[WHOLE] * 2,
        out_shape=[shaped((rows + gain.shape[0], LANES), jnp.float32), shaped(tokens.shape, tokens.dtype)],
        scratch_shapes=[pltpu.SemaphoreType.DMA((4,))],
        compiler_params=params(16),
        cost_estimate=cost(rows * width * 2, rows * width * 2),
        name="squares",
    )(place, frequency, gain, *in_hbm(tokens))


def tables_kernel(place_ref, lengths_ref, frequency_ref, wk_hbm, wv_hbm, wkv_ref, cos_ref, sin_ref, sems):
    loads = [
        pltpu.make_async_copy(wk_hbm, wkv_ref.at[:, :HEAD], sems.at[0]),
        pltpu.make_async_copy(wv_hbm, wkv_ref.at[:, HEAD:], sems.at[1]),
    ]
    for load in loads:
        load.start()
    row = lax.broadcasted_iota(jnp.int32, cos_ref.shape, 0)
    lane = lax.broadcasted_iota(jnp.int32, cos_ref.shape, 1)
    angles = (row - first_of_document(place_ref, lengths_ref, row)).astype(jnp.float32) * frequency_ref[...]
    cos_ref[...] = jnp.cos(angles)
    sine = jnp.sin(angles)
    sin_ref[...] = jnp.where(lane < HEAD // 2, -sine, sine)
    for load in loads:
        load.wait()


def tables_and_weights(place, lengths, frequency, wk, wv, rows):
    return pl.pallas_call(
        tables_kernel,
        in_specs=[SCALAR, SCALAR, WHOLE, HBM, HBM],
        out_specs=[WHOLE] * 3,
        out_shape=[
            shaped((wk.shape[0], 2 * HEAD), wk.dtype),
            shaped((rows, HEAD), jnp.float32),
            shaped((rows, HEAD), jnp.float32),
        ],
        scratch_shapes=[pltpu.SemaphoreType.DMA((2,))],
        compiler_params=params(16),
        cost_estimate=cost(rows * HEAD * 100, wk.shape[0] * HEAD * 4),
        name="tables",
    )(place, lengths, frequency, *in_hbm(wk, wv))


def normalize(block, inverse, gains_ref, gain_row):
    parts = []
    for j in range(block.shape[1] // LANES):
        wide = block[:, j * LANES : (j + 1) * LANES].astype(jnp.float32)
        gain = gains_ref[gain_row + j : gain_row + j + 1, :]
        parts.append((wide * inverse * gain).astype(jnp.bfloat16))
    return jnp.concatenate(parts, axis=1)


def turn(x, cosine, sine):
    return (x * cosine + pltpu.roll(x, HEAD // 2, 1) * sine).astype(jnp.bfloat16)


def partial_kernel(
    place_ref, tokens_ref, mine_ref, other_ref, wkv_ref, wq_hbm, normed_ref, inverse_ref, keep_ref, send_ref, wq_ref, acc, sem
):
    rows, width = tokens_ref.shape
    half = rows // 2
    step = 1024
    me = place_ref[0]
    load = pltpu.make_async_copy(wq_hbm, wq_ref, sem)
    load.start()
    mean = jnp.sum(mine_ref[0:rows, :] + other_ref[0:rows, :], axis=1, keepdims=True) * (0.5 / width)
    inverse_ref[...] = jnp.broadcast_to(lax.rsqrt(mean + 1e-05), inverse_ref.shape)
    inverse = inverse_ref[...]
    for c in range(width // step):
        columns = slice(c * step, (c + 1) * step)
        normed = normalize(tokens_ref[:, columns], inverse, mine_ref, rows + c * (step // LANES))
        normed_ref[:, columns] = normed
        depth = pl.ds(pl.multiple_of(me * width + c * step, step), step)
        term = jnp.dot(normed, wkv_ref[depth, :], preferred_element_type=jnp.float32)
        if c == 0:
            acc[...] = term
        else:
            acc[...] += term
    keep_ref[...] = acc[pl.ds(pl.multiple_of(me * half, half), half), :]
    send_ref[...] = acc[pl.ds(pl.multiple_of((1 - me) * half, half), half), :]
    load.wait()


def partial_keys(place, tokens, mine, other, wkv, wq):
    rows, width = tokens.shape
    both = 2 * HEAD
    return pl.pallas_call(
        partial_kernel,
        in_specs=[SCALAR] + [WHOLE] * 4 + [HBM],
        out_specs=[WHOLE] * 5,
        out_shape=[
            shaped(tokens.shape, jnp.bfloat16),
            shaped((rows, LANES), jnp.float32),
            shaped((rows // 2, both), jnp.float32),
            shaped((rows // 2, both), jnp.float32),
            shaped(wq.shape, wq.dtype),
        ],
        scratch_shapes=[pltpu.VMEM((rows, both), jnp.float32), pltpu.SemaphoreType.DMA],
        compiler_params=params(16),
        cost_estimate=cost(2 * rows * width * both, wq.size * 2),
        name="partial_keys",
    )(place, tokens, mine, other, wkv, *in_hbm(wq))


def keys_kernel(place_ref, mine_ref, other_ref, cos_ref, sin_ref, kv_ref):
    half = mine_ref.shape[0]
    here = pl.ds(pl.multiple_of(place_ref[0] * half, half), half)
    total = mine_ref[...] + other_ref[...]
    kv_ref[:, :HEAD] = turn(total[:, :HEAD], cos_ref[here, :], sin_ref[here, :])
    kv_ref[:, HEAD:] = total[:, HEAD:].astype(jnp.bfloat16)


def finish_keys(place, mine, other, tables):
    return pl.pallas_call(
        keys_kernel,
        in_specs=[SCALAR] + [WHOLE] * 4,
        out_specs=WHOLE,
        out_shape=shaped(mine.shape, jnp.bfloat16),
        compiler_params=params(8),
        cost_estimate=cost(mine.size * 8, mine.size * 8),
        name="keys",
    )(place, mine, other, *tables)


def queries_own_kernel(place_ref, normed_ref, wq_ref, wout_hbm, acc_ref, wsend_ref, sem):
    width = normed_ref.shape[1]
    me = place_ref[0]
    start = pl.multiple_of((1 - me) * width, width)
    load = pltpu.make_async_copy(wout_hbm.at[:, pl.ds(start, width)], wsend_ref, sem)
    load.start()
    depth = pl.ds(pl.multiple_of(me * width, width), width)
    acc_ref[...] = jnp.dot(normed_ref[...], wq_ref[depth, :], preferred_element_type=jnp.float32)
    load.wait()


def queries_own(place, normed, wq, w_out):
    rows, width = normed.shape
    nq = wq.shape[1]
    return pl.pallas_call(
        queries_own_kernel,
        in_specs=[SCALAR, WHOLE, WHOLE, HBM],
        out_specs=[WHOLE, WHOLE],
        out_shape=[shaped((rows, nq), jnp.float32), shaped((w_out.shape[0], width), w_out.dtype)],
        scratch_shapes=[pltpu.SemaphoreType.DMA],
        compiler_params=params(16),
        cost_estimate=cost(2 * rows * width * nq, w_out.size * 2),
        name="queries_own",
    )(place, normed, wq, *in_hbm(w_out))


def queries_kernel(
    place_ref, acc_ref, tokens_ref, gains_ref, inverse_ref, cos_ref, sin_ref, wq_ref, wout_hbm, q_ref, wkeep_ref, acc, sem
):
    rows, width = tokens_ref.shape
    step = 1024
    me = place_ref[0]
    load = pltpu.make_async_copy(wout_hbm.at[:, pl.ds(pl.multiple_of(me * width, width), width)], wkeep_ref, sem)
    load.start()
    inverse = inverse_ref[...]
    for c in range(width // step):
        normed = normalize(tokens_ref[:, c * step : (c + 1) * step], inverse, gains_ref, rows + c * (step // LANES))
        depth = pl.ds(pl.multiple_of((1 - me) * width + c * step, step), step)
        term = jnp.dot(normed, wq_ref[depth, :], preferred_element_type=jnp.float32)
        if c == 0:
            acc[...] = acc_ref[...] + term
        else:
            acc[...] += term
    for h in range(q_ref.shape[1] // HEAD):
        lanes = slice(h * HEAD, (h + 1) * HEAD)
        q_ref[:, lanes] = turn(acc[:, lanes], cos_ref[...], sin_ref[...])
    load.wait()


def finish_queries(place, acc, tokens_other, sums_other, inverse, tables, wq, w_out):
    rows, width = tokens_other.shape
    nq = wq.shape[1]
    return pl.pallas_call(
        queries_kernel,
        in_specs=[SCALAR] + [WHOLE] * 7 + [HBM],
        out_specs=[WHOLE, WHOLE],
        out_shape=[shaped((rows, nq), jnp.bfloat16), shaped((w_out.shape[0], width), w_out.dtype)],
        scratch_shapes=[pltpu.VMEM((rows, nq), jnp.float32), pltpu.SemaphoreType.DMA],
        compiler_params=params(16),
        cost_estimate=cost(2 * rows * width * nq, w_out.size * 2),
        name="queries",
    )(place, acc, tokens_other, sums_other, inverse, *tables, wq, *in_hbm(w_out))


def attend_kernel(reach, own, place_ref, lengths_ref, q_ref, *rest):
    count = 2 if own else 2 * reach
    blocks = rest[:count]
    rest = rest[count:]
    if own:
        acc, tops, sums, keys, values, stacked, scores = rest
    else:
        acc_ref, tops_ref, sums_ref, ctx_ref, keys, values, stacked, scores, acc, tops, sums = rest
    rows = q_ref.shape[0]
    tall = stacked.shape[0]
    heads = q_ref.shape[1] // HEAD
    tile_rows = tall // heads
    span = scores.shape[2]
    t = pl.program_id(0)

    @pl.when(t == 0)
    def _():
        part = rows // 2
        for b, block in enumerate(blocks):
            which = place_ref[0] if b % 2 == 0 else 1 - place_ref[0]
            at = pl.ds(pl.multiple_of((b // 2) * rows + which * part, part), part)
            keys[at, :] = block[:, :HEAD]
            values[at, :] = block[:, HEAD:]

    behind = 0 if own else reach * rows
    first_row = t * tile_rows
    row = first_row + lax.broadcasted_iota(jnp.int32, (tile_rows, span), 0)
    begin = first_of_document(place_ref, lengths_ref, row) + behind
    row = row + behind
    start = -place_ref[1]
    lowest = start
    for d in range(lengths_ref.shape[0] - 1):
        start = start + lengths_ref[d]
        lowest = jnp.where(first_row >= start, start, lowest)
    lane = lax.broadcasted_iota(jnp.int32, (tile_rows, span), 1)
    if own:
        low = jnp.maximum(lowest, 0) // span
        high = (first_row + tile_rows - 1) // span + 1
    else:
        low = jnp.minimum(lowest + behind, behind) // span
        high = behind // span
    q_rows = pl.ds(pl.multiple_of(first_row, tile_rows), tile_rows)
    for h in range(heads):
        stacked[h * tile_rows : (h + 1) * tile_rows, :] = q_ref[q_rows, h * HEAD : (h + 1) * HEAD]

    if own:
        tops[...] = jnp.full(tops.shape, -1e30, jnp.float32)
        sums[...] = jnp.zeros(sums.shape, jnp.float32)
        acc[...] = jnp.zeros(acc.shape, jnp.float32)
    else:
        tops[...] = tops_ref[...]

    def score(i, carry):
        place = lane + i * span
        allowed = place >= begin
        if own:
            allowed = allowed & (place <= row)
        s = lax.dot_general(
            stacked[...],
            keys[pl.ds(pl.multiple_of(i * span, span), span), :],
            (((1,), (1,)), ((), ())),
            preferred_element_type=jnp.float32,
        )
        for h in range(heads):
            part = slice(h * tile_rows, (h + 1) * tile_rows)
            masked = jnp.where(allowed, s[part, :], -1e30)
            scores[i, part, :] = masked
            top = tops[part, :]
            for j in range(span // LANES):
                top = jnp.maximum(top, masked[:, j * LANES : (j + 1) * LANES])
            tops[part, :] = top
        return carry

    lax.fori_loop(low, high, score, 0)
    top = jnp.max(tops[...], axis=1, keepdims=True)
    tops[...] = jnp.broadcast_to(top, tops.shape)
    if not own:
        rescale = jnp.exp2((tops_ref[...] - tops[...]) * EXP2_SCALE)
        acc[...] = acc_ref[...] * rescale
        sums[...] = sums_ref[...] * rescale

    def weigh(i, carry):
        top = tops[...] * EXP2_SCALE
        total = sums[...]
        rounded = []
        for j in range(span // LANES):
            w = jnp.exp2(scores[i, :, j * LANES : (j + 1) * LANES] * EXP2_SCALE - top)
            total = total + w
            rounded.append(w.astype(jnp.bfloat16))
        sums[...] = total
        acc[...] += jnp.dot(
            jnp.concatenate(rounded, axis=1),
            values[pl.ds(pl.multiple_of(i * span, span), span), :],
            preferred_element_type=jnp.float32,
        )
        return carry

    lax.fori_loop(low, high, weigh, 0)
    if not own:
        for h in range(heads):
            part = slice(h * tile_rows, (h + 1) * tile_rows)
            total = jnp.sum(sums[part, :], axis=1, keepdims=True)
            ctx_ref[:, h * HEAD : (h + 1) * HEAD] = (acc[part, :] / total).astype(jnp.bfloat16)


def attend(place, lengths, queries, blocks, state=None):
    rows, width = queries.shape
    own = state is None
    count = len(blocks) // 2
    tile_rows, span = 128, 512 if not own else 256
    heads = width // HEAD
    places = count * rows
    tall = heads * tile_rows
    state_spec = pl.BlockSpec((tall, LANES), lambda t: (t, 0))
    scratch = [
        pltpu.VMEM((places, HEAD), jnp.bfloat16),
        pltpu.VMEM((places, HEAD), jnp.bfloat16),
        pltpu.VMEM((tall, HEAD), jnp.bfloat16),
        pltpu.VMEM((places // span, tall, span), jnp.float32),
    ]
    in_specs = [SCALAR, SCALAR, WHOLE] + [WHOLE] * len(blocks)
    if own:
        out_specs = [state_spec] * 3
        out_shape = [shaped((heads * rows, LANES), jnp.float32)] * 3
    else:
        in_specs += [state_spec] * 3
        out_specs = pl.BlockSpec((tile_rows, width), lambda t: (t, 0))
        out_shape = shaped((rows, width), jnp.bfloat16)
        scratch += [pltpu.VMEM((tall, LANES), jnp.float32)] * 3
    return pl.pallas_call(
        functools.partial(attend_kernel, count, own),
        grid=(rows // tile_rows,),
        in_specs=in_specs,
        out_specs=out_specs,
        scratch_shapes=scratch,
        out_shape=out_shape,
        compiler_params=params(20),
        cost_estimate=cost(4 * rows * width * places, rows * width * 8),
        name="attend_own" if own else "attend",
    )(place, lengths, queries, *blocks, *(state or ()))


def term_kernel(context_ref, w_ref, term_ref):
    step = 1024
    for c in range(w_ref.shape[1] // step):
        part = slice(c * step, (c + 1) * step)
        term_ref[:, part] = jnp.dot(context_ref[...], w_ref[:, part], preferred_element_type=jnp.float32).astype(jnp.bfloat16)


def group_term(context, w):
    rows, depth = context.shape
    width = w.shape[1]
    return pl.pallas_call(
        term_kernel,
        in_specs=[WHOLE] * 2,
        out_specs=WHOLE,
        out_shape=shaped((rows, width), jnp.bfloat16),
        compiler_params=params(16),
        cost_estimate=cost(2 * rows * depth * width, rows * width * 2),
        name="own_term",
    )(context, w)


def output_kernel(tokens_ref, term_ref, context_ref, w_ref, out_ref):
    step = out_ref.shape[1]
    here = pl.ds(pl.multiple_of(pl.program_id(0) * step, step), step)
    other = jnp.dot(context_ref[...], w_ref[:, here], preferred_element_type=jnp.float32).astype(jnp.bfloat16)
    out = tokens_ref[:, here].astype(jnp.float32) + term_ref[:, here].astype(jnp.float32) + other.astype(jnp.float32)
    out_ref[...] = out.astype(jnp.bfloat16)


def output(tokens, term, context, w):
    rows, width = tokens.shape
    depth = context.shape[1]
    step = 1024
    return pl.pallas_call(
        output_kernel,
        grid=(width // step,),
        in_specs=[WHOLE] * 4,
        out_specs=pl.BlockSpec((rows, step), lambda j: (0, j)),
        out_shape=shaped((rows, width), jnp.bfloat16),
        compiler_params=params(20),
        cost_estimate=cost(2 * rows * width * depth, rows * width * 4),
        name="output",
    )(tokens, term, context, w)


def shift(value, axis, steps):
    count = lax.axis_size(axis)
    return lax.ppermute(value, axis, [(source, source + steps) for source in range(count - steps)])


def swap(value):
    return lax.ppermute(value, "tp", SWAP)


def local(tokens, norm_gain, lengths, w_query, w_key, w_value, w_out):
    rows = tokens.shape[0]
    reach = (rows + MOST - 2) // rows
    place = jnp.stack([lax.axis_index("tp"), lax.axis_index("dp") * rows]).astype(jnp.int32)
    frequency = 500000.0 ** (-jnp.arange(HEAD // 2, dtype=jnp.float32) * 2.0 / HEAD)
    frequency = jnp.concatenate([frequency, frequency])[None, :]

    sums, tokens = squares(place, frequency, norm_gain.reshape(-1, LANES), tokens)
    sums_other = swap(sums)
    wkv, *tables = tables_and_weights(place, lengths, frequency, w_key, w_value, rows)
    normed, inverse, kv_keep, kv_send, wq = partial_keys(place, tokens, sums, sums_other, wkv, w_query)
    kv_come = swap(kv_send)
    tokens, kv_come = lax.optimization_barrier((tokens, kv_come))
    tokens_other = swap(tokens)
    kv = finish_keys(place, kv_keep, kv_come, tables)
    kv, normed = lax.optimization_barrier((kv, normed))
    parts = [shift(kv, "dp", d) for d in range(reach, 0, -1)]
    kv_other = swap(kv)
    acc, w_send = queries_own(place, normed, wq, w_out)
    queries, w_mine = finish_queries(place, acc, tokens_other, sums_other, inverse, tables, wq, w_out)
    state = attend(place, lengths, queries, [kv, kv_other])
    parts, state = lax.optimization_barrier((parts, state))
    blocks = []
    for part in parts:
        blocks += [part, swap(part)]
    w_send, blocks = lax.optimization_barrier((w_send, blocks))
    w_other = swap(w_send)
    context = attend(place, lengths, queries, blocks, state)
    context_other = swap(context)
    term = group_term(context, w_mine)
    return output(tokens, term, context_other, w_other)


def solution(mesh):
    placed = (P(("grp", "dp"), "tp"), P("tp"), P("grp"), P(None, "tp"), P(), P(), P("tp", None))
    return jax.shard_map(
        local, mesh=mesh, in_specs=placed, out_specs=P(("grp", "dp"), "tp"), check_vma=False
    )
```

time: 54.8 us -> 53.5 us (0.976)
  the two profiles are of different devices: /device:TPU:13 before, /device:TPU:0 now
where the time goes in v2:
time: 53.5 us; the launch traced here: 52.8 us
  Pallas kernels  31.3 us (59%)
  starting transfers between devices  14.9 us (28%)
  waiting for transfers between devices  5.58 us (10%)
  local copies, waits for them, and re-layouts  0.7 us (1%)
    ppermute x3, starting transfers between devices, shift(): lax.ppermute(value, axis, [(source, source + steps) for source in range(c...  12.5 us
    pallas_call x2, Pallas kernels, attend(): pl.pallas_call(functools.partial(attend_kernel, count, own), grid=(rows /...  6.54 us
    ppermute x9, waiting for transfers between devices, swap(): return lax.ppermute(value, 'tp', SWAP)  5.57 us
    pallas_call x1, Pallas kernels, finish_queries(): pl.pallas_call(queries_kernel, in_specs=[SCALAR] + [WHOLE] * 7 + [HBM], o...  4.92 us
    pallas_call x1, Pallas kernels, output(): pl.pallas_call(output_kernel, grid=(width // step,), in_specs=[WHOLE] * 4...  4.29 us
    pallas_call x1, Pallas kernels, partial_keys(): pl.pallas_call(partial_kernel, in_specs=[SCALAR] + [WHOLE] * 4 + [HBM], o...  3.93 us
    pallas_call x1, Pallas kernels, squares(): pl.pallas_call(squares_kernel, in_specs=[SCALAR, WHOLE, WHOLE, HBM], out_...  2.97 us
    pallas_call x1, Pallas kernels, queries_own(): pl.pallas_call(queries_own_kernel, in_specs=[SCALAR, WHOLE, WHOLE, HBM],...  2.88 us
  transfers between devices with their start and end apart: 12, of which 5 were waited for; matrix products, arithmetic and copies ran while one was open for 0% of the time, Pallas kernels for 38%

profile of v2, /device:TPU:0, one launch (start us, length us, event | category | flops | bytes accessed | tf_op | source)
XLA Modules:
  0.0 52.8 jit_solution(12029338299260129030)
XLA Ops:
  0.2 0.7 %copy-done = bf16[4096]{0:T(1024)(128)(2,1)S(1)} copy-done((bf16[4096]{0:T(1024)(128)(2,1)S(1)}, bf16[4096]{0:T(1024)(128)(2,1)}, u32[]{:S(2)}) %copy-start) | copy-done | bytes 8216
  0.9 3.0 %squares.1 = (f32[544,128]{1,0:T(8,128)S(1)}, bf16[512,4096]{1,0:T(8,128)(2,1)S(1)}) custom-call(s32[2]{0:T(128)S(1)} %pad_add_fusion.place_ref, f32[1,128]{1,0:T(1,128)S(1)} %maximum_bitcast_fusion.frequency_ref, bf16[32,128]{1,0:T(8,128)(2,1)S(1)} %bitcast.5, bf16[512,4096]{1,0:T(8,128)(2,1)} %tokens_hbm.1), custom_call_target="tpu_custom_call" | custom-call | flops 4194304 | bytes 4194304 | tf_op jit(solution)/shard_map/squares/pallas_call | solution.py:69
  3.8 0.5 collective-permute-start
  4.4 2.8 %tables.1 = (bf16[8192,256]{1,0:T(8,128)(2,1)S(1)}, f32[512,128]{1,0:T(8,128)S(1)}, f32[512,128]{1,0:T(8,128)S(1)}) custom-call(s32[2]{0:T(128)S(1)} %pad_add_fusion.place_ref, s32[8]{0:T(128)S(1)} %copy-done.1, f32[1,128]{1,0:T(1,128)S(1)} %maximum_bitcast_fusion.frequency_ref, bf16[8192,128]{1,0:T(8,128)(2,1)} %wk_hbm.1, bf16[8192,128]{1,0:T(8,128)(2,1)} %wv_hbm.1), custom_call_target="tpu_custom_call" | custom-call | flops 6553600 | bytes 4194304 | tf_op jit(solution)/shard_map/tables/pallas_call | solution.py:99
  7.2 3.9 %partial_keys.1 = (bf16[512,4096]{1,0:T(8,128)(2,1)S(1)}, f32[512,128]{1,0:T(8,128)S(1)}, f32[256,256]{1,0:T(8,128)S(1)}, f32[256,256]{1,0:T(8,128)S(1)}, bf16[8192,512]{1,0:T(8,128)(2,1)S(1)}) custom-call(s32[2]{0:T(128)S(1)} %pad_add_fusion.place_ref, bf16[512,4096]{1,0:T(8,128)(2,1)S(1)} %get-tuple-element.43.tokens_ref, ...), custom_call_target="tpu_custom_call" | custom-call | flops 1073741824 | bytes 8388608 | tf_op jit(solution)/shard_map/partial_keys/pallas_call | solution.py:158
  11.2 1.5 %collective-permute-done.1.other_ref = f32[256,256]{1,0:T(8,128)S(1)} collective-permute-done((f32[256,256]{1,0:T(8,128)S(1)}, f32[256,256]{1,0:T(8,128)S(1)}, u32[]{:S(2)}, u32[]{:S(2)}) %collective-permute-start.1) | collective-permute-done | bytes 262176 | tf_op jit(solution)/shard_map/ppermute | solution.py:453
  12.8 0.6 %keys.1.rest_0_ = bf16[256,256]{1,0:T(8,128)(2,1)S(1)} custom-call(s32[2]{0:T(128)S(1)} %pad_add_fusion.place_ref, f32[256,256]{1,0:T(8,128)S(1)} %get-tuple-element.44.mine_ref, f32[256,256]{1,0:T(8,128)S(1)} %collective-permute-done.1.other_ref, f32[512,128]{1,0:T(8,128)S(1)} %get-tuple-element.46.cos_ref, f32[512,128]{1,0:T(8,128)S(1)} %get-tuple-element.47.sin_ref), custom_call_target="tpu_custom_call" | custom-call | flops 524288 | bytes 524288 | tf_op jit(solution)/shard_map/keys/pallas_call | solution.py:185
  13.5 0.4 collective-permute-start.6
  13.9 5.6 %collective-permute-start.3 = (bf16[256,256]{1,0:T(8,128)(2,1)S(1)}, bf16[256,256]{1,0:T(8,128)(2,1)S(1)}, u32[]{:S(2)}, u32[]{:S(2)}) collective-permute-start(bf16[256,256]{1,0:T(8,128)(2,1)S(1)} %keys.1.rest_0_), channel_id=1, source_target_pairs={{0,6},{2,8},{4,10},{6,12},{8,14},{1,7},{3,9},{5,11},{7,13},{9,15},... | collective-permute-start | bytes 393224 | tf_op jit(solution)/shard_map/ppermute | solution.py:449
  19.5 3.5 %collective-permute-start.4 = (bf16[256,256]{1,0:T(8,128)(2,1)S(1)}, bf16[256,256]{1,0:T(8,128)(2,1)S(1)}, u32[]{:S(2)}, u32[]{:S(2)}) collective-permute-start(bf16[256,256]{1,0:T(8,128)(2,1)S(1)} %keys.1.rest_0_), channel_id=1, source_target_pairs={{0,4},{2,6},{4,8},{6,10},{8,12},{10,14},{1,5},{3,7},{5,9},{7,11},{... | collective-permute-start | bytes 393224 | tf_op jit(solution)/shard_map/ppermute | solution.py:449
  23.0 3.4 %collective-permute-start.5 = (bf16[256,256]{1,0:T(8,128)(2,1)S(1)}, bf16[256,256]{1,0:T(8,128)(2,1)S(1)}, u32[]{:S(2)}, u32[]{:S(2)}) collective-permute-start(bf16[256,256]{1,0:T(8,128)(2,1)S(1)} %keys.1.rest_0_), channel_id=1, source_target_pairs={{0,2},{2,4},{4,6},{6,8},{8,10},{10,12},{12,14},{1,3},{3,5},{5,7},{... | collective-permute-start | bytes 393224 | tf_op jit(solution)/shard_map/ppermute | solution.py:449
  26.4 2.9 %queries_own.1 = (f32[512,512]{1,0:T(8,128)S(1)}, bf16[512,4096]{1,0:T(8,128)(2,1)S(1)}) custom-call(s32[2]{0:T(128)S(1)} %pad_add_fusion.place_ref, bf16[512,4096]{1,0:T(8,128)(2,1)S(1)} %get-tuple-element.49.normed_ref, bf16[8192,512]{1,0:T(8,128)(2,1)S(1)} %get-tuple-element.50.wq_ref, bf16[512,8192]{1,0:T(8,128)(2,1)} %wout_hbm.3), custom_call_target="tpu_custom_call" | custom-call | flops 2147483648 | bytes 8388608 | tf_op jit(solution)/shard_map/queries_own/pallas_call | solution.py:210
  29.3 4.9 %queries.1 = (bf16[512,512]{1,0:T(8,128)(2,1)S(1)}, bf16[512,4096]{1,0:T(8,128)(2,1)S(1)}) custom-call(s32[2]{0:T(128)S(1)} %pad_add_fusion.place_ref, f32[512,512]{1,0:T(8,128)S(1)} %get-tuple-element.51.acc_ref, bf16[512,4096]{1,0:T(8,128)(2,1)S(1)} %collective-permute-done.2.tokens_ref, f32[544,128]{1,0:T(8,128)S(1)} %collective-permute-done.other_ref.gains_ref, ...), custom_call_target="tpu_custom_call" | custom-call | flops 2147483648 | bytes 8388608 | tf_op jit(solution)/shard_map/queries/pallas_call | solution.py:248
  34.3 4.4 %attend_own.1 = (f32[2048,128]{1,0:T(8,128)S(1)}, f32[2048,128]{1,0:T(8,128)S(1)}, f32[2048,128]{1,0:T(8,128)S(1)}) custom-call(s32[2]{0:T(128)S(1)} %pad_add_fusion.place_ref, s32[8]{0:T(128)S(1)} %copy-done.1, bf16[512,512]{1,0:T(8,128)(2,1)S(1)} %get-tuple-element.53.q_ref, bf16[256,256]{1,0:T(8,128)(2,1)S(1)} %keys.1.rest_0_, ...), custom_call_target="tpu_custom_call" | custom-call | flops 536870912 | bytes 2097152 | tf_op jit(solution)/shard_map/attend_own/pallas_call | solution.py:389
  38.8 0.5 collective-permute-start.8
  39.4 0.8 %collective-permute-done.7.rest_1_ = bf16[256,256]{1,0:T(8,128)(2,1)S(1)} collective-permute-done((bf16[256,256]{1,0:T(8,128)(2,1)S(1)}, bf16[256,256]{1,0:T(8,128)(2,1)S(1)}, u32[]{:S(2)}, u32[]{:S(2)}) %collective-permute-start.7) | collective-permute-done | bytes 131104 | tf_op jit(solution)/shard_map/ppermute | solution.py:453
  40.1 0.2 collective-permute-done.8.rest_3_
  40.3 0.3 collective-permute-done.9.rest_5_
  40.6 0.2 collective-permute-start.11
  40.8 2.2 %attend.1.context_ref = bf16[512,512]{1,0:T(8,128)(2,1)S(1)} custom-call(s32[2]{0:T(128)S(1)} %pad_add_fusion.place_ref, s32[8]{0:T(128)S(1)} %copy-done.1, bf16[512,512]{1,0:T(8,128)(2,1)S(1)} %get-tuple-element.53.q_ref, bf16[256,256]{1,0:T(8,128)(2,1)S(1)} %collective-permute-done.3.rest_0_, bf16[256,256]{1,0:T(8,128)(2,1)S(1)} %collective-permute-done.7.rest_1_, ...), custom_call_target="tpu_custom_call" | custom-call | flops 1610612736 | bytes 2097152 | tf_op jit(solution)/shard_map/attend/pallas_call | solution.py:389
  43.0 0.4 collective-permute-start.10
  43.4 2.3 %own_term.1.term_ref = bf16[512,4096]{1,0:T(8,128)(2,1)S(1)} custom-call(bf16[512,512]{1,0:T(8,128)(2,1)S(1)} %attend.1.context_ref, bf16[512,4096]{1,0:T(8,128)(2,1)S(1)} %get-tuple-element.71.w_ref), custom_call_target="tpu_custom_call" | custom-call | flops 2147483648 | bytes 4194304 | tf_op jit(solution)/shard_map/own_term/pallas_call | solution.py:412
  45.7 2.8 %collective-permute-done.10.context_ref = bf16[512,512]{1,0:T(8,128)(2,1)S(1)} collective-permute-done((bf16[512,512]{1,0:T(8,128)(2,1)S(1)}, bf16[512,512]{1,0:T(8,128)(2,1)S(1)}, u32[]{:S(2)}, u32[]{:S(2)}) %collective-permute-start.10) | collective-permute-done | bytes 524320 | tf_op jit(solution)/shard_map/ppermute | solution.py:453
  48.5 4.3 %output.1 = bf16[512,4096]{1,0:T(8,128)(2,1)} custom-call(bf16[512,4096]{1,0:T(8,128)(2,1)S(1)} %get-tuple-element.43.tokens_ref, bf16[512,4096]{1,0:T(8,128)(2,1)S(1)} %own_term.1.term_ref, bf16[512,512]{1,0:T(8,128)(2,1)S(1)} %collective-permute-done.10.context_ref, bf16[512,4096]{1,0:T(8,128)(2,1)S(1)} %collective-permute-done.11.w_ref), custom_call_target="tpu_custom_call" | custom-call | flops 2147483648 | bytes 8388608 | tf_op jit(solution)/shard_map/output/pallas_call | solution.py:435
  (17 shorter events, 0.6 us)
Async XLA Ops:
  0.0 4.4 %copy-start.1 = (s32[8]{0:T(128)S(1)}, s32[8]{0:T(128)}, u32[]{:S(2)}) copy-start(s32[8]{0:T(128)} %lengths_ref.5) | copy-start | bytes 100
  0.2 0.7 %copy-start = (bf16[4096]{0:T(1024)(128)(2,1)S(1)}, bf16[4096]{0:T(1024)(128)(2,1)}, u32[]{:S(2)}) copy-start(bf16[4096]{0:T(1024)(128)(2,1)} %param.8) | copy-start | bytes 24580
  3.8 3.3 %collective-permute-start = (f32[544,128]{1,0:T(8,128)S(1)}, f32[544,128]{1,0:T(8,128)S(1)}, u32[]{:S(2)}, u32[]{:S(2)}) collective-permute-start(f32[544,128]{1,0:T(8,128)S(1)} %get-tuple-element.40.mine_ref), channel_id=1, source_target_pairs={{0,1},{1,0},{2,3},{3,2},{4,5},{5,4},{6,7},{7,6},{8,9},{9,8},{10,11... | collective-permute-start | bytes 835592 | tf_op jit(solution)/shard_map/ppermute | solution.py:453
  11.1 1.6 %collective-permute-start.1 = (f32[256,256]{1,0:T(8,128)S(1)}, f32[256,256]{1,0:T(8,128)S(1)}, u32[]{:S(2)}, u32[]{:S(2)}) collective-permute-start(f32[256,256]{1,0:T(8,128)S(1)} %get-tuple-element.42), channel_id=1, source_target_pairs={{0,1},{1,0},{2,3},{3,2},{4,5},{5,4},{6,7},{7,6},{8,9},{9,8},{10,11... | collective-permute-start | bytes 786440 | tf_op jit(solution)/shard_map/ppermute | solution.py:453
  12.7 16.6 %collective-permute-start.2 = (bf16[512,4096]{1,0:T(8,128)(2,1)S(1)}, bf16[512,4096]{1,0:T(8,128)(2,1)S(1)}, u32[]{:S(2)}, u32[]{:S(2)}) collective-permute-start(bf16[512,4096]{1,0:T(8,128)(2,1)S(1)} %get-tuple-element.43.tokens_ref), channel_id=1, source_target_pairs={{0,1},{1,0},{2,3},{3,2},{4,5},{5,4},{6,7},{7,6},{8,9},{9,8},{10,11... | collective-permute-start | bytes 12582920 | tf_op jit(solution)/shard_map/ppermute | solution.py:453
  13.5 20.8 %collective-permute-start.6 = (bf16[256,256]{1,0:T(8,128)(2,1)S(1)}, bf16[256,256]{1,0:T(8,128)(2,1)S(1)}, u32[]{:S(2)}, u32[]{:S(2)}) collective-permute-start(bf16[256,256]{1,0:T(8,128)(2,1)S(1)} %keys.1.rest_0_), channel_id=1, source_target_pairs={{0,1},{1,0},{2,3},{3,2},{4,5},{5,4},{6,7},{7,6},{8,9},{9,8},{10,11... | collective-permute-start | bytes 393224 | tf_op jit(solution)/shard_map/ppermute | solution.py:453
  13.9 24.7 %collective-permute-start.3 = (bf16[256,256]{1,0:T(8,128)(2,1)S(1)}, bf16[256,256]{1,0:T(8,128)(2,1)S(1)}, u32[]{:S(2)}, u32[]{:S(2)}) collective-permute-start(bf16[256,256]{1,0:T(8,128)(2,1)S(1)} %keys.1.rest_0_), channel_id=1, source_target_pairs={{0,6},{2,8},{4,10},{6,12},{8,14},{1,7},{3,9},{5,11},{7,13},{9,15},... | collective-permute-start | bytes 393224 | tf_op jit(solution)/shard_map/ppermute | solution.py:449
  19.5 19.2 %collective-permute-start.4 = (bf16[256,256]{1,0:T(8,128)(2,1)S(1)}, bf16[256,256]{1,0:T(8,128)(2,1)S(1)}, u32[]{:S(2)}, u32[]{:S(2)}) collective-permute-start(bf16[256,256]{1,0:T(8,128)(2,1)S(1)} %keys.1.rest_0_), channel_id=1, source_target_pairs={{0,4},{2,6},{4,8},{6,10},{8,12},{10,14},{1,5},{3,7},{5,9},{7,11},{... | collective-permute-start | bytes 393224 | tf_op jit(solution)/shard_map/ppermute | solution.py:449
  23.0 15.7 %collective-permute-start.5 = (bf16[256,256]{1,0:T(8,128)(2,1)S(1)}, bf16[256,256]{1,0:T(8,128)(2,1)S(1)}, u32[]{:S(2)}, u32[]{:S(2)}) collective-permute-start(bf16[256,256]{1,0:T(8,128)(2,1)S(1)} %keys.1.rest_0_), channel_id=1, source_target_pairs={{0,2},{2,4},{4,6},{6,8},{8,10},{10,12},{12,14},{1,3},{3,5},{5,7},{... | collective-permute-start | bytes 393224 | tf_op jit(solution)/shard_map/ppermute | solution.py:449
  38.7 1.4 %collective-permute-start.7 = (bf16[256,256]{1,0:T(8,128)(2,1)S(1)}, bf16[256,256]{1,0:T(8,128)(2,1)S(1)}, u32[]{:S(2)}, u32[]{:S(2)}) collective-permute-start(bf16[256,256]{1,0:T(8,128)(2,1)S(1)} %collective-permute-done.3.rest_0_), channel_id=1, source_target_pairs={{0,1},{1,0},{2,3},{3,2},{4,5},{5,4},{6,7},{7,6},{8,9},{9,8},{10,11... | collective-permute-start | bytes 393224 | tf_op jit(solution)/shard_map/ppermute | solution.py:453
  38.8 1.5 %collective-permute-start.8 = (bf16[256,256]{1,0:T(8,128)(2,1)S(1)}, bf16[256,256]{1,0:T(8,128)(2,1)S(1)}, u32[]{:S(2)}, u32[]{:S(2)}) collective-permute-start(bf16[256,256]{1,0:T(8,128)(2,1)S(1)} %collective-permute-done.4.rest_2_), channel_id=1, source_target_pairs={{0,1},{1,0},{2,3},{3,2},{4,5},{5,4},{6,7},{7,6},{8,9},{9,8},{10,11... | collective-permute-start | bytes 393224 | tf_op jit(solution)/shard_map/ppermute | solution.py:453
  39.3 1.3 %collective-permute-start.9 = (bf16[256,256]{1,0:T(8,128)(2,1)S(1)}, bf16[256,256]{1,0:T(8,128)(2,1)S(1)}, u32[]{:S(2)}, u32[]{:S(2)}) collective-permute-start(bf16[256,256]{1,0:T(8,128)(2,1)S(1)} %collective-permute-done.5.rest_4_), channel_id=1, source_target_pairs={{0,1},{1,0},{2,3},{3,2},{4,5},{5,4},{6,7},{7,6},{8,9},{9,8},{10,11... | collective-permute-start | bytes 393224 | tf_op jit(solution)/shard_map/ppermute | solution.py:453
  40.6 7.9 %collective-permute-start.11 = (bf16[512,4096]{1,0:T(8,128)(2,1)S(1)}, bf16[512,4096]{1,0:T(8,128)(2,1)S(1)}, u32[]{:S(2)}, u32[]{:S(2)}) collective-permute-start(bf16[512,4096]{1,0:T(8,128)(2,1)S(1)} %get-tuple-element.72), channel_id=1, source_target_pairs={{0,1},{1,0},{2,3},{3,2},{4,5},{5,4},{6,7},{7,6},{8,9},{9,8},{10,11... | collective-permute-start | bytes 12582920 | tf_op jit(solution)/shard_map/ppermute | solution.py:453
  43.0 5.6 %collective-permute-start.10 = (bf16[512,512]{1,0:T(8,128)(2,1)S(1)}, bf16[512,512]{1,0:T(8,128)(2,1)S(1)}, u32[]{:S(2)}, u32[]{:S(2)}) collective-permute-start(bf16[512,512]{1,0:T(8,128)(2,1)S(1)} %attend.1.context_ref), channel_id=1, source_target_pairs={{0,1},{1,0},{2,3},{3,2},{4,5},{5,4},{6,7},{7,6},{8,9},{9,8},{10,11... | collective-permute-start | bytes 1572872 | tf_op jit(solution)/shard_map/ppermute | solution.py:453

commit v3 on v2

v3 whole, which is shorter than its diff:
```python
import functools
import math

import jax
import jax.numpy as jnp
from jax import lax
from jax.experimental import pallas as pl
from jax.experimental.pallas import tpu as pltpu
from jax.sharding import PartitionSpec as P

HEAD = 128
MOST = 1536
LANES = 128
SWAP = [(0, 1), (1, 0)]
MIB = 1024 * 1024
EXP2_SCALE = math.log2(math.e) / HEAD**0.5

SCALAR = pl.BlockSpec(memory_space=pltpu.SMEM)
WHOLE = pl.BlockSpec(memory_space=pltpu.VMEM)
HBM = pl.BlockSpec(memory_space=pltpu.HBM)


def in_hbm(*arrays):
    return [pltpu.with_memory_space_constraint(array, pltpu.HBM) for array in arrays]


def params(mib):
    return pltpu.CompilerParams(vmem_limit_bytes=mib * MIB)


def cost(flops, moved):
    return pl.CostEstimate(flops=flops, bytes_accessed=moved, transcendentals=0)


def shaped(shape, dtype):
    return jax.ShapeDtypeStruct(shape, dtype)


def first_of_document(place_ref, lengths_ref, row):
    start = -place_ref[1]
    begin = jnp.full(row.shape, start, jnp.int32)
    for d in range(lengths_ref.shape[0] - 1):
        start = start + lengths_ref[d]
        begin = jnp.where(row >= start, start, begin)
    return begin


def squares_kernel(place_ref, frequency_ref, gain_ref, tokens_hbm, sums_ref, tokens_ref, sems):
    rows, width = tokens_ref.shape
    chunks = sems.shape[0]
    step = width // chunks
    loads = []
    for c in range(chunks):
        part = (slice(None), slice(c * step, (c + 1) * step))
        loads.append(pltpu.make_async_copy(tokens_hbm.at[part], tokens_ref.at[part], sems.at[c]))
        loads[c].start()
    sums_ref[rows:, :] = gain_ref[...].astype(jnp.float32)
    for c in range(chunks):
        loads[c].wait()
        total = sums_ref[0:rows, :] if c else jnp.zeros((rows, LANES), jnp.float32)
        for j in range(c * step // LANES, (c + 1) * step // LANES):
            wide = tokens_ref[:, j * LANES : (j + 1) * LANES].astype(jnp.float32)
            total = total + wide * wide
        sums_ref[0:rows, :] = total


def squares(place, frequency, gain, tokens):
    rows, width = tokens.shape
    return pl.pallas_call(
        squares_kernel,
        in_specs=[SCALAR, WHOLE, WHOLE, HBM],
        out_specs=[WHOLE] * 2,
        out_shape=[shaped((rows + gain.shape[0], LANES), jnp.float32), shaped(tokens.shape, tokens.dtype)],
        scratch_shapes=[pltpu.SemaphoreType.DMA((4,))],
        compiler_params=params(16),
        cost_estimate=cost(rows * width * 2, rows * width * 2),
        name="squares",
    )(place, frequency, gain, *in_hbm(tokens))


def tables_kernel(
    place_ref, lengths_ref, frequency_ref, wk_hbm, wv_hbm, wout_hbm, wkv_ref, wsend_ref, cos_ref, sin_ref, sems
):
    width = wsend_ref.shape[1]
    start = pl.multiple_of((1 - place_ref[0]) * width, width)
    loads = [
        pltpu.make_async_copy(wk_hbm, wkv_ref.at[:, :HEAD], sems.at[0]),
        pltpu.make_async_copy(wv_hbm, wkv_ref.at[:, HEAD:], sems.at[1]),
        pltpu.make_async_copy(wout_hbm.at[:, pl.ds(start, width)], wsend_ref, sems.at[2]),
    ]
    for load in loads:
        load.start()
    row = lax.broadcasted_iota(jnp.int32, cos_ref.shape, 0)
    lane = lax.broadcasted_iota(jnp.int32, cos_ref.shape, 1)
    angles = (row - first_of_document(place_ref, lengths_ref, row)).astype(jnp.float32) * frequency_ref[...]
    cos_ref[...] = jnp.cos(angles)
    sine = jnp.sin(angles)
    sin_ref[...] = jnp.where(lane < HEAD // 2, -sine, sine)
    for load in loads:
        load.wait()


def tables_and_weights(place, lengths, frequency, wk, wv, w_out, rows, width):
    return pl.pallas_call(
        tables_kernel,
        in_specs=[SCALAR, SCALAR, WHOLE, HBM, HBM, HBM],
        out_specs=[WHOLE] * 4,
        out_shape=[
            shaped((wk.shape[0], 2 * HEAD), wk.dtype),
            shaped((w_out.shape[0], width), w_out.dtype),
            shaped((rows, HEAD), jnp.float32),
            shaped((rows, HEAD), jnp.float32),
        ],
        scratch_shapes=[pltpu.SemaphoreType.DMA((3,))],
        compiler_params=params(16),
        cost_estimate=cost(rows * HEAD * 100, wk.size * 4 + w_out.size),
        name="tables",
    )(place, lengths, frequency, *in_hbm(wk, wv, w_out))


STEP = 1024


def normalize(out_ref, out_rows, out_column, tokens_ref, rows, column, inverse, gains_ref):
    for j in range(0, STEP, LANES):
        wide = tokens_ref[rows, column + j : column + j + LANES].astype(jnp.float32)
        gain_row = tokens_ref.shape[0] + (column + j) // LANES
        gain = gains_ref[gain_row : gain_row + 1, :]
        out_ref[out_rows, out_column + j : out_column + j + LANES] = (wide * inverse * gain).astype(jnp.bfloat16)


def inverse_norm(mine_ref, other_ref, rows, width):
    mean = jnp.sum(mine_ref[rows, :] + other_ref[rows, :], axis=1, keepdims=True) * (0.5 / width)
    return jnp.broadcast_to(lax.rsqrt(mean + 1e-05), (rows.size, LANES))


def turn(x, cosine, sine):
    return (x * cosine + pltpu.roll(x, HEAD // 2, 1) * sine).astype(jnp.bfloat16)


def keys_kernel(
    place_ref, tokens_ref, tokens_other_ref, mine_ref, other_ref, cos_ref, sin_ref, wkv_ref, wq_hbm, kv_ref, normed_ref, wq_ref, acc, sem
):
    rows, width = tokens_ref.shape
    half = rows // 2
    me = place_ref[0]
    load = pltpu.make_async_copy(wq_hbm, wq_ref, sem)
    load.start()
    here = pl.ds(pl.multiple_of(me * half, half), half)
    inverse = inverse_norm(mine_ref, other_ref, here, width)
    chunks = [
        (tokens, gains, base, column)
        for column in range(0, width, STEP)
        for tokens, gains, base in ((tokens_ref, mine_ref, me), (tokens_other_ref, other_ref, 1 - me))
    ]
    every = slice(None)

    def ready(c):
        tokens, gains, _, column = chunks[c]
        normalize(normed_ref, every, c * STEP, tokens, here, column, inverse, gains)

    ready(0)
    for c, (_, _, base, column) in enumerate(chunks):
        if c + 1 < len(chunks):
            ready(c + 1)
        depth = pl.ds(pl.multiple_of(base * width + column, STEP), STEP)
        term = jnp.dot(normed_ref[:, c * STEP : (c + 1) * STEP], wkv_ref[depth, :], preferred_element_type=jnp.float32)
        if c < 2:
            acc[c] = term
        else:
            acc[c % 2] += term
    total = acc[0] + acc[1]
    kv_ref[:, :HEAD] = turn(total[:, :HEAD], cos_ref[here, :], sin_ref[here, :])
    kv_ref[:, HEAD:] = total[:, HEAD:].astype(jnp.bfloat16)
    load.wait()


def keys_values(place, tokens, tokens_other, sums, sums_other, tables, wkv, wq):
    rows, width = tokens.shape
    half = rows // 2
    both = 2 * HEAD
    return pl.pallas_call(
        keys_kernel,
        in_specs=[SCALAR] + [WHOLE] * 7 + [HBM],
        out_specs=[WHOLE] * 3,
        out_shape=[
            shaped((half, both), jnp.bfloat16),
            shaped((half, 2 * width), jnp.bfloat16),
            shaped(wq.shape, wq.dtype),
        ],
        scratch_shapes=[pltpu.VMEM((2, half, both), jnp.float32), pltpu.SemaphoreType.DMA],
        compiler_params=params(16),
        cost_estimate=cost(2 * rows * width * both, wq.size * 2),
        name="keys",
    )(place, tokens, tokens_other, sums, sums_other, *tables, wkv, *in_hbm(wq))


def queries_kernel(
    place_ref,
    tokens_ref,
    tokens_other_ref,
    mine_ref,
    other_ref,
    normed_ref,
    cos_ref,
    sin_ref,
    wq_ref,
    wout_hbm,
    q_ref,
    wkeep_ref,
    even,
    odd,
    acc,
    sem,
):
    rows, width = tokens_ref.shape
    half = rows // 2
    me = place_ref[0]
    load = pltpu.make_async_copy(wout_hbm.at[:, pl.ds(pl.multiple_of(me * width, width), width)], wkeep_ref, sem)
    load.start()
    here = pl.ds(pl.multiple_of(me * half, half), half)
    there = pl.ds(pl.multiple_of((1 - me) * half, half), half)
    inverse = inverse_norm(mine_ref, other_ref, there, width)
    chunks = [
        (tokens, gains, base, column)
        for column in range(0, width, STEP)
        for tokens, gains, base in ((tokens_ref, mine_ref, me), (tokens_other_ref, other_ref, 1 - me))
    ]
    buffers = (even, odd)

    def ready(c):
        tokens, gains, _, column = chunks[c]
        buffer = buffers[c % 2]
        buffer[:half, :] = normed_ref[:, c * STEP : (c + 1) * STEP]
        normalize(buffer, slice(half, rows), 0, tokens, there, column, inverse, gains)

    ready(0)
    for c, (_, _, base, column) in enumerate(chunks):
        if c + 1 < len(chunks):
            ready(c + 1)
        depth = pl.ds(pl.multiple_of(base * width + column, STEP), STEP)
        term = jnp.dot(buffers[c % 2][...], wq_ref[depth, :], preferred_element_type=jnp.float32)
        if c == 0:
            acc[...] = term
        else:
            acc[...] += term
    for at, part in ((here, slice(0, half)), (there, slice(half, rows))):
        for h in range(q_ref.shape[1] // HEAD):
            lanes = slice(h * HEAD, (h + 1) * HEAD)
            q_ref[at, lanes] = turn(acc[part, lanes], cos_ref[at, :], sin_ref[at, :])
    load.wait()


def project_queries(place, tokens, tokens_other, sums, sums_other, normed, tables, wq, w_out):
    rows, width = tokens.shape
    nq = wq.shape[1]
    return pl.pallas_call(
        queries_kernel,
        in_specs=[SCALAR] + [WHOLE] * 8 + [HBM],
        out_specs=[WHOLE, WHOLE],
        out_shape=[shaped((rows, nq), jnp.bfloat16), shaped((w_out.shape[0], width), w_out.dtype)],
        scratch_shapes=[pltpu.VMEM((rows, STEP), jnp.bfloat16)] * 2
        + [pltpu.VMEM((rows, nq), jnp.float32), pltpu.SemaphoreType.DMA],
        compiler_params=params(16),
        cost_estimate=cost(4 * rows * width * nq, w_out.size),
        name="queries",
    )(place, tokens, tokens_other, sums, sums_other, normed, *tables, wq, *in_hbm(w_out))


TILE = 128


def attend_kernel(own, place_ref, lengths_ref, q_ref, *rest):
    if own:
        blocks, (acc_out, tops_out, sums_out, keys, values, stacked, scores) = rest[:2], rest[2:]
    else:
        blocks, (acc_in, tops_in, sums_in, ctx_ref, keys, values, stacked, scores, acc, tops, sums) = rest[:-11], rest[-11:]
    rows = q_ref.shape[0]
    heads = q_ref.shape[1] // HEAD
    tall = heads * TILE
    span = scores.shape[2]
    part = rows // 2
    for b, block in enumerate(blocks):
        which = place_ref[0] if b % 2 == 0 else 1 - place_ref[0]
        at = pl.ds(pl.multiple_of((b // 2) * rows + which * part, part), part)
        keys[at, :] = block[:, :HEAD]
        values[at, :] = block[:, HEAD:]
    behind = 0 if own else len(blocks) // 2 * rows
    lane = lax.broadcasted_iota(jnp.int32, (TILE, span), 1)

    def tile(t, carry):
        first_row = t * TILE
        state = pl.ds(pl.multiple_of(t * tall, tall), tall)
        q_rows = pl.ds(pl.multiple_of(first_row, TILE), TILE)
        row = first_row + lax.broadcasted_iota(jnp.int32, (TILE, span), 0)
        begin = first_of_document(place_ref, lengths_ref, row) + behind
        row = row + behind
        start = -place_ref[1]
        lowest = start
        for d in range(lengths_ref.shape[0] - 1):
            start = start + lengths_ref[d]
            lowest = jnp.where(first_row >= start, start, lowest)
        if own:
            acc, tops, sums = acc_out.at[state, :], tops_out.at[state, :], sums_out.at[state, :]
            low = jnp.maximum(lowest, 0) // span
            high = (first_row + TILE - 1) // span + 1
            tops[...] = jnp.full((tall, LANES), -1e30, jnp.float32)
            sums[...] = jnp.zeros((tall, LANES), jnp.float32)
            acc[...] = jnp.zeros((tall, HEAD), jnp.float32)
        else:
            acc, tops, sums = rest[-3:]
            low = jnp.minimum(lowest + behind, behind) // span
            high = behind // span

        def score(i, carry):
            place = lane + i * span
            allowed = place >= begin
            if own:
                allowed = allowed & (place <= row)
            s = lax.dot_general(
                stacked[...],
                keys[pl.ds(pl.multiple_of(i * span, span), span), :],
                (((1,), (1,)), ((), ())),
                preferred_element_type=jnp.float32,
            )
            for h in range(heads):
                block = slice(h * TILE, (h + 1) * TILE)
                masked = jnp.where(allowed, s[block, :], -1e30)
                scores[i, block, :] = masked
                top = tops[block, :]
                for j in range(0, span, LANES):
                    top = jnp.maximum(top, masked[:, j : j + LANES])
                tops[block, :] = top
            return carry

        def weigh(i, carry):
            top = tops[...] * EXP2_SCALE
            total = sums[...]
            rounded = []
            for j in range(0, span, LANES):
                w = jnp.exp2(scores[i, :, j : j + LANES] * EXP2_SCALE - top)
                total = total + w
                rounded.append(w.astype(jnp.bfloat16))
            sums[...] = total
            acc[...] += jnp.dot(
                jnp.concatenate(rounded, axis=1),
                values[pl.ds(pl.multiple_of(i * span, span), span), :],
                preferred_element_type=jnp.float32,
            )
            return carry

        def finish(acc_ref, sums_ref):
            for h in range(heads):
                block = slice(h * TILE, (h + 1) * TILE)
                total = jnp.sum(sums_ref[block, :], axis=1, keepdims=True)
                ctx_ref[q_rows, h * HEAD : (h + 1) * HEAD] = (acc_ref[block, :] / total).astype(jnp.bfloat16)

        def work():
            for h in range(heads):
                stacked[h * TILE : (h + 1) * TILE, :] = q_ref[q_rows, h * HEAD : (h + 1) * HEAD]
            if not own:
                tops[...] = tops_in[state, :]
            lax.fori_loop(low, high, score, 0)
            top = jnp.max(tops[...], axis=1, keepdims=True)
            tops[...] = jnp.broadcast_to(top, (tall, LANES))
            if not own:
                rescale = jnp.exp2((tops_in[state, :] - tops[...]) * EXP2_SCALE)
                acc[...] = acc_in[state, :] * rescale
                sums[...] = sums_in[state, :] * rescale
            lax.fori_loop(low, high, weigh, 0)

        if own:
            work()
        else:

            @pl.when(low < high)
            def _():
                work()
                finish(acc, sums)

            @pl.when(low >= high)
            def _():
                finish(acc_in.at[state, :], sums_in.at[state, :])

        return carry

    lax.fori_loop(0, rows // TILE, tile, 0)


def attend(place, lengths, queries, blocks, state=None):
    rows, width = queries.shape
    own = state is None
    places = len(blocks) // 2 * rows
    span = 256 if own else 512
    heads = width // HEAD
    tall = heads * TILE
    scratch = [
        pltpu.VMEM((places, HEAD), jnp.bfloat16),
        pltpu.VMEM((places, HEAD), jnp.bfloat16),
        pltpu.VMEM((tall, HEAD), jnp.bfloat16),
        pltpu.VMEM((places // span, tall, span), jnp.float32),
    ]
    if own:
        out_shape = [shaped((heads * rows, LANES), jnp.float32)] * 3
    else:
        out_shape = shaped((rows, width), jnp.bfloat16)
        scratch += [pltpu.VMEM((tall, LANES), jnp.float32)] * 3
    return pl.pallas_call(
        functools.partial(attend_kernel, own),
        in_specs=[SCALAR, SCALAR] + [WHOLE] * (1 + len(blocks) + (0 if own else 3)),
        out_specs=[WHOLE] * 3 if own else WHOLE,
        scratch_shapes=scratch,
        out_shape=out_shape,
        compiler_params=params(20),
        cost_estimate=cost(4 * rows * width * places, rows * width * 8),
        name="attend_own" if own else "attend",
    )(place, lengths, queries, *blocks, *(state or ()))


def term_kernel(context_ref, w_ref, term_ref):
    step = 1024
    for c in range(w_ref.shape[1] // step):
        part = slice(c * step, (c + 1) * step)
        term_ref[:, part] = jnp.dot(context_ref[...], w_ref[:, part], preferred_element_type=jnp.float32).astype(jnp.bfloat16)


def group_term(context, w):
    rows, depth = context.shape
    width = w.shape[1]
    return pl.pallas_call(
        term_kernel,
        in_specs=[WHOLE] * 2,
        out_specs=WHOLE,
        out_shape=shaped((rows, width), jnp.bfloat16),
        compiler_params=params(16),
        cost_estimate=cost(2 * rows * depth * width, rows * width * 2),
        name="own_term",
    )(context, w)


def output_kernel(tokens_ref, term_ref, context_ref, w_ref, out_ref):
    step = out_ref.shape[1]
    here = pl.ds(pl.multiple_of(pl.program_id(0) * step, step), step)
    other = jnp.dot(context_ref[...], w_ref[:, here], preferred_element_type=jnp.float32).astype(jnp.bfloat16)
    out = tokens_ref[:, here].astype(jnp.float32) + term_ref[:, here].astype(jnp.float32) + other.astype(jnp.float32)
    out_ref[...] = out.astype(jnp.bfloat16)


def output(tokens, term, context, w):
    rows, width = tokens.shape
    depth = context.shape[1]
    step = 1024
    return pl.pallas_call(
        output_kernel,
        grid=(width // step,),
        in_specs=[WHOLE] * 4,
        out_specs=pl.BlockSpec((rows, step), lambda j: (0, j)),
        out_shape=shaped((rows, width), jnp.bfloat16),
        compiler_params=params(20),
        cost_estimate=cost(2 * rows * width * depth, rows * width * 4),
        name="output",
    )(tokens, term, context, w)


def shift(value, axis, steps):
    count = lax.axis_size(axis)
    return lax.ppermute(value, axis, [(source, source + steps) for source in range(count - steps)])


def swap(value):
    return lax.ppermute(value, "tp", SWAP)


def local(tokens, norm_gain, lengths, w_query, w_key, w_value, w_out):
    rows = tokens.shape[0]
    reach = (rows + MOST - 2) // rows
    place = jnp.stack([lax.axis_index("tp"), lax.axis_index("dp") * rows]).astype(jnp.int32)
    frequency = 500000.0 ** (-jnp.arange(HEAD // 2, dtype=jnp.float32) * 2.0 / HEAD)
    frequency = jnp.concatenate([frequency, frequency])[None, :]

    tokens_other = swap(tokens)
    sums, tokens = squares(place, frequency, norm_gain.reshape(-1, LANES), tokens)
    sums_other = swap(sums)
    wkv, w_send, *tables = tables_and_weights(place, lengths, frequency, w_key, w_value, w_out, rows, tokens.shape[1])
    kv, normed, wq = keys_values(place, tokens, tokens_other, sums, sums_other, tables, wkv, w_query)
    kv, normed = lax.optimization_barrier((kv, normed))
    parts = [shift(kv, "dp", d) for d in range(reach, 0, -1)]
    kv_other = swap(kv)
    queries, w_mine = project_queries(place, tokens, tokens_other, sums, sums_other, normed, tables, wq, w_out)
    state = attend(place, lengths, queries, [kv, kv_other])
    parts, state = lax.optimization_barrier((parts, state))
    blocks = []
    for part in parts:
        blocks += [part, swap(part)]
    blocks, w_send = lax.optimization_barrier((blocks, w_send))
    w_other = swap(w_send)
    context = attend(place, lengths, queries, blocks, state)
    context_other = swap(context)
    term = group_term(context, w_mine)
    return output(tokens, term, context_other, w_other)


def solution(mesh):
    placed = (P(("grp", "dp"), "tp"), P("tp"), P("grp"), P(None, "tp"), P(), P(), P("tp", None))
    return jax.shard_map(
        local, mesh=mesh, in_specs=placed, out_specs=P(("grp", "dp"), "tp"), check_vma=False
    )
```

time: 53.5 us -> 56.6 us (1.058)
  Pallas kernels: 31.3 us -> 35.6 us
  waiting for transfers between devices: 5.58 us -> 4.79 us
    pallas_call x7 -> x5, Pallas kernels: 21.7 us -> 26 us  [the longest x1 9.2 us: project_queries(): pl.pallas_call(queries_kernel, in_specs=[SCALAR] + [WHOLE] * 8 + [HBM], o...]
    ppermute x9 -> x8, waiting for transfers between devices: 5.57 us -> 4.78 us  [swap(): return lax.ppermute(value, 'tp', SWAP)]
    ppermute x9 -> x8, starting transfers between devices: 2.44 us -> 2.31 us  [swap(): return lax.ppermute(value, 'tp', SWAP)]
  transfers between devices with their start and end apart: 12 -> 11, of which waited for: 5 -> 4; matrix products, arithmetic and copies ran while one was open for 0% -> 0% of each run, Pallas kernels for 38% -> 43%
where the time goes in v3:
time: 56.6 us; the launch traced here: 56.3 us
  Pallas kernels  35.6 us (63%)
  starting transfers between devices  14.9 us (26%)
  waiting for transfers between devices  4.79 us (8%)
  local copies, waits for them, and re-layouts  0.7 us (1%)
    ppermute x3, starting transfers between devices, shift(): lax.ppermute(value, axis, [(source, source + steps) for source in range(c...  12.5 us
    pallas_call x1, Pallas kernels, project_queries(): pl.pallas_call(queries_kernel, in_specs=[SCALAR] + [WHOLE] * 8 + [HBM], o...  9.2 us
    pallas_call x1, Pallas kernels, keys_values(): pl.pallas_call(keys_kernel, in_specs=[SCALAR] + [WHOLE] * 7 + [HBM], out_...  6.99 us
    pallas_call x2, Pallas kernels, attend(): pl.pallas_call(functools.partial(attend_kernel, own), in_specs=[SCALAR, S...  5.82 us
    ppermute x8, waiting for transfers between devices, swap(): return lax.ppermute(value, 'tp', SWAP)  4.78 us
    pallas_call x1, Pallas kernels, output(): pl.pallas_call(output_kernel, grid=(width // step,), in_specs=[WHOLE] * 4...  4.26 us
    pallas_call x1, Pallas kernels, tables_and_weights(): pl.pallas_call(tables_kernel, in_specs=[SCALAR, SCALAR, WHOLE, HBM, HBM,...  4.03 us
    pallas_call x1, Pallas kernels, squares(): pl.pallas_call(squares_kernel, in_specs=[SCALAR, WHOLE, WHOLE, HBM], out_...  2.97 us
  transfers between devices with their start and end apart: 11, of which 4 were waited for; matrix products, arithmetic and copies ran while one was open for 0% of the time, Pallas kernels for 43%

profile of v3, /device:TPU:0, one launch (start us, length us, event | category | flops | bytes accessed | tf_op | source)
XLA Modules:
  0.0 56.3 jit_solution(16594041521386166151)
XLA Ops:
  0.0 0.5 collective-permute-start
  0.5 0.1 maximum_bitcast_fusion.frequency_ref
  0.6 0.7 %copy-done = bf16[4096]{0:T(1024)(128)(2,1)S(1)} copy-done((bf16[4096]{0:T(1024)(128)(2,1)S(1)}, bf16[4096]{0:T(1024)(128)(2,1)}, u32[]{:S(2)}) %copy-start) | copy-done | bytes 8216
  1.3 3.0 %squares.1 = (f32[544,128]{1,0:T(8,128)S(1)}, bf16[512,4096]{1,0:T(8,128)(2,1)S(1)}) custom-call(s32[2]{0:T(128)S(1)} %pad_add_fusion.place_ref, f32[1,128]{1,0:T(1,128)S(1)} %maximum_bitcast_fusion.frequency_ref, bf16[32,128]{1,0:T(8,128)(2,1)S(1)} %bitcast.5, bf16[512,4096]{1,0:T(8,128)(2,1)} %tokens_hbm.1), custom_call_target="tpu_custom_call" | custom-call | flops 4194304 | bytes 4194304 | tf_op jit(solution)/shard_map/squares/pallas_call | solution.py:69
  4.3 0.1 collective-permute-start.1
  4.4 4.0 %tables.1 = (bf16[8192,256]{1,0:T(8,128)(2,1)S(1)}, bf16[512,4096]{1,0:T(8,128)(2,1)S(1)}, f32[512,128]{1,0:T(8,128)S(1)}, f32[512,128]{1,0:T(8,128)S(1)}) custom-call(s32[2]{0:T(128)S(1)} %pad_add_fusion.place_ref, s32[8]{0:T(128)S(1)} %copy-done.1, f32[1,128]{1,0:T(1,128)S(1)} %maximum_bitcast_fusion.frequency_ref, bf16[8192,128]{1,0:T(8,128)(2,1)} %wk_hbm.1, ...), custom_call_target="tpu_custom_call" | custom-call | flops 6553600 | bytes 8388608 | tf_op jit(solution)/shard_map/tables/pallas_call | solution.py:104
  8.5 7.0 %keys.1 = (bf16[256,256]{1,0:T(8,128)(2,1)S(1)}, bf16[256,8192]{1,0:T(8,128)(2,1)S(1)}, bf16[8192,512]{1,0:T(8,128)(2,1)S(1)}) custom-call(s32[2]{0:T(128)S(1)} %pad_add_fusion.place_ref, bf16[512,4096]{1,0:T(8,128)(2,1)S(1)} %get-tuple-element.34.tokens_ref, bf16[512,4096]{1,0:T(8,128)(2,1)} %collective-permute-done.tokens_other_ref, ...), custom_call_target="tpu_custom_call" | custom-call | flops 1073741824 | bytes 8388608 | tf_op jit(solution)/shard_map/keys/pallas_call | solution.py:182
  15.5 0.5 collective-permute-start.5
  16.0 4.4 %collective-permute-start.4 = (bf16[256,256]{1,0:T(8,128)(2,1)S(1)}, bf16[256,256]{1,0:T(8,128)(2,1)S(1)}, u32[]{:S(2)}, u32[]{:S(2)}) collective-permute-start(bf16[256,256]{1,0:T(8,128)(2,1)S(1)} %get-tuple-element.44.rest_0_), channel_id=1, source_target_pairs={{0,2},{2,4},{4,6},{6,8},{8,10},{10,12},{12,14},{1,3},{3,5},{5,7},{... | collective-permute-start | bytes 393224 | tf_op jit(solution)/shard_map/ppermute | solution.py:467
  20.4 3.5 %collective-permute-start.3 = (bf16[256,256]{1,0:T(8,128)(2,1)S(1)}, bf16[256,256]{1,0:T(8,128)(2,1)S(1)}, u32[]{:S(2)}, u32[]{:S(2)}) collective-permute-start(bf16[256,256]{1,0:T(8,128)(2,1)S(1)} %get-tuple-element.44.rest_0_), channel_id=1, source_target_pairs={{0,4},{2,6},{4,8},{6,10},{8,12},{10,14},{1,5},{3,7},{5,9},{7,11},{... | collective-permute-start | bytes 393224 | tf_op jit(solution)/shard_map/ppermute | solution.py:467
  23.9 4.6 %collective-permute-start.2 = (bf16[256,256]{1,0:T(8,128)(2,1)S(1)}, bf16[256,256]{1,0:T(8,128)(2,1)S(1)}, u32[]{:S(2)}, u32[]{:S(2)}) collective-permute-start(bf16[256,256]{1,0:T(8,128)(2,1)S(1)} %get-tuple-element.44.rest_0_), channel_id=1, source_target_pairs={{0,6},{2,8},{4,10},{6,12},{8,14},{1,7},{3,9},{5,11},{7,13},{9,15},... | collective-permute-start | bytes 393224 | tf_op jit(solution)/shard_map/ppermute | solution.py:467
  28.6 9.2 %queries.1 = (bf16[512,512]{1,0:T(8,128)(2,1)S(1)}, bf16[512,4096]{1,0:T(8,128)(2,1)S(1)}) custom-call(s32[2]{0:T(128)S(1)} %pad_add_fusion.place_ref, bf16[512,4096]{1,0:T(8,128)(2,1)S(1)} %get-tuple-element.34.tokens_ref, bf16[512,4096]{1,0:T(8,128)(2,1)} %collective-permute-done.tokens_other_ref, f32[544,128]{1,0:T(8,128)S(1)} %get-tuple-element.35.mine_ref, ...), custom_call_target="tpu_custom_call" | custom-call | flops 4294967296 | bytes 4194304 | tf_op jit(solution)/shard_map/queries/pallas_call | solution.py:257
  37.8 4.4 %attend_own.1 = (f32[2048,128]{1,0:T(8,128)S(1)}, f32[2048,128]{1,0:T(8,128)S(1)}, f32[2048,128]{1,0:T(8,128)S(1)}) custom-call(s32[2]{0:T(128)S(1)} %pad_add_fusion.place_ref, s32[8]{0:T(128)S(1)} %copy-done.1, bf16[512,512]{1,0:T(8,128)(2,1)S(1)} %get-tuple-element.43.q_ref, bf16[256,256]{1,0:T(8,128)(2,1)S(1)} %get-tuple-element.44.rest_0_, ...), custom_call_target="tpu_custom_call" | custom-call | flops 536870912 | bytes 2097152 | tf_op jit(solution)/shard_map/attend_own/pallas_call | solution.py:408
  42.3 0.5 collective-permute-start.7
  42.8 0.1 collective-permute-start.8
  42.8 0.8 %collective-permute-done.6.rest_1_ = bf16[256,256]{1,0:T(8,128)(2,1)S(1)} collective-permute-done((bf16[256,256]{1,0:T(8,128)(2,1)S(1)}, bf16[256,256]{1,0:T(8,128)(2,1)S(1)}, u32[]{:S(2)}, u32[]{:S(2)}) %collective-permute-start.6) | collective-permute-done | bytes 131104 | tf_op jit(solution)/shard_map/ppermute | solution.py:471
  43.6 0.2 collective-permute-done.7.rest_3_
  43.8 0.3 collective-permute-done.8.rest_5_
  44.1 0.2 collective-permute-start.10
  44.3 1.4 %attend.1.context_ref = bf16[512,512]{1,0:T(8,128)(2,1)S(1)} custom-call(s32[2]{0:T(128)S(1)} %pad_add_fusion.place_ref, s32[8]{0:T(128)S(1)} %copy-done.1, bf16[512,512]{1,0:T(8,128)(2,1)S(1)} %get-tuple-element.43.q_ref, bf16[256,256]{1,0:T(8,128)(2,1)S(1)} %collective-permute-done.2.rest_0_, bf16[256,256]{1,0:T(8,128)(2,1)S(1)} %collective-permute-done.6.rest_1_, ...), custom_call_target="tpu_custom_call" | custom-call | flops 1610612736 | bytes 2097152 | tf_op jit(solution)/shard_map/attend/pallas_call | solution.py:408
  45.8 0.4 collective-permute-start.9
  46.1 2.4 %own_term.1.term_ref = bf16[512,4096]{1,0:T(8,128)(2,1)S(1)} custom-call(bf16[512,512]{1,0:T(8,128)(2,1)S(1)} %attend.1.context_ref, bf16[512,4096]{1,0:T(8,128)(2,1)S(1)} %get-tuple-element.61.w_ref), custom_call_target="tpu_custom_call" | custom-call | flops 2147483648 | bytes 4194304 | tf_op jit(solution)/shard_map/own_term/pallas_call | solution.py:430
  48.5 3.5 %collective-permute-done.9.context_ref = bf16[512,512]{1,0:T(8,128)(2,1)S(1)} collective-permute-done((bf16[512,512]{1,0:T(8,128)(2,1)S(1)}, bf16[512,512]{1,0:T(8,128)(2,1)S(1)}, u32[]{:S(2)}, u32[]{:S(2)}) %collective-permute-start.9) | collective-permute-done | bytes 524320 | tf_op jit(solution)/shard_map/ppermute | solution.py:471
  52.0 4.3 %output.1 = bf16[512,4096]{1,0:T(8,128)(2,1)} custom-call(bf16[512,4096]{1,0:T(8,128)(2,1)S(1)} %get-tuple-element.34.tokens_ref, bf16[512,4096]{1,0:T(8,128)(2,1)S(1)} %own_term.1.term_ref, bf16[512,512]{1,0:T(8,128)(2,1)S(1)} %collective-permute-done.9.context_ref, bf16[512,4096]{1,0:T(8,128)(2,1)S(1)} %collective-permute-done.10.w_ref), custom_call_target="tpu_custom_call" | custom-call | flops 2147483648 | bytes 8388608 | tf_op jit(solution)/shard_map/output/pallas_call | solution.py:453
  (13 shorter events, 0.2 us)
Async XLA Ops:
  0.0 4.4 %copy-start.1 = (s32[8]{0:T(128)S(1)}, s32[8]{0:T(128)}, u32[]{:S(2)}) copy-start(s32[8]{0:T(128)} %lengths_ref.5) | copy-start | bytes 100
  0.0 8.5 %collective-permute-start = (bf16[512,4096]{1,0:T(8,128)(2,1)}, bf16[512,4096]{1,0:T(8,128)(2,1)}, u32[]{:S(2)}, u32[]{:S(2)}) collective-permute-start(bf16[512,4096]{1,0:T(8,128)(2,1)} %tokens_hbm.1), channel_id=1, source_target_pairs={{0,1},{1,0},{2,3},{3,2},{4,5},{5,4},{6,7},{7,6},{8,9},{9,8},{10,11... | collective-permute-start | bytes 12582920 | tf_op jit(solution)/shard_map/ppermute | solution.py:471
  0.6 0.7 %copy-start = (bf16[4096]{0:T(1024)(128)(2,1)S(1)}, bf16[4096]{0:T(1024)(128)(2,1)}, u32[]{:S(2)}) copy-start(bf16[4096]{0:T(1024)(128)(2,1)} %param.8) | copy-start | bytes 24580
  4.3 4.2 %collective-permute-start.1 = (f32[544,128]{1,0:T(8,128)S(1)}, f32[544,128]{1,0:T(8,128)S(1)}, u32[]{:S(2)}, u32[]{:S(2)}) collective-permute-start(f32[544,128]{1,0:T(8,128)S(1)} %get-tuple-element.35.mine_ref), channel_id=1, source_target_pairs={{0,1},{1,0},{2,3},{3,2},{4,5},{5,4},{6,7},{7,6},{8,9},{9,8},{10,11... | collective-permute-start | bytes 835592 | tf_op jit(solution)/shard_map/ppermute | solution.py:471
  15.5 22.3 %collective-permute-start.5 = (bf16[256,256]{1,0:T(8,128)(2,1)S(1)}, bf16[256,256]{1,0:T(8,128)(2,1)S(1)}, u32[]{:S(2)}, u32[]{:S(2)}) collective-permute-start(bf16[256,256]{1,0:T(8,128)(2,1)S(1)} %get-tuple-element.44.rest_0_), channel_id=1, source_target_pairs={{0,1},{1,0},{2,3},{3,2},{4,5},{5,4},{6,7},{7,6},{8,9},{9,8},{10,11... | collective-permute-start | bytes 393224 | tf_op jit(solution)/shard_map/ppermute | solution.py:471
  16.0 26.2 %collective-permute-start.4 = (bf16[256,256]{1,0:T(8,128)(2,1)S(1)}, bf16[256,256]{1,0:T(8,128)(2,1)S(1)}, u32[]{:S(2)}, u32[]{:S(2)}) collective-permute-start(bf16[256,256]{1,0:T(8,128)(2,1)S(1)} %get-tuple-element.44.rest_0_), channel_id=1, source_target_pairs={{0,2},{2,4},{4,6},{6,8},{8,10},{10,12},{12,14},{1,3},{3,5},{5,7},{... | collective-permute-start | bytes 393224 | tf_op jit(solution)/shard_map/ppermute | solution.py:467
  20.4 21.7 %collective-permute-start.3 = (bf16[256,256]{1,0:T(8,128)(2,1)S(1)}, bf16[256,256]{1,0:T(8,128)(2,1)S(1)}, u32[]{:S(2)}, u32[]{:S(2)}) collective-permute-start(bf16[256,256]{1,0:T(8,128)(2,1)S(1)} %get-tuple-element.44.rest_0_), channel_id=1, source_target_pairs={{0,4},{2,6},{4,8},{6,10},{8,12},{10,14},{1,5},{3,7},{5,9},{7,11},{... | collective-permute-start | bytes 393224 | tf_op jit(solution)/shard_map/ppermute | solution.py:467
  23.9 18.2 %collective-permute-start.2 = (bf16[256,256]{1,0:T(8,128)(2,1)S(1)}, bf16[256,256]{1,0:T(8,128)(2,1)S(1)}, u32[]{:S(2)}, u32[]{:S(2)}) collective-permute-start(bf16[256,256]{1,0:T(8,128)(2,1)S(1)} %get-tuple-element.44.rest_0_), channel_id=1, source_target_pairs={{0,6},{2,8},{4,10},{6,12},{8,14},{1,7},{3,9},{5,11},{7,13},{9,15},... | collective-permute-start | bytes 393224 | tf_op jit(solution)/shard_map/ppermute | solution.py:467
  42.2 1.4 %collective-permute-start.6 = (bf16[256,256]{1,0:T(8,128)(2,1)S(1)}, bf16[256,256]{1,0:T(8,128)(2,1)S(1)}, u32[]{:S(2)}, u32[]{:S(2)}) collective-permute-start(bf16[256,256]{1,0:T(8,128)(2,1)S(1)} %collective-permute-done.2.rest_0_), channel_id=1, source_target_pairs={{0,1},{1,0},{2,3},{3,2},{4,5},{5,4},{6,7},{7,6},{8,9},{9,8},{10,11... | collective-permute-start | bytes 393224 | tf_op jit(solution)/shard_map/ppermute | solution.py:471
  42.3 1.5 %collective-permute-start.7 = (bf16[256,256]{1,0:T(8,128)(2,1)S(1)}, bf16[256,256]{1,0:T(8,128)(2,1)S(1)}, u32[]{:S(2)}, u32[]{:S(2)}) collective-permute-start(bf16[256,256]{1,0:T(8,128)(2,1)S(1)} %collective-permute-done.3.rest_2_), channel_id=1, source_target_pairs={{0,1},{1,0},{2,3},{3,2},{4,5},{5,4},{6,7},{7,6},{8,9},{9,8},{10,11... | collective-permute-start | bytes 393224 | tf_op jit(solution)/shard_map/ppermute | solution.py:471
  42.8 1.3 %collective-permute-start.8 = (bf16[256,256]{1,0:T(8,128)(2,1)S(1)}, bf16[256,256]{1,0:T(8,128)(2,1)S(1)}, u32[]{:S(2)}, u32[]{:S(2)}) collective-permute-start(bf16[256,256]{1,0:T(8,128)(2,1)S(1)} %collective-permute-done.4.rest_4_), channel_id=1, source_target_pairs={{0,1},{1,0},{2,3},{3,2},{4,5},{5,4},{6,7},{7,6},{8,9},{9,8},{10,11... | collective-permute-start | bytes 393224 | tf_op jit(solution)/shard_map/ppermute | solution.py:471
  44.1 7.9 %collective-permute-start.10 = (bf16[512,4096]{1,0:T(8,128)(2,1)S(1)}, bf16[512,4096]{1,0:T(8,128)(2,1)S(1)}, u32[]{:S(2)}, u32[]{:S(2)}) collective-permute-start(bf16[512,4096]{1,0:T(8,128)(2,1)S(1)} %get-tuple-element.62), channel_id=1, source_target_pairs={{0,1},{1,0},{2,3},{3,2},{4,5},{5,4},{6,7},{7,6},{8,9},{9,8},{10,11... | collective-permute-start | bytes 12582920 | tf_op jit(solution)/shard_map/ppermute | solution.py:471
  45.8 6.3 %collective-permute-start.9 = (bf16[512,512]{1,0:T(8,128)(2,1)S(1)}, bf16[512,512]{1,0:T(8,128)(2,1)S(1)}, u32[]{:S(2)}, u32[]{:S(2)}) collective-permute-start(bf16[512,512]{1,0:T(8,128)(2,1)S(1)} %attend.1.context_ref), channel_id=1, source_target_pairs={{0,1},{1,0},{2,3},{3,2},{4,5},{5,4},{6,7},{7,6},{8,9},{9,8},{10,11... | collective-permute-start | bytes 1572872 | tf_op jit(solution)/shard_map/ppermute | solution.py:471

commit v4 on v3

--- a/solution.py
+++ b/solution.py
@@ -45,226 +45,231 @@
     return begin
 
 
-def squares_kernel(place_ref, frequency_ref, gain_ref, tokens_hbm, sums_ref, tokens_ref, sems):
+ROWS = 64
+
+
+def block_rows(start, r):
+    return pl.ds(pl.multiple_of(start + r * ROWS, ROWS), ROWS)
+
+
+def load_kernel(
+    place_ref, lengths_ref, frequency_ref, gain_ref, tokens_hbm, wk_hbm, wv_hbm,
+    sums_ref, tokens_ref, wkv_ref, cos_ref, sin_ref, sems,
+):
     rows, width = tokens_ref.shape
-    chunks = sems.shape[0]
-    step = width // chunks
-    loads = []
-    for c in range(chunks):
-        part = (slice(None), slice(c * step, (c + 1) * step))
-        loads.append(pltpu.make_async_copy(tokens_hbm.at[part], tokens_ref.at[part], sems.at[c]))
-        loads[c].start()
-    sums_ref[rows:, :] = gain_ref[...].astype(jnp.float32)
-    for c in range(chunks):
-        loads[c].wait()
-        total = sums_ref[0:rows, :] if c else jnp.zeros((rows, LANES), jnp.float32)
-        for j in range(c * step // LANES, (c + 1) * step // LANES):
-            wide = tokens_ref[:, j * LANES : (j + 1) * LANES].astype(jnp.float32)
-            total = total + wide * wide
-        sums_ref[0:rows, :] = total
-
-
-def squares(place, frequency, gain, tokens):
-    rows, width = tokens.shape
-    return pl.pallas_call(
-        squares_kernel,
-        in_specs=[SCALAR, WHOLE, WHOLE, HBM],
-        out_specs=[WHOLE] * 2,
-        out_shape=[shaped((rows + gain.shape[0], LANES), jnp.float32), shaped(tokens.shape, tokens.dtype)],
-        scratch_shapes=[pltpu.SemaphoreType.DMA((4,))],
-        compiler_params=params(16),
-        cost_estimate=cost(rows * width * 2, rows * width * 2),
-        name="squares",
-    )(place, frequency, gain, *in_hbm(tokens))
-
-
-def tables_kernel(
-    place_ref, lengths_ref, frequency_ref, wk_hbm, wv_hbm, wout_hbm, wkv_ref, wsend_ref, cos_ref, sin_ref, sems
-):
-    width = wsend_ref.shape[1]
-    start = pl.multiple_of((1 - place_ref[0]) * width, width)
+    half = rows // 2
+    chunks = sems.shape[0] - 2
+    height = rows // chunks
     loads = [
-        pltpu.make_async_copy(wk_hbm, wkv_ref.at[:, :HEAD], sems.at[0]),
-        pltpu.make_async_copy(wv_hbm, wkv_ref.at[:, HEAD:], sems.at[1]),
-        pltpu.make_async_copy(wout_hbm.at[:, pl.ds(start, width)], wsend_ref, sems.at[2]),
+        pltpu.make_async_copy(
+            tokens_hbm.at[c * height : (c + 1) * height], tokens_ref.at[c * height : (c + 1) * height], sems.at[c]
+        )
+        for c in range(chunks)
+    ]
+    loads += [
+        pltpu.make_async_copy(wk_hbm, wkv_ref.at[:, :HEAD], sems.at[chunks]),
+        pltpu.make_async_copy(wv_hbm, wkv_ref.at[:, HEAD:], sems.at[chunks + 1]),
     ]
     for load in loads:
         load.start()
-    row = lax.broadcasted_iota(jnp.int32, cos_ref.shape, 0)
-    lane = lax.broadcasted_iota(jnp.int32, cos_ref.shape, 1)
+    sums_ref[rows:, :] = gain_ref[...].astype(jnp.float32)
+
+    lane = lax.broadcasted_iota(jnp.int32, (half, HEAD), 1)
+    row = lax.broadcasted_iota(jnp.int32, (half, HEAD), 0) + jnp.where(lane < HEAD // 2, 0, half)
     angles = (row - first_of_document(place_ref, lengths_ref, row)).astype(jnp.float32) * frequency_ref[...]
-    cos_ref[...] = jnp.cos(angles)
-    sine = jnp.sin(angles)
-    sin_ref[...] = jnp.where(lane < HEAD // 2, -sine, sine)
-    for load in loads:
+    for table_ref, table, sign in ((cos_ref, jnp.cos(angles), 1.0), (sin_ref, jnp.sin(angles), -1.0)):
+        turned = pltpu.roll(table, HEAD // 2, 1)
+        low = lane < HEAD // 2
+        table_ref[:half, :] = jnp.where(low, sign * table, turned)
+        table_ref[half:, :] = jnp.where(low, sign * turned, table)
+
+    for c in range(chunks):
+        loads[c].wait()
+        for r in range(height // ROWS):
+            at = slice(c * height + r * ROWS, c * height + (r + 1) * ROWS)
+            total = jnp.zeros((ROWS, LANES), jnp.float32)
+            for j in range(0, width, LANES):
+                wide = tokens_ref[at, j : j + LANES].astype(jnp.float32)
+                total = total + wide * wide
+            sums_ref[at, :] = total
+    for load in loads[chunks:]:
         load.wait()
 
 
-def tables_and_weights(place, lengths, frequency, wk, wv, w_out, rows, width):
-    return pl.pallas_call(
-        tables_kernel,
-        in_specs=[SCALAR, SCALAR, WHOLE, HBM, HBM, HBM],
-        out_specs=[WHOLE] * 4,
+def load_own(place, lengths, frequency, gain, tokens, wk, wv):
+    rows, width = tokens.shape
+    return pl.pallas_call(
+        load_kernel,
+        in_specs=[SCALAR, SCALAR, WHOLE, WHOLE, HBM, HBM, HBM],
+        out_specs=[WHOLE] * 5,
         out_shape=[
+            shaped((rows + gain.shape[0], LANES), jnp.float32),
+            shaped(tokens.shape, tokens.dtype),
             shaped((wk.shape[0], 2 * HEAD), wk.dtype),
-            shaped((w_out.shape[0], width), w_out.dtype),
             shaped((rows, HEAD), jnp.float32),
             shaped((rows, HEAD), jnp.float32),
         ],
-        scratch_shapes=[pltpu.SemaphoreType.DMA((3,))],
+        scratch_shapes=[pltpu.SemaphoreType.DMA((4 + 2,))],
         compiler_params=params(16),
-        cost_estimate=cost(rows * HEAD * 100, wk.size * 4 + w_out.size),
-        name="tables",
-    )(place, lengths, frequency, *in_hbm(wk, wv, w_out))
-
-
-STEP = 1024
-
-
-def normalize(out_ref, out_rows, out_column, tokens_ref, rows, column, inverse, gains_ref):
-    for j in range(0, STEP, LANES):
-        wide = tokens_ref[rows, column + j : column + j + LANES].astype(jnp.float32)
-        gain_row = tokens_ref.shape[0] + (column + j) // LANES
-        gain = gains_ref[gain_row : gain_row + 1, :]
-        out_ref[out_rows, out_column + j : out_column + j + LANES] = (wide * inverse * gain).astype(jnp.bfloat16)
-
-
-def inverse_norm(mine_ref, other_ref, rows, width):
-    mean = jnp.sum(mine_ref[rows, :] + other_ref[rows, :], axis=1, keepdims=True) * (0.5 / width)
-    return jnp.broadcast_to(lax.rsqrt(mean + 1e-05), (rows.size, LANES))
+        cost_estimate=cost(rows * width * 2, rows * width * 2 + wk.size * 4),
+        name="load_own",
+    )(place, lengths, frequency, gain, *in_hbm(tokens, wk, wv))
+
+
+def normalize(out_ref, out_start, tokens_ref, start, count, inverse_ref, gains_ref):
+    rows, width = tokens_ref.shape
+
+    def block(r, carry):
+        at = block_rows(start, r)
+        out_at = block_rows(out_start, r)
+        inverse = inverse_ref[at, :]
+        for j in range(0, width, LANES):
+            wide = tokens_ref[at, j : j + LANES].astype(jnp.float32)
+            gain = gains_ref[rows + j // LANES : rows + j // LANES + 1, :]
+            out_ref[out_at, j : j + LANES] = (wide * inverse * gain).astype(jnp.bfloat16)
+        return carry
+
+    lax.fori_loop(0, count // ROWS, block, 0)
 
 
 def turn(x, cosine, sine):
     return (x * cosine + pltpu.roll(x, HEAD // 2, 1) * sine).astype(jnp.bfloat16)
 
 
-def keys_kernel(
-    place_ref, tokens_ref, tokens_other_ref, mine_ref, other_ref, cos_ref, sin_ref, wkv_ref, wq_hbm, kv_ref, normed_ref, wq_ref, acc, sem
+def own_rows(place_ref, rows):
+    half = rows // 2
+    return pl.ds(pl.multiple_of(place_ref[0] * half, half), half)
+
+
+def features(place_ref, width, other):
+    which = 1 - place_ref[0] if other else place_ref[0]
+    return pl.ds(pl.multiple_of(which * width, width), width)
+
+
+def keys_own_kernel(
+    place_ref, tokens_ref, mine_ref, other_ref, wkv_ref, wq_hbm, normed_ref, inverse_ref, acc_ref, wq_ref, sem
+):
+    rows, width = tokens_ref.shape
+    load = pltpu.make_async_copy(wq_hbm, wq_ref, sem)
+    load.start()
+    mean = jnp.sum(mine_ref[0:rows, :] + other_ref[0:rows, :], axis=1, keepdims=True) * (0.5 / width)
+    inverse_ref[...] = jnp.broadcast_to(lax.rsqrt(mean + 1e-05), (rows, LANES))
+    normalize(normed_ref, 0, tokens_ref, 0, rows, inverse_ref, mine_ref)
+    acc_ref[...] = jnp.dot(
+        normed_ref[own_rows(place_ref, rows), :],
+        wkv_ref[features(place_ref, width, False), :],
+        preferred_element_type=jnp.float32,
+    )
+    load.wait()
+
+
+def keys_own(place, tokens, sums, sums_other, wkv, wq):
+    rows, width = tokens.shape
+    return pl.pallas_call(
+        keys_own_kernel,
+        in_specs=[SCALAR] + [WHOLE] * 4 + [HBM],
+        out_specs=[WHOLE] * 4,
+        out_shape=[
+            shaped(tokens.shape, jnp.bfloat16),
+            shaped((rows, LANES), jnp.float32),
+            shaped((rows // 2, 2 * HEAD), jnp.float32),
+            shaped(wq.shape, wq.dtype),
+        ],
+        scratch_shapes=[pltpu.SemaphoreType.DMA],
+        compiler_params=params(16),
+        cost_estimate=cost(2 * rows * width * HEAD, wq.size * 2),
+        name="keys_own",
+    )(place, tokens, sums, sums_other, wkv, *in_hbm(wq))
+
+
+def keys_kernel(place_ref, tokens_ref, gains_ref, inverse_ref, acc_ref, wkv_ref, cos_ref, sin_ref, kv_ref, normed_ref):
+    rows, width = tokens_ref.shape
+    half = rows // 2
+    here = own_rows(place_ref, rows)
+    normalize(normed_ref, 0, tokens_ref, place_ref[0] * half, half, inverse_ref, gains_ref)
+    total = acc_ref[...] + jnp.dot(
+        normed_ref[...], wkv_ref[features(place_ref, width, True), :], preferred_element_type=jnp.float32
+    )
+    kv_ref[:, :HEAD] = turn(total[:, :HEAD], cos_ref[here, :], sin_ref[here, :])
+    kv_ref[:, HEAD:] = total[:, HEAD:].astype(jnp.bfloat16)
+
+
+def finish_keys(place, tokens_other, sums_other, inverse, acc, wkv, tables):
+    rows, width = tokens_other.shape
+    return pl.pallas_call(
+        keys_kernel,
+        in_specs=[SCALAR] + [WHOLE] * 7,
+        out_specs=[WHOLE] * 2,
+        out_shape=[shaped(acc.shape, jnp.bfloat16), shaped((rows // 2, width), jnp.bfloat16)],
+        compiler_params=params(16),
+        cost_estimate=cost(2 * rows * width * HEAD, rows * width),
+        name="keys",
+    )(place, tokens_other, sums_other, inverse, acc, wkv, *tables)
+
+
+def queries_own_kernel(place_ref, normed_ref, wq_ref, acc_ref):
+    width = normed_ref.shape[1]
+    acc_ref[...] = jnp.dot(
+        normed_ref[...], wq_ref[features(place_ref, width, False), :], preferred_element_type=jnp.float32
+    )
+
+
+def queries_own(place, normed, wq):
+    rows, width = normed.shape
+    nq = wq.shape[1]
+    return pl.pallas_call(
+        queries_own_kernel,
+        in_specs=[SCALAR, WHOLE, WHOLE],
+        out_specs=WHOLE,
+        out_shape=shaped((rows, nq), jnp.float32),
+        compiler_params=params(12),
+        cost_estimate=cost(2 * rows * width * nq, rows * nq * 4),
+        name="queries_own",
+    )(place, normed, wq)
+
+
+def queries_kernel(
+    place_ref, tokens_ref, gains_ref, inverse_ref, acc_ref, wq_ref, cos_ref, sin_ref, ready_ref, wout_hbm,
+    q_ref, wsend_ref, wkeep_ref, normed_ref, acc, sems,
 ):
     rows, width = tokens_ref.shape
     half = rows // 2
-    me = place_ref[0]
-    load = pltpu.make_async_copy(wq_hbm, wq_ref, sem)
-    load.start()
-    here = pl.ds(pl.multiple_of(me * half, half), half)
-    inverse = inverse_norm(mine_ref, other_ref, here, width)
-    chunks = [
-        (tokens, gains, base, column)
-        for column in range(0, width, STEP)
-        for tokens, gains, base in ((tokens_ref, mine_ref, me), (tokens_other_ref, other_ref, 1 - me))
+    loads = [
+        pltpu.make_async_copy(wout_hbm.at[:, features(place_ref, width, True)], wsend_ref, sems.at[0]),
+        pltpu.make_async_copy(wout_hbm.at[:, features(place_ref, width, False)], wkeep_ref, sems.at[1]),
     ]
-    every = slice(None)
-
-    def ready(c):
-        tokens, gains, _, column = chunks[c]
-        normalize(normed_ref, every, c * STEP, tokens, here, column, inverse, gains)
-
-    ready(0)
-    for c, (_, _, base, column) in enumerate(chunks):
-        if c + 1 < len(chunks):
-            ready(c + 1)
-        depth = pl.ds(pl.multiple_of(base * width + column, STEP), STEP)
-        term = jnp.dot(normed_ref[:, c * STEP : (c + 1) * STEP], wkv_ref[depth, :], preferred_element_type=jnp.float32)
-        if c < 2:
-            acc[c] = term
-        else:
-            acc[c % 2] += term
-    total = acc[0] + acc[1]
-    kv_ref[:, :HEAD] = turn(total[:, :HEAD], cos_ref[here, :], sin_ref[here, :])
-    kv_ref[:, HEAD:] = total[:, HEAD:].astype(jnp.bfloat16)
-    load.wait()
-
-
-def keys_values(place, tokens, tokens_other, sums, sums_other, tables, wkv, wq):
-    rows, width = tokens.shape
-    half = rows // 2
-    both = 2 * HEAD
-    return pl.pallas_call(
-        keys_kernel,
-        in_specs=[SCALAR] + [WHOLE] * 7 + [HBM],
-        out_specs=[WHOLE] * 3,
-        out_shape=[
-            shaped((half, both), jnp.bfloat16),
-            shaped((half, 2 * width), jnp.bfloat16),
-            shaped(wq.shape, wq.dtype),
-        ],
-        scratch_shapes=[pltpu.VMEM((2, half, both), jnp.float32), pltpu.SemaphoreType.DMA],
-        compiler_params=params(16),
-        cost_estimate=cost(2 * rows * width * both, wq.size * 2),
-        name="keys",
-    )(place, tokens, tokens_other, sums, sums_other, *tables, wkv, *in_hbm(wq))
-
-
-def queries_kernel(
-    place_ref,
-    tokens_ref,
-    tokens_other_ref,
-    mine_ref,
-    other_ref,
-    normed_ref,
-    cos_ref,
-    sin_ref,
-    wq_ref,
-    wout_hbm,
-    q_ref,
-    wkeep_ref,
-    even,
-    odd,
-    acc,
-    sem,
-):
-    rows, width = tokens_ref.shape
-    half = rows // 2
-    me = place_ref[0]
-    load = pltpu.make_async_copy(wout_hbm.at[:, pl.ds(pl.multiple_of(me * width, width), width)], wkeep_ref, sem)
-    load.start()
-    here = pl.ds(pl.multiple_of(me * half, half), half)
-    there = pl.ds(pl.multiple_of((1 - me) * half, half), half)
-    inverse = inverse_norm(mine_ref, other_ref, there, width)
-    chunks = [
-        (tokens, gains, base, column)
-        for column in range(0, width, STEP)
-        for tokens, gains, base in ((tokens_ref, mine_ref, me), (tokens_other_ref, other_ref, 1 - me))
-    ]
-    buffers = (even, odd)
-
-    def ready(c):
-        tokens, gains, _, column = chunks[c]
-        buffer = buffers[c % 2]
-        buffer[:half, :] = normed_ref[:, c * STEP : (c + 1) * STEP]
-        normalize(buffer, slice(half, rows), 0, tokens, there, column, inverse, gains)
-
-    ready(0)
-    for c, (_, _, base, column) in enumerate(chunks):
-        if c + 1 < len(chunks):
-            ready(c + 1)
-        depth = pl.ds(pl.multiple_of(base * width + column, STEP), STEP)
-        term = jnp.dot(buffers[c % 2][...], wq_ref[depth, :], preferred_element_type=jnp.float32)
-        if c == 0:
-            acc[...] = term
-        else:
-            acc[...] += term
-    for at, part in ((here, slice(0, half)), (there, slice(half, rows))):
-        for h in range(q_ref.shape[1] // HEAD):
-            lanes = slice(h * HEAD, (h + 1) * HEAD)
-            q_ref[at, lanes] = turn(acc[part, lanes], cos_ref[at, :], sin_ref[at, :])
-    load.wait()
-
-
-def project_queries(place, tokens, tokens_other, sums, sums_other, normed, tables, wq, w_out):
-    rows, width = tokens.shape
+    for load in loads:
+        load.start()
+    normed_ref[own_rows(place_ref, rows), :] = ready_ref[...]
+    normalize(normed_ref, (1 - place_ref[0]) * half, tokens_ref, (1 - place_ref[0]) * half, half, inverse_ref, gains_ref)
+    acc[...] = acc_ref[...] + jnp.dot(
+        normed_ref[...], wq_ref[features(place_ref, width, True), :], preferred_element_type=jnp.float32
+    )
+    for h in range(q_ref.shape[1] // HEAD):
+        lanes = slice(h * HEAD, (h + 1) * HEAD)
+        q_ref[:, lanes] = turn(acc[:, lanes], cos_ref[...], sin_ref[...])
+    for load in loads:
+        load.wait()
+
+
+def finish_queries(place, tokens_other, sums_other, inverse, acc, wq, tables, normed, w_out):
+    rows, width = tokens_other.shape
     nq = wq.shape[1]
+    half_out = shaped((w_out.shape[0], width), w_out.dtype)
     return pl.pallas_call(
         queries_kernel,
         in_specs=[SCALAR] + [WHOLE] * 8 + [HBM],
-        out_specs=[WHOLE, WHOLE],
-        out_shape=[shaped((rows, nq), jnp.bfloat16), shaped((w_out.shape[0], width), w_out.dtype)],
-        scratch_shapes=[pltpu.VMEM((rows, STEP), jnp.bfloat16)] * 2
-        + [pltpu.VMEM((rows, nq), jnp.float32), pltpu.SemaphoreType.DMA],
+        out_specs=[WHOLE] * 3,
+        out_shape=[shaped((rows, nq), jnp.bfloat16), half_out, half_out],
+        scratch_shapes=[
+            pltpu.VMEM((rows, width), jnp.bfloat16),
+            pltpu.VMEM((rows, nq), jnp.float32),
+            pltpu.SemaphoreType.DMA((2,)),
+        ],
         compiler_params=params(16),
-        cost_estimate=cost(4 * rows * width * nq, w_out.size),
+        cost_estimate=cost(2 * rows * width * nq, rows * width * 4),
         name="queries",
-    )(place, tokens, tokens_other, sums, sums_other, normed, *tables, wq, *in_hbm(w_out))
+    )(place, tokens_other, sums_other, inverse, acc, wq, *tables, normed, *in_hbm(w_out))
 
 
 TILE = 128
@@ -478,15 +483,22 @@
     frequency = 500000.0 ** (-jnp.arange(HEAD // 2, dtype=jnp.float32) * 2.0 / HEAD)
     frequency = jnp.concatenate([frequency, frequency])[None, :]
 
+    sums, tokens, wkv, *tables = load_own(
+        place, lengths, frequency, norm_gain.reshape(-1, LANES), tokens, w_key, w_value
+    )
+    sums_other = swap(sums)
+    tokens, sums_other = lax.optimization_barrier((tokens, sums_other))
     tokens_other = swap(tokens)
-    sums, tokens = squares(place, frequency, norm_gain.reshape(-1, LANES), tokens)
-    sums_other = swap(sums)
-    wkv, w_send, *tables = tables_and_weights(place, lengths, frequency, w_key, w_value, w_out, rows, tokens.shape[1])
-    kv, normed, wq = keys_values(place, tokens, tokens_other, sums, sums_other, tables, wkv, w_query)
+    normed, inverse, kv_partial, wq = keys_own(place, tokens, sums, sums_other, wkv, w_query)
+    partial = queries_own(place, normed, wq)
+    tokens_other, partial = lax.optimization_barrier((tokens_other, partial))
+    kv, normed = finish_keys(place, tokens_other, sums_other, inverse, kv_partial, wkv, tables)
     kv, normed = lax.optimization_barrier((kv, normed))
     parts = [shift(kv, "dp", d) for d in range(reach, 0, -1)]
     kv_other = swap(kv)
-    queries, w_mine = project_queries(place, tokens, tokens_other, sums, sums_other, normed, tables, wq, w_out)
+    queries, w_send, w_mine = finish_queries(
+        place, tokens_other, sums_other, inverse, partial, wq, tables, normed, w_out
+    )
     state = attend(place, lengths, queries, [kv, kv_other])
     parts, state = lax.optimization_barrier((parts, state))
     blocks = []

time: 56.6 us -> 52.8 us (0.933)
  the two profiles are of different devices: /device:TPU:0 before, /device:TPU:25 now
where the time goes in v4:
time: 52.8 us; the launch traced here: 53.4 us
  Pallas kernels  38 us (72%)
  starting transfers between devices  9.23 us (17%)
  waiting for transfers between devices  4.51 us (9%)
  local copies, waits for them, and re-layouts  1.36 us (3%)
    pallas_call x2, Pallas kernels, attend(): pl.pallas_call(functools.partial(attend_kernel, own), in_specs=[SCALAR, S...  14.2 us
    ppermute x3, starting transfers between devices, shift(): lax.ppermute(value, axis, [(source, source + steps) for source in range(c...  5.72 us
    pallas_call x1, Pallas kernels, load_own(): pl.pallas_call(load_kernel, in_specs=[SCALAR, SCALAR, WHOLE, WHOLE, HBM,...  4.35 us
    pallas_call x1, Pallas kernels, output(): pl.pallas_call(output_kernel, grid=(width // step,), in_specs=[WHOLE] * 4...  4.28 us
    pallas_call x1, Pallas kernels, finish_queries(): pl.pallas_call(queries_kernel, in_specs=[SCALAR] + [WHOLE] * 8 + [HBM], o...  4.03 us
    pallas_call x1, Pallas kernels, keys_own(): pl.pallas_call(keys_own_kernel, in_specs=[SCALAR] + [WHOLE] * 4 + [HBM],...  3.93 us
    ppermute x8, starting transfers between devices, swap(): return lax.ppermute(value, 'tp', SWAP)  3.51 us
    pallas_call x1, Pallas kernels, queries_own(): pl.pallas_call(queries_own_kernel, in_specs=[SCALAR, WHOLE, WHOLE], out_s...  2.87 us
  transfers between devices with their start and end apart: 11, of which 5 were waited for; matrix products, arithmetic and copies ran while one was open for 0% of the time, Pallas kernels for 51%

profile of v4, /device:TPU:25, one launch (start us, length us, event | category | flops | bytes accessed | tf_op | source)
XLA Modules:
  0.0 53.4 jit_solution(5711345395730095293)
XLA Ops:
  0.2 0.7 %copy-done = bf16[4096]{0:T(1024)(128)(2,1)S(1)} copy-done((bf16[4096]{0:T(1024)(128)(2,1)S(1)}, bf16[4096]{0:T(1024)(128)(2,1)}, u32[]{:S(2)}) %copy-start) | copy-done | bytes 8216
  0.9 0.7 %copy-done.1 = s32[8]{0:T(128)S(1)} copy-done((s32[8]{0:T(128)S(1)}, s32[8]{0:T(128)}, u32[]{:S(2)}) %copy-start.1) | copy-done | bytes 56
  1.5 4.4 %load_own.1 = (f32[544,128]{1,0:T(8,128)S(1)}, bf16[512,4096]{1,0:T(8,128)(2,1)S(1)}, bf16[8192,256]{1,0:T(8,128)(2,1)S(1)}, f32[512,128]{1,0:T(8,128)S(1)}, f32[512,128]{1,0:T(8,128)S(1)}) custom-call(s32[2]{0:T(128)S(1)} %pad_add_fusion.place_ref, s32[8]{0:T(128)S(1)} %copy-done.1, f32[1,128]{1,0:T(1,128)S(1)} %maximum_bitcast_fusion.frequency_ref, ...), custom_call_target="tpu_custom_call" | custom-call | flops 4194304 | bytes 8388608 | tf_op jit(solution)/shard_map/load_own/pallas_call | solution.py:101
  5.9 0.7 %collective-permute-start = (f32[544,128]{1,0:T(8,128)S(1)}, f32[544,128]{1,0:T(8,128)S(1)}, u32[]{:S(2)}, u32[]{:S(2)}) collective-permute-start(f32[544,128]{1,0:T(8,128)S(1)} %get-tuple-element.40.mine_ref), channel_id=1, source_target_pairs={{0,1},{1,0},{2,3},{3,2},{4,5},{5,4},{6,7},{7,6},{8,9},{9,8},{10,11... | collective-permute-start | bytes 835592 | tf_op jit(solution)/shard_map/ppermute | solution.py:476
  6.6 1.2 %collective-permute-done.other_ref.gains_ref = f32[544,128]{1,0:T(8,128)S(1)} collective-permute-done((f32[544,128]{1,0:T(8,128)S(1)}, f32[544,128]{1,0:T(8,128)S(1)}, u32[]{:S(2)}, u32[]{:S(2)}) %collective-permute-start) | collective-permute-done | bytes 278560 | tf_op jit(solution)/shard_map/ppermute | solution.py:476
  7.8 0.4 collective-permute-start.1
  8.2 3.9 %keys_own.1 = (bf16[512,4096]{1,0:T(8,128)(2,1)S(1)}, f32[512,128]{1,0:T(8,128)S(1)}, f32[256,256]{1,0:T(8,128)S(1)}, bf16[8192,512]{1,0:T(8,128)(2,1)S(1)}) custom-call(s32[2]{0:T(128)S(1)} %pad_add_fusion.place_ref, bf16[512,4096]{1,0:T(8,128)(2,1)S(1)} %get-tuple-element.41.tokens_ref, f32[544,128]{1,0:T(8,128)S(1)} %get-tuple-element.40.mine_ref, ...), custom_call_target="tpu_custom_call" | custom-call | flops 536870912 | bytes 8388608 | tf_op jit(solution)/shard_map/keys_own/pallas_call | solution.py:168
  12.1 2.9 %queries_own.1.acc_ref = f32[512,512]{1,0:T(8,128)S(1)} custom-call(s32[2]{0:T(128)S(1)} %pad_add_fusion.place_ref, bf16[512,4096]{1,0:T(8,128)(2,1)S(1)} %get-tuple-element.44.normed_ref, bf16[8192,512]{1,0:T(8,128)(2,1)S(1)} %get-tuple-element.45.wq_ref), custom_call_target="tpu_custom_call" | custom-call | flops 2147483648 | bytes 1048576 | tf_op jit(solution)/shard_map/queries_own/pallas_call | solution.py:220
  15.0 1.9 %keys.1 = (bf16[256,256]{1,0:T(8,128)(2,1)S(1)}, bf16[256,4096]{1,0:T(8,128)(2,1)S(1)}) custom-call(s32[2]{0:T(128)S(1)} %pad_add_fusion.place_ref, bf16[512,4096]{1,0:T(8,128)(2,1)S(1)} %collective-permute-done.1.tokens_ref, f32[544,128]{1,0:T(8,128)S(1)} %collective-permute-done.other_ref.gains_ref, f32[512,128]{1,0:T(8,128)S(1)} %get-tuple-element.47.inverse_ref, ...), custom_call_target="tpu_custom_call" | custom-call | flops 536870912 | bytes 2097152 | tf_op jit(solution)/shard_map/keys/pallas_call | solution.py:199
  16.9 0.4 collective-permute-start.5
  17.3 3.1 %collective-permute-start.4 = (bf16[256,256]{1,0:T(8,128)(2,1)S(1)}, bf16[256,256]{1,0:T(8,128)(2,1)S(1)}, u32[]{:S(2)}, u32[]{:S(2)}) collective-permute-start(bf16[256,256]{1,0:T(8,128)(2,1)S(1)} %get-tuple-element.54.rest_0_), channel_id=1, source_target_pairs={{0,2},{2,4},{4,6},{6,8},{8,10},{10,12},{12,14},{1,3},{3,5},{5,7},{... | collective-permute-start | bytes 393224 | tf_op jit(solution)/shard_map/ppermute | solution.py:472
  20.5 1.3 %collective-permute-start.3 = (bf16[256,256]{1,0:T(8,128)(2,1)S(1)}, bf16[256,256]{1,0:T(8,128)(2,1)S(1)}, u32[]{:S(2)}, u32[]{:S(2)}) collective-permute-start(bf16[256,256]{1,0:T(8,128)(2,1)S(1)} %get-tuple-element.54.rest_0_), channel_id=1, source_target_pairs={{0,4},{2,6},{4,8},{6,10},{8,12},{10,14},{1,5},{3,7},{5,9},{7,11},{... | collective-permute-start | bytes 393224 | tf_op jit(solution)/shard_map/ppermute | solution.py:472
  21.8 1.3 %collective-permute-start.2 = (bf16[256,256]{1,0:T(8,128)(2,1)S(1)}, bf16[256,256]{1,0:T(8,128)(2,1)S(1)}, u32[]{:S(2)}, u32[]{:S(2)}) collective-permute-start(bf16[256,256]{1,0:T(8,128)(2,1)S(1)} %get-tuple-element.54.rest_0_), channel_id=1, source_target_pairs={{0,6},{2,8},{4,10},{6,12},{8,14},{1,7},{3,9},{5,11},{7,13},{9,15},... | collective-permute-start | bytes 393224 | tf_op jit(solution)/shard_map/ppermute | solution.py:472
  23.1 4.0 %queries.1 = (bf16[512,512]{1,0:T(8,128)(2,1)S(1)}, bf16[512,4096]{1,0:T(8,128)(2,1)S(1)}, bf16[512,4096]{1,0:T(8,128)(2,1)S(1)}) custom-call(s32[2]{0:T(128)S(1)} %pad_add_fusion.place_ref, bf16[512,4096]{1,0:T(8,128)(2,1)S(1)} %collective-permute-done.1.tokens_ref, f32[544,128]{1,0:T(8,128)S(1)} %collective-permute-done.other_ref.gains_ref, ...), custom_call_target="tpu_custom_call" | custom-call | flops 2147483648 | bytes 8388608 | tf_op jit(solution)/shard_map/queries/pallas_call | solution.py:259
  27.2 4.4 %attend_own.1 = (f32[2048,128]{1,0:T(8,128)S(1)}, f32[2048,128]{1,0:T(8,128)S(1)}, f32[2048,128]{1,0:T(8,128)S(1)}) custom-call(s32[2]{0:T(128)S(1)} %pad_add_fusion.place_ref, s32[8]{0:T(128)S(1)} %copy-done.2, bf16[512,512]{1,0:T(8,128)(2,1)S(1)} %get-tuple-element.53.q_ref, bf16[256,256]{1,0:T(8,128)(2,1)S(1)} %get-tuple-element.54.rest_0_, ...), custom_call_target="tpu_custom_call" | custom-call | flops 536870912 | bytes 2097152 | tf_op jit(solution)/shard_map/attend_own/pallas_call | solution.py:413
  31.6 2.3 %collective-permute-done.2.rest_0_ = bf16[256,256]{1,0:T(8,128)(2,1)S(1)} collective-permute-done((bf16[256,256]{1,0:T(8,128)(2,1)S(1)}, bf16[256,256]{1,0:T(8,128)(2,1)S(1)}, u32[]{:S(2)}, u32[]{:S(2)}) %collective-permute-start.2) | collective-permute-done | bytes 131104 | tf_op jit(solution)/shard_map/ppermute | solution.py:472
  33.9 0.9 %collective-permute-start.6 = (bf16[256,256]{1,0:T(8,128)(2,1)S(1)}, bf16[256,256]{1,0:T(8,128)(2,1)S(1)}, u32[]{:S(2)}, u32[]{:S(2)}) collective-permute-start(bf16[256,256]{1,0:T(8,128)(2,1)S(1)} %collective-permute-done.2.rest_0_), channel_id=1, source_target_pairs={{0,1},{1,0},{2,3},{3,2},{4,5},{5,4},{6,7},{7,6},{8,9},{9,8},{10,11... | collective-permute-start | bytes 393224 | tf_op jit(solution)/shard_map/ppermute | solution.py:476
  34.8 0.5 collective-permute-start.8
  35.3 0.5 collective-permute-done.6.rest_1_
  35.7 0.4 collective-permute-done.7.rest_3_
  36.3 0.3 collective-permute-start.10
  36.6 9.9 %attend.1.context_ref = bf16[512,512]{1,0:T(8,128)(2,1)S(1)} custom-call(s32[2]{0:T(128)S(1)} %pad_add_fusion.place_ref, s32[8]{0:T(128)S(1)} %copy-done.2, bf16[512,512]{1,0:T(8,128)(2,1)S(1)} %get-tuple-element.53.q_ref, bf16[256,256]{1,0:T(8,128)(2,1)S(1)} %collective-permute-done.2.rest_0_, bf16[256,256]{1,0:T(8,128)(2,1)S(1)} %collective-permute-done.6.rest_1_, ...), custom_call_target="tpu_custom_call" | custom-call | flops 1610612736 | bytes 2097152 | tf_op jit(solution)/shard_map/attend/pallas_call | solution.py:413
  46.7 2.4 %own_term.1.term_ref = bf16[512,4096]{1,0:T(8,128)(2,1)S(1)} custom-call(bf16[512,512]{1,0:T(8,128)(2,1)S(1)} %attend.1.context_ref, bf16[512,4096]{1,0:T(8,128)(2,1)S(1)} %get-tuple-element.71.w_ref), custom_call_target="tpu_custom_call" | custom-call | flops 2147483648 | bytes 4194304 | tf_op jit(solution)/shard_map/own_term/pallas_call | solution.py:435
  49.1 4.3 %output.1 = bf16[512,4096]{1,0:T(8,128)(2,1)} custom-call(bf16[512,4096]{1,0:T(8,128)(2,1)S(1)} %get-tuple-element.41.tokens_ref, bf16[512,4096]{1,0:T(8,128)(2,1)S(1)} %own_term.1.term_ref, bf16[512,512]{1,0:T(8,128)(2,1)S(1)} %collective-permute-done.9.context_ref, bf16[512,4096]{1,0:T(8,128)(2,1)S(1)} %collective-permute-done.10.w_ref), custom_call_target="tpu_custom_call" | custom-call | flops 2147483648 | bytes 8388608 | tf_op jit(solution)/shard_map/output/pallas_call | solution.py:458
  (16 shorter events, 0.6 us)
Async XLA Ops:
  0.2 0.7 %copy-start = (bf16[4096]{0:T(1024)(128)(2,1)S(1)}, bf16[4096]{0:T(1024)(128)(2,1)}, u32[]{:S(2)}) copy-start(bf16[4096]{0:T(1024)(128)(2,1)} %param.8) | copy-start | bytes 24580
  0.9 0.7 %copy-start.1 = (s32[8]{0:T(128)S(1)}, s32[8]{0:T(128)}, u32[]{:S(2)}) copy-start(s32[8]{0:T(128)} %lengths_ref.5) | copy-start | bytes 100
  5.9 1.9 %collective-permute-start = (f32[544,128]{1,0:T(8,128)S(1)}, f32[544,128]{1,0:T(8,128)S(1)}, u32[]{:S(2)}, u32[]{:S(2)}) collective-permute-start(f32[544,128]{1,0:T(8,128)S(1)} %get-tuple-element.40.mine_ref), channel_id=1, source_target_pairs={{0,1},{1,0},{2,3},{3,2},{4,5},{5,4},{6,7},{7,6},{8,9},{9,8},{10,11... | collective-permute-start | bytes 835592 | tf_op jit(solution)/shard_map/ppermute | solution.py:476
  7.8 7.2 %collective-permute-start.1 = (bf16[512,4096]{1,0:T(8,128)(2,1)S(1)}, bf16[512,4096]{1,0:T(8,128)(2,1)S(1)}, u32[]{:S(2)}, u32[]{:S(2)}) collective-permute-start(bf16[512,4096]{1,0:T(8,128)(2,1)S(1)} %get-tuple-element.41.tokens_ref), channel_id=1, source_target_pairs={{0,1},{1,0},{2,3},{3,2},{4,5},{5,4},{6,7},{7,6},{8,9},{9,8},{10,11... | collective-permute-start | bytes 12582920 | tf_op jit(solution)/shard_map/ppermute | solution.py:476
  16.9 10.2 %collective-permute-start.5 = (bf16[256,256]{1,0:T(8,128)(2,1)S(1)}, bf16[256,256]{1,0:T(8,128)(2,1)S(1)}, u32[]{:S(2)}, u32[]{:S(2)}) collective-permute-start(bf16[256,256]{1,0:T(8,128)(2,1)S(1)} %get-tuple-element.54.rest_0_), channel_id=1, source_target_pairs={{0,1},{1,0},{2,3},{3,2},{4,5},{5,4},{6,7},{7,6},{8,9},{9,8},{10,11... | collective-permute-start | bytes 393224 | tf_op jit(solution)/shard_map/ppermute | solution.py:476
  17.3 14.2 %collective-permute-start.4 = (bf16[256,256]{1,0:T(8,128)(2,1)S(1)}, bf16[256,256]{1,0:T(8,128)(2,1)S(1)}, u32[]{:S(2)}, u32[]{:S(2)}) collective-permute-start(bf16[256,256]{1,0:T(8,128)(2,1)S(1)} %get-tuple-element.54.rest_0_), channel_id=1, source_target_pairs={{0,2},{2,4},{4,6},{6,8},{8,10},{10,12},{12,14},{1,3},{3,5},{5,7},{... | collective-permute-start | bytes 393224 | tf_op jit(solution)/shard_map/ppermute | solution.py:472
  20.5 11.1 %collective-permute-start.3 = (bf16[256,256]{1,0:T(8,128)(2,1)S(1)}, bf16[256,256]{1,0:T(8,128)(2,1)S(1)}, u32[]{:S(2)}, u32[]{:S(2)}) collective-permute-start(bf16[256,256]{1,0:T(8,128)(2,1)S(1)} %get-tuple-element.54.rest_0_), channel_id=1, source_target_pairs={{0,4},{2,6},{4,8},{6,10},{8,12},{10,14},{1,5},{3,7},{5,9},{7,11},{... | collective-permute-start | bytes 393224 | tf_op jit(solution)/shard_map/ppermute | solution.py:472
  21.8 12.1 %collective-permute-start.2 = (bf16[256,256]{1,0:T(8,128)(2,1)S(1)}, bf16[256,256]{1,0:T(8,128)(2,1)S(1)}, u32[]{:S(2)}, u32[]{:S(2)}) collective-permute-start(bf16[256,256]{1,0:T(8,128)(2,1)S(1)} %get-tuple-element.54.rest_0_), channel_id=1, source_target_pairs={{0,6},{2,8},{4,10},{6,12},{8,14},{1,7},{3,9},{5,11},{7,13},{9,15},... | collective-permute-start | bytes 393224 | tf_op jit(solution)/shard_map/ppermute | solution.py:472
  23.1 4.1 %copy-start.2 = (s32[8]{0:T(128)S(1)}, s32[8]{0:T(128)}, u32[]{:S(2)}) copy-start(s32[8]{0:T(128)} %lengths_ref.5) | copy-start | bytes 100
  33.9 1.9 %collective-permute-start.6 = (bf16[256,256]{1,0:T(8,128)(2,1)S(1)}, bf16[256,256]{1,0:T(8,128)(2,1)S(1)}, u32[]{:S(2)}, u32[]{:S(2)}) collective-permute-start(bf16[256,256]{1,0:T(8,128)(2,1)S(1)} %collective-permute-done.2.rest_0_), channel_id=1, source_target_pairs={{0,1},{1,0},{2,3},{3,2},{4,5},{5,4},{6,7},{7,6},{8,9},{9,8},{10,11... | collective-permute-start | bytes 393224 | tf_op jit(solution)/shard_map/ppermute | solution.py:476
  34.8 1.3 %collective-permute-start.7 = (bf16[256,256]{1,0:T(8,128)(2,1)S(1)}, bf16[256,256]{1,0:T(8,128)(2,1)S(1)}, u32[]{:S(2)}, u32[]{:S(2)}) collective-permute-start(bf16[256,256]{1,0:T(8,128)(2,1)S(1)} %collective-permute-done.3.rest_2_), channel_id=1, source_target_pairs={{0,1},{1,0},{2,3},{3,2},{4,5},{5,4},{6,7},{7,6},{8,9},{9,8},{10,11... | collective-permute-start | bytes 393224 | tf_op jit(solution)/shard_map/ppermute | solution.py:476
  34.8 1.5 %collective-permute-start.8 = (bf16[256,256]{1,0:T(8,128)(2,1)S(1)}, bf16[256,256]{1,0:T(8,128)(2,1)S(1)}, u32[]{:S(2)}, u32[]{:S(2)}) collective-permute-start(bf16[256,256]{1,0:T(8,128)(2,1)S(1)} %collective-permute-done.4.rest_4_), channel_id=1, source_target_pairs={{0,1},{1,0},{2,3},{3,2},{4,5},{5,4},{6,7},{7,6},{8,9},{9,8},{10,11... | collective-permute-start | bytes 393224 | tf_op jit(solution)/shard_map/ppermute | solution.py:476
  36.3 12.8 %collective-permute-start.10 = (bf16[512,4096]{1,0:T(8,128)(2,1)S(1)}, bf16[512,4096]{1,0:T(8,128)(2,1)S(1)}, u32[]{:S(2)}, u32[]{:S(2)}) collective-permute-start(bf16[512,4096]{1,0:T(8,128)(2,1)S(1)} %get-tuple-element.72), channel_id=1, source_target_pairs={{0,1},{1,0},{2,3},{3,2},{4,5},{5,4},{6,7},{7,6},{8,9},{9,8},{10,11... | collective-permute-start | bytes 12582920 | tf_op jit(solution)/shard_map/ppermute | solution.py:476
  46.5 2.6 %collective-permute-start.9 = (bf16[512,512]{1,0:T(8,128)(2,1)S(1)}, bf16[512,512]{1,0:T(8,128)(2,1)S(1)}, u32[]{:S(2)}, u32[]{:S(2)}) collective-permute-start(bf16[512,512]{1,0:T(8,128)(2,1)S(1)} %attend.1.context_ref), channel_id=1, source_target_pairs={{0,1},{1,0},{2,3},{3,2},{4,5},{5,4},{6,7},{7,6},{8,9},{9,8},{10,11... | collective-permute-start | bytes 1572872 | tf_op jit(solution)/shard_map/ppermute | solution.py:476

commit v5 on v4

--- a/solution.py
+++ b/solution.py
@@ -32,33 +32,38 @@
     return pl.CostEstimate(flops=flops, bytes_accessed=moved, transcendentals=0)
 
 
+SMALL = cost(1, 1)
+
+
 def shaped(shape, dtype):
     return jax.ShapeDtypeStruct(shape, dtype)
 
 
-def first_of_document(place_ref, lengths_ref, row):
+def first_of_document(place_ref, row):
     start = -place_ref[1]
-    begin = jnp.full(row.shape, start, jnp.int32)
-    for d in range(lengths_ref.shape[0] - 1):
-        start = start + lengths_ref[d]
+    begin = jnp.full(jnp.shape(row), start, jnp.int32)
+    for d in range(2, place_ref.shape[0] - 1):
+        start = start + place_ref[d]
         begin = jnp.where(row >= start, start, begin)
     return begin
 
 
 ROWS = 64
+WIDE = 256
 
 
 def block_rows(start, r):
     return pl.ds(pl.multiple_of(start + r * ROWS, ROWS), ROWS)
 
 
-def load_kernel(
-    place_ref, lengths_ref, frequency_ref, gain_ref, tokens_hbm, wk_hbm, wv_hbm,
-    sums_ref, tokens_ref, wkv_ref, cos_ref, sin_ref, sems,
-):
+def wide_slice(ref, at, j):
+    wide = ref[at, j : j + WIDE].astype(jnp.float32)
+    return [wide[:, i : i + LANES] for i in range(0, WIDE, LANES)]
+
+
+def squares_kernel(place_ref, frequency_ref, gain_hbm, tokens_hbm, sums_ref, tokens_ref, gain_ref, sems):
     rows, width = tokens_ref.shape
-    half = rows // 2
-    chunks = sems.shape[0] - 2
+    chunks = sems.shape[0] - 1
     height = rows // chunks
     loads = [
         pltpu.make_async_copy(
@@ -66,54 +71,72 @@
         )
         for c in range(chunks)
     ]
-    loads += [
-        pltpu.make_async_copy(wk_hbm, wkv_ref.at[:, :HEAD], sems.at[chunks]),
-        pltpu.make_async_copy(wv_hbm, wkv_ref.at[:, HEAD:], sems.at[chunks + 1]),
+    loads.append(pltpu.make_async_copy(gain_hbm, gain_ref, sems.at[chunks]))
+    for load in loads:
+        load.start()
+    for c in range(chunks):
+        loads[c].wait()
+        for r in range(height // ROWS):
+            at = slice(c * height + r * ROWS, c * height + (r + 1) * ROWS)
+            total = jnp.zeros((ROWS, LANES), jnp.float32)
+            for j in range(0, width, WIDE):
+                for wide in wide_slice(tokens_ref, at, j):
+                    total = total + wide * wide
+            sums_ref[at, :] = total
+    loads[chunks].wait()
+    sums_ref[rows:, :] = gain_ref[...].astype(jnp.float32)
+
+
+def squares(place, frequency, gain, tokens):
+    rows, width = tokens.shape
+    return pl.pallas_call(
+        squares_kernel,
+        in_specs=[SCALAR, WHOLE, HBM, HBM],
+        out_specs=[WHOLE] * 2,
+        out_shape=[shaped((rows + gain.shape[0], LANES), jnp.float32), shaped(tokens.shape, tokens.dtype)],
+        scratch_shapes=[pltpu.VMEM(gain.shape, gain.dtype), pltpu.SemaphoreType.DMA((8 + 1,))],
+        compiler_params=params(16),
+        cost_estimate=cost(rows * width * 2, rows * width * 2),
+        name="squares",
+    )(place, frequency, *in_hbm(gain, tokens))
+
+
+def tables_kernel(place_ref, frequency_ref, wk_hbm, wv_hbm, wkv_ref, cos_ref, sin_ref, sems):
+    rows = cos_ref.shape[0]
+    half = rows // 2
+    loads = [
+        pltpu.make_async_copy(wk_hbm, wkv_ref.at[:, :HEAD], sems.at[0]),
+        pltpu.make_async_copy(wv_hbm, wkv_ref.at[:, HEAD:], sems.at[1]),
     ]
     for load in loads:
         load.start()
-    sums_ref[rows:, :] = gain_ref[...].astype(jnp.float32)
-
     lane = lax.broadcasted_iota(jnp.int32, (half, HEAD), 1)
     row = lax.broadcasted_iota(jnp.int32, (half, HEAD), 0) + jnp.where(lane < HEAD // 2, 0, half)
-    angles = (row - first_of_document(place_ref, lengths_ref, row)).astype(jnp.float32) * frequency_ref[...]
+    angles = (row - first_of_document(place_ref, row)).astype(jnp.float32) * frequency_ref[...]
     for table_ref, table, sign in ((cos_ref, jnp.cos(angles), 1.0), (sin_ref, jnp.sin(angles), -1.0)):
         turned = pltpu.roll(table, HEAD // 2, 1)
         low = lane < HEAD // 2
         table_ref[:half, :] = jnp.where(low, sign * table, turned)
         table_ref[half:, :] = jnp.where(low, sign * turned, table)
-
-    for c in range(chunks):
-        loads[c].wait()
-        for r in range(height // ROWS):
-            at = slice(c * height + r * ROWS, c * height + (r + 1) * ROWS)
-            total = jnp.zeros((ROWS, LANES), jnp.float32)
-            for j in range(0, width, LANES):
-                wide = tokens_ref[at, j : j + LANES].astype(jnp.float32)
-                total = total + wide * wide
-            sums_ref[at, :] = total
-    for load in loads[chunks:]:
+    for load in loads:
         load.wait()
 
 
-def load_own(place, lengths, frequency, gain, tokens, wk, wv):
-    rows, width = tokens.shape
-    return pl.pallas_call(
-        load_kernel,
-        in_specs=[SCALAR, SCALAR, WHOLE, WHOLE, HBM, HBM, HBM],
-        out_specs=[WHOLE] * 5,
+def tables_and_weights(place, frequency, wk, wv, rows):
+    return pl.pallas_call(
+        tables_kernel,
+        in_specs=[SCALAR, WHOLE, HBM, HBM],
+        out_specs=[WHOLE] * 3,
         out_shape=[
-            shaped((rows + gain.shape[0], LANES), jnp.float32),
-            shaped(tokens.shape, tokens.dtype),
             shaped((wk.shape[0], 2 * HEAD), wk.dtype),
             shaped((rows, HEAD), jnp.float32),
             shaped((rows, HEAD), jnp.float32),
         ],
-        scratch_shapes=[pltpu.SemaphoreType.DMA((4 + 2,))],
+        scratch_shapes=[pltpu.SemaphoreType.DMA((2,))],
         compiler_params=params(16),
-        cost_estimate=cost(rows * width * 2, rows * width * 2 + wk.size * 4),
-        name="load_own",
-    )(place, lengths, frequency, gain, *in_hbm(tokens, wk, wv))
+        cost_estimate=cost(rows * HEAD * 100, wk.size * 4),
+        name="tables",
+    )(place, frequency, *in_hbm(wk, wv))
 
 
 def normalize(out_ref, out_start, tokens_ref, start, count, inverse_ref, gains_ref):
@@ -123,10 +146,12 @@
         at = block_rows(start, r)
         out_at = block_rows(out_start, r)
         inverse = inverse_ref[at, :]
-        for j in range(0, width, LANES):
-            wide = tokens_ref[at, j : j + LANES].astype(jnp.float32)
-            gain = gains_ref[rows + j // LANES : rows + j // LANES + 1, :]
-            out_ref[out_at, j : j + LANES] = (wide * inverse * gain).astype(jnp.bfloat16)
+        for j in range(0, width, WIDE):
+            normed = []
+            for i, wide in enumerate(wide_slice(tokens_ref, at, j)):
+                gain_row = rows + j // LANES + i
+                normed.append(wide * inverse * gains_ref[gain_row : gain_row + 1, :])
+            out_ref[out_at, j : j + WIDE] = jnp.concatenate(normed, axis=1).astype(jnp.bfloat16)
         return carry
 
     lax.fori_loop(0, count // ROWS, block, 0)
@@ -207,6 +232,25 @@
     )(place, tokens_other, sums_other, inverse, acc, wkv, *tables)
 
 
+def join_kernel(place_ref, mine_ref, other_ref, out_ref):
+    half = mine_ref.shape[0]
+    for block, which in ((mine_ref, place_ref[0]), (other_ref, 1 - place_ref[0])):
+        out_ref[pl.ds(pl.multiple_of(which * half, half), half), :] = block[...]
+
+
+def join(place, mine, other):
+    half, width = mine.shape
+    return pl.pallas_call(
+        join_kernel,
+        in_specs=[SCALAR] + [WHOLE] * 2,
+        out_specs=WHOLE,
+        out_shape=shaped((2 * half, width), mine.dtype),
+        compiler_params=params(8),
+        cost_estimate=SMALL,
+        name="join",
+    )(place, mine, other)
+
+
 def queries_own_kernel(place_ref, normed_ref, wq_ref, acc_ref):
     width = normed_ref.shape[1]
     acc_ref[...] = jnp.dot(
@@ -230,13 +274,15 @@
 
 def queries_kernel(
     place_ref, tokens_ref, gains_ref, inverse_ref, acc_ref, wq_ref, cos_ref, sin_ref, ready_ref, wout_hbm,
-    q_ref, wsend_ref, wkeep_ref, normed_ref, acc, sems,
+    q_ref, wsend_ref, wlater_ref, wkeep_ref, normed_ref, acc, sems,
 ):
     rows, width = tokens_ref.shape
     half = rows // 2
+    send = pl.multiple_of((1 - place_ref[0]) * width, width)
     loads = [
-        pltpu.make_async_copy(wout_hbm.at[:, features(place_ref, width, True)], wsend_ref, sems.at[0]),
-        pltpu.make_async_copy(wout_hbm.at[:, features(place_ref, width, False)], wkeep_ref, sems.at[1]),
+        pltpu.make_async_copy(wout_hbm.at[:, pl.ds(send, width // 2)], wsend_ref, sems.at[0]),
+        pltpu.make_async_copy(wout_hbm.at[:, pl.ds(send + width // 2, width // 2)], wlater_ref, sems.at[1]),
+        pltpu.make_async_copy(wout_hbm.at[:, features(place_ref, width, False)], wkeep_ref, sems.at[2]),
     ]
     for load in loads:
         load.start()
@@ -255,16 +301,21 @@
 def finish_queries(place, tokens_other, sums_other, inverse, acc, wq, tables, normed, w_out):
     rows, width = tokens_other.shape
     nq = wq.shape[1]
-    half_out = shaped((w_out.shape[0], width), w_out.dtype)
+    depth = w_out.shape[0]
     return pl.pallas_call(
         queries_kernel,
         in_specs=[SCALAR] + [WHOLE] * 8 + [HBM],
-        out_specs=[WHOLE] * 3,
-        out_shape=[shaped((rows, nq), jnp.bfloat16), half_out, half_out],
+        out_specs=[WHOLE] * 4,
+        out_shape=[
+            shaped((rows, nq), jnp.bfloat16),
+            shaped((depth, width // 2), w_out.dtype),
+            shaped((depth, width // 2), w_out.dtype),
+            shaped((depth, width), w_out.dtype),
+        ],
         scratch_shapes=[
             pltpu.VMEM((rows, width), jnp.bfloat16),
             pltpu.VMEM((rows, nq), jnp.float32),
-            pltpu.SemaphoreType.DMA((2,)),
+            pltpu.SemaphoreType.DMA((3,)),
         ],
         compiler_params=params(16),
         cost_estimate=cost(2 * rows * width * nq, rows * width * 4),
@@ -275,22 +326,25 @@
 TILE = 128
 
 
-def attend_kernel(own, place_ref, lengths_ref, q_ref, *rest):
+def attend_kernel(own, place_ref, q_ref, *rest):
+    rows = q_ref.shape[0]
+    half = rows // 2
     if own:
         blocks, (acc_out, tops_out, sums_out, keys, values, stacked, scores) = rest[:2], rest[2:]
     else:
         blocks, (acc_in, tops_in, sums_in, ctx_ref, keys, values, stacked, scores, acc, tops, sums) = rest[:-11], rest[-11:]
-    rows = q_ref.shape[0]
     heads = q_ref.shape[1] // HEAD
     tall = heads * TILE
     span = scores.shape[2]
-    part = rows // 2
-    for b, block in enumerate(blocks):
-        which = place_ref[0] if b % 2 == 0 else 1 - place_ref[0]
-        at = pl.ds(pl.multiple_of((b // 2) * rows + which * part, part), part)
+    me = place_ref[0]
+    places = [me * half, (1 - me) * half]
+    if not own:
+        places += [rows * (2 - me), rows * (1 + me)]
+    for block, start in zip(blocks, places, strict=True):
+        at = pl.ds(pl.multiple_of(start, half), block.shape[0])
         keys[at, :] = block[:, :HEAD]
         values[at, :] = block[:, HEAD:]
-    behind = 0 if own else len(blocks) // 2 * rows
+    behind = 0 if own else keys.shape[0]
     lane = lax.broadcasted_iota(jnp.int32, (TILE, span), 1)
 
     def tile(t, carry):
@@ -298,13 +352,9 @@
         state = pl.ds(pl.multiple_of(t * tall, tall), tall)
         q_rows = pl.ds(pl.multiple_of(first_row, TILE), TILE)
         row = first_row + lax.broadcasted_iota(jnp.int32, (TILE, span), 0)
-        begin = first_of_document(place_ref, lengths_ref, row) + behind
+        begin = first_of_document(place_ref, row) + behind
         row = row + behind
-        start = -place_ref[1]
-        lowest = start
-        for d in range(lengths_ref.shape[0] - 1):
-            start = start + lengths_ref[d]
-            lowest = jnp.where(first_row >= start, start, lowest)
+        lowest = first_of_document(place_ref, first_row)
         if own:
             acc, tops, sums = acc_out.at[state, :], tops_out.at[state, :], sums_out.at[state, :]
             low = jnp.maximum(lowest, 0) // span
@@ -392,10 +442,10 @@
     lax.fori_loop(0, rows // TILE, tile, 0)
 
 
-def attend(place, lengths, queries, blocks, state=None):
+def attend(place, queries, blocks, state=None):
     rows, width = queries.shape
     own = state is None
-    places = len(blocks) // 2 * rows
+    places = sum(block.shape[0] for block in blocks)
     span = 256 if own else 512
     heads = width // HEAD
     tall = heads * TILE
@@ -412,14 +462,14 @@
         scratch += [pltpu.VMEM((tall, LANES), jnp.float32)] * 3
     return pl.pallas_call(
         functools.partial(attend_kernel, own),
-        in_specs=[SCALAR, SCALAR] + [WHOLE] * (1 + len(blocks) + (0 if own else 3)),
+        in_specs=[SCALAR] + [WHOLE] * (1 + len(blocks) + (0 if own else 3)),
         out_specs=[WHOLE] * 3 if own else WHOLE,
         scratch_shapes=scratch,
         out_shape=out_shape,
         compiler_params=params(20),
         cost_estimate=cost(4 * rows * width * places, rows * width * 8),
         name="attend_own" if own else "attend",
-    )(place, lengths, queries, *blocks, *(state or ()))
+    )(place, queries, *blocks, *(state or ()))
 
 
 def term_kernel(context_ref, w_ref, term_ref):
@@ -443,73 +493,85 @@
     )(context, w)
 
 
-def output_kernel(tokens_ref, term_ref, context_ref, w_ref, out_ref):
+def output_kernel(tokens_ref, term_ref, context_ref, w_ref, w_later_ref, out_ref):
     step = out_ref.shape[1]
-    here = pl.ds(pl.multiple_of(pl.program_id(0) * step, step), step)
-    other = jnp.dot(context_ref[...], w_ref[:, here], preferred_element_type=jnp.float32).astype(jnp.bfloat16)
-    out = tokens_ref[:, here].astype(jnp.float32) + term_ref[:, here].astype(jnp.float32) + other.astype(jnp.float32)
-    out_ref[...] = out.astype(jnp.bfloat16)
-
-
-def output(tokens, term, context, w):
+    j = pl.program_id(0)
+    here = pl.ds(pl.multiple_of(j * step, step), step)
+
+    def work(weights_ref, first):
+        part = pl.ds(pl.multiple_of((j - first) * step, step), step)
+        other = jnp.dot(context_ref[...], weights_ref[:, part], preferred_element_type=jnp.float32).astype(jnp.bfloat16)
+        out = tokens_ref[:, here].astype(jnp.float32) + term_ref[:, here].astype(jnp.float32) + other.astype(jnp.float32)
+        out_ref[...] = out.astype(jnp.bfloat16)
+
+    middle = w_ref.shape[1] // step
+    pl.when(j < middle)(lambda: work(w_ref, 0))
+    pl.when(j >= middle)(lambda: work(w_later_ref, middle))
+
+
+def output(tokens, term, context, w, w_later):
     rows, width = tokens.shape
     depth = context.shape[1]
     step = 1024
     return pl.pallas_call(
         output_kernel,
         grid=(width // step,),
-        in_specs=[WHOLE] * 4,
+        in_specs=[WHOLE] * 5,
         out_specs=pl.BlockSpec((rows, step), lambda j: (0, j)),
         out_shape=shaped((rows, width), jnp.bfloat16),
         compiler_params=params(20),
         cost_estimate=cost(2 * rows * width * depth, rows * width * 4),
         name="output",
-    )(tokens, term, context, w)
-
-
-def shift(value, axis, steps):
-    count = lax.axis_size(axis)
-    return lax.ppermute(value, axis, [(source, source + steps) for source in range(count - steps)])
+    )(tokens, term, context, w, w_later)
 
 
 def swap(value):
     return lax.ppermute(value, "tp", SWAP)
 
 
+def onward(value, distances):
+    count, cores = lax.axis_size("dp"), len(distances)
+    pairs = [
+        (source * cores + core, (source + distance) * cores + core)
+        for core, distance in enumerate(distances)
+        for source in range(count - distance)
+    ]
+    return lax.ppermute(value, ("dp", "tp"), pairs)
+
+
 def local(tokens, norm_gain, lengths, w_query, w_key, w_value, w_out):
     rows = tokens.shape[0]
-    reach = (rows + MOST - 2) // rows
-    place = jnp.stack([lax.axis_index("tp"), lax.axis_index("dp") * rows]).astype(jnp.int32)
+    first_here = lax.axis_index("dp") * rows
+    place = jnp.concatenate([lax.axis_index("tp")[None], first_here[None], lengths]).astype(jnp.int32)
     frequency = 500000.0 ** (-jnp.arange(HEAD // 2, dtype=jnp.float32) * 2.0 / HEAD)
     frequency = jnp.concatenate([frequency, frequency])[None, :]
 
-    sums, tokens, wkv, *tables = load_own(
-        place, lengths, frequency, norm_gain.reshape(-1, LANES), tokens, w_key, w_value
-    )
+    sums, tokens = squares(place, frequency, norm_gain.reshape(-1, LANES), tokens)
     sums_other = swap(sums)
-    tokens, sums_other = lax.optimization_barrier((tokens, sums_other))
+    wkv, *tables = tables_and_weights(place, frequency, w_key, w_value, rows)
+    tokens, sums_other, wkv = lax.optimization_barrier((tokens, sums_other, wkv))
     tokens_other = swap(tokens)
     normed, inverse, kv_partial, wq = keys_own(place, tokens, sums, sums_other, wkv, w_query)
     partial = queries_own(place, normed, wq)
     tokens_other, partial = lax.optimization_barrier((tokens_other, partial))
     kv, normed = finish_keys(place, tokens_other, sums_other, inverse, kv_partial, wkv, tables)
-    kv, normed = lax.optimization_barrier((kv, normed))
-    parts = [shift(kv, "dp", d) for d in range(reach, 0, -1)]
+    assert (rows + MOST - 2) // rows == 3
     kv_other = swap(kv)
-    queries, w_send, w_mine = finish_queries(
+    third = onward(kv, (3, 3))
+    block = onward(join(place, kv, kv_other), (1, 2))
+    queries, w_send, w_later, w_mine = finish_queries(
         place, tokens_other, sums_other, inverse, partial, wq, tables, normed, w_out
     )
-    state = attend(place, lengths, queries, [kv, kv_other])
-    parts, state = lax.optimization_barrier((parts, state))
-    blocks = []
-    for part in parts:
-        blocks += [part, swap(part)]
-    blocks, w_send = lax.optimization_barrier((blocks, w_send))
     w_other = swap(w_send)
-    context = attend(place, lengths, queries, blocks, state)
+    state = attend(place, queries, [kv, kv_other])
+    third, block, state = lax.optimization_barrier((third, block, state))
+    blocks = [third, swap(third), block, swap(block)]
+    blocks, w_later = lax.optimization_barrier((blocks, w_later))
+    w_other_later = swap(w_later)
+    context = attend(place, queries, blocks, state)
     context_other = swap(context)
     term = group_term(context, w_mine)
-    return output(tokens, term, context_other, w_other)
+    return output(tokens, term, context_other, w_other, w_other_later)
 
 
 def solution(mesh):

time: 52.8 us -> 52.8 us (level)
  the two profiles are of different devices: /device:TPU:25 before, /device:TPU:15 now
where the time goes in v5:
time: 52.8 us; the launch traced here: 53.4 us
  Pallas kernels  39.8 us (75%)
  starting transfers between devices  9.76 us (18%)
  waiting for transfers between devices  2.88 us (5%)
  other arithmetic  0.82 us (2%)
    pallas_call x2, Pallas kernels, attend(): pl.pallas_call(functools.partial(attend_kernel, own), in_specs=[SCALAR] +...  14.2 us
    ppermute x2, starting transfers between devices, onward(): return lax.ppermute(value, ('dp', 'tp'), pairs)  5.45 us
    ppermute x8, starting transfers between devices, swap(): return lax.ppermute(value, 'tp', SWAP)  4.31 us
    pallas_call x1, Pallas kernels, output(): pl.pallas_call(output_kernel, grid=(width // step,), in_specs=[WHOLE] * 5...  4.29 us
    pallas_call x1, Pallas kernels, finish_queries(): pl.pallas_call(queries_kernel, in_specs=[SCALAR] + [WHOLE] * 8 + [HBM], o...  4.04 us
    pallas_call x1, Pallas kernels, keys_own(): pl.pallas_call(keys_own_kernel, in_specs=[SCALAR] + [WHOLE] * 4 + [HBM],...  3.93 us
    pallas_call x1, Pallas kernels, squares(): pl.pallas_call(squares_kernel, in_specs=[SCALAR, WHOLE, HBM, HBM], out_sp...  2.89 us
    pallas_call x1, Pallas kernels, queries_own(): pl.pallas_call(queries_own_kernel, in_specs=[SCALAR, WHOLE, WHOLE], out_s...  2.87 us
  transfers between devices with their start and end apart: 10, of which 4 were waited for; matrix products, arithmetic and copies ran while one was open for 0% of the time, Pallas kernels for 57%

profile of v5, /device:TPU:15, one launch (start us, length us, event | category | flops | bytes accessed | tf_op | source)
XLA Modules:
  0.0 53.4 jit_solution(13066978193267117251)
XLA Ops:
  0.1 0.7 %pad_add_fusion.place_ref = s32[10]{0:T(128)S(1)} fusion(s32[8]{0:T(128)} %param.9, s32[1]{0:T(128)} %bitcast.1, s32[1]{0:T(128)} %bitcast), kind=kLoop, calls=%fused_computation | loop fusion | flops 20 | bytes 80 | tf_op jit(solution)/shard_map/concatenate | solution.py:545
  0.8 2.9 %squares.1 = (f32[544,128]{1,0:T(8,128)S(1)}, bf16[512,4096]{1,0:T(8,128)(2,1)S(1)}) custom-call(s32[10]{0:T(128)S(1)} %pad_add_fusion.place_ref, f32[1,128]{1,0:T(1,128)S(1)} %maximum_bitcast_fusion.frequency_ref, bf16[32,128]{1,0:T(8,128)(2,1)} %bitcast.5, bf16[512,4096]{1,0:T(8,128)(2,1)} %tokens_hbm.1), custom_call_target="tpu_custom_call" | custom-call | flops 4194304 | bytes 4194304 | tf_op jit(solution)/shard_map/squares/pallas_call | solution.py:92
  3.7 0.7 %collective-permute-start = (f32[544,128]{1,0:T(8,128)S(1)}, f32[544,128]{1,0:T(8,128)S(1)}, u32[]{:S(2)}, u32[]{:S(2)}) collective-permute-start(f32[544,128]{1,0:T(8,128)S(1)} %get-tuple-element.39.mine_ref), channel_id=1, source_target_pairs={{0,1},{1,0},{2,3},{3,2},{4,5},{5,4},{6,7},{7,6},{8,9},{9,8},{10,11... | collective-permute-start | bytes 835592 | tf_op jit(solution)/shard_map/ppermute | solution.py:529
  4.5 2.8 %tables.1 = (bf16[8192,256]{1,0:T(8,128)(2,1)S(1)}, f32[512,128]{1,0:T(8,128)S(1)}, f32[512,128]{1,0:T(8,128)S(1)}) custom-call(s32[10]{0:T(128)S(1)} %pad_add_fusion.place_ref, f32[1,128]{1,0:T(1,128)S(1)} %maximum_bitcast_fusion.frequency_ref, bf16[8192,128]{1,0:T(8,128)(2,1)} %wk_hbm.1, bf16[8192,128]{1,0:T(8,128)(2,1)} %wv_hbm.1), custom_call_target="tpu_custom_call" | custom-call | flops 6553600 | bytes 4194304 | tf_op jit(solution)/shard_map/tables/pallas_call | solution.py:126
  7.3 3.9 %keys_own.1 = (bf16[512,4096]{1,0:T(8,128)(2,1)S(1)}, f32[512,128]{1,0:T(8,128)S(1)}, f32[256,256]{1,0:T(8,128)S(1)}, bf16[8192,512]{1,0:T(8,128)(2,1)S(1)}) custom-call(s32[10]{0:T(128)S(1)} %pad_add_fusion.place_ref, bf16[512,4096]{1,0:T(8,128)(2,1)S(1)} %get-tuple-element.41.tokens_ref, f32[544,128]{1,0:T(8,128)S(1)} %get-tuple-element.39.mine_ref, ...), custom_call_target="tpu_custom_call" | custom-call | flops 536870912 | bytes 8388608 | tf_op jit(solution)/shard_map/keys_own/pallas_call | solution.py:193
  11.3 2.9 %queries_own.1.acc_ref = f32[512,512]{1,0:T(8,128)S(1)} custom-call(s32[10]{0:T(128)S(1)} %pad_add_fusion.place_ref, bf16[512,4096]{1,0:T(8,128)(2,1)S(1)} %get-tuple-element.44.normed_ref, bf16[8192,512]{1,0:T(8,128)(2,1)S(1)} %get-tuple-element.45.wq_ref), custom_call_target="tpu_custom_call" | custom-call | flops 2147483648 | bytes 1048576 | tf_op jit(solution)/shard_map/queries_own/pallas_call | solution.py:264
  14.2 0.3 collective-permute-done.1.tokens_ref
  14.5 1.8 %keys.1 = (bf16[256,256]{1,0:T(8,128)(2,1)S(1)}, bf16[256,4096]{1,0:T(8,128)(2,1)S(1)}) custom-call(s32[10]{0:T(128)S(1)} %pad_add_fusion.place_ref, bf16[512,4096]{1,0:T(8,128)(2,1)S(1)} %collective-permute-done.1.tokens_ref, f32[544,128]{1,0:T(8,128)S(1)} %collective-permute-done.other_ref.gains_ref, f32[512,128]{1,0:T(8,128)S(1)} %get-tuple-element.47.inverse_ref, ...), custom_call_target="tpu_custom_call" | custom-call | flops 536870912 | bytes 2097152 | tf_op jit(solution)/shard_map/keys/pallas_call | solution.py:224
  16.3 0.2 collective-permute-start.3
  16.5 1.2 %collective-permute-done.3.other_ref.rest_1_ = bf16[256,256]{1,0:T(8,128)(2,1)S(1)} collective-permute-done((bf16[256,256]{1,0:T(8,128)(2,1)S(1)}, bf16[256,256]{1,0:T(8,128)(2,1)S(1)}, u32[]{:S(2)}, u32[]{:S(2)}) %collective-permute-start.3) | collective-permute-done | bytes 131104 | tf_op jit(solution)/shard_map/ppermute | solution.py:529
  17.7 0.6 %join.1 = bf16[512,256]{1,0:T(8,128)(2,1)S(1)} custom-call(s32[10]{0:T(128)S(1)} %pad_add_fusion.place_ref, bf16[256,256]{1,0:T(8,128)(2,1)S(1)} %get-tuple-element.54.mine_ref.rest_0_, bf16[256,256]{1,0:T(8,128)(2,1)S(1)} %collective-permute-done.3.other_ref.rest_1_), custom_call_target="tpu_custom_call" | custom-call | flops 1 | bytes 1 | tf_op jit(solution)/shard_map/join/pallas_call | solution.py:243
  18.3 3.2 %collective-permute-start.4 = (bf16[512,256]{1,0:T(8,128)(2,1)S(1)}, bf16[512,256]{1,0:T(8,128)(2,1)S(1)}, u32[]{:S(2)}, u32[]{:S(2)}) collective-permute-start(bf16[512,256]{1,0:T(8,128)(2,1)S(1)} %join.1), channel_id=1, source_target_pairs={{0,2},{2,4},{4,6},{6,8},{8,10},{10,12},{12,14},{1,5},{3,7},{5,9},{... | collective-permute-start | bytes 786440 | tf_op jit(solution)/shard_map/ppermute | solution.py:539
  21.5 2.2 %collective-permute-start.2 = (bf16[256,256]{1,0:T(8,128)(2,1)S(1)}, bf16[256,256]{1,0:T(8,128)(2,1)S(1)}, u32[]{:S(2)}, u32[]{:S(2)}) collective-permute-start(bf16[256,256]{1,0:T(8,128)(2,1)S(1)} %get-tuple-element.54.mine_ref.rest_0_), channel_id=1, source_target_pairs={{0,6},{2,8},{4,10},{6,12},{8,14},{1,7},{3,9},{5,11},{7,13},{9,15},... | collective-permute-start | bytes 393224 | tf_op jit(solution)/shard_map/ppermute | solution.py:539
  23.8 4.0 %queries.1 = (bf16[512,512]{1,0:T(8,128)(2,1)S(1)}, bf16[512,2048]{1,0:T(8,128)(2,1)S(1)}, bf16[512,2048]{1,0:T(8,128)(2,1)S(1)}, bf16[512,4096]{1,0:T(8,128)(2,1)S(1)}) custom-call(s32[10]{0:T(128)S(1)} %pad_add_fusion.place_ref, bf16[512,4096]{1,0:T(8,128)(2,1)S(1)} %collective-permute-done.1.tokens_ref, ...), custom_call_target="tpu_custom_call" | custom-call | flops 2147483648 | bytes 8388608 | tf_op jit(solution)/shard_map/queries/pallas_call | solution.py:305
  27.8 4.4 %attend_own.1 = (f32[2048,128]{1,0:T(8,128)S(1)}, f32[2048,128]{1,0:T(8,128)S(1)}, f32[2048,128]{1,0:T(8,128)S(1)}) custom-call(s32[10]{0:T(128)S(1)} %pad_add_fusion.place_ref, bf16[512,512]{1,0:T(8,128)(2,1)S(1)} %get-tuple-element.53.q_ref, bf16[256,256]{1,0:T(8,128)(2,1)S(1)} %get-tuple-element.54.mine_ref.rest_0_, ...), custom_call_target="tpu_custom_call" | custom-call | flops 536870912 | bytes 2097152 | tf_op jit(solution)/shard_map/attend_own/pallas_call | solution.py:463
  32.2 0.5 collective-permute-done.2.rest_0_
  32.7 2.2 %collective-permute-start.6 = (bf16[512,256]{1,0:T(8,128)(2,1)S(1)}, bf16[512,256]{1,0:T(8,128)(2,1)S(1)}, u32[]{:S(2)}, u32[]{:S(2)}) collective-permute-start(bf16[512,256]{1,0:T(8,128)(2,1)S(1)} %collective-permute-done.4.rest_2_), channel_id=1, source_target_pairs={{0,1},{1,0},{2,3},{3,2},{4,5},{5,4},{6,7},{7,6},{8,9},{9,8},{10,11... | collective-permute-start | bytes 786440 | tf_op jit(solution)/shard_map/ppermute | solution.py:529
  35.0 0.4 collective-permute-start.8
  35.4 0.8 %collective-permute-done.5.rest_1_ = bf16[256,256]{1,0:T(8,128)(2,1)S(1)} collective-permute-done((bf16[256,256]{1,0:T(8,128)(2,1)S(1)}, bf16[256,256]{1,0:T(8,128)(2,1)S(1)}, u32[]{:S(2)}, u32[]{:S(2)}) %collective-permute-start.5) | collective-permute-done | bytes 131104 | tf_op jit(solution)/shard_map/ppermute | solution.py:529
  36.2 0.4 collective-permute-start.9
  36.6 9.9 %attend.1.context_ref = bf16[512,512]{1,0:T(8,128)(2,1)S(1)} custom-call(s32[10]{0:T(128)S(1)} %pad_add_fusion.place_ref, bf16[512,512]{1,0:T(8,128)(2,1)S(1)} %get-tuple-element.53.q_ref, bf16[256,256]{1,0:T(8,128)(2,1)S(1)} %collective-permute-done.2.rest_0_, bf16[256,256]{1,0:T(8,128)(2,1)S(1)} %collective-permute-done.5.rest_1_, ...), custom_call_target="tpu_custom_call" | custom-call | flops 1610612736 | bytes 2097152 | tf_op jit(solution)/shard_map/attend/pallas_call | solution.py:463
  46.5 0.2 collective-permute-start.7
  46.7 2.4 %own_term.1.term_ref = bf16[512,4096]{1,0:T(8,128)(2,1)S(1)} custom-call(bf16[512,512]{1,0:T(8,128)(2,1)S(1)} %attend.1.context_ref, bf16[512,4096]{1,0:T(8,128)(2,1)S(1)} %get-tuple-element.68.w_ref), custom_call_target="tpu_custom_call" | custom-call | flops 2147483648 | bytes 4194304 | tf_op jit(solution)/shard_map/own_term/pallas_call | solution.py:485
  49.1 4.3 %output.1 = bf16[512,4096]{1,0:T(8,128)(2,1)} custom-call(bf16[512,4096]{1,0:T(8,128)(2,1)S(1)} %get-tuple-element.41.tokens_ref, bf16[512,4096]{1,0:T(8,128)(2,1)S(1)} %own_term.1.term_ref, bf16[512,512]{1,0:T(8,128)(2,1)S(1)} %collective-permute-done.7.context_ref, bf16[512,2048]{1,0:T(8,128)(2,1)S(1)} %collective-permute-done.8.w_ref, ...), custom_call_target="tpu_custom_call" | custom-call | flops 2147483648 | bytes 8388608 | tf_op jit(solution)/shard_map/output/pallas_call | solution.py:516
  (10 shorter events, 0.3 us)
Async XLA Ops:
  3.7 3.5 %collective-permute-start = (f32[544,128]{1,0:T(8,128)S(1)}, f32[544,128]{1,0:T(8,128)S(1)}, u32[]{:S(2)}, u32[]{:S(2)}) collective-permute-start(f32[544,128]{1,0:T(8,128)S(1)} %get-tuple-element.39.mine_ref), channel_id=1, source_target_pairs={{0,1},{1,0},{2,3},{3,2},{4,5},{5,4},{6,7},{7,6},{8,9},{9,8},{10,11... | collective-permute-start | bytes 835592 | tf_op jit(solution)/shard_map/ppermute | solution.py:529
  7.3 7.2 %collective-permute-start.1 = (bf16[512,4096]{1,0:T(8,128)(2,1)S(1)}, bf16[512,4096]{1,0:T(8,128)(2,1)S(1)}, u32[]{:S(2)}, u32[]{:S(2)}) collective-permute-start(bf16[512,4096]{1,0:T(8,128)(2,1)S(1)} %get-tuple-element.41.tokens_ref), channel_id=1, source_target_pairs={{0,1},{1,0},{2,3},{3,2},{4,5},{5,4},{6,7},{7,6},{8,9},{9,8},{10,11... | collective-permute-start | bytes 12582920 | tf_op jit(solution)/shard_map/ppermute | solution.py:529
  16.3 1.4 %collective-permute-start.3 = (bf16[256,256]{1,0:T(8,128)(2,1)S(1)}, bf16[256,256]{1,0:T(8,128)(2,1)S(1)}, u32[]{:S(2)}, u32[]{:S(2)}) collective-permute-start(bf16[256,256]{1,0:T(8,128)(2,1)S(1)} %get-tuple-element.54.mine_ref.rest_0_), channel_id=1, source_target_pairs={{0,1},{1,0},{2,3},{3,2},{4,5},{5,4},{6,7},{7,6},{8,9},{9,8},{10,11... | collective-permute-start | bytes 393224 | tf_op jit(solution)/shard_map/ppermute | solution.py:529
  18.3 14.4 %collective-permute-start.4 = (bf16[512,256]{1,0:T(8,128)(2,1)S(1)}, bf16[512,256]{1,0:T(8,128)(2,1)S(1)}, u32[]{:S(2)}, u32[]{:S(2)}) collective-permute-start(bf16[512,256]{1,0:T(8,128)(2,1)S(1)} %join.1), channel_id=1, source_target_pairs={{0,2},{2,4},{4,6},{6,8},{8,10},{10,12},{12,14},{1,5},{3,7},{5,9},{... | collective-permute-start | bytes 786440 | tf_op jit(solution)/shard_map/ppermute | solution.py:539
  21.5 11.2 %collective-permute-start.2 = (bf16[256,256]{1,0:T(8,128)(2,1)S(1)}, bf16[256,256]{1,0:T(8,128)(2,1)S(1)}, u32[]{:S(2)}, u32[]{:S(2)}) collective-permute-start(bf16[256,256]{1,0:T(8,128)(2,1)S(1)} %get-tuple-element.54.mine_ref.rest_0_), channel_id=1, source_target_pairs={{0,6},{2,8},{4,10},{6,12},{8,14},{1,7},{3,9},{5,11},{7,13},{9,15},... | collective-permute-start | bytes 393224 | tf_op jit(solution)/shard_map/ppermute | solution.py:539
  32.7 3.5 %collective-permute-start.6 = (bf16[512,256]{1,0:T(8,128)(2,1)S(1)}, bf16[512,256]{1,0:T(8,128)(2,1)S(1)}, u32[]{:S(2)}, u32[]{:S(2)}) collective-permute-start(bf16[512,256]{1,0:T(8,128)(2,1)S(1)} %collective-permute-done.4.rest_2_), channel_id=1, source_target_pairs={{0,1},{1,0},{2,3},{3,2},{4,5},{5,4},{6,7},{7,6},{8,9},{9,8},{10,11... | collective-permute-start | bytes 786440 | tf_op jit(solution)/shard_map/ppermute | solution.py:529
  34.9 1.3 %collective-permute-start.5 = (bf16[256,256]{1,0:T(8,128)(2,1)S(1)}, bf16[256,256]{1,0:T(8,128)(2,1)S(1)}, u32[]{:S(2)}, u32[]{:S(2)}) collective-permute-start(bf16[256,256]{1,0:T(8,128)(2,1)S(1)} %collective-permute-done.2.rest_0_), channel_id=1, source_target_pairs={{0,1},{1,0},{2,3},{3,2},{4,5},{5,4},{6,7},{7,6},{8,9},{9,8},{10,11... | collective-permute-start | bytes 393224 | tf_op jit(solution)/shard_map/ppermute | solution.py:529
  35.0 14.1 %collective-permute-start.8 = (bf16[512,2048]{1,0:T(8,128)(2,1)S(1)}, bf16[512,2048]{1,0:T(8,128)(2,1)S(1)}, u32[]{:S(2)}, u32[]{:S(2)}) collective-permute-start(bf16[512,2048]{1,0:T(8,128)(2,1)S(1)} %get-tuple-element.69), channel_id=1, source_target_pairs={{0,1},{1,0},{2,3},{3,2},{4,5},{5,4},{6,7},{7,6},{8,9},{9,8},{10,11... | collective-permute-start | bytes 6291464 | tf_op jit(solution)/shard_map/ppermute | solution.py:529
  36.2 12.8 %collective-permute-start.9 = (bf16[512,2048]{1,0:T(8,128)(2,1)S(1)}, bf16[512,2048]{1,0:T(8,128)(2,1)S(1)}, u32[]{:S(2)}, u32[]{:S(2)}) collective-permute-start(bf16[512,2048]{1,0:T(8,128)(2,1)S(1)} %get-tuple-element.70), channel_id=1, source_target_pairs={{0,1},{1,0},{2,3},{3,2},{4,5},{5,4},{6,7},{7,6},{8,9},{9,8},{10,11... | collective-permute-start | bytes 6291464 | tf_op jit(solution)/shard_map/ppermute | solution.py:529
  46.5 2.6 %collective-permute-start.7 = (bf16[512,512]{1,0:T(8,128)(2,1)S(1)}, bf16[512,512]{1,0:T(8,128)(2,1)S(1)}, u32[]{:S(2)}, u32[]{:S(2)}) collective-permute-start(bf16[512,512]{1,0:T(8,128)(2,1)S(1)} %attend.1.context_ref), channel_id=1, source_target_pairs={{0,1},{1,0},{2,3},{3,2},{4,5},{5,4},{6,7},{7,6},{8,9},{9,8},{10,11... | collective-permute-start | bytes 1572872 | tf_op jit(solution)/shard_map/ppermute | solution.py:529

commit v6 on v5

v6 whole, which is shorter than its diff:
```python
import functools
import math

import jax
import jax.numpy as jnp
from jax import lax
from jax.experimental import pallas as pl
from jax.experimental.pallas import tpu as pltpu
from jax.sharding import PartitionSpec as P

HEAD = 128
MOST = 1536
LANES = 128
SWAP = [(0, 1), (1, 0)]
MIB = 1024 * 1024
EXP2_SCALE = math.log2(math.e) / HEAD**0.5

SCALAR = pl.BlockSpec(memory_space=pltpu.SMEM)
WHOLE = pl.BlockSpec(memory_space=pltpu.VMEM)
HBM = pl.BlockSpec(memory_space=pltpu.HBM)


def in_hbm(*arrays):
    return [pltpu.with_memory_space_constraint(array, pltpu.HBM) for array in arrays]


def params(mib):
    return pltpu.CompilerParams(vmem_limit_bytes=mib * MIB)


def cost(flops, moved):
    return pl.CostEstimate(flops=flops, bytes_accessed=moved, transcendentals=0)


SMALL = cost(1, 1)


def shaped(shape, dtype):
    return jax.ShapeDtypeStruct(shape, dtype)


def first_of_document(place_ref, row):
    start = -place_ref[1]
    begin = jnp.full(jnp.shape(row), start, jnp.int32)
    for d in range(2, place_ref.shape[0] - 1):
        start = start + place_ref[d]
        begin = jnp.where(row >= start, start, begin)
    return begin


ROWS = 64
WIDE = 256


def block_rows(start, r):
    return pl.ds(pl.multiple_of(start + r * ROWS, ROWS), ROWS)


def wide_slice(ref, at, j):
    wide = ref[at, j : j + WIDE].astype(jnp.float32)
    return [wide[:, i : i + LANES] for i in range(0, WIDE, LANES)]


def squares_kernel(place_ref, frequency_ref, gain_hbm, tokens_hbm, sums_ref, tokens_ref, gain_ref, sems):
    rows, width = tokens_ref.shape
    chunks = sems.shape[0] - 1
    height = rows // chunks
    loads = [
        pltpu.make_async_copy(
            tokens_hbm.at[c * height : (c + 1) * height], tokens_ref.at[c * height : (c + 1) * height], sems.at[c]
        )
        for c in range(chunks)
    ]
    loads.append(pltpu.make_async_copy(gain_hbm, gain_ref, sems.at[chunks]))
    for load in loads:
        load.start()
    for c in range(chunks):
        loads[c].wait()
        for r in range(height // ROWS):
            at = slice(c * height + r * ROWS, c * height + (r + 1) * ROWS)
            total = jnp.zeros((ROWS, LANES), jnp.float32)
            for j in range(0, width, WIDE):
                for wide in wide_slice(tokens_ref, at, j):
                    total = total + wide * wide
            sums_ref[at, :] = total
    loads[chunks].wait()
    sums_ref[rows:, :] = gain_ref[...].astype(jnp.float32)


def squares(place, frequency, gain, tokens):
    rows, width = tokens.shape
    return pl.pallas_call(
        squares_kernel,
        in_specs=[SCALAR, WHOLE, HBM, HBM],
        out_specs=[WHOLE] * 2,
        out_shape=[shaped((rows + gain.shape[0], LANES), jnp.float32), shaped(tokens.shape, tokens.dtype)],
        scratch_shapes=[pltpu.VMEM(gain.shape, gain.dtype), pltpu.SemaphoreType.DMA((8 + 1,))],
        compiler_params=params(16),
        cost_estimate=cost(rows * width * 2, rows * width * 2),
        name="squares",
    )(place, frequency, *in_hbm(gain, tokens))


def tables_kernel(place_ref, frequency_ref, wk_hbm, wv_hbm, wk_ref, wv_ref, cos_ref, sin_ref, sems):
    rows = cos_ref.shape[0]
    half = rows // 2
    loads = [
        pltpu.make_async_copy(wk_hbm, wk_ref, sems.at[0]),
        pltpu.make_async_copy(wv_hbm, wv_ref, sems.at[1]),
    ]
    for load in loads:
        load.start()
    lane = lax.broadcasted_iota(jnp.int32, (half, HEAD), 1)
    row = lax.broadcasted_iota(jnp.int32, (half, HEAD), 0) + jnp.where(lane < HEAD // 2, 0, half)
    angles = (row - first_of_document(place_ref, row)).astype(jnp.float32) * frequency_ref[...]
    for table_ref, table, sign in ((cos_ref, jnp.cos(angles), 1.0), (sin_ref, jnp.sin(angles), -1.0)):
        turned = pltpu.roll(table, HEAD // 2, 1)
        low = lane < HEAD // 2
        table_ref[:half, :] = jnp.where(low, sign * table, turned)
        table_ref[half:, :] = jnp.where(low, sign * turned, table)
    for load in loads:
        load.wait()


def tables_and_weights(place, frequency, wk, wv, rows):
    return pl.pallas_call(
        tables_kernel,
        in_specs=[SCALAR, WHOLE, HBM, HBM],
        out_specs=[WHOLE] * 4,
        out_shape=[
            shaped(wk.shape, wk.dtype),
            shaped(wv.shape, wv.dtype),
            shaped((rows, HEAD), jnp.float32),
            shaped((rows, HEAD), jnp.float32),
        ],
        scratch_shapes=[pltpu.SemaphoreType.DMA((2,))],
        compiler_params=params(16),
        cost_estimate=cost(rows * HEAD * 100, wk.size * 4),
        name="tables",
    )(place, frequency, *in_hbm(wk, wv))


def normalize(out_ref, out_start, tokens_ref, start, count, inverse_ref, gains_ref):
    rows, width = tokens_ref.shape

    def block(r, carry):
        at = block_rows(start, r)
        out_at = block_rows(out_start, r)
        inverse = inverse_ref[at, :]
        for j in range(0, width, WIDE):
            normed = []
            for i, wide in enumerate(wide_slice(tokens_ref, at, j)):
                gain_row = rows + j // LANES + i
                normed.append(wide * inverse * gains_ref[gain_row : gain_row + 1, :])
            out_ref[out_at, j : j + WIDE] = jnp.concatenate(normed, axis=1).astype(jnp.bfloat16)
        return carry

    lax.fori_loop(0, count // ROWS, block, 0)


def turn(x, cosine, sine):
    return (x * cosine + pltpu.roll(x, HEAD // 2, 1) * sine).astype(jnp.bfloat16)


def own_rows(rows):
    half = rows // 2
    return pl.ds(pl.multiple_of(lax.axis_index("tp") * half, half), half)


def features(width, other):
    me = lax.axis_index("tp")
    which = 1 - me if other else me
    return pl.ds(pl.multiple_of(which * width, width), width)


def keys_own_kernel(
    tokens_ref, mine_ref, other_ref, wk_ref, wv_ref, wq_hbm, normed_ref, inverse_ref, acc_ref, wq_ref, sem
):
    rows, width = tokens_ref.shape
    load = pltpu.make_async_copy(wq_hbm, wq_ref, sem)
    load.start()
    mean = jnp.sum(mine_ref[0:rows, :] + other_ref[0:rows, :], axis=1, keepdims=True) * (0.5 / width)
    inverse_ref[...] = jnp.broadcast_to(lax.rsqrt(mean + 1e-05), (rows, LANES))
    normalize(normed_ref, 0, tokens_ref, 0, rows, inverse_ref, mine_ref)
    acc_ref[...] = jnp.dot(
        normed_ref[own_rows(rows), :],
        both_weights(wk_ref, wv_ref, features(width, False)),
        preferred_element_type=jnp.float32,
    )
    load.wait()


def keys_own(tokens, sums, sums_other, wk, wv, wq):
    rows, width = tokens.shape
    return pl.pallas_call(
        keys_own_kernel,
        in_specs=[WHOLE] * 5 + [HBM],
        out_specs=[WHOLE] * 4,
        out_shape=[
            shaped(tokens.shape, jnp.bfloat16),
            shaped((rows, LANES), jnp.float32),
            shaped((rows // 2, 2 * HEAD), jnp.float32),
            shaped(wq.shape, wq.dtype),
        ],
        scratch_shapes=[pltpu.SemaphoreType.DMA],
        compiler_params=params(16),
        cost_estimate=cost(2 * rows * width * HEAD, wq.size * 2),
        name="keys_own",
    )(tokens, sums, sums_other, wk, wv, *in_hbm(wq))


def both_weights(wk_ref, wv_ref, depth):
    return jnp.concatenate([wk_ref[depth, :], wv_ref[depth, :]], axis=1)


def keys_kernel(tokens_ref, gains_ref, inverse_ref, acc_ref, wk_ref, wv_ref, cos_ref, sin_ref, kv_ref, normed_ref):
    rows, width = tokens_ref.shape
    half = rows // 2
    here = own_rows(rows)
    normalize(normed_ref, 0, tokens_ref, lax.axis_index("tp") * half, half, inverse_ref, gains_ref)
    total = acc_ref[...] + jnp.dot(
        normed_ref[...], both_weights(wk_ref, wv_ref, features(width, True)), preferred_element_type=jnp.float32
    )
    kv_ref[:, :HEAD] = turn(total[:, :HEAD], cos_ref[here, :], sin_ref[here, :])
    kv_ref[:, HEAD:] = total[:, HEAD:].astype(jnp.bfloat16)


def finish_keys(tokens_other, sums_other, inverse, acc, wk, wv, tables):
    rows, width = tokens_other.shape
    return pl.pallas_call(
        keys_kernel,
        in_specs=[WHOLE] * 8,
        out_specs=[WHOLE] * 2,
        out_shape=[shaped(acc.shape, jnp.bfloat16), shaped((rows // 2, width), jnp.bfloat16)],
        compiler_params=params(16),
        cost_estimate=cost(2 * rows * width * HEAD, rows * width),
        name="keys",
    )(tokens_other, sums_other, inverse, acc, wk, wv, *tables)


def join_kernel(mine_ref, other_ref, out_ref):
    half = mine_ref.shape[0]
    me = lax.axis_index("tp")
    for block, which in ((mine_ref, me), (other_ref, 1 - me)):
        out_ref[pl.ds(pl.multiple_of(which * half, half), half), :] = block[...]


def join(mine, other):
    half, width = mine.shape
    return pl.pallas_call(
        join_kernel,
        in_specs=[WHOLE] * 2,
        out_specs=WHOLE,
        out_shape=shaped((2 * half, width), mine.dtype),
        compiler_params=params(8),
        cost_estimate=SMALL,
        name="join",
    )(mine, other)


def queries_own_kernel(normed_ref, wq_ref, acc_ref):
    width = normed_ref.shape[1]
    acc_ref[...] = jnp.dot(
        normed_ref[...], wq_ref[features(width, False), :], preferred_element_type=jnp.float32
    )


def queries_own(normed, wq):
    rows, width = normed.shape
    nq = wq.shape[1]
    return pl.pallas_call(
        queries_own_kernel,
        in_specs=[WHOLE, WHOLE],
        out_specs=WHOLE,
        out_shape=shaped((rows, nq), jnp.float32),
        compiler_params=params(12),
        cost_estimate=cost(2 * rows * width * nq, rows * nq * 4),
        name="queries_own",
    )(normed, wq)


def queries_kernel(
    tokens_ref, gains_ref, inverse_ref, acc_ref, wq_ref, cos_ref, sin_ref, ready_ref, wout_hbm,
    q_ref, wsend_ref, wlater_ref, wkeep_ref, normed_ref, acc, sems,
):
    rows, width = tokens_ref.shape
    half = rows // 2
    send = pl.multiple_of((1 - lax.axis_index("tp")) * width, width)
    loads = [
        pltpu.make_async_copy(wout_hbm.at[:, pl.ds(send, width // 2)], wsend_ref, sems.at[0]),
        pltpu.make_async_copy(wout_hbm.at[:, pl.ds(send + width // 2, width // 2)], wlater_ref, sems.at[1]),
        pltpu.make_async_copy(wout_hbm.at[:, features(width, False)], wkeep_ref, sems.at[2]),
    ]
    for load in loads:
        load.start()
    normed_ref[own_rows(rows), :] = ready_ref[...]
    there = (1 - lax.axis_index("tp")) * half
    normalize(normed_ref, there, tokens_ref, there, half, inverse_ref, gains_ref)
    acc[...] = acc_ref[...] + jnp.dot(
        normed_ref[...], wq_ref[features(width, True), :], preferred_element_type=jnp.float32
    )
    for h in range(q_ref.shape[1] // HEAD):
        lanes = slice(h * HEAD, (h + 1) * HEAD)
        q_ref[:, lanes] = turn(acc[:, lanes], cos_ref[...], sin_ref[...])
    for load in loads:
        load.wait()


def finish_queries(tokens_other, sums_other, inverse, acc, wq, tables, normed, w_out):
    rows, width = tokens_other.shape
    nq = wq.shape[1]
    depth = w_out.shape[0]
    return pl.pallas_call(
        queries_kernel,
        in_specs=[WHOLE] * 8 + [HBM],
        out_specs=[WHOLE] * 4,
        out_shape=[
            shaped((rows, nq), jnp.bfloat16),
            shaped((depth, width // 2), w_out.dtype),
            shaped((depth, width // 2), w_out.dtype),
            shaped((depth, width), w_out.dtype),
        ],
        scratch_shapes=[
            pltpu.VMEM((rows, width), jnp.bfloat16),
            pltpu.VMEM((rows, nq), jnp.float32),
            pltpu.SemaphoreType.DMA((3,)),
        ],
        compiler_params=params(16),
        cost_estimate=cost(2 * rows * width * nq, rows * width * 4),
        name="queries",
    )(tokens_other, sums_other, inverse, acc, wq, *tables, normed, *in_hbm(w_out))


TILE = 128
SPAN = 512


def place_blocks(blocks, starts, keys, values):
    for block, start in zip(blocks, starts, strict=True):
        at = pl.ds(pl.multiple_of(start, block.shape[0]), block.shape[0])
        keys[at, :] = block[:, :HEAD]
        values[at, :] = block[:, HEAD:]


def lanes_max(x):
    return jnp.broadcast_to(jnp.max(x, axis=1, keepdims=True), x.shape)


def weigh(scores, probs, at, first, count, top):
    scaled = top * EXP2_SCALE
    total = jnp.zeros((ROWS, LANES), jnp.float32)
    for j in range(0, count, WIDE):
        weights = []
        for i in range(j, j + WIDE, LANES):
            w = jnp.exp2(scores[at, first + i : first + i + LANES] * EXP2_SCALE - scaled)
            total = total + w
            weights.append(w)
        probs[at, first + j : first + j + WIDE] = jnp.concatenate(weights, axis=1).astype(jnp.bfloat16)
    return total


def attend_own_kernel(place_ref, q_ref, mine_ref, other_ref, acc_ref, tops_ref, sums_ref, keys, values, bias, scores, probs):
    rows = q_ref.shape[0]
    half = rows // 2
    me = lax.axis_index("tp")
    place_blocks([mine_ref, other_ref], [me * half, (1 - me) * half], keys, values)
    row = lax.broadcasted_iota(jnp.int32, (rows, LANES), 0)
    lane = lax.broadcasted_iota(jnp.int32, (rows, LANES), 1)
    begin = first_of_document(place_ref, row)
    for j in range(0, rows, LANES):
        allowed = (lane + j >= begin) & (lane + j <= row)
        bias[:, j : j + LANES] = jnp.where(allowed, 0.0, -1e30)
    for h in range(q_ref.shape[1] // HEAD):
        for first, count in ((0, half), (half, rows)):
            scores[:, :count] = lax.dot_general(
                q_ref[first : first + half, h * HEAD : (h + 1) * HEAD],
                keys[:count, :],
                (((1,), (1,)), ((), ())),
                preferred_element_type=jnp.float32,
            )
            out = h * rows + first

            def block(r, carry):
                at = block_rows(0, r)
                out_at = block_rows(out, r)
                top = jnp.full((ROWS, LANES), -1e30, jnp.float32)
                for j in range(0, count, LANES):
                    s = scores[at, j : j + LANES] + bias[block_rows(first, r), j : j + LANES]
                    scores[at, j : j + LANES] = s
                    top = jnp.maximum(top, s)
                top = lanes_max(top)
                tops_ref[out_at, :] = top
                sums_ref[out_at, :] = weigh(scores, probs, at, 0, count, top)
                return carry

            lax.fori_loop(0, half // ROWS, block, 0, unroll=True)
            acc_ref[out : out + half, :] = jnp.dot(
                probs[:, :count], values[:count, :], preferred_element_type=jnp.float32
            )


def attend_kernel(
    place_ref, q_ref, third_ref, third_other_ref, block_ref, block_other_ref, acc_in, tops_in, sums_in,
    ctx_ref, keys, values, stacked, scores, probs, acc, sums,
):
    rows = q_ref.shape[0]
    half = rows // 2
    heads = q_ref.shape[1] // HEAD
    tall = heads * TILE
    behind = keys.shape[0]
    me = lax.axis_index("tp")
    place_blocks(
        [third_ref, third_other_ref, block_ref, block_other_ref],
        [me * half, (1 - me) * half, rows * (2 - me), rows * (1 + me)],
        keys,
        values,
    )
    start = -place_ref[1]
    begin, end = start, jnp.int32(rows)
    for d in range(2, place_ref.shape[0] - 1):
        start = start + place_ref[d]
        begin = jnp.where(start <= 0, start, begin)
        end = jnp.where(start > 0, jnp.minimum(end, start), end)
    low = begin + behind
    lane = lax.broadcasted_iota(jnp.int32, (ROWS, LANES), 1)
    line = lax.broadcasted_iota(jnp.int32, (ROWS, LANES), 0)

    def alone(at, q_at, h):
        total = jnp.sum(sums_in[at, :], axis=1, keepdims=True)
        ctx_ref[q_at, h * HEAD : (h + 1) * HEAD] = (acc_in[at, :] / total).astype(jnp.bfloat16)

    def tile(t, carry):
        reached = (t * TILE < end) & (low < behind)

        @pl.when(jnp.logical_not(reached))
        def _():
            for h in range(heads):
                for r in range(TILE // ROWS):
                    alone(block_rows(h * rows + t * TILE, r), block_rows(t * TILE, r), h)

        def merge(first):
            for h in range(heads):
                stacked[h * TILE : (h + 1) * TILE, :] = q_ref[
                    pl.ds(pl.multiple_of(t * TILE, TILE), TILE), h * HEAD : (h + 1) * HEAD
                ]
            scores[:, first:] = lax.dot_general(
                stacked[...], keys[first:, :], (((1,), (1,)), ((), ())), preferred_element_type=jnp.float32
            )
            for h in range(heads):
                for r in range(TILE // ROWS):
                    at = slice(h * TILE + r * ROWS, h * TILE + (r + 1) * ROWS)
                    state = block_rows(h * rows + t * TILE, r)
                    own_top = tops_in[state, :]
                    top = own_top
                    for j in range(first, behind, LANES):
                        s = scores[at, j : j + LANES]
                        if j < first + SPAN:
                            s = jnp.where(lane + j >= low, s, -1e30)
                            scores[at, j : j + LANES] = s
                        top = jnp.maximum(top, s)
                    top = lanes_max(top)
                    rescale = jnp.exp2((own_top - top) * EXP2_SCALE)
                    acc[at, :] = acc_in[state, :] * rescale
                    sums[at, :] = sums_in[state, :] * rescale + weigh(scores, probs, at, first, behind - first, top)
            acc[...] += jnp.dot(probs[:, first:], values[first:, :], preferred_element_type=jnp.float32)
            for h in range(heads):
                for r in range(TILE // ROWS):
                    at = slice(h * TILE + r * ROWS, h * TILE + (r + 1) * ROWS)
                    state = block_rows(h * rows + t * TILE, r)
                    merged = line + (t * TILE + r * ROWS) < end
                    total = jnp.sum(jnp.where(merged, sums[at, :], sums_in[state, :]), axis=1, keepdims=True)
                    context = jnp.where(merged, acc[at, :], acc_in[state, :]) / total
                    ctx_ref[block_rows(t * TILE, r), h * HEAD : (h + 1) * HEAD] = context.astype(jnp.bfloat16)

        for first in range(0, behind, SPAN):
            inside = (low >= first) & (low < first + SPAN)
            pl.when(reached & inside)(functools.partial(merge, first))
        return carry

    lax.fori_loop(0, rows // TILE, tile, 0)


def attend_own(place, queries, blocks):
    rows, width = queries.shape
    half = rows // 2
    heads = width // HEAD
    return pl.pallas_call(
        attend_own_kernel,
        in_specs=[SCALAR] + [WHOLE] * 3,
        out_specs=[WHOLE] * 3,
        scratch_shapes=[
            pltpu.VMEM((rows, HEAD), jnp.bfloat16),
            pltpu.VMEM((rows, HEAD), jnp.bfloat16),
            pltpu.VMEM((rows, rows), jnp.float32),
            pltpu.VMEM((half, rows), jnp.float32),
            pltpu.VMEM((half, rows), jnp.bfloat16),
        ],
        out_shape=[shaped((heads * rows, LANES), jnp.float32)] * 3,
        compiler_params=params(16),
        cost_estimate=cost(4 * rows * width * rows, rows * width * 8),
        name="attend_own",
    )(place, queries, *blocks)


def attend(place, queries, blocks, state):
    rows, width = queries.shape
    heads = width // HEAD
    tall = heads * TILE
    places = sum(block.shape[0] for block in blocks)
    return pl.pallas_call(
        attend_kernel,
        in_specs=[SCALAR] + [WHOLE] * (1 + len(blocks) + len(state)),
        out_specs=WHOLE,
        scratch_shapes=[
            pltpu.VMEM((places, HEAD), jnp.bfloat16),
            pltpu.VMEM((places, HEAD), jnp.bfloat16),
            pltpu.VMEM((tall, HEAD), jnp.bfloat16),
            pltpu.VMEM((tall, places), jnp.float32),
            pltpu.VMEM((tall, places), jnp.bfloat16),
            pltpu.VMEM((tall, HEAD), jnp.float32),
            pltpu.VMEM((tall, LANES), jnp.float32),
        ],
        out_shape=shaped((rows, width), jnp.bfloat16),
        compiler_params=params(20),
        cost_estimate=cost(4 * rows * width * places, rows * width * 8),
        name="attend",
    )(place, queries, *blocks, *state)


def term_kernel(context_ref, w_ref, term_ref):
    step = 1024
    for c in range(w_ref.shape[1] // step):
        part = slice(c * step, (c + 1) * step)
        term_ref[:, part] = jnp.dot(context_ref[...], w_ref[:, part], preferred_element_type=jnp.float32).astype(jnp.bfloat16)


def group_term(context, w):
    rows, depth = context.shape
    width = w.shape[1]
    return pl.pallas_call(
        term_kernel,
        in_specs=[WHOLE] * 2,
        out_specs=WHOLE,
        out_shape=shaped((rows, width), jnp.bfloat16),
        compiler_params=params(16),
        cost_estimate=cost(2 * rows * depth * width, rows * width * 2),
        name="own_term",
    )(context, w)


def output_kernel(tokens_ref, term_ref, context_ref, w_ref, w_later_ref, out_ref):
    step = out_ref.shape[1]
    j = pl.program_id(0)
    here = pl.ds(pl.multiple_of(j * step, step), step)

    def work(weights_ref, first):
        part = pl.ds(pl.multiple_of((j - first) * step, step), step)
        other = jnp.dot(context_ref[...], weights_ref[:, part], preferred_element_type=jnp.float32).astype(jnp.bfloat16)
        out = tokens_ref[:, here].astype(jnp.float32) + term_ref[:, here].astype(jnp.float32) + other.astype(jnp.float32)
        out_ref[...] = out.astype(jnp.bfloat16)

    middle = w_ref.shape[1] // step
    pl.when(j < middle)(lambda: work(w_ref, 0))
    pl.when(j >= middle)(lambda: work(w_later_ref, middle))


def output(tokens, term, context, w, w_later):
    rows, width = tokens.shape
    depth = context.shape[1]
    step = 1024
    return pl.pallas_call(
        output_kernel,
        grid=(width // step,),
        in_specs=[WHOLE] * 5,
        out_specs=pl.BlockSpec((rows, step), lambda j: (0, j)),
        out_shape=shaped((rows, width), jnp.bfloat16),
        compiler_params=params(20),
        cost_estimate=cost(2 * rows * width * depth, rows * width * 4),
        name="output",
    )(tokens, term, context, w, w_later)


def swap(value):
    return lax.ppermute(value, "tp", SWAP)


def onward(value, distances):
    count, cores = lax.axis_size("dp"), len(distances)
    pairs = [
        (source * cores + core, (source + distance) * cores + core)
        for core, distance in enumerate(distances)
        for source in range(count - distance)
    ]
    return lax.ppermute(value, ("dp", "tp"), pairs)


def local(tokens, norm_gain, lengths, w_query, w_key, w_value, w_out):
    rows = tokens.shape[0]
    first_here = lax.axis_index("dp") * rows
    place = jnp.concatenate([lax.axis_index("tp")[None], first_here[None], lengths]).astype(jnp.int32)
    frequency = 500000.0 ** (-jnp.arange(HEAD // 2, dtype=jnp.float32) * 2.0 / HEAD)
    frequency = jnp.concatenate([frequency, frequency])[None, :]

    sums, tokens = squares(place, frequency, norm_gain.reshape(-1, LANES), tokens)
    sums_other = swap(sums)
    wk, wv, *tables = tables_and_weights(place, frequency, w_key, w_value, rows)
    tokens, sums_other, wk = lax.optimization_barrier((tokens, sums_other, wk))
    tokens_other = swap(tokens)
    normed, inverse, kv_partial, wq = keys_own(tokens, sums, sums_other, wk, wv, w_query)
    partial = queries_own(normed, wq)
    tokens_other, partial = lax.optimization_barrier((tokens_other, partial))
    kv, normed = finish_keys(tokens_other, sums_other, inverse, kv_partial, wk, wv, tables)
    assert (rows + MOST - 2) // rows == 3
    kv_other = swap(kv)
    third = onward(kv, (3, 3))
    block = onward(join(kv, kv_other), (1, 2))
    queries, w_send, w_later, w_mine = finish_queries(
        tokens_other, sums_other, inverse, partial, wq, tables, normed, w_out
    )
    w_other = swap(w_send)
    state = attend_own(place, queries, [kv, kv_other])
    third, block, state = lax.optimization_barrier((third, block, state))
    blocks = [third, swap(third), block, swap(block)]
    blocks, w_later = lax.optimization_barrier((blocks, w_later))
    w_other_later = swap(w_later)
    context = attend(place, queries, blocks, state)
    context_other = swap(context)
    term = group_term(context, w_mine)
    return output(tokens, term, context_other, w_other, w_other_later)


def solution(mesh):
    placed = (P(("grp", "dp"), "tp"), P("tp"), P("grp"), P(None, "tp"), P(), P(), P("tp", None))
    return jax.shard_map(
        local, mesh=mesh, in_specs=placed, out_specs=P(("grp", "dp"), "tp"), check_vma=False
    )
```

time: 52.8 us -> 47 us (0.89)
  the two profiles are of different devices: /device:TPU:15 before, /device:TPU:25 now
where the time goes in v6:
time: 47 us
  Pallas kernels  30.1 us (64%)
  waiting for transfers between devices  10.2 us (22%)
  starting transfers between devices  5.76 us (12%)
  other arithmetic  0.82 us (2%)
    ppermute x2, waiting for transfers between devices, onward(): return lax.ppermute(value, ('dp', 'tp'), pairs)  6.71 us
    pallas_call x1, Pallas kernels, output(): pl.pallas_call(output_kernel, grid=(width // step,), in_specs=[WHOLE] * 5...  4.23 us
    pallas_call x1, Pallas kernels, attend(): pl.pallas_call(attend_kernel, in_specs=[SCALAR] + [WHOLE] * (1 + len(bloc...  4.16 us
    pallas_call x1, Pallas kernels, finish_queries(): pl.pallas_call(queries_kernel, in_specs=[WHOLE] * 8 + [HBM], out_specs=[W...  3.51 us
    ppermute x8, waiting for transfers between devices, swap(): return lax.ppermute(value, 'tp', SWAP)  3.47 us
    pallas_call x1, Pallas kernels, keys_own(): pl.pallas_call(keys_own_kernel, in_specs=[WHOLE] * 5 + [HBM], out_specs=[...  3.39 us
    pallas_call x1, Pallas kernels, attend_own(): pl.pallas_call(attend_own_kernel, in_specs=[SCALAR] + [WHOLE] * 3, out_sp...  3.18 us
    ppermute x8, starting transfers between devices, swap(): return lax.ppermute(value, 'tp', SWAP)  2.99 us
  transfers between devices with their start and end apart: 10, of which 4 were waited for; matrix products, arithmetic and copies ran while one was open for 0% of the time, Pallas kernels for 46%

profile of v6, /device:TPU:25, one launch (start us, length us, event | category | flops | bytes accessed | tf_op | source)
XLA Modules:
  0.0 47.0 jit_solution(1419369606803147356)
XLA Ops:
  0.1 0.7 %pad_add_fusion.place_ref = s32[10]{0:T(128)S(1)} fusion(s32[8]{0:T(128)} %param.9, s32[1]{0:T(128)} %bitcast.1, s32[1]{0:T(128)} %bitcast), kind=kLoop, calls=%fused_computation | loop fusion | flops 20 | bytes 80 | tf_op jit(solution)/shard_map/concatenate | solution.py:600
  0.8 2.9 %squares.1 = (f32[544,128]{1,0:T(8,128)S(1)}, bf16[512,4096]{1,0:T(8,128)(2,1)S(1)}) custom-call(s32[10]{0:T(128)S(1)} %pad_add_fusion.place_ref, f32[1,128]{1,0:T(1,128)S(1)} %maximum_bitcast_fusion.frequency_ref, bf16[32,128]{1,0:T(8,128)(2,1)} %bitcast.5, bf16[512,4096]{1,0:T(8,128)(2,1)} %tokens_hbm.1), custom_call_target="tpu_custom_call" | custom-call | flops 4194304 | bytes 4194304 | tf_op jit(solution)/shard_map/squares/pallas_call | solution.py:92
  3.7 0.7 %collective-permute-start = (f32[544,128]{1,0:T(8,128)S(1)}, f32[544,128]{1,0:T(8,128)S(1)}, u32[]{:S(2)}, u32[]{:S(2)}) collective-permute-start(f32[544,128]{1,0:T(8,128)S(1)} %get-tuple-element.40.mine_ref), channel_id=1, source_target_pairs={{0,1},{1,0},{2,3},{3,2},{4,5},{5,4},{6,7},{7,6},{8,9},{9,8},{10,11... | collective-permute-start | bytes 835592 | tf_op jit(solution)/shard_map/ppermute | solution.py:584
  4.5 2.8 %tables.1 = (bf16[8192,128]{1,0:T(8,128)(2,1)S(1)}, bf16[8192,128]{1,0:T(8,128)(2,1)S(1)}, f32[512,128]{1,0:T(8,128)S(1)}, f32[512,128]{1,0:T(8,128)S(1)}) custom-call(s32[10]{0:T(128)S(1)} %pad_add_fusion.place_ref, f32[1,128]{1,0:T(1,128)S(1)} %maximum_bitcast_fusion.frequency_ref, bf16[8192,128]{1,0:T(8,128)(2,1)} %wk_hbm.1, bf16[8192,128]{1,0:T(8,128)(2,1)} %wv_hbm.1), custom_call_target="tpu_custom_call" | custom-call | flops 6553600 | bytes 4194304 | tf_op jit(solution)/shard_map/tables/pallas_call | solution.py:126
  7.3 0.1 collective-permute-start.1
  7.3 3.4 %keys_own.1 = (bf16[512,4096]{1,0:T(8,128)(2,1)S(1)}, f32[512,128]{1,0:T(8,128)S(1)}, f32[256,256]{1,0:T(8,128)S(1)}, bf16[8192,512]{1,0:T(8,128)(2,1)S(1)}) custom-call(bf16[512,4096]{1,0:T(8,128)(2,1)S(1)} %get-tuple-element.42.tokens_ref, f32[544,128]{1,0:T(8,128)S(1)} %get-tuple-element.40.mine_ref, ...), custom_call_target="tpu_custom_call" | custom-call | flops 536870912 | bytes 8388608 | tf_op jit(solution)/shard_map/keys_own/pallas_call | solution.py:195
  10.7 2.3 %queries_own.1.acc_ref = f32[512,512]{1,0:T(8,128)S(1)} custom-call(bf16[512,4096]{1,0:T(8,128)(2,1)S(1)} %get-tuple-element.46.normed_ref, bf16[8192,512]{1,0:T(8,128)(2,1)S(1)} %get-tuple-element.47.wq_ref), custom_call_target="tpu_custom_call" | custom-call | flops 2147483648 | bytes 1048576 | tf_op jit(solution)/shard_map/queries_own/pallas_call | solution.py:271
  13.1 1.4 %collective-permute-done.1.tokens_ref = bf16[512,4096]{1,0:T(8,128)(2,1)S(1)} collective-permute-done((bf16[512,4096]{1,0:T(8,128)(2,1)S(1)}, bf16[512,4096]{1,0:T(8,128)(2,1)S(1)}, u32[]{:S(2)}, u32[]{:S(2)}) %collective-permute-start.1) | collective-permute-done | bytes 4194336 | tf_op jit(solution)/shard_map/ppermute | solution.py:584
  14.5 1.3 %keys.1 = (bf16[256,256]{1,0:T(8,128)(2,1)S(1)}, bf16[256,4096]{1,0:T(8,128)(2,1)S(1)}) custom-call(bf16[512,4096]{1,0:T(8,128)(2,1)S(1)} %collective-permute-done.1.tokens_ref, f32[544,128]{1,0:T(8,128)S(1)} %collective-permute-done.other_ref.gains_ref, f32[512,128]{1,0:T(8,128)S(1)} %get-tuple-element.49.inverse_ref, ...), custom_call_target="tpu_custom_call" | custom-call | flops 536870912 | bytes 2097152 | tf_op jit(solution)/shard_map/keys/pallas_call | solution.py:230
  15.8 0.2 collective-permute-start.3
  16.0 1.2 %collective-permute-done.3.other_ref = bf16[256,256]{1,0:T(8,128)(2,1)S(1)} collective-permute-done((bf16[256,256]{1,0:T(8,128)(2,1)S(1)}, bf16[256,256]{1,0:T(8,128)(2,1)S(1)}, u32[]{:S(2)}, u32[]{:S(2)}) %collective-permute-start.3) | collective-permute-done | bytes 131104 | tf_op jit(solution)/shard_map/ppermute | solution.py:584
  17.2 1.3 %collective-permute-start.4 = (bf16[512,256]{1,0:T(8,128)(2,1)S(1)}, bf16[512,256]{1,0:T(8,128)(2,1)S(1)}, u32[]{:S(2)}, u32[]{:S(2)}) collective-permute-start(bf16[512,256]{1,0:T(8,128)(2,1)S(1)} %join.1), channel_id=1, source_target_pairs={{0,2},{2,4},{4,6},{6,8},{8,10},{10,12},{12,14},{1,5},{3,7},{5,9},{... | collective-permute-start | bytes 786440 | tf_op jit(solution)/shard_map/ppermute | solution.py:594
  18.5 1.5 %collective-permute-start.2 = (bf16[256,256]{1,0:T(8,128)(2,1)S(1)}, bf16[256,256]{1,0:T(8,128)(2,1)S(1)}, u32[]{:S(2)}, u32[]{:S(2)}) collective-permute-start(bf16[256,256]{1,0:T(8,128)(2,1)S(1)} %get-tuple-element.56.mine_ref), channel_id=1, source_target_pairs={{0,6},{2,8},{4,10},{6,12},{8,14},{1,7},{3,9},{5,11},{7,13},{9,15},... | collective-permute-start | bytes 393224 | tf_op jit(solution)/shard_map/ppermute | solution.py:594
  20.0 3.5 %queries.1 = (bf16[512,512]{1,0:T(8,128)(2,1)S(1)}, bf16[512,2048]{1,0:T(8,128)(2,1)S(1)}, bf16[512,2048]{1,0:T(8,128)(2,1)S(1)}, bf16[512,4096]{1,0:T(8,128)(2,1)S(1)}) custom-call(bf16[512,4096]{1,0:T(8,128)(2,1)S(1)} %collective-permute-done.1.tokens_ref, f32[544,128]{1,0:T(8,128)S(1)} %collective-permute-done.other_ref.gains_ref, ...), custom_call_target="tpu_custom_call" | custom-call | flops 2147483648 | bytes 8388608 | tf_op jit(solution)/shard_map/queries/pallas_call | solution.py:313
  23.5 3.2 %attend_own.1 = (f32[2048,128]{1,0:T(8,128)S(1)}, f32[2048,128]{1,0:T(8,128)S(1)}, f32[2048,128]{1,0:T(8,128)S(1)}) custom-call(s32[10]{0:T(128)S(1)} %pad_add_fusion.place_ref, bf16[512,512]{1,0:T(8,128)(2,1)S(1)} %get-tuple-element.55.q_ref, bf16[256,256]{1,0:T(8,128)(2,1)S(1)} %get-tuple-element.56.mine_ref, ...), custom_call_target="tpu_custom_call" | custom-call | flops 536870912 | bytes 2097152 | tf_op jit(solution)/shard_map/attend_own/pallas_call | solution.py:487
  26.7 6.7 %collective-permute-done.2.third_ref = bf16[256,256]{1,0:T(8,128)(2,1)S(1)} collective-permute-done((bf16[256,256]{1,0:T(8,128)(2,1)S(1)}, bf16[256,256]{1,0:T(8,128)(2,1)S(1)}, u32[]{:S(2)}, u32[]{:S(2)}) %collective-permute-start.2) | collective-permute-done | bytes 131104 | tf_op jit(solution)/shard_map/ppermute | solution.py:594
  33.4 0.9 %collective-permute-start.6 = (bf16[512,256]{1,0:T(8,128)(2,1)S(1)}, bf16[512,256]{1,0:T(8,128)(2,1)S(1)}, u32[]{:S(2)}, u32[]{:S(2)}) collective-permute-start(bf16[512,256]{1,0:T(8,128)(2,1)S(1)} %collective-permute-done.4.block_ref), channel_id=1, source_target_pairs={{0,1},{1,0},{2,3},{3,2},{4,5},{5,4},{6,7},{7,6},{8,9},{9,8},{10,11... | collective-permute-start | bytes 786440 | tf_op jit(solution)/shard_map/ppermute | solution.py:584
  34.3 0.5 %collective-permute-start.8 = (bf16[512,2048]{1,0:T(8,128)(2,1)S(1)}, bf16[512,2048]{1,0:T(8,128)(2,1)S(1)}, u32[]{:S(2)}, u32[]{:S(2)}) collective-permute-start(bf16[512,2048]{1,0:T(8,128)(2,1)S(1)} %get-tuple-element.71), channel_id=1, source_target_pairs={{0,1},{1,0},{2,3},{3,2},{4,5},{5,4},{6,7},{7,6},{8,9},{9,8},{10,11... | collective-permute-start | bytes 6291464 | tf_op jit(solution)/shard_map/ppermute | solution.py:584
  34.8 0.8 %collective-permute-done.5.third_other_ref = bf16[256,256]{1,0:T(8,128)(2,1)S(1)} collective-permute-done((bf16[256,256]{1,0:T(8,128)(2,1)S(1)}, bf16[256,256]{1,0:T(8,128)(2,1)S(1)}, u32[]{:S(2)}, u32[]{:S(2)}) %collective-permute-start.5) | collective-permute-done | bytes 131104 | tf_op jit(solution)/shard_map/ppermute | solution.py:584
  35.6 0.4 collective-permute-start.9
  36.0 4.2 %attend.1.context_ref = bf16[512,512]{1,0:T(8,128)(2,1)S(1)} custom-call(s32[10]{0:T(128)S(1)} %pad_add_fusion.place_ref, bf16[512,512]{1,0:T(8,128)(2,1)S(1)} %get-tuple-element.55.q_ref, bf16[256,256]{1,0:T(8,128)(2,1)S(1)} %collective-permute-done.2.third_ref, bf16[256,256]{1,0:T(8,128)(2,1)S(1)} %collective-permute-done.5.third_other_ref, ...), custom_call_target="tpu_custom_call" | custom-call | flops 1610612736 | bytes 2097152 | tf_op jit(solution)/shard_map/attend/pallas_call | solution.py:510
  40.2 0.2 collective-permute-start.7
  40.4 2.3 %own_term.1.term_ref = bf16[512,4096]{1,0:T(8,128)(2,1)S(1)} custom-call(bf16[512,512]{1,0:T(8,128)(2,1)S(1)} %attend.1.context_ref, bf16[512,4096]{1,0:T(8,128)(2,1)S(1)} %get-tuple-element.70.w_ref), custom_call_target="tpu_custom_call" | custom-call | flops 2147483648 | bytes 4194304 | tf_op jit(solution)/shard_map/own_term/pallas_call | solution.py:540
  42.8 4.2 %output.1 = bf16[512,4096]{1,0:T(8,128)(2,1)} custom-call(bf16[512,4096]{1,0:T(8,128)(2,1)S(1)} %get-tuple-element.42.tokens_ref, bf16[512,4096]{1,0:T(8,128)(2,1)S(1)} %own_term.1.term_ref, bf16[512,512]{1,0:T(8,128)(2,1)S(1)} %collective-permute-done.7.context_ref, bf16[512,2048]{1,0:T(8,128)(2,1)S(1)} %collective-permute-done.8.w_ref, ...), custom_call_target="tpu_custom_call" | custom-call | flops 2147483648 | bytes 8388608 | tf_op jit(solution)/shard_map/output/pallas_call | solution.py:571
  (10 shorter events, 0.1 us)
Async XLA Ops:
  3.7 3.5 %collective-permute-start = (f32[544,128]{1,0:T(8,128)S(1)}, f32[544,128]{1,0:T(8,128)S(1)}, u32[]{:S(2)}, u32[]{:S(2)}) collective-permute-start(f32[544,128]{1,0:T(8,128)S(1)} %get-tuple-element.40.mine_ref), channel_id=1, source_target_pairs={{0,1},{1,0},{2,3},{3,2},{4,5},{5,4},{6,7},{7,6},{8,9},{9,8},{10,11... | collective-permute-start | bytes 835592 | tf_op jit(solution)/shard_map/ppermute | solution.py:584
  7.3 7.2 %collective-permute-start.1 = (bf16[512,4096]{1,0:T(8,128)(2,1)S(1)}, bf16[512,4096]{1,0:T(8,128)(2,1)S(1)}, u32[]{:S(2)}, u32[]{:S(2)}) collective-permute-start(bf16[512,4096]{1,0:T(8,128)(2,1)S(1)} %get-tuple-element.42.tokens_ref), channel_id=1, source_target_pairs={{0,1},{1,0},{2,3},{3,2},{4,5},{5,4},{6,7},{7,6},{8,9},{9,8},{10,11... | collective-permute-start | bytes 12582920 | tf_op jit(solution)/shard_map/ppermute | solution.py:584
  15.8 1.4 %collective-permute-start.3 = (bf16[256,256]{1,0:T(8,128)(2,1)S(1)}, bf16[256,256]{1,0:T(8,128)(2,1)S(1)}, u32[]{:S(2)}, u32[]{:S(2)}) collective-permute-start(bf16[256,256]{1,0:T(8,128)(2,1)S(1)} %get-tuple-element.56.mine_ref), channel_id=1, source_target_pairs={{0,1},{1,0},{2,3},{3,2},{4,5},{5,4},{6,7},{7,6},{8,9},{9,8},{10,11... | collective-permute-start | bytes 393224 | tf_op jit(solution)/shard_map/ppermute | solution.py:584
  17.2 16.2 %collective-permute-start.4 = (bf16[512,256]{1,0:T(8,128)(2,1)S(1)}, bf16[512,256]{1,0:T(8,128)(2,1)S(1)}, u32[]{:S(2)}, u32[]{:S(2)}) collective-permute-start(bf16[512,256]{1,0:T(8,128)(2,1)S(1)} %join.1), channel_id=1, source_target_pairs={{0,2},{2,4},{4,6},{6,8},{8,10},{10,12},{12,14},{1,5},{3,7},{5,9},{... | collective-permute-start | bytes 786440 | tf_op jit(solution)/shard_map/ppermute | solution.py:594
  18.5 14.9 %collective-permute-start.2 = (bf16[256,256]{1,0:T(8,128)(2,1)S(1)}, bf16[256,256]{1,0:T(8,128)(2,1)S(1)}, u32[]{:S(2)}, u32[]{:S(2)}) collective-permute-start(bf16[256,256]{1,0:T(8,128)(2,1)S(1)} %get-tuple-element.56.mine_ref), channel_id=1, source_target_pairs={{0,6},{2,8},{4,10},{6,12},{8,14},{1,7},{3,9},{5,11},{7,13},{9,15},... | collective-permute-start | bytes 393224 | tf_op jit(solution)/shard_map/ppermute | solution.py:594
  33.4 2.2 %collective-permute-start.6 = (bf16[512,256]{1,0:T(8,128)(2,1)S(1)}, bf16[512,256]{1,0:T(8,128)(2,1)S(1)}, u32[]{:S(2)}, u32[]{:S(2)}) collective-permute-start(bf16[512,256]{1,0:T(8,128)(2,1)S(1)} %collective-permute-done.4.block_ref), channel_id=1, source_target_pairs={{0,1},{1,0},{2,3},{3,2},{4,5},{5,4},{6,7},{7,6},{8,9},{9,8},{10,11... | collective-permute-start | bytes 786440 | tf_op jit(solution)/shard_map/ppermute | solution.py:584
  34.3 1.3 %collective-permute-start.5 = (bf16[256,256]{1,0:T(8,128)(2,1)S(1)}, bf16[256,256]{1,0:T(8,128)(2,1)S(1)}, u32[]{:S(2)}, u32[]{:S(2)}) collective-permute-start(bf16[256,256]{1,0:T(8,128)(2,1)S(1)} %collective-permute-done.2.third_ref), channel_id=1, source_target_pairs={{0,1},{1,0},{2,3},{3,2},{4,5},{5,4},{6,7},{7,6},{8,9},{9,8},{10,11... | collective-permute-start | bytes 393224 | tf_op jit(solution)/shard_map/ppermute | solution.py:584
  34.3 8.5 %collective-permute-start.8 = (bf16[512,2048]{1,0:T(8,128)(2,1)S(1)}, bf16[512,2048]{1,0:T(8,128)(2,1)S(1)}, u32[]{:S(2)}, u32[]{:S(2)}) collective-permute-start(bf16[512,2048]{1,0:T(8,128)(2,1)S(1)} %get-tuple-element.71), channel_id=1, source_target_pairs={{0,1},{1,0},{2,3},{3,2},{4,5},{5,4},{6,7},{7,6},{8,9},{9,8},{10,11... | collective-permute-start | bytes 6291464 | tf_op jit(solution)/shard_map/ppermute | solution.py:584
  35.6 7.1 %collective-permute-start.9 = (bf16[512,2048]{1,0:T(8,128)(2,1)S(1)}, bf16[512,2048]{1,0:T(8,128)(2,1)S(1)}, u32[]{:S(2)}, u32[]{:S(2)}) collective-permute-start(bf16[512,2048]{1,0:T(8,128)(2,1)S(1)} %get-tuple-element.72), channel_id=1, source_target_pairs={{0,1},{1,0},{2,3},{3,2},{4,5},{5,4},{6,7},{7,6},{8,9},{9,8},{10,11... | collective-permute-start | bytes 6291464 | tf_op jit(solution)/shard_map/ppermute | solution.py:584
  40.2 2.6 %collective-permute-start.7 = (bf16[512,512]{1,0:T(8,128)(2,1)S(1)}, bf16[512,512]{1,0:T(8,128)(2,1)S(1)}, u32[]{:S(2)}, u32[]{:S(2)}) collective-permute-start(bf16[512,512]{1,0:T(8,128)(2,1)S(1)} %attend.1.context_ref), channel_id=1, source_target_pairs={{0,1},{1,0},{2,3},{3,2},{4,5},{5,4},{6,7},{7,6},{8,9},{9,8},{10,11... | collective-permute-start | bytes 1572872 | tf_op jit(solution)/shard_map/ppermute | solution.py:584

commit v7 on v6

--- a/solution.py
+++ b/solution.py
@@ -15,7 +15,6 @@
 MIB = 1024 * 1024
 EXP2_SCALE = math.log2(math.e) / HEAD**0.5
 
-SCALAR = pl.BlockSpec(memory_space=pltpu.SMEM)
 WHOLE = pl.BlockSpec(memory_space=pltpu.VMEM)
 HBM = pl.BlockSpec(memory_space=pltpu.HBM)
 
@@ -39,11 +38,11 @@
     return jax.ShapeDtypeStruct(shape, dtype)
 
 
-def first_of_document(place_ref, row):
-    start = -place_ref[1]
+def first_of_document(lengths_ref, first_here, row):
+    start = -first_here
     begin = jnp.full(jnp.shape(row), start, jnp.int32)
-    for d in range(2, place_ref.shape[0] - 1):
-        start = start + place_ref[d]
+    for d in range(lengths_ref.shape[0] - 1):
+        start = start + lengths_ref[d]
         begin = jnp.where(row >= start, start, begin)
     return begin
 
@@ -61,7 +60,7 @@
     return [wide[:, i : i + LANES] for i in range(0, WIDE, LANES)]
 
 
-def squares_kernel(place_ref, frequency_ref, gain_hbm, tokens_hbm, sums_ref, tokens_ref, gain_ref, sems):
+def squares_kernel(frequency_ref, gain_hbm, tokens_hbm, sums_ref, gain_ref, tokens_ref, narrow, sems):
     rows, width = tokens_ref.shape
     chunks = sems.shape[0] - 1
     height = rows // chunks
@@ -71,7 +70,7 @@
         )
         for c in range(chunks)
     ]
-    loads.append(pltpu.make_async_copy(gain_hbm, gain_ref, sems.at[chunks]))
+    loads.append(pltpu.make_async_copy(gain_hbm, narrow, sems.at[chunks]))
     for load in loads:
         load.start()
     for c in range(chunks):
@@ -84,140 +83,176 @@
                     total = total + wide * wide
             sums_ref[at, :] = total
     loads[chunks].wait()
-    sums_ref[rows:, :] = gain_ref[...].astype(jnp.float32)
-
-
-def squares(place, frequency, gain, tokens):
+    gain_ref[...] = narrow[...].astype(jnp.float32)
+
+
+def squares(frequency, gain, tokens):
     rows, width = tokens.shape
     return pl.pallas_call(
         squares_kernel,
-        in_specs=[SCALAR, WHOLE, HBM, HBM],
-        out_specs=[WHOLE] * 2,
-        out_shape=[shaped((rows + gain.shape[0], LANES), jnp.float32), shaped(tokens.shape, tokens.dtype)],
+        in_specs=[WHOLE, HBM, HBM],
+        out_specs=[WHOLE] * 3,
+        out_shape=[
+            shaped((rows, LANES), jnp.float32),
+            shaped(gain.shape, jnp.float32),
+            shaped(tokens.shape, tokens.dtype),
+        ],
         scratch_shapes=[pltpu.VMEM(gain.shape, gain.dtype), pltpu.SemaphoreType.DMA((8 + 1,))],
         compiler_params=params(16),
         cost_estimate=cost(rows * width * 2, rows * width * 2),
         name="squares",
-    )(place, frequency, *in_hbm(gain, tokens))
-
-
-def tables_kernel(place_ref, frequency_ref, wk_hbm, wv_hbm, wk_ref, wv_ref, cos_ref, sin_ref, sems):
+    )(frequency, *in_hbm(gain, tokens))
+
+
+def sine_and_cosine(x):
+    turns = jnp.floor(x * (2.0 / math.pi) + 0.5)
+    r = ((x - turns * 1.5703125) - turns * 4.837512969970703125e-4) - turns * 7.54978995489188e-8
+    z = r * r
+    s = ((-1.9515295891e-4 * z + 8.3321608736e-3) * z - 1.6666654611e-1) * z * r + r
+    c = ((2.443315711809948e-5 * z - 1.388731625493765e-3) * z + 4.166664568298827e-2) * z * z - 0.5 * z + 1.0
+    quadrant = turns.astype(jnp.int32)
+    odd = (quadrant & 1) == 1
+    sine = jnp.where(odd, c, s)
+    cosine = jnp.where(odd, s, c)
+    sine = jnp.where((quadrant & 2) == 2, -sine, sine)
+    cosine = jnp.where(((quadrant + 1) & 2) == 2, -cosine, cosine)
+    return sine, cosine
+
+
+def tables_kernel(frequency_ref, lengths_hbm, cos_ref, sin_ref, lengths_ref, sem):
     rows = cos_ref.shape[0]
     half = rows // 2
+    load = pltpu.make_async_copy(lengths_hbm, lengths_ref, sem)
+    load.start()
+    lane = lax.broadcasted_iota(jnp.int32, (half, HEAD), 1)
+    row = lax.broadcasted_iota(jnp.int32, (half, HEAD), 0) + jnp.where(lane < HEAD // 2, 0, half)
+    low = lane < HEAD // 2
+    load.wait()
+    begin = first_of_document(lengths_ref, lax.axis_index("dp") * rows, row)
+    sine, cosine = sine_and_cosine((row - begin).astype(jnp.float32) * frequency_ref[...])
+    for table_ref, table, sign in ((cos_ref, cosine, 1.0), (sin_ref, sine, -1.0)):
+        turned = pltpu.roll(table, HEAD // 2, 1)
+        table_ref[:half, :] = jnp.where(low, sign * table, turned)
+        table_ref[half:, :] = jnp.where(low, sign * turned, table)
+
+
+def rotary_tables(frequency, lengths, rows):
+    return pl.pallas_call(
+        tables_kernel,
+        in_specs=[WHOLE, HBM],
+        out_specs=[WHOLE] * 2,
+        out_shape=[shaped((rows, HEAD), jnp.float32)] * 2,
+        scratch_shapes=[pltpu.SMEM(lengths.shape, lengths.dtype), pltpu.SemaphoreType.DMA],
+        compiler_params=params(16),
+        cost_estimate=cost(rows * HEAD * 100, rows * HEAD * 8),
+        name="tables",
+    )(frequency, *in_hbm(lengths))
+
+
+def normalize(out_ref, tokens_ref, start, inverse_ref, gains_ref):
+    count, width = out_ref.shape
+
+    def block(r, carry):
+        at = block_rows(start, r)
+        inverse = inverse_ref[at, :]
+        for j in range(0, width, WIDE):
+            normed = []
+            for i, wide in enumerate(wide_slice(tokens_ref, at, j)):
+                gain_row = j // LANES + i
+                normed.append(wide * inverse * gains_ref[gain_row : gain_row + 1, :])
+            out_ref[block_rows(0, r), j : j + WIDE] = jnp.concatenate(normed, axis=1).astype(jnp.bfloat16)
+        return carry
+
+    lax.fori_loop(0, count // ROWS, block, 0)
+
+
+def turn(x, cosine, sine):
+    return (x * cosine + pltpu.roll(x, HEAD // 2, 1) * sine).astype(jnp.bfloat16)
+
+
+def half_rows(rows, other):
+    me = lax.axis_index("tp")
+    half = rows // 2
+    return pl.ds(pl.multiple_of((1 - me if other else me) * half, half), half)
+
+
+def features(width, other):
+    me = lax.axis_index("tp")
+    return pl.ds(pl.multiple_of((1 - me if other else me) * width, width), width)
+
+
+def both_weights(wk_ref, wv_ref, depth):
+    return jnp.concatenate([wk_ref[depth, :], wv_ref[depth, :]], axis=1)
+
+
+def normalize_other_kernel(
+    tokens_ref, mine_ref, other_ref, gain_ref, wk_hbm, wv_hbm, normed_ref, inverse_ref, wk_ref, wv_ref, sems
+):
+    rows, width = tokens_ref.shape
     loads = [
         pltpu.make_async_copy(wk_hbm, wk_ref, sems.at[0]),
         pltpu.make_async_copy(wv_hbm, wv_ref, sems.at[1]),
     ]
     for load in loads:
         load.start()
-    lane = lax.broadcasted_iota(jnp.int32, (half, HEAD), 1)
-    row = lax.broadcasted_iota(jnp.int32, (half, HEAD), 0) + jnp.where(lane < HEAD // 2, 0, half)
-    angles = (row - first_of_document(place_ref, row)).astype(jnp.float32) * frequency_ref[...]
-    for table_ref, table, sign in ((cos_ref, jnp.cos(angles), 1.0), (sin_ref, jnp.sin(angles), -1.0)):
-        turned = pltpu.roll(table, HEAD // 2, 1)
-        low = lane < HEAD // 2
-        table_ref[:half, :] = jnp.where(low, sign * table, turned)
-        table_ref[half:, :] = jnp.where(low, sign * turned, table)
+    mean = jnp.sum(mine_ref[...] + other_ref[...], axis=1, keepdims=True) * (0.5 / width)
+    inverse_ref[...] = jnp.broadcast_to(lax.rsqrt(mean + 1e-05), (rows, LANES))
+    normalize(normed_ref, tokens_ref, half_rows(rows, True).start, inverse_ref, gain_ref)
     for load in loads:
         load.wait()
 
 
-def tables_and_weights(place, frequency, wk, wv, rows):
-    return pl.pallas_call(
-        tables_kernel,
-        in_specs=[SCALAR, WHOLE, HBM, HBM],
+def normalize_other(tokens, sums, sums_other, gain, wk, wv):
+    rows, width = tokens.shape
+    return pl.pallas_call(
+        normalize_other_kernel,
+        in_specs=[WHOLE] * 4 + [HBM] * 2,
         out_specs=[WHOLE] * 4,
         out_shape=[
+            shaped((rows // 2, width), jnp.bfloat16),
+            shaped((rows, LANES), jnp.float32),
             shaped(wk.shape, wk.dtype),
             shaped(wv.shape, wv.dtype),
-            shaped((rows, HEAD), jnp.float32),
-            shaped((rows, HEAD), jnp.float32),
         ],
         scratch_shapes=[pltpu.SemaphoreType.DMA((2,))],
-        compiler_params=params(16),
-        cost_estimate=cost(rows * HEAD * 100, wk.size * 4),
-        name="tables",
-    )(place, frequency, *in_hbm(wk, wv))
-
-
-def normalize(out_ref, out_start, tokens_ref, start, count, inverse_ref, gains_ref):
-    rows, width = tokens_ref.shape
-
-    def block(r, carry):
-        at = block_rows(start, r)
-        out_at = block_rows(out_start, r)
-        inverse = inverse_ref[at, :]
-        for j in range(0, width, WIDE):
-            normed = []
-            for i, wide in enumerate(wide_slice(tokens_ref, at, j)):
-                gain_row = rows + j // LANES + i
-                normed.append(wide * inverse * gains_ref[gain_row : gain_row + 1, :])
-            out_ref[out_at, j : j + WIDE] = jnp.concatenate(normed, axis=1).astype(jnp.bfloat16)
-        return carry
-
-    lax.fori_loop(0, count // ROWS, block, 0)
-
-
-def turn(x, cosine, sine):
-    return (x * cosine + pltpu.roll(x, HEAD // 2, 1) * sine).astype(jnp.bfloat16)
-
-
-def own_rows(rows):
-    half = rows // 2
-    return pl.ds(pl.multiple_of(lax.axis_index("tp") * half, half), half)
-
-
-def features(width, other):
-    me = lax.axis_index("tp")
-    which = 1 - me if other else me
-    return pl.ds(pl.multiple_of(which * width, width), width)
-
-
-def keys_own_kernel(
-    tokens_ref, mine_ref, other_ref, wk_ref, wv_ref, wq_hbm, normed_ref, inverse_ref, acc_ref, wq_ref, sem
-):
+        compiler_params=params(12),
+        cost_estimate=cost(rows * width * 2, wk.size * 4),
+        name="normalize_other",
+    )(tokens, sums, sums_other, gain, *in_hbm(wk, wv))
+
+
+def normalize_own_kernel(tokens_ref, gain_ref, inverse_ref, wk_ref, wv_ref, wq_hbm, normed_ref, acc_ref, wq_ref, sem):
     rows, width = tokens_ref.shape
     load = pltpu.make_async_copy(wq_hbm, wq_ref, sem)
     load.start()
-    mean = jnp.sum(mine_ref[0:rows, :] + other_ref[0:rows, :], axis=1, keepdims=True) * (0.5 / width)
-    inverse_ref[...] = jnp.broadcast_to(lax.rsqrt(mean + 1e-05), (rows, LANES))
-    normalize(normed_ref, 0, tokens_ref, 0, rows, inverse_ref, mine_ref)
+    normalize(normed_ref, tokens_ref, half_rows(rows, False).start, inverse_ref, gain_ref)
     acc_ref[...] = jnp.dot(
-        normed_ref[own_rows(rows), :],
-        both_weights(wk_ref, wv_ref, features(width, False)),
-        preferred_element_type=jnp.float32,
+        normed_ref[...], both_weights(wk_ref, wv_ref, features(width, False)), preferred_element_type=jnp.float32
     )
     load.wait()
 
 
-def keys_own(tokens, sums, sums_other, wk, wv, wq):
+def normalize_own(tokens, gain, inverse, wk, wv, wq):
     rows, width = tokens.shape
     return pl.pallas_call(
-        keys_own_kernel,
+        normalize_own_kernel,
         in_specs=[WHOLE] * 5 + [HBM],
-        out_specs=[WHOLE] * 4,
+        out_specs=[WHOLE] * 3,
         out_shape=[
-            shaped(tokens.shape, jnp.bfloat16),
-            shaped((rows, LANES), jnp.float32),
+            shaped((rows // 2, width), jnp.bfloat16),
             shaped((rows // 2, 2 * HEAD), jnp.float32),
             shaped(wq.shape, wq.dtype),
         ],
         scratch_shapes=[pltpu.SemaphoreType.DMA],
-        compiler_params=params(16),
+        compiler_params=params(12),
         cost_estimate=cost(2 * rows * width * HEAD, wq.size * 2),
-        name="keys_own",
-    )(tokens, sums, sums_other, wk, wv, *in_hbm(wq))
-
-
-def both_weights(wk_ref, wv_ref, depth):
-    return jnp.concatenate([wk_ref[depth, :], wv_ref[depth, :]], axis=1)
-
-
-def keys_kernel(tokens_ref, gains_ref, inverse_ref, acc_ref, wk_ref, wv_ref, cos_ref, sin_ref, kv_ref, normed_ref):
-    rows, width = tokens_ref.shape
-    half = rows // 2
-    here = own_rows(rows)
-    normalize(normed_ref, 0, tokens_ref, lax.axis_index("tp") * half, half, inverse_ref, gains_ref)
+        name="normalize_own",
+    )(tokens, gain, inverse, wk, wv, *in_hbm(wq))
+
+
+def keys_kernel(normed_ref, acc_ref, wk_ref, wv_ref, cos_ref, sin_ref, kv_ref):
+    half, width = normed_ref.shape
+    here = half_rows(2 * half, False)
     total = acc_ref[...] + jnp.dot(
         normed_ref[...], both_weights(wk_ref, wv_ref, features(width, True)), preferred_element_type=jnp.float32
     )
@@ -225,24 +260,22 @@
     kv_ref[:, HEAD:] = total[:, HEAD:].astype(jnp.bfloat16)
 
 
-def finish_keys(tokens_other, sums_other, inverse, acc, wk, wv, tables):
-    rows, width = tokens_other.shape
+def finish_keys(normed_come, acc, wk, wv, tables):
     return pl.pallas_call(
         keys_kernel,
-        in_specs=[WHOLE] * 8,
-        out_specs=[WHOLE] * 2,
-        out_shape=[shaped(acc.shape, jnp.bfloat16), shaped((rows // 2, width), jnp.bfloat16)],
-        compiler_params=params(16),
-        cost_estimate=cost(2 * rows * width * HEAD, rows * width),
+        in_specs=[WHOLE] * 6,
+        out_specs=WHOLE,
+        out_shape=shaped(acc.shape, jnp.bfloat16),
+        compiler_params=params(12),
+        cost_estimate=cost(normed_come.size * 4 * HEAD, acc.size * 4),
         name="keys",
-    )(tokens_other, sums_other, inverse, acc, wk, wv, *tables)
+    )(normed_come, acc, wk, wv, *tables)
 
 
 def join_kernel(mine_ref, other_ref, out_ref):
-    half = mine_ref.shape[0]
-    me = lax.axis_index("tp")
-    for block, which in ((mine_ref, me), (other_ref, 1 - me)):
-        out_ref[pl.ds(pl.multiple_of(which * half, half), half), :] = block[...]
+    rows = out_ref.shape[0]
+    out_ref[half_rows(rows, False), :] = mine_ref[...]
+    out_ref[half_rows(rows, True), :] = other_ref[...]
 
 
 def join(mine, other):
@@ -258,34 +291,32 @@
     )(mine, other)
 
 
-def queries_own_kernel(normed_ref, wq_ref, acc_ref):
-    width = normed_ref.shape[1]
-    acc_ref[...] = jnp.dot(
-        normed_ref[...], wq_ref[features(width, False), :], preferred_element_type=jnp.float32
-    )
-
-
-def queries_own(normed, wq):
-    rows, width = normed.shape
+def queries_own_kernel(mine_ref, other_ref, wq_ref, acc_ref):
+    half, width = mine_ref.shape
+    weights = wq_ref[features(width, False), :]
+    acc_ref[:half, :] = jnp.dot(mine_ref[...], weights, preferred_element_type=jnp.float32)
+    acc_ref[half:, :] = jnp.dot(other_ref[...], weights, preferred_element_type=jnp.float32)
+
+
+def queries_own(mine, other, wq):
+    half, width = mine.shape
     nq = wq.shape[1]
     return pl.pallas_call(
         queries_own_kernel,
-        in_specs=[WHOLE, WHOLE],
+        in_specs=[WHOLE] * 3,
         out_specs=WHOLE,
-        out_shape=shaped((rows, nq), jnp.float32),
+        out_shape=shaped((2 * half, nq), jnp.float32),
         compiler_params=params(12),
-        cost_estimate=cost(2 * rows * width * nq, rows * nq * 4),
+        cost_estimate=cost(4 * half * width * nq, half * nq * 8),
         name="queries_own",
-    )(normed, wq)
+    )(mine, other, wq)
 
 
 def queries_kernel(
-    tokens_ref, gains_ref, inverse_ref, acc_ref, wq_ref, cos_ref, sin_ref, ready_ref, wout_hbm,
-    q_ref, wsend_ref, wlater_ref, wkeep_ref, normed_ref, acc, sems,
+    mine_ref, other_ref, acc_ref, wq_ref, cos_ref, sin_ref, wout_hbm, q_ref, wsend_ref, wlater_ref, wkeep_ref, acc, sems
 ):
-    rows, width = tokens_ref.shape
-    half = rows // 2
-    send = pl.multiple_of((1 - lax.axis_index("tp")) * width, width)
+    half, width = mine_ref.shape
+    send = features(width, True).start
     loads = [
         pltpu.make_async_copy(wout_hbm.at[:, pl.ds(send, width // 2)], wsend_ref, sems.at[0]),
         pltpu.make_async_copy(wout_hbm.at[:, pl.ds(send + width // 2, width // 2)], wlater_ref, sems.at[1]),
@@ -293,42 +324,36 @@
     ]
     for load in loads:
         load.start()
-    normed_ref[own_rows(rows), :] = ready_ref[...]
-    there = (1 - lax.axis_index("tp")) * half
-    normalize(normed_ref, there, tokens_ref, there, half, inverse_ref, gains_ref)
-    acc[...] = acc_ref[...] + jnp.dot(
-        normed_ref[...], wq_ref[features(width, True), :], preferred_element_type=jnp.float32
-    )
-    for h in range(q_ref.shape[1] // HEAD):
-        lanes = slice(h * HEAD, (h + 1) * HEAD)
-        q_ref[:, lanes] = turn(acc[:, lanes], cos_ref[...], sin_ref[...])
+    weights = wq_ref[features(width, True), :]
+    for part, normed_ref, other in ((slice(0, half), mine_ref, False), (slice(half, 2 * half), other_ref, True)):
+        acc[part, :] = acc_ref[part, :] + jnp.dot(normed_ref[...], weights, preferred_element_type=jnp.float32)
+        at = half_rows(2 * half, other)
+        for h in range(q_ref.shape[1] // HEAD):
+            lanes = slice(h * HEAD, (h + 1) * HEAD)
+            q_ref[at, lanes] = turn(acc[part, lanes], cos_ref[at, :], sin_ref[at, :])
     for load in loads:
         load.wait()
 
 
-def finish_queries(tokens_other, sums_other, inverse, acc, wq, tables, normed, w_out):
-    rows, width = tokens_other.shape
+def finish_queries(mine, other, acc, wq, tables, w_out):
+    half, width = mine.shape
     nq = wq.shape[1]
     depth = w_out.shape[0]
     return pl.pallas_call(
         queries_kernel,
-        in_specs=[WHOLE] * 8 + [HBM],
+        in_specs=[WHOLE] * 6 + [HBM],
         out_specs=[WHOLE] * 4,
         out_shape=[
-            shaped((rows, nq), jnp.bfloat16),
+            shaped((2 * half, nq), jnp.bfloat16),
             shaped((depth, width // 2), w_out.dtype),
             shaped((depth, width // 2), w_out.dtype),
             shaped((depth, width), w_out.dtype),
         ],
-        scratch_shapes=[
-            pltpu.VMEM((rows, width), jnp.bfloat16),
-            pltpu.VMEM((rows, nq), jnp.float32),
-            pltpu.SemaphoreType.DMA((3,)),
-        ],
-        compiler_params=params(16),
-        cost_estimate=cost(2 * rows * width * nq, rows * width * 4),
+        scratch_shapes=[pltpu.VMEM((2 * half, nq), jnp.float32), pltpu.SemaphoreType.DMA((3,))],
+        compiler_params=params(12),
+        cost_estimate=cost(4 * half * width * nq, w_out.size * 2),
         name="queries",
-    )(tokens_other, sums_other, inverse, acc, wq, *tables, normed, *in_hbm(w_out))
+    )(mine, other, acc, wq, *tables, *in_hbm(w_out))
 
 
 TILE = 128
@@ -359,14 +384,19 @@
     return total
 
 
-def attend_own_kernel(place_ref, q_ref, mine_ref, other_ref, acc_ref, tops_ref, sums_ref, keys, values, bias, scores, probs):
+def attend_own_kernel(
+    lengths_hbm, q_ref, mine_ref, other_ref, acc_ref, tops_ref, sums_ref, keys, values, bias, scores, probs, lengths_ref, sem
+):
+    load = pltpu.make_async_copy(lengths_hbm, lengths_ref, sem)
+    load.start()
     rows = q_ref.shape[0]
     half = rows // 2
     me = lax.axis_index("tp")
     place_blocks([mine_ref, other_ref], [me * half, (1 - me) * half], keys, values)
+    load.wait()
     row = lax.broadcasted_iota(jnp.int32, (rows, LANES), 0)
     lane = lax.broadcasted_iota(jnp.int32, (rows, LANES), 1)
-    begin = first_of_document(place_ref, row)
+    begin = first_of_document(lengths_ref, lax.axis_index("dp") * rows, row)
     for j in range(0, rows, LANES):
         allowed = (lane + j >= begin) & (lane + j <= row)
         bias[:, j : j + LANES] = jnp.where(allowed, 0.0, -1e30)
@@ -400,13 +430,14 @@
 
 
 def attend_kernel(
-    place_ref, q_ref, third_ref, third_other_ref, block_ref, block_other_ref, acc_in, tops_in, sums_in,
-    ctx_ref, keys, values, stacked, scores, probs, acc, sums,
+    lengths_hbm, q_ref, third_ref, third_other_ref, block_ref, block_other_ref, acc_in, tops_in, sums_in,
+    ctx_ref, keys, values, stacked, scores, probs, acc, sums, lengths_ref, sem,
 ):
+    load = pltpu.make_async_copy(lengths_hbm, lengths_ref, sem)
+    load.start()
     rows = q_ref.shape[0]
     half = rows // 2
     heads = q_ref.shape[1] // HEAD
-    tall = heads * TILE
     behind = keys.shape[0]
     me = lax.axis_index("tp")
     place_blocks(
@@ -415,10 +446,11 @@
         keys,
         values,
     )
-    start = -place_ref[1]
+    load.wait()
+    start = -lax.axis_index("dp") * rows
     begin, end = start, jnp.int32(rows)
-    for d in range(2, place_ref.shape[0] - 1):
-        start = start + place_ref[d]
+    for d in range(lengths_ref.shape[0] - 1):
+        start = start + lengths_ref[d]
         begin = jnp.where(start <= 0, start, begin)
         end = jnp.where(start > 0, jnp.minimum(end, start), end)
     low = begin + behind
@@ -480,13 +512,13 @@
     lax.fori_loop(0, rows // TILE, tile, 0)
 
 
-def attend_own(place, queries, blocks):
+def attend_own(lengths, queries, blocks):
     rows, width = queries.shape
     half = rows // 2
     heads = width // HEAD
     return pl.pallas_call(
         attend_own_kernel,
-        in_specs=[SCALAR] + [WHOLE] * 3,
+        in_specs=[HBM] + [WHOLE] * 3,
         out_specs=[WHOLE] * 3,
         scratch_shapes=[
             pltpu.VMEM((rows, HEAD), jnp.bfloat16),
@@ -494,22 +526,24 @@
             pltpu.VMEM((rows, rows), jnp.float32),
             pltpu.VMEM((half, rows), jnp.float32),
             pltpu.VMEM((half, rows), jnp.bfloat16),
+            pltpu.SMEM(lengths.shape, lengths.dtype),
+            pltpu.SemaphoreType.DMA,
         ],
         out_shape=[shaped((heads * rows, LANES), jnp.float32)] * 3,
         compiler_params=params(16),
         cost_estimate=cost(4 * rows * width * rows, rows * width * 8),
         name="attend_own",
-    )(place, queries, *blocks)
-
-
-def attend(place, queries, blocks, state):
+    )(*in_hbm(lengths), queries, *blocks)
+
+
+def attend(lengths, queries, blocks, state):
     rows, width = queries.shape
     heads = width // HEAD
     tall = heads * TILE
     places = sum(block.shape[0] for block in blocks)
     return pl.pallas_call(
         attend_kernel,
-        in_specs=[SCALAR] + [WHOLE] * (1 + len(blocks) + len(state)),
+        in_specs=[HBM] + [WHOLE] * (1 + len(blocks) + len(state)),
         out_specs=WHOLE,
         scratch_shapes=[
             pltpu.VMEM((places, HEAD), jnp.bfloat16),
@@ -519,12 +553,14 @@
             pltpu.VMEM((tall, places), jnp.bfloat16),
             pltpu.VMEM((tall, HEAD), jnp.float32),
             pltpu.VMEM((tall, LANES), jnp.float32),
+            pltpu.SMEM(lengths.shape, lengths.dtype),
+            pltpu.SemaphoreType.DMA,
         ],
         out_shape=shaped((rows, width), jnp.bfloat16),
         compiler_params=params(20),
         cost_estimate=cost(4 * rows * width * places, rows * width * 8),
         name="attend",
-    )(place, queries, *blocks, *state)
+    )(*in_hbm(lengths), queries, *blocks, *state)
 
 
 def term_kernel(context_ref, w_ref, term_ref):
@@ -596,34 +632,33 @@
 
 def local(tokens, norm_gain, lengths, w_query, w_key, w_value, w_out):
     rows = tokens.shape[0]
-    first_here = lax.axis_index("dp") * rows
-    place = jnp.concatenate([lax.axis_index("tp")[None], first_here[None], lengths]).astype(jnp.int32)
     frequency = 500000.0 ** (-jnp.arange(HEAD // 2, dtype=jnp.float32) * 2.0 / HEAD)
     frequency = jnp.concatenate([frequency, frequency])[None, :]
 
-    sums, tokens = squares(place, frequency, norm_gain.reshape(-1, LANES), tokens)
+    sums, gain, tokens = squares(frequency, norm_gain.reshape(-1, LANES), tokens)
     sums_other = swap(sums)
-    wk, wv, *tables = tables_and_weights(place, frequency, w_key, w_value, rows)
-    tokens, sums_other, wk = lax.optimization_barrier((tokens, sums_other, wk))
-    tokens_other = swap(tokens)
-    normed, inverse, kv_partial, wq = keys_own(tokens, sums, sums_other, wk, wv, w_query)
-    partial = queries_own(normed, wq)
-    tokens_other, partial = lax.optimization_barrier((tokens_other, partial))
-    kv, normed = finish_keys(tokens_other, sums_other, inverse, kv_partial, wk, wv, tables)
+    tables = rotary_tables(frequency, lengths, rows)
+    sums_other, tables = lax.optimization_barrier((sums_other, tables))
+    normed_other, inverse, wk, wv = normalize_other(tokens, sums, sums_other, gain, w_key, w_value)
+    come_mine = swap(normed_other)
+    normed_mine, kv_partial, wq = normalize_own(tokens, gain, inverse, wk, wv, w_query)
+    come_other = swap(normed_mine)
+    come_mine, kv_partial = lax.optimization_barrier((come_mine, kv_partial))
+    kv = finish_keys(come_mine, kv_partial, wk, wv, tables)
     assert (rows + MOST - 2) // rows == 3
+    kv, normed_mine = lax.optimization_barrier((kv, normed_mine))
+    third = onward(kv, (3, 3))
     kv_other = swap(kv)
-    third = onward(kv, (3, 3))
     block = onward(join(kv, kv_other), (1, 2))
-    queries, w_send, w_later, w_mine = finish_queries(
-        tokens_other, sums_other, inverse, partial, wq, tables, normed, w_out
-    )
+    partial = queries_own(normed_mine, normed_other, wq)
+    queries, w_send, w_later, w_mine = finish_queries(come_mine, come_other, partial, wq, tables, w_out)
     w_other = swap(w_send)
-    state = attend_own(place, queries, [kv, kv_other])
+    state = attend_own(lengths, queries, [kv, kv_other])
     third, block, state = lax.optimization_barrier((third, block, state))
     blocks = [third, swap(third), block, swap(block)]
     blocks, w_later = lax.optimization_barrier((blocks, w_later))
     w_other_later = swap(w_later)
-    context = attend(place, queries, blocks, state)
+    context = attend(lengths, queries, blocks, state)
     context_other = swap(context)
     term = group_term(context, w_mine)
     return output(tokens, term, context_other, w_other, w_other_later)

time: 47 us -> 45.9 us (0.977)
  the two profiles are of different devices: /device:TPU:25 before, /device:TPU:0 now
where the time goes in v7:
time: 45.9 us; the launch traced here: 45.4 us
  Pallas kernels  29.4 us (64%)
  starting transfers between devices  12 us (26%)
  waiting for transfers between devices  3.8 us (8%)
    ppermute x2, starting transfers between devices, onward(): return lax.ppermute(value, ('dp', 'tp'), pairs)  9.2 us
    pallas_call x1, Pallas kernels, finish_queries(): pl.pallas_call(queries_kernel, in_specs=[WHOLE] * 6 + [HBM], out_specs=[W...  5.9 us
    pallas_call x1, Pallas kernels, output(): pl.pallas_call(output_kernel, grid=(width // step,), in_specs=[WHOLE] * 5...  4.22 us
    ppermute x9, waiting for transfers between devices, swap(): return lax.ppermute(value, 'tp', SWAP)  3.8 us
    pallas_call x1, Pallas kernels, normalize_own(): pl.pallas_call(normalize_own_kernel, in_specs=[WHOLE] * 5 + [HBM], out_sp...  3.39 us
    pallas_call x1, Pallas kernels, attend_own(): pl.pallas_call(attend_own_kernel, in_specs=[HBM] + [WHOLE] * 3, out_specs...  3.29 us
    ppermute x9, starting transfers between devices, swap(): return lax.ppermute(value, 'tp', SWAP)  2.82 us
    pallas_call x1, Pallas kernels, squares(): pl.pallas_call(squares_kernel, in_specs=[WHOLE, HBM, HBM], out_specs=[WHO...  2.35 us
  transfers between devices with their start and end apart: 11, of which 4 were waited for; matrix products, arithmetic and copies ran while one was open for 0% of the time, Pallas kernels for 45%

profile of v7, /device:TPU:0, one launch (start us, length us, event | category | flops | bytes accessed | tf_op | source)
XLA Modules:
  0.0 45.4 jit_solution(10658223934248803052)
XLA Ops:
  0.1 2.3 %squares.1 = (f32[512,128]{1,0:T(8,128)S(1)}, f32[32,128]{1,0:T(8,128)S(1)}, bf16[512,4096]{1,0:T(8,128)(2,1)S(1)}) custom-call(f32[1,128]{1,0:T(1,128)S(1)} %maximum_bitcast_fusion.frequency_ref, bf16[32,128]{1,0:T(8,128)(2,1)} %bitcast.3, bf16[512,4096]{1,0:T(8,128)(2,1)} %tokens_hbm.1), custom_call_target="tpu_custom_call" | custom-call | flops 4194304 | bytes 4194304 | tf_op jit(solution)/shard_map/squares/pallas_call | solution.py:91
  2.4 0.5 %collective-permute-start = (f32[512,128]{1,0:T(8,128)S(1)}, f32[512,128]{1,0:T(8,128)S(1)}, u32[]{:S(2)}, u32[]{:S(2)}) collective-permute-start(f32[512,128]{1,0:T(8,128)S(1)} %get-tuple-element.42.mine_ref), channel_id=1, source_target_pairs={{0,1},{1,0},{2,3},{3,2},{4,5},{5,4},{6,7},{7,6},{8,9},{9,8},{10,11... | collective-permute-start | bytes 786440 | tf_op jit(solution)/shard_map/ppermute | solution.py:620
  3.0 1.0 %tables.1 = (f32[512,128]{1,0:T(8,128)S(1)}, f32[512,128]{1,0:T(8,128)S(1)}) custom-call(f32[1,128]{1,0:T(1,128)S(1)} %maximum_bitcast_fusion.frequency_ref, s32[8]{0:T(128)} %lengths_hbm.5), custom_call_target="tpu_custom_call" | custom-call | flops 6553600 | bytes 524288 | tf_op jit(solution)/shard_map/tables/pallas_call | solution.py:140
  4.0 0.1 collective-permute-done.other_ref
  4.1 2.2 %normalize_other.1 = (bf16[256,4096]{1,0:T(8,128)(2,1)S(1)}, f32[512,128]{1,0:T(8,128)S(1)}, bf16[8192,128]{1,0:T(8,128)(2,1)S(1)}, bf16[8192,128]{1,0:T(8,128)(2,1)S(1)}) custom-call(bf16[512,4096]{1,0:T(8,128)(2,1)S(1)} %get-tuple-element.41.tokens_ref, f32[512,128]{1,0:T(8,128)S(1)} %get-tuple-element.42.mine_ref, ...), custom_call_target="tpu_custom_call" | custom-call | flops 4194304 | bytes 4194304 | tf_op jit(solution)/shard_map/normalize_other/pallas_call | solution.py:207
  6.4 0.4 collective-permute-start.1
  6.8 3.4 %normalize_own.1 = (bf16[256,4096]{1,0:T(8,128)(2,1)S(1)}, f32[256,256]{1,0:T(8,128)S(1)}, bf16[8192,512]{1,0:T(8,128)(2,1)S(1)}) custom-call(bf16[512,4096]{1,0:T(8,128)(2,1)S(1)} %get-tuple-element.41.tokens_ref, f32[32,128]{1,0:T(8,128)S(1)} %get-tuple-element.46.gain_ref, f32[512,128]{1,0:T(8,128)S(1)} %get-tuple-element.48.inverse_ref, ...), custom_call_target="tpu_custom_call" | custom-call | flops 536870912 | bytes 8388608 | tf_op jit(solution)/shard_map/normalize_own/pallas_call | solution.py:237
  10.2 0.2 collective-permute-start.2
  10.4 0.2 collective-permute-done.1.normed_ref.mine_ref
  10.6 0.8 %keys.1.mine_ref = bf16[256,256]{1,0:T(8,128)(2,1)S(1)} custom-call(bf16[256,4096]{1,0:T(8,128)(2,1)S(1)} %collective-permute-done.1.normed_ref.mine_ref, f32[256,256]{1,0:T(8,128)S(1)} %get-tuple-element.54.acc_ref, bf16[8192,128]{1,0:T(8,128)(2,1)S(1)} %get-tuple-element.49.wk_ref, bf16[8192,128]{1,0:T(8,128)(2,1)S(1)} %get-tuple-element.50.wv_ref, ...), custom_call_target="tpu_custom_call" | custom-call | flops 536870912 | bytes 262144 | tf_op jit(solution)/shard_map/keys/pallas_call | solution.py:264
  11.4 0.4 collective-permute-start.4
  11.8 5.6 %collective-permute-start.3 = (bf16[256,256]{1,0:T(8,128)(2,1)S(1)}, bf16[256,256]{1,0:T(8,128)(2,1)S(1)}, u32[]{:S(2)}, u32[]{:S(2)}) collective-permute-start(bf16[256,256]{1,0:T(8,128)(2,1)S(1)} %keys.1.mine_ref), channel_id=1, source_target_pairs={{0,6},{2,8},{4,10},{6,12},{8,14},{1,7},{3,9},{5,11},{7,13},{9,15},... | collective-permute-start | bytes 393224 | tf_op jit(solution)/shard_map/ppermute | solution.py:630
  17.5 3.6 %collective-permute-start.5 = (bf16[512,256]{1,0:T(8,128)(2,1)S(1)}, bf16[512,256]{1,0:T(8,128)(2,1)S(1)}, u32[]{:S(2)}, u32[]{:S(2)}) collective-permute-start(bf16[512,256]{1,0:T(8,128)(2,1)S(1)} %join.1), channel_id=1, source_target_pairs={{0,2},{2,4},{4,6},{6,8},{8,10},{10,12},{12,14},{1,5},{3,7},{5,9},{... | collective-permute-start | bytes 786440 | tf_op jit(solution)/shard_map/ppermute | solution.py:630
  21.1 2.3 %queries_own.1.acc_ref = f32[512,512]{1,0:T(8,128)S(1)} custom-call(bf16[256,4096]{1,0:T(8,128)(2,1)S(1)} %get-tuple-element.57.mine_ref, bf16[256,4096]{1,0:T(8,128)(2,1)S(1)} %get-tuple-element.47.other_ref, bf16[8192,512]{1,0:T(8,128)(2,1)S(1)} %get-tuple-element.58.wq_ref), custom_call_target="tpu_custom_call" | custom-call | flops 2147483648 | bytes 1048576 | tf_op jit(solution)/shard_map/queries_own/pallas_call | solution.py:304
  23.4 5.9 %queries.1 = (bf16[512,512]{1,0:T(8,128)(2,1)S(1)}, bf16[512,2048]{1,0:T(8,128)(2,1)S(1)}, bf16[512,2048]{1,0:T(8,128)(2,1)S(1)}, bf16[512,4096]{1,0:T(8,128)(2,1)S(1)}) custom-call(bf16[256,4096]{1,0:T(8,128)(2,1)S(1)} %collective-permute-done.1.normed_ref.mine_ref, bf16[256,4096]{1,0:T(8,128)(2,1)S(1)} %collective-permute-done.2.other_ref, ...), custom_call_target="tpu_custom_call" | custom-call | flops 2147483648 | bytes 8388608 | tf_op jit(solution)/shard_map/queries/pallas_call | solution.py:342
  29.3 3.3 %attend_own.1 = (f32[2048,128]{1,0:T(8,128)S(1)}, f32[2048,128]{1,0:T(8,128)S(1)}, f32[2048,128]{1,0:T(8,128)S(1)}) custom-call(s32[8]{0:T(128)} %lengths_hbm.5, bf16[512,512]{1,0:T(8,128)(2,1)S(1)} %get-tuple-element.59.q_ref, bf16[256,256]{1,0:T(8,128)(2,1)S(1)} %keys.1.mine_ref, bf16[256,256]{1,0:T(8,128)(2,1)S(1)} %collective-permute-done.4.other_ref), custom_call_target="tpu_custom_call" | custom-call | flops 536870912 | bytes 2097152 | tf_op jit(solution)/shard_map/attend_own/pallas_call | solution.py:519
  32.7 0.5 %collective-permute-start.6 = (bf16[256,256]{1,0:T(8,128)(2,1)S(1)}, bf16[256,256]{1,0:T(8,128)(2,1)S(1)}, u32[]{:S(2)}, u32[]{:S(2)}) collective-permute-start(bf16[256,256]{1,0:T(8,128)(2,1)S(1)} %collective-permute-done.3.third_ref), channel_id=1, source_target_pairs={{0,1},{1,0},{2,3},{3,2},{4,5},{5,4},{6,7},{7,6},{8,9},{9,8},{10,11... | collective-permute-start | bytes 393224 | tf_op jit(solution)/shard_map/ppermute | solution.py:620
  33.3 1.1 %collective-permute-done.6.third_other_ref = bf16[256,256]{1,0:T(8,128)(2,1)S(1)} collective-permute-done((bf16[256,256]{1,0:T(8,128)(2,1)S(1)}, bf16[256,256]{1,0:T(8,128)(2,1)S(1)}, u32[]{:S(2)}, u32[]{:S(2)}) %collective-permute-start.6) | collective-permute-done | bytes 131104 | tf_op jit(solution)/shard_map/ppermute | solution.py:620
  34.4 0.1 collective-permute-start.10
  34.6 1.5 %attend.1.context_ref = bf16[512,512]{1,0:T(8,128)(2,1)S(1)} custom-call(s32[8]{0:T(128)} %lengths_hbm.5, bf16[512,512]{1,0:T(8,128)(2,1)S(1)} %get-tuple-element.59.q_ref, bf16[256,256]{1,0:T(8,128)(2,1)S(1)} %collective-permute-done.3.third_ref, bf16[256,256]{1,0:T(8,128)(2,1)S(1)} %collective-permute-done.6.third_other_ref, ...), custom_call_target="tpu_custom_call" | custom-call | flops 1610612736 | bytes 2097152 | tf_op jit(solution)/shard_map/attend/pallas_call | solution.py:544
  36.1 0.4 collective-permute-start.8
  36.5 2.3 %own_term.1.term_ref = bf16[512,4096]{1,0:T(8,128)(2,1)S(1)} custom-call(bf16[512,512]{1,0:T(8,128)(2,1)S(1)} %attend.1.context_ref, bf16[512,4096]{1,0:T(8,128)(2,1)S(1)} %get-tuple-element.74.w_ref), custom_call_target="tpu_custom_call" | custom-call | flops 2147483648 | bytes 4194304 | tf_op jit(solution)/shard_map/own_term/pallas_call | solution.py:576
  38.8 2.3 %collective-permute-done.8.context_ref = bf16[512,512]{1,0:T(8,128)(2,1)S(1)} collective-permute-done((bf16[512,512]{1,0:T(8,128)(2,1)S(1)}, bf16[512,512]{1,0:T(8,128)(2,1)S(1)}, u32[]{:S(2)}, u32[]{:S(2)}) %collective-permute-start.8) | collective-permute-done | bytes 524320 | tf_op jit(solution)/shard_map/ppermute | solution.py:620
  41.2 4.2 %output.1 = bf16[512,4096]{1,0:T(8,128)(2,1)} custom-call(bf16[512,4096]{1,0:T(8,128)(2,1)S(1)} %get-tuple-element.41.tokens_ref, bf16[512,4096]{1,0:T(8,128)(2,1)S(1)} %own_term.1.term_ref, bf16[512,512]{1,0:T(8,128)(2,1)S(1)} %collective-permute-done.8.context_ref, bf16[512,2048]{1,0:T(8,128)(2,1)S(1)} %collective-permute-done.9.w_ref, ...), custom_call_target="tpu_custom_call" | custom-call | flops 2147483648 | bytes 8388608 | tf_op jit(solution)/shard_map/output/pallas_call | solution.py:607
  (12 shorter events, 0.3 us)
Async XLA Ops:
  2.4 1.7 %collective-permute-start = (f32[512,128]{1,0:T(8,128)S(1)}, f32[512,128]{1,0:T(8,128)S(1)}, u32[]{:S(2)}, u32[]{:S(2)}) collective-permute-start(f32[512,128]{1,0:T(8,128)S(1)} %get-tuple-element.42.mine_ref), channel_id=1, source_target_pairs={{0,1},{1,0},{2,3},{3,2},{4,5},{5,4},{6,7},{7,6},{8,9},{9,8},{10,11... | collective-permute-start | bytes 786440 | tf_op jit(solution)/shard_map/ppermute | solution.py:620
  6.4 4.2 %collective-permute-start.1 = (bf16[256,4096]{1,0:T(8,128)(2,1)S(1)}, bf16[256,4096]{1,0:T(8,128)(2,1)S(1)}, u32[]{:S(2)}, u32[]{:S(2)}) collective-permute-start(bf16[256,4096]{1,0:T(8,128)(2,1)S(1)} %get-tuple-element.47.other_ref), channel_id=1, source_target_pairs={{0,1},{1,0},{2,3},{3,2},{4,5},{5,4},{6,7},{7,6},{8,9},{9,8},{10,11... | collective-permute-start | bytes 6291464 | tf_op jit(solution)/shard_map/ppermute | solution.py:620
  10.2 13.2 %collective-permute-start.2 = (bf16[256,4096]{1,0:T(8,128)(2,1)S(1)}, bf16[256,4096]{1,0:T(8,128)(2,1)S(1)}, u32[]{:S(2)}, u32[]{:S(2)}) collective-permute-start(bf16[256,4096]{1,0:T(8,128)(2,1)S(1)} %get-tuple-element.57.mine_ref), channel_id=1, source_target_pairs={{0,1},{1,0},{2,3},{3,2},{4,5},{5,4},{6,7},{7,6},{8,9},{9,8},{10,11... | collective-permute-start | bytes 6291464 | tf_op jit(solution)/shard_map/ppermute | solution.py:620
  11.4 6.0 %collective-permute-start.4 = (bf16[256,256]{1,0:T(8,128)(2,1)S(1)}, bf16[256,256]{1,0:T(8,128)(2,1)S(1)}, u32[]{:S(2)}, u32[]{:S(2)}) collective-permute-start(bf16[256,256]{1,0:T(8,128)(2,1)S(1)} %keys.1.mine_ref), channel_id=1, source_target_pairs={{0,1},{1,0},{2,3},{3,2},{4,5},{5,4},{6,7},{7,6},{8,9},{9,8},{10,11... | collective-permute-start | bytes 393224 | tf_op jit(solution)/shard_map/ppermute | solution.py:620
  11.8 20.8 %collective-permute-start.3 = (bf16[256,256]{1,0:T(8,128)(2,1)S(1)}, bf16[256,256]{1,0:T(8,128)(2,1)S(1)}, u32[]{:S(2)}, u32[]{:S(2)}) collective-permute-start(bf16[256,256]{1,0:T(8,128)(2,1)S(1)} %keys.1.mine_ref), channel_id=1, source_target_pairs={{0,6},{2,8},{4,10},{6,12},{8,14},{1,7},{3,9},{5,11},{7,13},{9,15},... | collective-permute-start | bytes 393224 | tf_op jit(solution)/shard_map/ppermute | solution.py:630
  17.5 15.2 %collective-permute-start.5 = (bf16[512,256]{1,0:T(8,128)(2,1)S(1)}, bf16[512,256]{1,0:T(8,128)(2,1)S(1)}, u32[]{:S(2)}, u32[]{:S(2)}) collective-permute-start(bf16[512,256]{1,0:T(8,128)(2,1)S(1)} %join.1), channel_id=1, source_target_pairs={{0,2},{2,4},{4,6},{6,8},{8,10},{10,12},{12,14},{1,5},{3,7},{5,9},{... | collective-permute-start | bytes 786440 | tf_op jit(solution)/shard_map/ppermute | solution.py:630
  32.6 1.8 %collective-permute-start.7 = (bf16[512,256]{1,0:T(8,128)(2,1)S(1)}, bf16[512,256]{1,0:T(8,128)(2,1)S(1)}, u32[]{:S(2)}, u32[]{:S(2)}) collective-permute-start(bf16[512,256]{1,0:T(8,128)(2,1)S(1)} %collective-permute-done.5.block_ref), channel_id=1, source_target_pairs={{0,1},{1,0},{2,3},{3,2},{4,5},{5,4},{6,7},{7,6},{8,9},{9,8},{10,11... | collective-permute-start | bytes 786440 | tf_op jit(solution)/shard_map/ppermute | solution.py:620
  32.7 1.7 %collective-permute-start.6 = (bf16[256,256]{1,0:T(8,128)(2,1)S(1)}, bf16[256,256]{1,0:T(8,128)(2,1)S(1)}, u32[]{:S(2)}, u32[]{:S(2)}) collective-permute-start(bf16[256,256]{1,0:T(8,128)(2,1)S(1)} %collective-permute-done.3.third_ref), channel_id=1, source_target_pairs={{0,1},{1,0},{2,3},{3,2},{4,5},{5,4},{6,7},{7,6},{8,9},{9,8},{10,11... | collective-permute-start | bytes 393224 | tf_op jit(solution)/shard_map/ppermute | solution.py:620
  33.2 8.0 %collective-permute-start.9 = (bf16[512,2048]{1,0:T(8,128)(2,1)S(1)}, bf16[512,2048]{1,0:T(8,128)(2,1)S(1)}, u32[]{:S(2)}, u32[]{:S(2)}) collective-permute-start(bf16[512,2048]{1,0:T(8,128)(2,1)S(1)} %get-tuple-element.75), channel_id=1, source_target_pairs={{0,1},{1,0},{2,3},{3,2},{4,5},{5,4},{6,7},{7,6},{8,9},{9,8},{10,11... | collective-permute-start | bytes 6291464 | tf_op jit(solution)/shard_map/ppermute | solution.py:620
  34.4 6.8 %collective-permute-start.10 = (bf16[512,2048]{1,0:T(8,128)(2,1)S(1)}, bf16[512,2048]{1,0:T(8,128)(2,1)S(1)}, u32[]{:S(2)}, u32[]{:S(2)}) collective-permute-start(bf16[512,2048]{1,0:T(8,128)(2,1)S(1)} %get-tuple-element.76), channel_id=1, source_target_pairs={{0,1},{1,0},{2,3},{3,2},{4,5},{5,4},{6,7},{7,6},{8,9},{9,8},{10,11... | collective-permute-start | bytes 6291464 | tf_op jit(solution)/shard_map/ppermute | solution.py:620
  36.1 5.1 %collective-permute-start.8 = (bf16[512,512]{1,0:T(8,128)(2,1)S(1)}, bf16[512,512]{1,0:T(8,128)(2,1)S(1)}, u32[]{:S(2)}, u32[]{:S(2)}) collective-permute-start(bf16[512,512]{1,0:T(8,128)(2,1)S(1)} %attend.1.context_ref), channel_id=1, source_target_pairs={{0,1},{1,0},{2,3},{3,2},{4,5},{5,4},{6,7},{7,6},{8,9},{9,8},{10,11... | collective-permute-start | bytes 1572872 | tf_op jit(solution)/shard_map/ppermute | solution.py:620

commit v8 on v7

--- a/solution.py
+++ b/solution.py
@@ -185,9 +185,27 @@
     return jnp.concatenate([wk_ref[depth, :], wv_ref[depth, :]], axis=1)
 
 
-def normalize_other_kernel(
-    tokens_ref, mine_ref, other_ref, gain_ref, wk_hbm, wv_hbm, normed_ref, inverse_ref, wk_ref, wv_ref, sems
-):
+def normalize_other_kernel(tokens_ref, mine_ref, other_ref, gain_ref, normed_ref, inverse_ref):
+    rows, width = tokens_ref.shape
+    mean = jnp.sum(mine_ref[...] + other_ref[...], axis=1, keepdims=True) * (0.5 / width)
+    inverse_ref[...] = jnp.broadcast_to(lax.rsqrt(mean + 1e-05), (rows, LANES))
+    normalize(normed_ref, tokens_ref, half_rows(rows, True).start, inverse_ref, gain_ref)
+
+
+def normalize_other(tokens, sums, sums_other, gain):
+    rows, width = tokens.shape
+    return pl.pallas_call(
+        normalize_other_kernel,
+        in_specs=[WHOLE] * 4,
+        out_specs=[WHOLE] * 2,
+        out_shape=[shaped((rows // 2, width), jnp.bfloat16), shaped((rows, LANES), jnp.float32)],
+        compiler_params=params(12),
+        cost_estimate=cost(rows * width * 2, rows * width * 2),
+        name="normalize_other",
+    )(tokens, sums, sums_other, gain)
+
+
+def normalize_own_kernel(tokens_ref, gain_ref, inverse_ref, wk_hbm, wv_hbm, normed_ref, acc_ref, wk_ref, wv_ref, sems):
     rows, width = tokens_ref.shape
     loads = [
         pltpu.make_async_copy(wk_hbm, wk_ref, sems.at[0]),
@@ -195,59 +213,31 @@
     ]
     for load in loads:
         load.start()
-    mean = jnp.sum(mine_ref[...] + other_ref[...], axis=1, keepdims=True) * (0.5 / width)
-    inverse_ref[...] = jnp.broadcast_to(lax.rsqrt(mean + 1e-05), (rows, LANES))
-    normalize(normed_ref, tokens_ref, half_rows(rows, True).start, inverse_ref, gain_ref)
+    normalize(normed_ref, tokens_ref, half_rows(rows, False).start, inverse_ref, gain_ref)
     for load in loads:
         load.wait()
-
-
-def normalize_other(tokens, sums, sums_other, gain, wk, wv):
+    acc_ref[...] = jnp.dot(
+        normed_ref[...], both_weights(wk_ref, wv_ref, features(width, False)), preferred_element_type=jnp.float32
+    )
+
+
+def normalize_own(tokens, gain, inverse, wk, wv):
     rows, width = tokens.shape
     return pl.pallas_call(
-        normalize_other_kernel,
-        in_specs=[WHOLE] * 4 + [HBM] * 2,
+        normalize_own_kernel,
+        in_specs=[WHOLE] * 3 + [HBM] * 2,
         out_specs=[WHOLE] * 4,
         out_shape=[
             shaped((rows // 2, width), jnp.bfloat16),
-            shaped((rows, LANES), jnp.float32),
+            shaped((rows // 2, 2 * HEAD), jnp.float32),
             shaped(wk.shape, wk.dtype),
             shaped(wv.shape, wv.dtype),
         ],
         scratch_shapes=[pltpu.SemaphoreType.DMA((2,))],
         compiler_params=params(12),
-        cost_estimate=cost(rows * width * 2, wk.size * 4),
-        name="normalize_other",
-    )(tokens, sums, sums_other, gain, *in_hbm(wk, wv))
-
-
-def normalize_own_kernel(tokens_ref, gain_ref, inverse_ref, wk_ref, wv_ref, wq_hbm, normed_ref, acc_ref, wq_ref, sem):
-    rows, width = tokens_ref.shape
-    load = pltpu.make_async_copy(wq_hbm, wq_ref, sem)
-    load.start()
-    normalize(normed_ref, tokens_ref, half_rows(rows, False).start, inverse_ref, gain_ref)
-    acc_ref[...] = jnp.dot(
-        normed_ref[...], both_weights(wk_ref, wv_ref, features(width, False)), preferred_element_type=jnp.float32
-    )
-    load.wait()
-
-
-def normalize_own(tokens, gain, inverse, wk, wv, wq):
-    rows, width = tokens.shape
-    return pl.pallas_call(
-        normalize_own_kernel,
-        in_specs=[WHOLE] * 5 + [HBM],
-        out_specs=[WHOLE] * 3,
-        out_shape=[
-            shaped((rows // 2, width), jnp.bfloat16),
-            shaped((rows // 2, 2 * HEAD), jnp.float32),
-            shaped(wq.shape, wq.dtype),
-        ],
-        scratch_shapes=[pltpu.SemaphoreType.DMA],
-        compiler_params=params(12),
-        cost_estimate=cost(2 * rows * width * HEAD, wq.size * 2),
+        cost_estimate=cost(2 * rows * width * HEAD, wk.size * 4),
         name="normalize_own",
-    )(tokens, gain, inverse, wk, wv, *in_hbm(wq))
+    )(tokens, gain, inverse, *in_hbm(wk, wv))
 
 
 def keys_kernel(normed_ref, acc_ref, wk_ref, wv_ref, cos_ref, sin_ref, kv_ref):
@@ -312,25 +302,23 @@
     )(mine, other, wq)
 
 
-def queries_kernel(
-    mine_ref, other_ref, acc_ref, wq_ref, cos_ref, sin_ref, wout_hbm, q_ref, wsend_ref, wlater_ref, wkeep_ref, acc, sems
-):
+def queries_kernel(mine_ref, other_ref, acc_ref, wq_ref, cos_ref, sin_ref, wout_hbm, q_ref, wsend_ref, wlater_ref, acc, sems):
     half, width = mine_ref.shape
     send = features(width, True).start
     loads = [
         pltpu.make_async_copy(wout_hbm.at[:, pl.ds(send, width // 2)], wsend_ref, sems.at[0]),
         pltpu.make_async_copy(wout_hbm.at[:, pl.ds(send + width // 2, width // 2)], wlater_ref, sems.at[1]),
-        pltpu.make_async_copy(wout_hbm.at[:, features(width, False)], wkeep_ref, sems.at[2]),
     ]
     for load in loads:
         load.start()
     weights = wq_ref[features(width, True), :]
-    for part, normed_ref, other in ((slice(0, half), mine_ref, False), (slice(half, 2 * half), other_ref, True)):
-        acc[part, :] = acc_ref[part, :] + jnp.dot(normed_ref[...], weights, preferred_element_type=jnp.float32)
+    acc[:half, :] = jnp.dot(mine_ref[...], weights, preferred_element_type=jnp.float32)
+    acc[half:, :] = jnp.dot(other_ref[...], weights, preferred_element_type=jnp.float32)
+    for part, other in ((slice(0, half), False), (slice(half, 2 * half), True)):
         at = half_rows(2 * half, other)
         for h in range(q_ref.shape[1] // HEAD):
             lanes = slice(h * HEAD, (h + 1) * HEAD)
-            q_ref[at, lanes] = turn(acc[part, lanes], cos_ref[at, :], sin_ref[at, :])
+            q_ref[at, lanes] = turn(acc_ref[part, lanes] + acc[part, lanes], cos_ref[at, :], sin_ref[at, :])
     for load in loads:
         load.wait()
 
@@ -342,16 +330,15 @@
     return pl.pallas_call(
         queries_kernel,
         in_specs=[WHOLE] * 6 + [HBM],
-        out_specs=[WHOLE] * 4,
+        out_specs=[WHOLE] * 3,
         out_shape=[
             shaped((2 * half, nq), jnp.bfloat16),
             shaped((depth, width // 2), w_out.dtype),
             shaped((depth, width // 2), w_out.dtype),
-            shaped((depth, width), w_out.dtype),
         ],
-        scratch_shapes=[pltpu.VMEM((2 * half, nq), jnp.float32), pltpu.SemaphoreType.DMA((3,))],
+        scratch_shapes=[pltpu.VMEM((2 * half, nq), jnp.float32), pltpu.SemaphoreType.DMA((2,))],
         compiler_params=params(12),
-        cost_estimate=cost(4 * half * width * nq, w_out.size * 2),
+        cost_estimate=cost(4 * half * width * nq, w_out.size),
         name="queries",
     )(mine, other, acc, wq, *tables, *in_hbm(w_out))
 
@@ -385,10 +372,13 @@
 
 
 def attend_own_kernel(
-    lengths_hbm, q_ref, mine_ref, other_ref, acc_ref, tops_ref, sums_ref, keys, values, bias, scores, probs, lengths_ref, sem
+    lengths_hbm, q_ref, mine_ref, other_ref, wout_hbm, acc_ref, tops_ref, sums_ref, wkeep_ref,
+    keys, values, bias, scores, probs, lengths_ref, sems,
 ):
-    load = pltpu.make_async_copy(lengths_hbm, lengths_ref, sem)
+    load = pltpu.make_async_copy(lengths_hbm, lengths_ref, sems.at[0])
     load.start()
+    keep = pltpu.make_async_copy(wout_hbm.at[:, features(wkeep_ref.shape[1], False)], wkeep_ref, sems.at[1])
+    keep.start()
     rows = q_ref.shape[0]
     half = rows // 2
     me = lax.axis_index("tp")
@@ -427,6 +417,7 @@
             acc_ref[out : out + half, :] = jnp.dot(
                 probs[:, :count], values[:count, :], preferred_element_type=jnp.float32
             )
+    keep.wait()
 
 
 def attend_kernel(
@@ -512,14 +503,14 @@
     lax.fori_loop(0, rows // TILE, tile, 0)
 
 
-def attend_own(lengths, queries, blocks):
+def attend_own(lengths, queries, blocks, w_out):
     rows, width = queries.shape
     half = rows // 2
     heads = width // HEAD
     return pl.pallas_call(
         attend_own_kernel,
-        in_specs=[HBM] + [WHOLE] * 3,
-        out_specs=[WHOLE] * 3,
+        in_specs=[HBM] + [WHOLE] * 3 + [HBM],
+        out_specs=[WHOLE] * 4,
         scratch_shapes=[
             pltpu.VMEM((rows, HEAD), jnp.bfloat16),
             pltpu.VMEM((rows, HEAD), jnp.bfloat16),
@@ -527,13 +518,14 @@
             pltpu.VMEM((half, rows), jnp.float32),
             pltpu.VMEM((half, rows), jnp.bfloat16),
             pltpu.SMEM(lengths.shape, lengths.dtype),
-            pltpu.SemaphoreType.DMA,
+            pltpu.SemaphoreType.DMA((2,)),
         ],
-        out_shape=[shaped((heads * rows, LANES), jnp.float32)] * 3,
+        out_shape=[shaped((heads * rows, LANES), jnp.float32)] * 3
+        + [shaped((w_out.shape[0], w_out.shape[1] // 2), w_out.dtype)],
         compiler_params=params(16),
         cost_estimate=cost(4 * rows * width * rows, rows * width * 8),
         name="attend_own",
-    )(*in_hbm(lengths), queries, *blocks)
+    )(*in_hbm(lengths), queries, *blocks, *in_hbm(w_out))
 
 
 def attend(lengths, queries, blocks, state):
@@ -584,32 +576,33 @@
     )(context, w)
 
 
-def output_kernel(tokens_ref, term_ref, context_ref, w_ref, w_later_ref, out_ref):
-    step = out_ref.shape[1]
-    j = pl.program_id(0)
-    here = pl.ds(pl.multiple_of(j * step, step), step)
-
-    def work(weights_ref, first):
-        part = pl.ds(pl.multiple_of((j - first) * step, step), step)
-        other = jnp.dot(context_ref[...], weights_ref[:, part], preferred_element_type=jnp.float32).astype(jnp.bfloat16)
-        out = tokens_ref[:, here].astype(jnp.float32) + term_ref[:, here].astype(jnp.float32) + other.astype(jnp.float32)
-        out_ref[...] = out.astype(jnp.bfloat16)
-
-    middle = w_ref.shape[1] // step
-    pl.when(j < middle)(lambda: work(w_ref, 0))
-    pl.when(j >= middle)(lambda: work(w_later_ref, middle))
+def output_kernel(tokens_ref, term_ref, context_ref, w_ref, w_later_ref, out_hbm, out, sems):
+    width = out.shape[1]
+    half = width // 2
+    chunks = sems.shape[0]
+    step = width // chunks
+    stores = []
+    for c in range(chunks):
+        here = slice(c * step, (c + 1) * step)
+        weights = w_ref[:, here] if c < chunks // 2 else w_later_ref[:, c * step - half : (c + 1) * step - half]
+        other = jnp.dot(context_ref[...], weights, preferred_element_type=jnp.float32).astype(jnp.bfloat16)
+        total = tokens_ref[:, here].astype(jnp.float32) + term_ref[:, here].astype(jnp.float32) + other.astype(jnp.float32)
+        out[:, here] = total.astype(jnp.bfloat16)
+        stores.append(pltpu.make_async_copy(out.at[:, here], out_hbm.at[:, here], sems.at[c]))
+        stores[c].start()
+    for store in stores:
+        store.wait()
 
 
 def output(tokens, term, context, w, w_later):
     rows, width = tokens.shape
     depth = context.shape[1]
-    step = 1024
     return pl.pallas_call(
         output_kernel,
-        grid=(width // step,),
         in_specs=[WHOLE] * 5,
-        out_specs=pl.BlockSpec((rows, step), lambda j: (0, j)),
+        out_specs=HBM,
         out_shape=shaped((rows, width), jnp.bfloat16),
+        scratch_shapes=[pltpu.VMEM((rows, width), jnp.bfloat16), pltpu.SemaphoreType.DMA((8,))],
         compiler_params=params(20),
         cost_estimate=cost(2 * rows * width * depth, rows * width * 4),
         name="output",
@@ -639,9 +632,9 @@
     sums_other = swap(sums)
     tables = rotary_tables(frequency, lengths, rows)
     sums_other, tables = lax.optimization_barrier((sums_other, tables))
-    normed_other, inverse, wk, wv = normalize_other(tokens, sums, sums_other, gain, w_key, w_value)
+    normed_other, inverse = normalize_other(tokens, sums, sums_other, gain)
     come_mine = swap(normed_other)
-    normed_mine, kv_partial, wq = normalize_own(tokens, gain, inverse, wk, wv, w_query)
+    normed_mine, kv_partial, wk, wv = normalize_own(tokens, gain, inverse, w_key, w_value)
     come_other = swap(normed_mine)
     come_mine, kv_partial = lax.optimization_barrier((come_mine, kv_partial))
     kv = finish_keys(come_mine, kv_partial, wk, wv, tables)
@@ -650,10 +643,10 @@
     third = onward(kv, (3, 3))
     kv_other = swap(kv)
     block = onward(join(kv, kv_other), (1, 2))
-    partial = queries_own(normed_mine, normed_other, wq)
-    queries, w_send, w_later, w_mine = finish_queries(come_mine, come_other, partial, wq, tables, w_out)
+    partial = queries_own(normed_mine, normed_other, w_query)
+    queries, w_send, w_later = finish_queries(come_mine, come_other, partial, w_query, tables, w_out)
     w_other = swap(w_send)
-    state = attend_own(lengths, queries, [kv, kv_other])
+    *state, w_mine = attend_own(lengths, queries, [kv, kv_other], w_out)
     third, block, state = lax.optimization_barrier((third, block, state))
     blocks = [third, swap(third), block, swap(block)]
     blocks, w_later = lax.optimization_barrier((blocks, w_later))

time: 45.9 us -> 41.9 us (0.913)
  Pallas kernels: 29.4 us -> 25.5 us
    pallas_call x4, Pallas kernels: 13.1 us -> 10.4 us  [the longest x1 3.31 us: output(): pl.pallas_call(output_kernel, in_specs=[WHOLE] * 5, out_specs=HBM, out_sh...]
    pallas_call x1, Pallas kernels: 5.9 us -> 4.65 us  [finish_queries(): pl.pallas_call(queries_kernel, in_specs=[WHOLE] * 6 + [HBM], out_specs=[W...]
  transfers between devices with their start and end apart: 11 -> 11, of which waited for: 4 -> 4; matrix products, arithmetic and copies ran while one was open for 0% -> 0% of each run, Pallas kernels for 45% -> 46%
where the time goes in v8:
time: 41.9 us; the launch traced here: 41.7 us
  Pallas kernels  25.5 us (61%)
  starting transfers between devices  12.1 us (29%)
  waiting for transfers between devices  3.67 us (9%)
    ppermute x2, starting transfers between devices, onward(): return lax.ppermute(value, ('dp', 'tp'), pairs)  9.02 us
    pallas_call x1, Pallas kernels, finish_queries(): pl.pallas_call(queries_kernel, in_specs=[WHOLE] * 6 + [HBM], out_specs=[W...  4.65 us
    ppermute x9, waiting for transfers between devices, swap(): return lax.ppermute(value, 'tp', SWAP)  3.66 us
    pallas_call x1, Pallas kernels, output(): pl.pallas_call(output_kernel, in_specs=[WHOLE] * 5, out_specs=HBM, out_sh...  3.31 us
    pallas_call x1, Pallas kernels, attend_own(): pl.pallas_call(attend_own_kernel, in_specs=[HBM] + [WHOLE] * 3 + [HBM], o...  3.28 us
    pallas_call x1, Pallas kernels, normalize_own(): pl.pallas_call(normalize_own_kernel, in_specs=[WHOLE] * 3 + [HBM] * 2, ou...  3.11 us
    ppermute x9, starting transfers between devices, swap(): return lax.ppermute(value, 'tp', SWAP)  3.06 us
    pallas_call x1, Pallas kernels, squares(): pl.pallas_call(squares_kernel, in_specs=[WHOLE, HBM, HBM], out_specs=[WHO...  2.35 us
  transfers between devices with their start and end apart: 11, of which 4 were waited for; matrix products, arithmetic and copies ran while one was open for 0% of the time, Pallas kernels for 46%

profile of v8, /device:TPU:0, one launch (start us, length us, event | category | flops | bytes accessed | tf_op | source)
XLA Modules:
  0.0 41.7 jit_solution(8384456788676347418)
XLA Ops:
  0.1 2.3 %squares.1 = (f32[512,128]{1,0:T(8,128)S(1)}, f32[32,128]{1,0:T(8,128)S(1)}, bf16[512,4096]{1,0:T(8,128)(2,1)S(1)}) custom-call(f32[1,128]{1,0:T(1,128)S(1)} %maximum_bitcast_fusion.frequency_ref, bf16[32,128]{1,0:T(8,128)(2,1)} %bitcast.5, bf16[512,4096]{1,0:T(8,128)(2,1)} %tokens_hbm.1), custom_call_target="tpu_custom_call" | custom-call | flops 4194304 | bytes 4194304 | tf_op jit(solution)/shard_map/squares/pallas_call | solution.py:91
  2.4 0.5 %collective-permute-start = (f32[512,128]{1,0:T(8,128)S(1)}, f32[512,128]{1,0:T(8,128)S(1)}, u32[]{:S(2)}, u32[]{:S(2)}) collective-permute-start(f32[512,128]{1,0:T(8,128)S(1)} %get-tuple-element.41.mine_ref), channel_id=1, source_target_pairs={{0,1},{1,0},{2,3},{3,2},{4,5},{5,4},{6,7},{7,6},{8,9},{9,8},{10,11... | collective-permute-start | bytes 786440 | tf_op jit(solution)/shard_map/ppermute | solution.py:613
  3.0 1.0 %tables.1 = (f32[512,128]{1,0:T(8,128)S(1)}, f32[512,128]{1,0:T(8,128)S(1)}) custom-call(f32[1,128]{1,0:T(1,128)S(1)} %maximum_bitcast_fusion.frequency_ref, s32[8]{0:T(128)} %lengths_hbm.5), custom_call_target="tpu_custom_call" | custom-call | flops 6553600 | bytes 524288 | tf_op jit(solution)/shard_map/tables/pallas_call | solution.py:140
  4.0 0.1 collective-permute-done.other_ref
  4.1 0.7 %normalize_other.1 = (bf16[256,4096]{1,0:T(8,128)(2,1)S(1)}, f32[512,128]{1,0:T(8,128)S(1)}) custom-call(bf16[512,4096]{1,0:T(8,128)(2,1)S(1)} %get-tuple-element.40.tokens_ref, f32[512,128]{1,0:T(8,128)S(1)} %get-tuple-element.41.mine_ref, f32[512,128]{1,0:T(8,128)S(1)} %collective-permute-done.other_ref, f32[32,128]{1,0:T(8,128)S(1)} %get-tuple-element.45.gain_ref), custom_call_target="tpu_custom_call" | custom-call | flops 4194304 | bytes 4194304 | tf_op jit(solution)/shard_map/normalize_other/pallas_call | solution.py:197
  4.8 0.4 %collective-permute-start.1 = (bf16[256,4096]{1,0:T(8,128)(2,1)S(1)}, bf16[256,4096]{1,0:T(8,128)(2,1)S(1)}, u32[]{:S(2)}, u32[]{:S(2)}) collective-permute-start(bf16[256,4096]{1,0:T(8,128)(2,1)S(1)} %get-tuple-element.46.other_ref), channel_id=1, source_target_pairs={{0,1},{1,0},{2,3},{3,2},{4,5},{5,4},{6,7},{7,6},{8,9},{9,8},{10,11... | collective-permute-start | bytes 6291464 | tf_op jit(solution)/shard_map/ppermute | solution.py:613
  5.2 3.1 %normalize_own.1 = (bf16[256,4096]{1,0:T(8,128)(2,1)S(1)}, f32[256,256]{1,0:T(8,128)S(1)}, bf16[8192,128]{1,0:T(8,128)(2,1)S(1)}, bf16[8192,128]{1,0:T(8,128)(2,1)S(1)}) custom-call(bf16[512,4096]{1,0:T(8,128)(2,1)S(1)} %get-tuple-element.40.tokens_ref, f32[32,128]{1,0:T(8,128)S(1)} %get-tuple-element.45.gain_ref, ...), custom_call_target="tpu_custom_call" | custom-call | flops 536870912 | bytes 4194304 | tf_op jit(solution)/shard_map/normalize_own/pallas_call | solution.py:226
  8.3 0.4 %collective-permute-start.2 = (bf16[256,4096]{1,0:T(8,128)(2,1)S(1)}, bf16[256,4096]{1,0:T(8,128)(2,1)S(1)}, u32[]{:S(2)}, u32[]{:S(2)}) collective-permute-start(bf16[256,4096]{1,0:T(8,128)(2,1)S(1)} %get-tuple-element.56.mine_ref), channel_id=1, source_target_pairs={{0,1},{1,0},{2,3},{3,2},{4,5},{5,4},{6,7},{7,6},{8,9},{9,8},{10,11... | collective-permute-start | bytes 6291464 | tf_op jit(solution)/shard_map/ppermute | solution.py:613
  8.8 0.2 collective-permute-done.1.normed_ref.mine_ref
  9.0 0.8 %keys.1.mine_ref = bf16[256,256]{1,0:T(8,128)(2,1)S(1)} custom-call(bf16[256,4096]{1,0:T(8,128)(2,1)S(1)} %collective-permute-done.1.normed_ref.mine_ref, f32[256,256]{1,0:T(8,128)S(1)} %get-tuple-element.51.acc_ref, bf16[8192,128]{1,0:T(8,128)(2,1)S(1)} %get-tuple-element.52.wk_ref, bf16[8192,128]{1,0:T(8,128)(2,1)S(1)} %get-tuple-element.53.wv_ref, ...), custom_call_target="tpu_custom_call" | custom-call | flops 536870912 | bytes 262144 | tf_op jit(solution)/shard_map/keys/pallas_call | solution.py:254
  9.8 0.4 %collective-permute-start.4 = (bf16[256,256]{1,0:T(8,128)(2,1)S(1)}, bf16[256,256]{1,0:T(8,128)(2,1)S(1)}, u32[]{:S(2)}, u32[]{:S(2)}) collective-permute-start(bf16[256,256]{1,0:T(8,128)(2,1)S(1)} %keys.1.mine_ref), channel_id=1, source_target_pairs={{0,1},{1,0},{2,3},{3,2},{4,5},{5,4},{6,7},{7,6},{8,9},{9,8},{10,11... | collective-permute-start | bytes 393224 | tf_op jit(solution)/shard_map/ppermute | solution.py:613
  10.2 5.6 %collective-permute-start.3 = (bf16[256,256]{1,0:T(8,128)(2,1)S(1)}, bf16[256,256]{1,0:T(8,128)(2,1)S(1)}, u32[]{:S(2)}, u32[]{:S(2)}) collective-permute-start(bf16[256,256]{1,0:T(8,128)(2,1)S(1)} %keys.1.mine_ref), channel_id=1, source_target_pairs={{0,6},{2,8},{4,10},{6,12},{8,14},{1,7},{3,9},{5,11},{7,13},{9,15},... | collective-permute-start | bytes 393224 | tf_op jit(solution)/shard_map/ppermute | solution.py:623
  15.9 3.4 %collective-permute-start.5 = (bf16[512,256]{1,0:T(8,128)(2,1)S(1)}, bf16[512,256]{1,0:T(8,128)(2,1)S(1)}, u32[]{:S(2)}, u32[]{:S(2)}) collective-permute-start(bf16[512,256]{1,0:T(8,128)(2,1)S(1)} %join.1), channel_id=1, source_target_pairs={{0,2},{2,4},{4,6},{6,8},{8,10},{10,12},{12,14},{1,5},{3,7},{5,9},{... | collective-permute-start | bytes 786440 | tf_op jit(solution)/shard_map/ppermute | solution.py:623
  19.3 2.3 %queries_own.1.acc_ref = f32[512,512]{1,0:T(8,128)S(1)} custom-call(bf16[256,4096]{1,0:T(8,128)(2,1)S(1)} %get-tuple-element.56.mine_ref, bf16[256,4096]{1,0:T(8,128)(2,1)S(1)} %get-tuple-element.46.other_ref, bf16[8192,512]{1,0:T(8,128)(2,1)S(1)} %bitcast.4), custom_call_target="tpu_custom_call" | custom-call | flops 2147483648 | bytes 1048576 | tf_op jit(solution)/shard_map/queries_own/pallas_call | solution.py:294
  21.7 4.7 %queries.1 = (bf16[512,512]{1,0:T(8,128)(2,1)S(1)}, bf16[512,2048]{1,0:T(8,128)(2,1)S(1)}, bf16[512,2048]{1,0:T(8,128)(2,1)S(1)}) custom-call(bf16[256,4096]{1,0:T(8,128)(2,1)S(1)} %collective-permute-done.1.normed_ref.mine_ref, bf16[256,4096]{1,0:T(8,128)(2,1)S(1)} %collective-permute-done.2.other_ref, f32[512,512]{1,0:T(8,128)S(1)} %queries_own.1.acc_ref, ...), custom_call_target="tpu_custom_call" | custom-call | flops 2147483648 | bytes 4194304 | tf_op jit(solution)/shard_map/queries/pallas_call | solution.py:330
  26.4 3.3 %attend_own.1 = (f32[2048,128]{1,0:T(8,128)S(1)}, f32[2048,128]{1,0:T(8,128)S(1)}, f32[2048,128]{1,0:T(8,128)S(1)}, bf16[512,4096]{1,0:T(8,128)(2,1)S(1)}) custom-call(s32[8]{0:T(128)} %lengths_hbm.5, bf16[512,512]{1,0:T(8,128)(2,1)S(1)} %get-tuple-element.57.q_ref, bf16[256,256]{1,0:T(8,128)(2,1)S(1)} %keys.1.mine_ref, ...), custom_call_target="tpu_custom_call" | custom-call | flops 536870912 | bytes 2097152 | tf_op jit(solution)/shard_map/attend_own/pallas_call | solution.py:510
  29.7 0.5 %collective-permute-start.6 = (bf16[256,256]{1,0:T(8,128)(2,1)S(1)}, bf16[256,256]{1,0:T(8,128)(2,1)S(1)}, u32[]{:S(2)}, u32[]{:S(2)}) collective-permute-start(bf16[256,256]{1,0:T(8,128)(2,1)S(1)} %collective-permute-done.3.third_ref), channel_id=1, source_target_pairs={{0,1},{1,0},{2,3},{3,2},{4,5},{5,4},{6,7},{7,6},{8,9},{9,8},{10,11... | collective-permute-start | bytes 393224 | tf_op jit(solution)/shard_map/ppermute | solution.py:613
  30.3 1.1 %collective-permute-done.6.third_other_ref = bf16[256,256]{1,0:T(8,128)(2,1)S(1)} collective-permute-done((bf16[256,256]{1,0:T(8,128)(2,1)S(1)}, bf16[256,256]{1,0:T(8,128)(2,1)S(1)}, u32[]{:S(2)}, u32[]{:S(2)}) %collective-permute-start.6) | collective-permute-done | bytes 131104 | tf_op jit(solution)/shard_map/ppermute | solution.py:613
  31.5 0.1 collective-permute-start.10
  31.6 1.7 %attend.1.context_ref = bf16[512,512]{1,0:T(8,128)(2,1)S(1)} custom-call(s32[8]{0:T(128)} %lengths_hbm.5, bf16[512,512]{1,0:T(8,128)(2,1)S(1)} %get-tuple-element.57.q_ref, bf16[256,256]{1,0:T(8,128)(2,1)S(1)} %collective-permute-done.3.third_ref, bf16[256,256]{1,0:T(8,128)(2,1)S(1)} %collective-permute-done.6.third_other_ref, ...), custom_call_target="tpu_custom_call" | custom-call | flops 1610612736 | bytes 2097152 | tf_op jit(solution)/shard_map/attend/pallas_call | solution.py:536
  33.2 0.4 %collective-permute-start.8 = (bf16[512,512]{1,0:T(8,128)(2,1)S(1)}, bf16[512,512]{1,0:T(8,128)(2,1)S(1)}, u32[]{:S(2)}, u32[]{:S(2)}) collective-permute-start(bf16[512,512]{1,0:T(8,128)(2,1)S(1)} %attend.1.context_ref), channel_id=1, source_target_pairs={{0,1},{1,0},{2,3},{3,2},{4,5},{5,4},{6,7},{7,6},{8,9},{9,8},{10,11... | collective-permute-start | bytes 1572872 | tf_op jit(solution)/shard_map/ppermute | solution.py:613
  33.7 2.3 %own_term.1.term_ref = bf16[512,4096]{1,0:T(8,128)(2,1)S(1)} custom-call(bf16[512,512]{1,0:T(8,128)(2,1)S(1)} %attend.1.context_ref, bf16[512,4096]{1,0:T(8,128)(2,1)S(1)} %get-tuple-element.72.w_ref), custom_call_target="tpu_custom_call" | custom-call | flops 2147483648 | bytes 4194304 | tf_op jit(solution)/shard_map/own_term/pallas_call | solution.py:568
  36.0 2.2 %collective-permute-done.8.context_ref = bf16[512,512]{1,0:T(8,128)(2,1)S(1)} collective-permute-done((bf16[512,512]{1,0:T(8,128)(2,1)S(1)}, bf16[512,512]{1,0:T(8,128)(2,1)S(1)}, u32[]{:S(2)}, u32[]{:S(2)}) %collective-permute-start.8) | collective-permute-done | bytes 524320 | tf_op jit(solution)/shard_map/ppermute | solution.py:613
  38.2 3.3 %output.1 = bf16[512,4096]{1,0:T(8,128)(2,1)} custom-call(bf16[512,4096]{1,0:T(8,128)(2,1)S(1)} %get-tuple-element.40.tokens_ref, bf16[512,4096]{1,0:T(8,128)(2,1)S(1)} %own_term.1.term_ref, bf16[512,512]{1,0:T(8,128)(2,1)S(1)} %collective-permute-done.8.context_ref, bf16[512,2048]{1,0:T(8,128)(2,1)S(1)} %collective-permute-done.9.w_ref, ...), custom_call_target="tpu_custom_call" | custom-call | flops 2147483648 | bytes 8388608 | tf_op jit(solution)/shard_map/output/pallas_call | solution.py:600
  (17 shorter events, 0.3 us)
Async XLA Ops:
  2.4 1.7 %collective-permute-start = (f32[512,128]{1,0:T(8,128)S(1)}, f32[512,128]{1,0:T(8,128)S(1)}, u32[]{:S(2)}, u32[]{:S(2)}) collective-permute-start(f32[512,128]{1,0:T(8,128)S(1)} %get-tuple-element.41.mine_ref), channel_id=1, source_target_pairs={{0,1},{1,0},{2,3},{3,2},{4,5},{5,4},{6,7},{7,6},{8,9},{9,8},{10,11... | collective-permute-start | bytes 786440 | tf_op jit(solution)/shard_map/ppermute | solution.py:613
  4.1 15.2 %slice-start = ((s8[8388608]{0:T(1024)(128)(4,1)}), s8[4194304]{0:T(1024)(128)(4,1)S(1)}, s32[]{:S(2)}) async-start(s8[8388608]{0:T(1024)(128)(4,1)} %bitcast.3), calls=%async_computation | async-start | bytes 8388608
  4.8 4.2 %collective-permute-start.1 = (bf16[256,4096]{1,0:T(8,128)(2,1)S(1)}, bf16[256,4096]{1,0:T(8,128)(2,1)S(1)}, u32[]{:S(2)}, u32[]{:S(2)}) collective-permute-start(bf16[256,4096]{1,0:T(8,128)(2,1)S(1)} %get-tuple-element.46.other_ref), channel_id=1, source_target_pairs={{0,1},{1,0},{2,3},{3,2},{4,5},{5,4},{6,7},{7,6},{8,9},{9,8},{10,11... | collective-permute-start | bytes 6291464 | tf_op jit(solution)/shard_map/ppermute | solution.py:613
  5.2 14.1 %slice-start.1 = ((s8[8388608]{0:T(1024)(128)(4,1)}), s8[4194304]{0:T(1024)(128)(4,1)S(1)}, s32[]{:S(2)}) async-start(s8[8388608]{0:T(1024)(128)(4,1)} %bitcast.3), calls=%async_computation.1 | async-start | bytes 8388608
  8.3 13.3 %collective-permute-start.2 = (bf16[256,4096]{1,0:T(8,128)(2,1)S(1)}, bf16[256,4096]{1,0:T(8,128)(2,1)S(1)}, u32[]{:S(2)}, u32[]{:S(2)}) collective-permute-start(bf16[256,4096]{1,0:T(8,128)(2,1)S(1)} %get-tuple-element.56.mine_ref), channel_id=1, source_target_pairs={{0,1},{1,0},{2,3},{3,2},{4,5},{5,4},{6,7},{7,6},{8,9},{9,8},{10,11... | collective-permute-start | bytes 6291464 | tf_op jit(solution)/shard_map/ppermute | solution.py:613
  9.8 6.0 %collective-permute-start.4 = (bf16[256,256]{1,0:T(8,128)(2,1)S(1)}, bf16[256,256]{1,0:T(8,128)(2,1)S(1)}, u32[]{:S(2)}, u32[]{:S(2)}) collective-permute-start(bf16[256,256]{1,0:T(8,128)(2,1)S(1)} %keys.1.mine_ref), channel_id=1, source_target_pairs={{0,1},{1,0},{2,3},{3,2},{4,5},{5,4},{6,7},{7,6},{8,9},{9,8},{10,11... | collective-permute-start | bytes 393224 | tf_op jit(solution)/shard_map/ppermute | solution.py:613
  10.2 19.4 %collective-permute-start.3 = (bf16[256,256]{1,0:T(8,128)(2,1)S(1)}, bf16[256,256]{1,0:T(8,128)(2,1)S(1)}, u32[]{:S(2)}, u32[]{:S(2)}) collective-permute-start(bf16[256,256]{1,0:T(8,128)(2,1)S(1)} %keys.1.mine_ref), channel_id=1, source_target_pairs={{0,6},{2,8},{4,10},{6,12},{8,14},{1,7},{3,9},{5,11},{7,13},{9,15},... | collective-permute-start | bytes 393224 | tf_op jit(solution)/shard_map/ppermute | solution.py:623
  15.9 13.8 %collective-permute-start.5 = (bf16[512,256]{1,0:T(8,128)(2,1)S(1)}, bf16[512,256]{1,0:T(8,128)(2,1)S(1)}, u32[]{:S(2)}, u32[]{:S(2)}) collective-permute-start(bf16[512,256]{1,0:T(8,128)(2,1)S(1)} %join.1), channel_id=1, source_target_pairs={{0,2},{2,4},{4,6},{6,8},{8,10},{10,12},{12,14},{1,5},{3,7},{5,9},{... | collective-permute-start | bytes 786440 | tf_op jit(solution)/shard_map/ppermute | solution.py:623
  29.7 1.8 %collective-permute-start.7 = (bf16[512,256]{1,0:T(8,128)(2,1)S(1)}, bf16[512,256]{1,0:T(8,128)(2,1)S(1)}, u32[]{:S(2)}, u32[]{:S(2)}) collective-permute-start(bf16[512,256]{1,0:T(8,128)(2,1)S(1)} %collective-permute-done.5.block_ref), channel_id=1, source_target_pairs={{0,1},{1,0},{2,3},{3,2},{4,5},{5,4},{6,7},{7,6},{8,9},{9,8},{10,11... | collective-permute-start | bytes 786440 | tf_op jit(solution)/shard_map/ppermute | solution.py:613
  29.7 1.7 %collective-permute-start.6 = (bf16[256,256]{1,0:T(8,128)(2,1)S(1)}, bf16[256,256]{1,0:T(8,128)(2,1)S(1)}, u32[]{:S(2)}, u32[]{:S(2)}) collective-permute-start(bf16[256,256]{1,0:T(8,128)(2,1)S(1)} %collective-permute-done.3.third_ref), channel_id=1, source_target_pairs={{0,1},{1,0},{2,3},{3,2},{4,5},{5,4},{6,7},{7,6},{8,9},{9,8},{10,11... | collective-permute-start | bytes 393224 | tf_op jit(solution)/shard_map/ppermute | solution.py:613
  30.2 8.0 %collective-permute-start.9 = (bf16[512,2048]{1,0:T(8,128)(2,1)S(1)}, bf16[512,2048]{1,0:T(8,128)(2,1)S(1)}, u32[]{:S(2)}, u32[]{:S(2)}) collective-permute-start(bf16[512,2048]{1,0:T(8,128)(2,1)S(1)} %get-tuple-element.73), channel_id=1, source_target_pairs={{0,1},{1,0},{2,3},{3,2},{4,5},{5,4},{6,7},{7,6},{8,9},{9,8},{10,11... | collective-permute-start | bytes 6291464 | tf_op jit(solution)/shard_map/ppermute | solution.py:613
  31.5 6.8 %collective-permute-start.10 = (bf16[512,2048]{1,0:T(8,128)(2,1)S(1)}, bf16[512,2048]{1,0:T(8,128)(2,1)S(1)}, u32[]{:S(2)}, u32[]{:S(2)}) collective-permute-start(bf16[512,2048]{1,0:T(8,128)(2,1)S(1)} %get-tuple-element.74), channel_id=1, source_target_pairs={{0,1},{1,0},{2,3},{3,2},{4,5},{5,4},{6,7},{7,6},{8,9},{9,8},{10,11... | collective-permute-start | bytes 6291464 | tf_op jit(solution)/shard_map/ppermute | solution.py:613
  33.2 4.9 %collective-permute-start.8 = (bf16[512,512]{1,0:T(8,128)(2,1)S(1)}, bf16[512,512]{1,0:T(8,128)(2,1)S(1)}, u32[]{:S(2)}, u32[]{:S(2)}) collective-permute-start(bf16[512,512]{1,0:T(8,128)(2,1)S(1)} %attend.1.context_ref), channel_id=1, source_target_pairs={{0,1},{1,0},{2,3},{3,2},{4,5},{5,4},{6,7},{7,6},{8,9},{9,8},{10,11... | collective-permute-start | bytes 1572872 | tf_op jit(solution)/shard_map/ppermute | solution.py:613

commit v9 on v8

--- a/solution.py
+++ b/solution.py
@@ -281,28 +281,7 @@
     )(mine, other)
 
 
-def queries_own_kernel(mine_ref, other_ref, wq_ref, acc_ref):
-    half, width = mine_ref.shape
-    weights = wq_ref[features(width, False), :]
-    acc_ref[:half, :] = jnp.dot(mine_ref[...], weights, preferred_element_type=jnp.float32)
-    acc_ref[half:, :] = jnp.dot(other_ref[...], weights, preferred_element_type=jnp.float32)
-
-
-def queries_own(mine, other, wq):
-    half, width = mine.shape
-    nq = wq.shape[1]
-    return pl.pallas_call(
-        queries_own_kernel,
-        in_specs=[WHOLE] * 3,
-        out_specs=WHOLE,
-        out_shape=shaped((2 * half, nq), jnp.float32),
-        compiler_params=params(12),
-        cost_estimate=cost(4 * half * width * nq, half * nq * 8),
-        name="queries_own",
-    )(mine, other, wq)
-
-
-def queries_kernel(mine_ref, other_ref, acc_ref, wq_ref, cos_ref, sin_ref, wout_hbm, q_ref, wsend_ref, wlater_ref, acc, sems):
+def queries_own_kernel(mine_ref, other_ref, wq_ref, wout_hbm, acc_ref, wsend_ref, wlater_ref, sems):
     half, width = mine_ref.shape
     send = features(width, True).start
     loads = [
@@ -311,36 +290,63 @@
     ]
     for load in loads:
         load.start()
+    weights = wq_ref[features(width, False), :]
+    acc_ref[:half, :] = jnp.dot(mine_ref[...], weights, preferred_element_type=jnp.float32)
+    acc_ref[half:, :] = jnp.dot(other_ref[...], weights, preferred_element_type=jnp.float32)
+    for load in loads:
+        load.wait()
+
+
+def queries_own(mine, other, wq, w_out):
+    half, width = mine.shape
+    nq = wq.shape[1]
+    depth = w_out.shape[0]
+    return pl.pallas_call(
+        queries_own_kernel,
+        in_specs=[WHOLE] * 3 + [HBM],
+        out_specs=[WHOLE] * 3,
+        out_shape=[
+            shaped((2 * half, nq), jnp.float32),
+            shaped((depth, width // 2), w_out.dtype),
+            shaped((depth, width // 2), w_out.dtype),
+        ],
+        scratch_shapes=[pltpu.SemaphoreType.DMA((2,))],
+        compiler_params=params(12),
+        cost_estimate=cost(4 * half * width * nq, w_out.size),
+        name="queries_own",
+    )(mine, other, wq, *in_hbm(w_out))
+
+
+def queries_kernel(mine_ref, other_ref, acc_ref, wq_ref, cos_ref, sin_ref, q_ref, acc):
+    half, width = mine_ref.shape
     weights = wq_ref[features(width, True), :]
     acc[:half, :] = jnp.dot(mine_ref[...], weights, preferred_element_type=jnp.float32)
     acc[half:, :] = jnp.dot(other_ref[...], weights, preferred_element_type=jnp.float32)
-    for part, other in ((slice(0, half), False), (slice(half, 2 * half), True)):
-        at = half_rows(2 * half, other)
-        for h in range(q_ref.shape[1] // HEAD):
-            lanes = slice(h * HEAD, (h + 1) * HEAD)
-            q_ref[at, lanes] = turn(acc_ref[part, lanes] + acc[part, lanes], cos_ref[at, :], sin_ref[at, :])
-    for load in loads:
-        load.wait()
-
-
-def finish_queries(mine, other, acc, wq, tables, w_out):
+
+    def finish(me):
+        for part, which in ((slice(0, half), me), (slice(half, 2 * half), 1 - me)):
+            at = slice(which * half, (which + 1) * half)
+            for h in range(q_ref.shape[1] // HEAD):
+                lanes = slice(h * HEAD, (h + 1) * HEAD)
+                q_ref[at, lanes] = turn(acc_ref[part, lanes] + acc[part, lanes], cos_ref[at, :], sin_ref[at, :])
+
+    for core in range(2):
+        pl.when(lax.axis_index("tp") == core)(functools.partial(finish, core))
+
+
+def finish_queries(mine, other, acc, wq, tables):
     half, width = mine.shape
     nq = wq.shape[1]
-    depth = w_out.shape[0]
     return pl.pallas_call(
         queries_kernel,
-        in_specs=[WHOLE] * 6 + [HBM],
-        out_specs=[WHOLE] * 3,
-        out_shape=[
-            shaped((2 * half, nq), jnp.bfloat16),
-            shaped((depth, width // 2), w_out.dtype),
-            shaped((depth, width // 2), w_out.dtype),
-        ],
-        scratch_shapes=[pltpu.VMEM((2 * half, nq), jnp.float32), pltpu.SemaphoreType.DMA((2,))],
+        in_specs=[WHOLE] * 6,
+        out_specs=WHOLE,
+        out_shape=shaped((2 * half, nq), jnp.bfloat16),
+        scratch_shapes=[pltpu.VMEM((2 * half, nq), jnp.float32)],
         compiler_params=params(12),
-        cost_estimate=cost(4 * half * width * nq, w_out.size),
+        cost_estimate=cost(4 * half * width * nq, half * nq * 16),
         name="queries",
-    )(mine, other, acc, wq, *tables, *in_hbm(w_out))
+    )(mine, other, acc, wq, *tables)
 
 
 TILE = 128
@@ -350,7 +356,7 @@
 def place_blocks(blocks, starts, keys, values):
     for block, start in zip(blocks, starts, strict=True):
         at = pl.ds(pl.multiple_of(start, block.shape[0]), block.shape[0])
-        keys[at, :] = block[:, :HEAD]
+        keys[:, at] = block[:, :HEAD].T
         values[at, :] = block[:, HEAD:]
 
 
@@ -373,7 +379,7 @@
 
 def attend_own_kernel(
     lengths_hbm, q_ref, mine_ref, other_ref, wout_hbm, acc_ref, tops_ref, sums_ref, wkeep_ref,
-    keys, values, bias, scores, probs, lengths_ref, sems,
+    keys, values, stacked, bias, scores, probs, lengths_ref, sems,
 ):
     load = pltpu.make_async_copy(lengths_hbm, lengths_ref, sems.at[0])
     load.start()
@@ -390,33 +396,30 @@
     for j in range(0, rows, LANES):
         allowed = (lane + j >= begin) & (lane + j <= row)
         bias[:, j : j + LANES] = jnp.where(allowed, 0.0, -1e30)
-    for h in range(q_ref.shape[1] // HEAD):
-        for first, count in ((0, half), (half, rows)):
-            scores[:, :count] = lax.dot_general(
-                q_ref[first : first + half, h * HEAD : (h + 1) * HEAD],
-                keys[:count, :],
-                (((1,), (1,)), ((), ())),
-                preferred_element_type=jnp.float32,
-            )
-            out = h * rows + first
-
-            def block(r, carry):
-                at = block_rows(0, r)
-                out_at = block_rows(out, r)
-                top = jnp.full((ROWS, LANES), -1e30, jnp.float32)
-                for j in range(0, count, LANES):
-                    s = scores[at, j : j + LANES] + bias[block_rows(first, r), j : j + LANES]
-                    scores[at, j : j + LANES] = s
-                    top = jnp.maximum(top, s)
-                top = lanes_max(top)
-                tops_ref[out_at, :] = top
-                sums_ref[out_at, :] = weigh(scores, probs, at, 0, count, top)
-                return carry
-
-            lax.fori_loop(0, half // ROWS, block, 0, unroll=True)
-            acc_ref[out : out + half, :] = jnp.dot(
-                probs[:, :count], values[:count, :], preferred_element_type=jnp.float32
-            )
+    heads = q_ref.shape[1] // HEAD
+    for first, count in ((0, half), (half, rows)):
+        for h in range(heads):
+            stacked[h * half : (h + 1) * half, :] = q_ref[first : first + half, h * HEAD : (h + 1) * HEAD]
+        scores[:, :count] = jnp.dot(stacked[...], keys[:, :count], preferred_element_type=jnp.float32)
+
+        def block(r, carry):
+            h, within = r // (half // ROWS), lax.rem(r, half // ROWS)
+            at = block_rows(0, r)
+            out_at = block_rows(h * rows + first, within)
+            top = jnp.full((ROWS, LANES), -1e30, jnp.float32)
+            for j in range(0, count, LANES):
+                s = scores[at, j : j + LANES] + bias[block_rows(first, within), j : j + LANES]
+                scores[at, j : j + LANES] = s
+                top = jnp.maximum(top, s)
+            top = lanes_max(top)
+            tops_ref[out_at, :] = top
+            sums_ref[out_at, :] = weigh(scores, probs, at, 0, count, top)
+            return carry
+
+        lax.fori_loop(0, heads * half // ROWS, block, 0, unroll=4)
+        term = jnp.dot(probs[:, :count], values[:count, :], preferred_element_type=jnp.float32)
+        for h in range(heads):
+            acc_ref[h * rows + first : h * rows + first + half, :] = term[h * half : (h + 1) * half, :]
     keep.wait()
 
 
@@ -429,7 +432,7 @@
     rows = q_ref.shape[0]
     half = rows // 2
     heads = q_ref.shape[1] // HEAD
-    behind = keys.shape[0]
+    behind = keys.shape[1]
     me = lax.axis_index("tp")
     place_blocks(
         [third_ref, third_other_ref, block_ref, block_other_ref],
@@ -466,9 +469,7 @@
                 stacked[h * TILE : (h + 1) * TILE, :] = q_ref[
                     pl.ds(pl.multiple_of(t * TILE, TILE), TILE), h * HEAD : (h + 1) * HEAD
                 ]
-            scores[:, first:] = lax.dot_general(
-                stacked[...], keys[first:, :], (((1,), (1,)), ((), ())), preferred_element_type=jnp.float32
-            )
+            scores[:, first:] = jnp.dot(stacked[...], keys[:, first:], preferred_element_type=jnp.float32)
             for h in range(heads):
                 for r in range(TILE // ROWS):
                     at = slice(h * TILE + r * ROWS, h * TILE + (r + 1) * ROWS)
@@ -512,11 +513,12 @@
         in_specs=[HBM] + [WHOLE] * 3 + [HBM],
         out_specs=[WHOLE] * 4,
         scratch_shapes=[
+            pltpu.VMEM((HEAD, rows), jnp.bfloat16),
             pltpu.VMEM((rows, HEAD), jnp.bfloat16),
-            pltpu.VMEM((rows, HEAD), jnp.bfloat16),
+            pltpu.VMEM((heads * half, HEAD), jnp.bfloat16),
             pltpu.VMEM((rows, rows), jnp.float32),
-            pltpu.VMEM((half, rows), jnp.float32),
-            pltpu.VMEM((half, rows), jnp.bfloat16),
+            pltpu.VMEM((heads * half, rows), jnp.float32),
+            pltpu.VMEM((heads * half, rows), jnp.bfloat16),
             pltpu.SMEM(lengths.shape, lengths.dtype),
             pltpu.SemaphoreType.DMA((2,)),
         ],
@@ -538,7 +540,7 @@
         in_specs=[HBM] + [WHOLE] * (1 + len(blocks) + len(state)),
         out_specs=WHOLE,
         scratch_shapes=[
-            pltpu.VMEM((places, HEAD), jnp.bfloat16),
+            pltpu.VMEM((HEAD, places), jnp.bfloat16),
             pltpu.VMEM((places, HEAD), jnp.bfloat16),
             pltpu.VMEM((tall, HEAD), jnp.bfloat16),
             pltpu.VMEM((tall, places), jnp.float32),
@@ -643,8 +645,8 @@
     third = onward(kv, (3, 3))
     kv_other = swap(kv)
     block = onward(join(kv, kv_other), (1, 2))
-    partial = queries_own(normed_mine, normed_other, w_query)
-    queries, w_send, w_later = finish_queries(come_mine, come_other, partial, w_query, tables, w_out)
+    partial, w_send, w_later = queries_own(normed_mine, normed_other, w_query, w_out)
+    queries = finish_queries(come_mine, come_other, partial, w_query, tables)
     w_other = swap(w_send)
     *state, w_mine = attend_own(lengths, queries, [kv, kv_other], w_out)
     third, block, state = lax.optimization_barrier((third, block, state))

time: 41.9 us -> 42.7 us (1.019)
  Pallas kernels: 25.5 us -> 26 us
    pallas_call x1, Pallas kernels: 3.28 us -> 4.19 us  [attend_own(): pl.pallas_call(attend_own_kernel, in_specs=[HBM] + [WHOLE] * 3 + [HBM], o...]
where the time goes in v9:
time: 42.7 us; the launch traced here: 42.4 us
  Pallas kernels  26 us (61%)
  starting transfers between devices  12.1 us (28%)
  waiting for transfers between devices  3.85 us (9%)
    ppermute x2, starting transfers between devices, onward(): return lax.ppermute(value, ('dp', 'tp'), pairs)  9.02 us
    pallas_call x1, Pallas kernels, attend_own(): pl.pallas_call(attend_own_kernel, in_specs=[HBM] + [WHOLE] * 3 + [HBM], o...  4.19 us
    pallas_call x1, Pallas kernels, queries_own(): pl.pallas_call(queries_own_kernel, in_specs=[WHOLE] * 3 + [HBM], out_spec...  3.85 us
    ppermute x9, waiting for transfers between devices, swap(): return lax.ppermute(value, 'tp', SWAP)  3.85 us
    pallas_call x1, Pallas kernels, output(): pl.pallas_call(output_kernel, in_specs=[WHOLE] * 5, out_specs=HBM, out_sh...  3.31 us
    pallas_call x1, Pallas kernels, normalize_own(): pl.pallas_call(normalize_own_kernel, in_specs=[WHOLE] * 3 + [HBM] * 2, ou...  3.11 us
    ppermute x9, starting transfers between devices, swap(): return lax.ppermute(value, 'tp', SWAP)  3.06 us
    pallas_call x1, Pallas kernels, finish_queries(): pl.pallas_call(queries_kernel, in_specs=[WHOLE] * 6, out_specs=WHOLE, out...  2.89 us
  transfers between devices with their start and end apart: 11, of which 4 were waited for; matrix products, arithmetic and copies ran while one was open for 0% of the time, Pallas kernels for 46%

profile of v9, /device:TPU:0, one launch (start us, length us, event | category | flops | bytes accessed | tf_op | source)
XLA Modules:
  0.0 42.4 jit_solution(4636358224830950378)
XLA Ops:
  0.1 2.3 %squares.1 = (f32[512,128]{1,0:T(8,128)S(1)}, f32[32,128]{1,0:T(8,128)S(1)}, bf16[512,4096]{1,0:T(8,128)(2,1)S(1)}) custom-call(f32[1,128]{1,0:T(1,128)S(1)} %maximum_bitcast_fusion.frequency_ref, bf16[32,128]{1,0:T(8,128)(2,1)} %bitcast.5, bf16[512,4096]{1,0:T(8,128)(2,1)} %tokens_hbm.1), custom_call_target="tpu_custom_call" | custom-call | flops 4194304 | bytes 4194304 | tf_op jit(solution)/shard_map/squares/pallas_call | solution.py:91
  2.4 0.5 %collective-permute-start = (f32[512,128]{1,0:T(8,128)S(1)}, f32[512,128]{1,0:T(8,128)S(1)}, u32[]{:S(2)}, u32[]{:S(2)}) collective-permute-start(f32[512,128]{1,0:T(8,128)S(1)} %get-tuple-element.41.mine_ref), channel_id=1, source_target_pairs={{0,1},{1,0},{2,3},{3,2},{4,5},{5,4},{6,7},{7,6},{8,9},{9,8},{10,11... | collective-permute-start | bytes 786440 | tf_op jit(solution)/shard_map/ppermute | solution.py:615
  3.0 1.0 %tables.1 = (f32[512,128]{1,0:T(8,128)S(1)}, f32[512,128]{1,0:T(8,128)S(1)}) custom-call(f32[1,128]{1,0:T(1,128)S(1)} %maximum_bitcast_fusion.frequency_ref, s32[8]{0:T(128)} %lengths_hbm.5), custom_call_target="tpu_custom_call" | custom-call | flops 6553600 | bytes 524288 | tf_op jit(solution)/shard_map/tables/pallas_call | solution.py:140
  4.0 0.1 collective-permute-done.other_ref
  4.1 0.7 %normalize_other.1 = (bf16[256,4096]{1,0:T(8,128)(2,1)S(1)}, f32[512,128]{1,0:T(8,128)S(1)}) custom-call(bf16[512,4096]{1,0:T(8,128)(2,1)S(1)} %get-tuple-element.40.tokens_ref, f32[512,128]{1,0:T(8,128)S(1)} %get-tuple-element.41.mine_ref, f32[512,128]{1,0:T(8,128)S(1)} %collective-permute-done.other_ref, f32[32,128]{1,0:T(8,128)S(1)} %get-tuple-element.45.gain_ref), custom_call_target="tpu_custom_call" | custom-call | flops 4194304 | bytes 4194304 | tf_op jit(solution)/shard_map/normalize_other/pallas_call | solution.py:197
  4.8 0.4 %collective-permute-start.1 = (bf16[256,4096]{1,0:T(8,128)(2,1)S(1)}, bf16[256,4096]{1,0:T(8,128)(2,1)S(1)}, u32[]{:S(2)}, u32[]{:S(2)}) collective-permute-start(bf16[256,4096]{1,0:T(8,128)(2,1)S(1)} %get-tuple-element.46.other_ref), channel_id=1, source_target_pairs={{0,1},{1,0},{2,3},{3,2},{4,5},{5,4},{6,7},{7,6},{8,9},{9,8},{10,11... | collective-permute-start | bytes 6291464 | tf_op jit(solution)/shard_map/ppermute | solution.py:615
  5.2 3.1 %normalize_own.1 = (bf16[256,4096]{1,0:T(8,128)(2,1)S(1)}, f32[256,256]{1,0:T(8,128)S(1)}, bf16[8192,128]{1,0:T(8,128)(2,1)S(1)}, bf16[8192,128]{1,0:T(8,128)(2,1)S(1)}) custom-call(bf16[512,4096]{1,0:T(8,128)(2,1)S(1)} %get-tuple-element.40.tokens_ref, f32[32,128]{1,0:T(8,128)S(1)} %get-tuple-element.45.gain_ref, ...), custom_call_target="tpu_custom_call" | custom-call | flops 536870912 | bytes 4194304 | tf_op jit(solution)/shard_map/normalize_own/pallas_call | solution.py:226
  8.3 0.4 %collective-permute-start.2 = (bf16[256,4096]{1,0:T(8,128)(2,1)S(1)}, bf16[256,4096]{1,0:T(8,128)(2,1)S(1)}, u32[]{:S(2)}, u32[]{:S(2)}) collective-permute-start(bf16[256,4096]{1,0:T(8,128)(2,1)S(1)} %get-tuple-element.56.mine_ref), channel_id=1, source_target_pairs={{0,1},{1,0},{2,3},{3,2},{4,5},{5,4},{6,7},{7,6},{8,9},{9,8},{10,11... | collective-permute-start | bytes 6291464 | tf_op jit(solution)/shard_map/ppermute | solution.py:615
  8.8 0.2 collective-permute-done.1.normed_ref.mine_ref
  9.0 0.8 %keys.1.mine_ref = bf16[256,256]{1,0:T(8,128)(2,1)S(1)} custom-call(bf16[256,4096]{1,0:T(8,128)(2,1)S(1)} %collective-permute-done.1.normed_ref.mine_ref, f32[256,256]{1,0:T(8,128)S(1)} %get-tuple-element.51.acc_ref, bf16[8192,128]{1,0:T(8,128)(2,1)S(1)} %get-tuple-element.52.wk_ref, bf16[8192,128]{1,0:T(8,128)(2,1)S(1)} %get-tuple-element.53.wv_ref, ...), custom_call_target="tpu_custom_call" | custom-call | flops 536870912 | bytes 262144 | tf_op jit(solution)/shard_map/keys/pallas_call | solution.py:254
  9.8 0.4 %collective-permute-start.4 = (bf16[256,256]{1,0:T(8,128)(2,1)S(1)}, bf16[256,256]{1,0:T(8,128)(2,1)S(1)}, u32[]{:S(2)}, u32[]{:S(2)}) collective-permute-start(bf16[256,256]{1,0:T(8,128)(2,1)S(1)} %keys.1.mine_ref), channel_id=1, source_target_pairs={{0,1},{1,0},{2,3},{3,2},{4,5},{5,4},{6,7},{7,6},{8,9},{9,8},{10,11... | collective-permute-start | bytes 393224 | tf_op jit(solution)/shard_map/ppermute | solution.py:615
  10.2 5.6 %collective-permute-start.3 = (bf16[256,256]{1,0:T(8,128)(2,1)S(1)}, bf16[256,256]{1,0:T(8,128)(2,1)S(1)}, u32[]{:S(2)}, u32[]{:S(2)}) collective-permute-start(bf16[256,256]{1,0:T(8,128)(2,1)S(1)} %keys.1.mine_ref), channel_id=1, source_target_pairs={{0,6},{2,8},{4,10},{6,12},{8,14},{1,7},{3,9},{5,11},{7,13},{9,15},... | collective-permute-start | bytes 393224 | tf_op jit(solution)/shard_map/ppermute | solution.py:625
  15.9 3.4 %collective-permute-start.5 = (bf16[512,256]{1,0:T(8,128)(2,1)S(1)}, bf16[512,256]{1,0:T(8,128)(2,1)S(1)}, u32[]{:S(2)}, u32[]{:S(2)}) collective-permute-start(bf16[512,256]{1,0:T(8,128)(2,1)S(1)} %join.1), channel_id=1, source_target_pairs={{0,2},{2,4},{4,6},{6,8},{8,10},{10,12},{12,14},{1,5},{3,7},{5,9},{... | collective-permute-start | bytes 786440 | tf_op jit(solution)/shard_map/ppermute | solution.py:625
  19.3 3.9 %queries_own.1 = (f32[512,512]{1,0:T(8,128)S(1)}, bf16[512,2048]{1,0:T(8,128)(2,1)S(1)}, bf16[512,2048]{1,0:T(8,128)(2,1)S(1)}) custom-call(bf16[256,4096]{1,0:T(8,128)(2,1)S(1)} %get-tuple-element.56.mine_ref, bf16[256,4096]{1,0:T(8,128)(2,1)S(1)} %get-tuple-element.46.other_ref, bf16[8192,512]{1,0:T(8,128)(2,1)S(1)} %bitcast.4, bf16[512,8192]{1,0:T(8,128)(2,1)} %wout_hbm.3), custom_call_target="tpu_custom_call" | custom-call | flops 2147483648 | bytes 4194304 | tf_op jit(solution)/shard_map/queries_own/pallas_call | solution.py:304
  23.2 2.9 %queries.1.q_ref = bf16[512,512]{1,0:T(8,128)(2,1)S(1)} custom-call(bf16[256,4096]{1,0:T(8,128)(2,1)S(1)} %collective-permute-done.1.normed_ref.mine_ref, bf16[256,4096]{1,0:T(8,128)(2,1)S(1)} %collective-permute-done.2.other_ref, f32[512,512]{1,0:T(8,128)S(1)} %get-tuple-element.57.acc_ref, bf16[8192,512]{1,0:T(8,128)(2,1)S(1)} %bitcast.4, ...), custom_call_target="tpu_custom_call" | custom-call | flops 2147483648 | bytes 2097152 | tf_op jit(solution)/shard_map/queries/pallas_call | solution.py:340
  26.1 4.2 %attend_own.1 = (f32[2048,128]{1,0:T(8,128)S(1)}, f32[2048,128]{1,0:T(8,128)S(1)}, f32[2048,128]{1,0:T(8,128)S(1)}, bf16[512,4096]{1,0:T(8,128)(2,1)S(1)}) custom-call(s32[8]{0:T(128)} %lengths_hbm.5, bf16[512,512]{1,0:T(8,128)(2,1)S(1)} %queries.1.q_ref, bf16[256,256]{1,0:T(8,128)(2,1)S(1)} %keys.1.mine_ref, ...), custom_call_target="tpu_custom_call" | custom-call | flops 536870912 | bytes 2097152 | tf_op jit(solution)/shard_map/attend_own/pallas_call | solution.py:511
  30.4 0.5 %collective-permute-start.6 = (bf16[256,256]{1,0:T(8,128)(2,1)S(1)}, bf16[256,256]{1,0:T(8,128)(2,1)S(1)}, u32[]{:S(2)}, u32[]{:S(2)}) collective-permute-start(bf16[256,256]{1,0:T(8,128)(2,1)S(1)} %collective-permute-done.3.third_ref), channel_id=1, source_target_pairs={{0,1},{1,0},{2,3},{3,2},{4,5},{5,4},{6,7},{7,6},{8,9},{9,8},{10,11... | collective-permute-start | bytes 393224 | tf_op jit(solution)/shard_map/ppermute | solution.py:615
  31.0 1.1 %collective-permute-done.6.third_other_ref = bf16[256,256]{1,0:T(8,128)(2,1)S(1)} collective-permute-done((bf16[256,256]{1,0:T(8,128)(2,1)S(1)}, bf16[256,256]{1,0:T(8,128)(2,1)S(1)}, u32[]{:S(2)}, u32[]{:S(2)}) %collective-permute-start.6) | collective-permute-done | bytes 131104 | tf_op jit(solution)/shard_map/ppermute | solution.py:615
  32.1 0.1 collective-permute-start.10
  32.3 1.5 %attend.1.context_ref = bf16[512,512]{1,0:T(8,128)(2,1)S(1)} custom-call(s32[8]{0:T(128)} %lengths_hbm.5, bf16[512,512]{1,0:T(8,128)(2,1)S(1)} %queries.1.q_ref, bf16[256,256]{1,0:T(8,128)(2,1)S(1)} %collective-permute-done.3.third_ref, bf16[256,256]{1,0:T(8,128)(2,1)S(1)} %collective-permute-done.6.third_other_ref, ...), custom_call_target="tpu_custom_call" | custom-call | flops 1610612736 | bytes 2097152 | tf_op jit(solution)/shard_map/attend/pallas_call | solution.py:538
  33.7 0.4 %collective-permute-start.8 = (bf16[512,512]{1,0:T(8,128)(2,1)S(1)}, bf16[512,512]{1,0:T(8,128)(2,1)S(1)}, u32[]{:S(2)}, u32[]{:S(2)}) collective-permute-start(bf16[512,512]{1,0:T(8,128)(2,1)S(1)} %attend.1.context_ref), channel_id=1, source_target_pairs={{0,1},{1,0},{2,3},{3,2},{4,5},{5,4},{6,7},{7,6},{8,9},{9,8},{10,11... | collective-permute-start | bytes 1572872 | tf_op jit(solution)/shard_map/ppermute | solution.py:615
  34.2 2.3 %own_term.1.term_ref = bf16[512,4096]{1,0:T(8,128)(2,1)S(1)} custom-call(bf16[512,512]{1,0:T(8,128)(2,1)S(1)} %attend.1.context_ref, bf16[512,4096]{1,0:T(8,128)(2,1)S(1)} %get-tuple-element.72.w_ref), custom_call_target="tpu_custom_call" | custom-call | flops 2147483648 | bytes 4194304 | tf_op jit(solution)/shard_map/own_term/pallas_call | solution.py:570
  36.5 2.3 %collective-permute-done.8.context_ref = bf16[512,512]{1,0:T(8,128)(2,1)S(1)} collective-permute-done((bf16[512,512]{1,0:T(8,128)(2,1)S(1)}, bf16[512,512]{1,0:T(8,128)(2,1)S(1)}, u32[]{:S(2)}, u32[]{:S(2)}) %collective-permute-start.8) | collective-permute-done | bytes 524320 | tf_op jit(solution)/shard_map/ppermute | solution.py:615
  38.9 3.3 %output.1 = bf16[512,4096]{1,0:T(8,128)(2,1)} custom-call(bf16[512,4096]{1,0:T(8,128)(2,1)S(1)} %get-tuple-element.40.tokens_ref, bf16[512,4096]{1,0:T(8,128)(2,1)S(1)} %own_term.1.term_ref, bf16[512,512]{1,0:T(8,128)(2,1)S(1)} %collective-permute-done.8.context_ref, bf16[512,2048]{1,0:T(8,128)(2,1)S(1)} %collective-permute-done.9.w_ref, ...), custom_call_target="tpu_custom_call" | custom-call | flops 2147483648 | bytes 8388608 | tf_op jit(solution)/shard_map/output/pallas_call | solution.py:602
  (17 shorter events, 0.3 us)
Async XLA Ops:
  2.4 1.7 %collective-permute-start = (f32[512,128]{1,0:T(8,128)S(1)}, f32[512,128]{1,0:T(8,128)S(1)}, u32[]{:S(2)}, u32[]{:S(2)}) collective-permute-start(f32[512,128]{1,0:T(8,128)S(1)} %get-tuple-element.41.mine_ref), channel_id=1, source_target_pairs={{0,1},{1,0},{2,3},{3,2},{4,5},{5,4},{6,7},{7,6},{8,9},{9,8},{10,11... | collective-permute-start | bytes 786440 | tf_op jit(solution)/shard_map/ppermute | solution.py:615
  4.1 15.2 %slice-start = ((s8[8388608]{0:T(1024)(128)(4,1)}), s8[4194304]{0:T(1024)(128)(4,1)S(1)}, s32[]{:S(2)}) async-start(s8[8388608]{0:T(1024)(128)(4,1)} %bitcast.3), calls=%async_computation | async-start | bytes 8388608
  4.8 4.2 %collective-permute-start.1 = (bf16[256,4096]{1,0:T(8,128)(2,1)S(1)}, bf16[256,4096]{1,0:T(8,128)(2,1)S(1)}, u32[]{:S(2)}, u32[]{:S(2)}) collective-permute-start(bf16[256,4096]{1,0:T(8,128)(2,1)S(1)} %get-tuple-element.46.other_ref), channel_id=1, source_target_pairs={{0,1},{1,0},{2,3},{3,2},{4,5},{5,4},{6,7},{7,6},{8,9},{9,8},{10,11... | collective-permute-start | bytes 6291464 | tf_op jit(solution)/shard_map/ppermute | solution.py:615
  5.2 14.1 %slice-start.1 = ((s8[8388608]{0:T(1024)(128)(4,1)}), s8[4194304]{0:T(1024)(128)(4,1)S(1)}, s32[]{:S(2)}) async-start(s8[8388608]{0:T(1024)(128)(4,1)} %bitcast.3), calls=%async_computation.1 | async-start | bytes 8388608
  8.3 14.9 %collective-permute-start.2 = (bf16[256,4096]{1,0:T(8,128)(2,1)S(1)}, bf16[256,4096]{1,0:T(8,128)(2,1)S(1)}, u32[]{:S(2)}, u32[]{:S(2)}) collective-permute-start(bf16[256,4096]{1,0:T(8,128)(2,1)S(1)} %get-tuple-element.56.mine_ref), channel_id=1, source_target_pairs={{0,1},{1,0},{2,3},{3,2},{4,5},{5,4},{6,7},{7,6},{8,9},{9,8},{10,11... | collective-permute-start | bytes 6291464 | tf_op jit(solution)/shard_map/ppermute | solution.py:615
  9.8 6.0 %collective-permute-start.4 = (bf16[256,256]{1,0:T(8,128)(2,1)S(1)}, bf16[256,256]{1,0:T(8,128)(2,1)S(1)}, u32[]{:S(2)}, u32[]{:S(2)}) collective-permute-start(bf16[256,256]{1,0:T(8,128)(2,1)S(1)} %keys.1.mine_ref), channel_id=1, source_target_pairs={{0,1},{1,0},{2,3},{3,2},{4,5},{5,4},{6,7},{7,6},{8,9},{9,8},{10,11... | collective-permute-start | bytes 393224 | tf_op jit(solution)/shard_map/ppermute | solution.py:615
  10.2 20.1 %collective-permute-start.3 = (bf16[256,256]{1,0:T(8,128)(2,1)S(1)}, bf16[256,256]{1,0:T(8,128)(2,1)S(1)}, u32[]{:S(2)}, u32[]{:S(2)}) collective-permute-start(bf16[256,256]{1,0:T(8,128)(2,1)S(1)} %keys.1.mine_ref), channel_id=1, source_target_pairs={{0,6},{2,8},{4,10},{6,12},{8,14},{1,7},{3,9},{5,11},{7,13},{9,15},... | collective-permute-start | bytes 393224 | tf_op jit(solution)/shard_map/ppermute | solution.py:625
  15.9 14.5 %collective-permute-start.5 = (bf16[512,256]{1,0:T(8,128)(2,1)S(1)}, bf16[512,256]{1,0:T(8,128)(2,1)S(1)}, u32[]{:S(2)}, u32[]{:S(2)}) collective-permute-start(bf16[512,256]{1,0:T(8,128)(2,1)S(1)} %join.1), channel_id=1, source_target_pairs={{0,2},{2,4},{4,6},{6,8},{8,10},{10,12},{12,14},{1,5},{3,7},{5,9},{... | collective-permute-start | bytes 786440 | tf_op jit(solution)/shard_map/ppermute | solution.py:625
  30.3 1.8 %collective-permute-start.7 = (bf16[512,256]{1,0:T(8,128)(2,1)S(1)}, bf16[512,256]{1,0:T(8,128)(2,1)S(1)}, u32[]{:S(2)}, u32[]{:S(2)}) collective-permute-start(bf16[512,256]{1,0:T(8,128)(2,1)S(1)} %collective-permute-done.5.block_ref), channel_id=1, source_target_pairs={{0,1},{1,0},{2,3},{3,2},{4,5},{5,4},{6,7},{7,6},{8,9},{9,8},{10,11... | collective-permute-start | bytes 786440 | tf_op jit(solution)/shard_map/ppermute | solution.py:615
  30.4 1.7 %collective-permute-start.6 = (bf16[256,256]{1,0:T(8,128)(2,1)S(1)}, bf16[256,256]{1,0:T(8,128)(2,1)S(1)}, u32[]{:S(2)}, u32[]{:S(2)}) collective-permute-start(bf16[256,256]{1,0:T(8,128)(2,1)S(1)} %collective-permute-done.3.third_ref), channel_id=1, source_target_pairs={{0,1},{1,0},{2,3},{3,2},{4,5},{5,4},{6,7},{7,6},{8,9},{9,8},{10,11... | collective-permute-start | bytes 393224 | tf_op jit(solution)/shard_map/ppermute | solution.py:615
  30.9 8.0 %collective-permute-start.9 = (bf16[512,2048]{1,0:T(8,128)(2,1)S(1)}, bf16[512,2048]{1,0:T(8,128)(2,1)S(1)}, u32[]{:S(2)}, u32[]{:S(2)}) collective-permute-start(bf16[512,2048]{1,0:T(8,128)(2,1)S(1)} %get-tuple-element.73), channel_id=1, source_target_pairs={{0,1},{1,0},{2,3},{3,2},{4,5},{5,4},{6,7},{7,6},{8,9},{9,8},{10,11... | collective-permute-start | bytes 6291464 | tf_op jit(solution)/shard_map/ppermute | solution.py:615
  32.1 6.8 %collective-permute-start.10 = (bf16[512,2048]{1,0:T(8,128)(2,1)S(1)}, bf16[512,2048]{1,0:T(8,128)(2,1)S(1)}, u32[]{:S(2)}, u32[]{:S(2)}) collective-permute-start(bf16[512,2048]{1,0:T(8,128)(2,1)S(1)} %get-tuple-element.74), channel_id=1, source_target_pairs={{0,1},{1,0},{2,3},{3,2},{4,5},{5,4},{6,7},{7,6},{8,9},{9,8},{10,11... | collective-permute-start | bytes 6291464 | tf_op jit(solution)/shard_map/ppermute | solution.py:615
  33.7 5.1 %collective-permute-start.8 = (bf16[512,512]{1,0:T(8,128)(2,1)S(1)}, bf16[512,512]{1,0:T(8,128)(2,1)S(1)}, u32[]{:S(2)}, u32[]{:S(2)}) collective-permute-start(bf16[512,512]{1,0:T(8,128)(2,1)S(1)} %attend.1.context_ref), channel_id=1, source_target_pairs={{0,1},{1,0},{2,3},{3,2},{4,5},{5,4},{6,7},{7,6},{8,9},{9,8},{10,11... | collective-permute-start | bytes 1572872 | tf_op jit(solution)/shard_map/ppermute | solution.py:615
